TPU v7x, 128 devices: a whole 4x4x4 slice. The times are simulated.
128 devices in a mesh: leaf: 8 (over y, core), front: 16 (over x, z).
Axes of the slice: x: 4, y: 4, z: 4, core: 2. Of those that a mesh axis runs over, the one named last changes fastest.
Arguments:
- inv_factors: bfloat16 [8, 2, 1024, 1024], P('leaf', None, 'front')
- panel_rows: bfloat16 [8, 1024, 1024], P('leaf', 'front'), may hold values from -6 to 6
- border: bfloat16 [8, 2048, 2048], P('leaf', 'front'), may hold values from -6 to 6
- tail: bfloat16 [8, 2048, 2048], P('leaf', 'front'), may hold values from -6 to 6
- front_sizes: int32 [8], replicated, may hold values from 1024 to 2048, as said below
- block_map: int32 [8, 16], replicated, may hold values from 0 to 31, as said below
- block_owner: int32 [8, 32], replicated, may hold values from 0 to 47, as said below
Outputs:
- link_factor: bfloat16 [8, 1024, 1024], P('leaf', 'front')
- border_factor: bfloat16 [8, 2048, 2048], P('leaf', 'front')
- parent_update: float32 [8, 4096, 6144], P('leaf', None, 'front')
Inputs may be any that keep to these rules, and one draw needn't show every extreme that they name: `front_sizes`: the live rows of some child always equal 2048; every child has at least 1024. `block_map`: the entries of one child's row are distinct. `block_owner`: the entries of one parent's row are distinct; slot s belongs to front index s // 3, so no front index owns more than 3 blocks of a parent, and in every parent's row one front index owns exactly 3.
All inputs are finite; a program needn't handle non-finite values.
Results may differ from a plain program's by a relative error of at most 0.0055.
Values may be sent and summed in bfloat16 or wider, within the bound.
No kernel may reach another device: no remote copies, remote signals or barrier semaphores. Data moves between devices by JAX's collectives and lax.ppermute only.
A program may use at most 64 MiB of HBM per device.

v0:
```python
import jax
import jax.numpy as jnp
from jax import lax
from jax.sharding import PartitionSpec as P

PANEL = 1024
BLOCK = 128
SLOTS = 3


def passed_along(value, axis, by):
    devices = lax.axis_size(axis)
    return lax.ppermute(value, axis, [(i, (i + by) % devices) for i in range(devices)])


def dot_rows(left_rows, right_rows):
    return lax.dot_general(
        left_rows, right_rows, (((1,), (1,)), ((), ())), preferred_element_type=jnp.float32
    )


def against(left_rows, piece):
    return dot_rows(left_rows, piece)


def pick_row(table, index):
    chooser = (jnp.arange(table.shape[0], dtype=jnp.int32)[:, None] == index).astype(jnp.int32)
    return jnp.sum(chooser * table, axis=0)


def route_tiles(contribution, owner_line, child_map, nfront, parent_blocks):
    block_pick = (child_map[:, None] == jnp.arange(parent_blocks, dtype=jnp.int32)[None, :]).astype(
        jnp.int32
    )
    slot_index = jnp.sum(block_pick * owner_line[None, :], axis=1)
    owner_front = slot_index // SLOTS
    owner_slot = slot_index % SLOTS
    select = (jnp.arange(nfront, dtype=jnp.int32)[:, None, None] == owner_front[None, None, :]) & (
        jnp.arange(SLOTS, dtype=jnp.int32)[None, :, None] == owner_slot[None, None, :]
    )
    tiles = contribution.reshape(BLOCK, nfront, BLOCK)
    return jnp.einsum(
        "ocb,rbd->orcd", select.astype(jnp.bfloat16), tiles, preferred_element_type=jnp.float32
    ).astype(jnp.bfloat16)


def place_rows(arrived, child_map, nfront, parent_blocks):
    row_hot = (jnp.arange(parent_blocks, dtype=jnp.int32)[:, None] == child_map[None, :]).astype(
        jnp.bfloat16
    )
    merged = jnp.dot(
        row_hot, arrived.reshape(nfront, BLOCK * SLOTS * BLOCK), preferred_element_type=jnp.float32
    )
    return merged.reshape(parent_blocks * BLOCK, SLOTS * BLOCK)


def per_device(inv_factors, panel_rows, border, tail, front_sizes, block_map, block_owner):
    nfront = lax.axis_size("front")
    nleaf = lax.axis_size("leaf")
    half_leaf = nleaf // 2
    leaf_group = lax.axis_index("leaf")
    front_place = lax.axis_index("front")
    first_inv = inv_factors[0, 0]
    second_inv = inv_factors[0, 1]
    upper_rows = panel_rows[0]
    left_cols = border[0, :, :PANEL]
    right_cols = border[0, :, PANEL:]
    stacked = jnp.concatenate([upper_rows, left_cols], axis=0)
    upper_count = upper_rows.shape[0]
    projected = against(stacked, lax.all_gather(first_inv, "front", axis=0, tiled=True))
    projected = projected.astype(jnp.bfloat16)
    link_local = projected[:upper_count]
    first_local = projected[upper_count:]
    coupled = against(first_local, lax.all_gather(link_local, "front", axis=0, tiled=True))
    updated = (right_cols.astype(jnp.float32) - coupled).astype(jnp.bfloat16)
    second_local = against(updated, lax.all_gather(second_inv, "front", axis=0, tiled=True))
    second_local = second_local.astype(jnp.bfloat16)
    factor_local = jnp.concatenate([first_local, second_local], axis=1)
    schur = tail[0].astype(jnp.float32) - against(
        factor_local, lax.all_gather(factor_local, "front", axis=0, tiled=True)
    )
    contrib_rows = BLOCK * nfront
    live = front_sizes[leaf_group]
    row_global = front_place * BLOCK + jnp.arange(BLOCK, dtype=jnp.int32)
    col_global = jnp.arange(contrib_rows, dtype=jnp.int32)
    keep = (row_global[:, None] < live) & (col_global[None, :] < live)
    contribution = jnp.where(keep, schur, jnp.float32(0.0)).astype(jnp.bfloat16)
    parent_blocks = 2 * nfront
    parent_group = (leaf_group + half_leaf) % nleaf
    child_group = (leaf_group + nleaf - half_leaf) % nleaf
    child_map_here = pick_row(block_map, child_group)
    own_map = pick_row(block_map, leaf_group)
    routed = route_tiles(
        contribution, pick_row(block_owner, parent_group), own_map, nfront, parent_blocks
    )
    sorted_tiles = lax.all_to_all(routed, "front", split_axis=0, concat_axis=0, tiled=True)
    arrived = passed_along(sorted_tiles, "leaf", half_leaf)
    merged = place_rows(arrived, child_map_here, nfront, parent_blocks)
    return (link_local[None], factor_local[None], merged[None])


def solution(mesh):
    return jax.shard_map(
        per_device,
        mesh=mesh,
        in_specs=(
            P("leaf", None, "front", None),
            P("leaf", "front", None),
            P("leaf", "front", None),
            P("leaf", "front", None),
            P(),
            P(),
            P(),
        ),
        out_specs=(P("leaf", "front", None), P("leaf", "front", None), P("leaf", None, "front")),
        check_vma=False,
    )
```

profile of v0, /device:TPU:0, one launch (start us, length us, event | category | flops | bytes accessed | tf_op | source)
XLA Modules:
  0.0 320.9 jit_solution(9470419997501196426)
XLA Ops:
  7.2 0.0 all-gather.11.cloned.1.call-start
  7.2 1.7 fusion.33
  8.9 0.0 all-gather.13.cloned.1.call-start
  9.0 0.7 all-gather.13.cloned.1.call-update
  9.7 0.0 all-gather.7.cloned.1.call-start
  9.7 1.0 slice_bitcast_fusion
  10.7 47.8 %all-gather.11.cloned.1.call-done = bf16[1,1,1024,1024]{3,2,1,0:T(8,128)(2,1)} async-done(((bf16[1,1,64,1024]{3,2,1,0:T(8,128)(2,1)}), bf16[1,1,1024,1024]{3,2,1,0:T(8,128)(2,1)}) %all-gather.11.cloned.1.call-update) | async-done | bytes 2097168 | tf_op jit(solution)/shard_map/all_gather | solution.py:70
  58.5 2.5 fusion.7
  61.0 0.7 fusion.32
  61.7 0.0 all-gather.9.cloned.1.call-start
  61.8 43.9 %all-gather.13.cloned.1.call-done = bf16[1,1,1024,1024]{3,2,1,0:T(8,128)(2,1)} async-done(((bf16[1,1,64,1024]{3,2,1,0:T(8,128)(2,1)}), bf16[1,1,1024,1024]{3,2,1,0:T(8,128)(2,1)}) %all-gather.13.cloned.1.call-update) | async-done | bytes 2097168 | tf_op jit(solution)/shard_map/all_gather | solution.py:76
  105.7 47.3 %all-gather.7.cloned.1.call-done = bf16[1024,1024]{1,0:T(8,128)(2,1)} async-done(((bf16[64,1024]{1,0:T(8,128)(2,1)}), bf16[1024,1024]{1,0:T(8,128)(2,1)}) %all-gather.7.cloned.1.call-update) | async-done | bytes 2097168 | tf_op jit(solution)/shard_map/all_gather | solution.py:74
  153.0 3.7 %fusion.11 = bf16[128,1024]{1,0:T(8,128)(2,1)S(1)} fusion(bf16[1,1,1024,1024]{3,2,1,0:T(8,128)(2,1)} %all-gather.13.cloned.1.call-done, bf16[1024,1024]{1,0:T(8,128)(2,1)} %all-gather.7.cloned.1.call-done, bf16[1,128,2048]{2,1,0:T(8,128)(2,1)S(1)} %copy-done.1, bf16[192,1024]{1,0:T(8,128)(2,1)S(1)} %fusion.7), kind=kOutput, calls=%fused_computation.12 | convolution fusion | flops 537395200 | bytes 4980736 | tf_op jit(solution)/shard_map/dot_general | solution.py:17
  156.8 1.1 pad_maximum_fusion
  158.0 0.7 dynamic_slice.3
  158.6 0.7 add_compare_fusion
  159.3 0.7 iota_compare_fusion.4
  160.1 0.1 multiply_reduce_fusion
  160.1 0.1 multiply_reduce_fusion.2
  160.2 0.2 select_reduce_fusion
  160.5 67.8 %all-gather.9.cloned.1.call-done = bf16[2048,2048]{1,0:T(8,128)(2,1)} async-done(((bf16[128,2048]{1,0:T(8,128)(2,1)}), bf16[2048,2048]{1,0:T(8,128)(2,1)}) %all-gather.9.cloned.1.call-update) | async-done | bytes 8388624 | tf_op jit(solution)/shard_map/all_gather | solution.py:80
  228.2 6.3 %fusion.10 = bf16[16,8,16,128]{3,1,2,0:T(8,128)(2,1)S(1)} fusion(bf16[2048,2048]{1,0:T(8,128)(2,1)} %all-gather.9.cloned.1.call-done, bf16[1,128,2048]{2,1,0:T(8,128)(2,1)S(1)} %copy-done, pred[2048]{0:T(1024)(128)(4,1)S(1)} %iota_compare_fusion.4, pred[128]{0:T(512)(128)(4,1)S(1)} %add_compare_fusion, bf16[128,1024]{1,0:T(8,128)(2,1)S(1)} %fusion.11, ...), kind=kOutput, calls=%fused_computation.11 | convolution fusion | flops 1076101120 | bytes 9963648 | tf_op jit(solution)/shard_map/dot_general | solution.py:17
  234.5 0.1 copy.17
  234.7 0.5 fusion.6
  235.2 0.4 copy.14
  235.6 27.6 %all_to_all.5 = bf16[16,128,3,128]{3,1,2,0:T(8,128)(2,1)S(1)} all-to-all(bf16[16,128,3,128]{3,1,2,0:T(8,128)(2,1)S(1)} %copy.14), channel_id=1, replica_groups=mesh['leaf'=8,'front'=16] {'front'}, dimensions={0} | all-to-all | bytes 3145728 | tf_op jit(solution)/shard_map/all_to_all | solution.py:96
  263.2 3.0 collective-permute-start
  266.2 33.3 %collective-permute-done = bf16[16,128,3,128]{3,1,2,0:T(8,128)(2,1)S(1)} collective-permute-done((bf16[16,128,3,128]{3,1,2,0:T(8,128)(2,1)S(1)}, bf16[16,128,3,128]{3,1,2,0:T(8,128)(2,1)S(1)}, u32[]{:S(2)}, u32[]{:S(2)}) %collective-permute-start) | collective-permute-done | bytes 1572896 | tf_op jit(solution)/shard_map/ppermute | solution.py:13
  299.5 1.4 copy.15
  300.9 2.4 reshape.114
  303.3 5.0 %fusion.24 = f32[32,49152]{1,0:T(8,128)} fusion(bf16[16,49152]{1,0:T(8,128)(2,1)} %reshape.114, s32[16]{0:T(128)S(1)} %get-tuple-element.3), kind=kOutput, calls=%fused_computation.26 | convolution fusion | flops 50332160 | bytes 7864384 | tf_op jit(solution)/shard_map/dot_general | solution.py:51
  308.3 6.1 %broadcast_in_dim_reshape.3 = f32[1,4096,384]{2,1,0:T(8,128)} reshape(f32[32,49152]{1,0:T(8,128)} %fusion.24) | data formatting | bytes 12582912 | tf_op jit(solution)/shard_map/broadcast_in_dim;reshape | solution.py:99
  (18 shorter events, 0.1 us)
Async XLA Ops:
  7.2 51.3 %all-gather.11.cloned.1.call-start = ((), (), s32[]{:S(2)}) async-start(), calls=%async_computation.3 | async-start | bytes 2228224 | tf_op jit(solution)/shard_map/all_gather | solution.py:70
  8.9 96.8 %all-gather.13.cloned.1.call-start = ((), (), s32[]{:S(2)}) async-start(), calls=%async_computation.4 | async-start | bytes 2228224 | tf_op jit(solution)/shard_map/all_gather | solution.py:76
  9.7 143.4 %all-gather.7.cloned.1.call-start = ((), (), s32[]{:S(2)}) async-start(), calls=%async_computation.1 | async-start | bytes 2228224 | tf_op jit(solution)/shard_map/all_gather | solution.py:74
  10.7 142.3 %copy-start.1 = (bf16[1,128,2048]{2,1,0:T(8,128)(2,1)S(1)}, bf16[1,128,2048]{2,1,0:T(8,128)(2,1)}, u32[]{:S(2)}) copy-start(bf16[1,128,2048]{2,1,0:T(8,128)(2,1)} %param.9) | copy-start | bytes 1572868
  61.7 166.5 %all-gather.9.cloned.1.call-start = ((), (), s32[]{:S(2)}) async-start(), calls=%async_computation.2 | async-start | bytes 8912896 | tf_op jit(solution)/shard_map/all_gather | solution.py:80
  156.8 1.2 copy-start.4
  156.8 3.3 %copy-start.2 = (s32[8,32]{1,0:T(8,128)S(1)}, s32[8,32]{1,0:T(8,128)}, u32[]{:S(2)}) copy-start(s32[8,32]{1,0:T(8,128)} %param.13) | copy-start | bytes 3076
  156.8 3.3 %copy-start.3 = (s32[8,16]{1,0:T(8,128)S(1)}, s32[8,16]{1,0:T(8,128)}, u32[]{:S(2)}) copy-start(s32[8,16]{1,0:T(8,128)} %param.12) | copy-start | bytes 1540
  156.8 71.4 %copy-start = (bf16[1,128,2048]{2,1,0:T(8,128)(2,1)S(1)}, bf16[1,128,2048]{2,1,0:T(8,128)(2,1)}, u32[]{:S(2)}) copy-start(bf16[1,128,2048]{2,1,0:T(8,128)(2,1)} %param.10) | copy-start | bytes 1572868
  263.2 36.3 %collective-permute-start = (bf16[16,128,3,128]{3,1,2,0:T(8,128)(2,1)S(1)}, bf16[16,128,3,128]{3,1,2,0:T(8,128)(2,1)S(1)}, u32[]{:S(2)}, u32[]{:S(2)}) collective-permute-start(bf16[16,128,3,128]{3,1,2,0:T(8,128)(2,1)S(1)} %all_to_all.5), channel_id=1, source_target_pairs={{0,64},{16,80},{32,96},{48,112},{64,0},{80,16},{96,32},{112,48},{1... | collective-permute-start | bytes 4718600 | tf_op jit(solution)/shard_map/ppermute | solution.py:13
Sparse Core Ops, SparseCore 0:
  10.7 47.7 all-gather.10
  61.2 44.5 all-gather.12
  108.5 44.5 all-gather.6
  158.1 70.1 all-gather.8
where the time goes:
time: 321 us
  waiting for transfers between devices  241 us (75%)
  blocking collectives  27.6 us (9%)
  matrix products  18.1 us (6%)
  local copies, waits for them, and re-layouts  14.5 us (5%)
  between operations  13.9 us (4%)
    all_gather x1, waiting for transfers between devices, per_device(): lax.all_gather(factor_local, 'front', axis=0, tiled=True)  67.8 us
    all_gather x1, waiting for transfers between devices, per_device(): lax.all_gather(first_inv, 'front', axis=0, tiled=True)  47.8 us
    all_gather x1, waiting for transfers between devices, per_device(): lax.all_gather(link_local, 'front', axis=0, tiled=True)  47.3 us
    all_gather x1, waiting for transfers between devices, per_device(): lax.all_gather(second_inv, 'front', axis=0, tiled=True)  43.9 us
    ppermute x1, waiting for transfers between devices, passed_along(): lax.ppermute(value, axis, [(i, (i + by) % devices) for i in range(devices)])  33.3 us
    all_to_all x1, blocking collectives, per_device(): lax.all_to_all(routed, 'front', split_axis=0, concat_axis=0, tiled=True)  27.6 us
    dot_general x3, matrix products, dot_rows(): lax.dot_general(left_rows, right_rows, (((1,), (1,)), ((), ())), preferre...  12.6 us
  transfers between devices with their start and end apart: 5, of which 5 were waited for; matrix products, arithmetic and copies ran while one was open for 2% of the time, Pallas kernels for 0%

commit v1 on v0

v1 whole, which is shorter than its diff:
```python
import functools

import jax
import jax.numpy as jnp
from jax import lax
from jax.experimental import pallas as pl
from jax.experimental.pallas import tpu as pltpu
from jax.sharding import PartitionSpec as P

PANEL = 1024
BLOCK = 128
SLOTS = 3
SIDE = 4
FRONT = SIDE * SIDE
CONTRIB = BLOCK * FRONT
ROWS = PANEL // FRONT
MIB = 1024 * 1024


def dot_nt(left, right):
    return lax.dot_general(
        left, right, (((1,), (1,)), ((), ())), preferred_element_type=jnp.float32
    )


def shift(value, axis, by):
    dx, dz = (by, 0) if axis == "x" else (0, by)
    pairs = [
        (x * SIDE + z, (x + dx) % SIDE * SIDE + (z + dz) % SIDE)
        for x in range(SIDE)
        for z in range(SIDE)
    ]
    return lax.ppermute(value, "front", pairs)


def to_parent(value):
    groups = lax.axis_size("leaf")
    return lax.ppermute(
        value, "leaf", [(g, (g + groups // 2) % groups) for g in range(groups)]
    )


RING = (0, -1, 1, 2)


def gather_half(own, first_axis, second_axis):
    rows = own.shape[0]
    half = rows // 2
    from_left = shift(own, first_axis, 1)
    from_right = shift(own, first_axis, -1)
    far_top = shift(from_left[:half], first_axis, 1)
    far_bottom = shift(from_right[half:], first_axis, -1)
    bundle = jnp.concatenate([own, from_left, from_right, far_top, far_bottom], axis=0)
    left_bundle = shift(bundle, second_axis, 1)
    right_bundle = shift(bundle, second_axis, -1)
    far_low = shift(left_bundle[: 2 * rows], second_axis, 1)
    far_high = shift(right_bundle[2 * rows :], second_axis, -1)

    def places(first, second):
        return [(f, second) if first_axis == "x" else (second, f) for f in first]

    return [
        (bundle, places(RING, 0)),
        (left_bundle, places(RING, -1)),
        (right_bundle, places(RING, 1)),
        (far_low, places(RING[:2], 2)),
        (far_high, places(RING[2:], 2)),
    ]


def gather_pieces(top, bottom):
    bundles, layout = [], []
    for half, parts in enumerate((gather_half(top, "x", "z"), gather_half(bottom, "z", "x"))):
        rows = (top, bottom)[half].shape[0]
        for array, places in parts:
            bundles.append(array)
            layout.append([(half, at * rows, dx, dz) for at, (dx, dz) in enumerate(places)])
    return bundles, layout


def place_of(front, dx, dz):
    x, z = front // SIDE, front % SIDE
    return lax.rem(x + dx + SIDE, SIDE) * SIDE + lax.rem(z + dz + SIDE, SIDE)


def panel_kernel(layout, info, border, *refs):
    count = len(layout)
    bundles = refs[:count]
    link_out, factor_out = refs[count : count + 2]
    mats, link, updated, sems = refs[count + 2 :]
    front = info[1]
    part = ROWS // 2
    copies = [[], [], []]
    for bundle, places in zip(bundles, layout, strict=True):
        for half, at, dx, dz in places:
            row = pl.multiple_of(place_of(front, dx, dz) * ROWS + half * part, part)
            for which in (0, 2, 1):
                copy = pltpu.make_async_copy(
                    bundle.at[pl.ds(at + which * part, part), :],
                    mats.at[which, pl.ds(row, part), :],
                    sems.at[which, len(copies[which])],
                )
                copies[which].append(copy)
    for which in (0, 2, 1):
        for copy in copies[which]:
            copy.start()
    for copy in copies[0]:
        copy.wait()
    wide = 256
    for at in range(0, PANEL, wide):
        factor_out[:, at : at + wide] = dot_nt(
            border[:, :PANEL], mats[0, at : at + wide, :]
        ).astype(jnp.bfloat16)
    for copy in copies[2]:
        copy.wait()

    @pl.loop(0, PANEL // wide)
    def _(step):
        at = pl.multiple_of(step * wide, wide)
        for up in range(0, PANEL, wide):
            link[up : up + wide, pl.ds(at, wide)] = dot_nt(
                mats[2, up : up + wide, :], mats[0, pl.ds(at, wide), :]
            ).astype(jnp.bfloat16)

    link_out[...] = link[pl.ds(pl.multiple_of(front * ROWS, ROWS), ROWS), :]
    for at in range(0, PANEL, wide):
        coupled = dot_nt(factor_out[:, :PANEL], link[at : at + wide, :])
        updated[:, at : at + wide] = (
            border[:, PANEL + at : PANEL + at + wide].astype(jnp.float32) - coupled
        ).astype(jnp.bfloat16)
    for copy in copies[1]:
        copy.wait()
    for at in range(0, PANEL, wide):
        factor_out[:, PANEL + at : PANEL + at + wide] = dot_nt(
            updated[...], mats[1, at : at + wide, :]
        ).astype(jnp.bfloat16)


def eliminate(info, border, bundles, layout):
    blocks = FRONT * 2
    vmem = pl.BlockSpec(memory_space=pltpu.VMEM)
    return pl.pallas_call(
        functools.partial(panel_kernel, layout),
        out_shape=(
            jax.ShapeDtypeStruct((ROWS, PANEL), jnp.bfloat16),
            jax.ShapeDtypeStruct((BLOCK, 2 * PANEL), jnp.bfloat16),
        ),
        in_specs=[pl.BlockSpec(memory_space=pltpu.SMEM), vmem]
        + [pl.BlockSpec(memory_space=pl.ANY)] * len(bundles),
        out_specs=(vmem, vmem),
        scratch_shapes=[
            pltpu.VMEM((3, PANEL, PANEL), jnp.bfloat16),
            pltpu.VMEM((PANEL, PANEL), jnp.bfloat16),
            pltpu.VMEM((BLOCK, PANEL), jnp.bfloat16),
            pltpu.SemaphoreType.DMA((3, blocks)),
        ],
        compiler_params=pltpu.CompilerParams(vmem_limit_bytes=24 * MIB),
        cost_estimate=pl.CostEstimate(
            flops=2 * PANEL**3 + 6 * BLOCK * PANEL**2,
            bytes_accessed=8 * MIB,
            transcendentals=0,
        ),
        name="panels",
    )(info, border, *bundles)


def pack_kernel(info, block_map, block_owner, tail, out):
    parent, child = info[0], info[2]
    for block in range(FRONT):
        slot = block_owner[parent, block_map[child, block]]
        out[slot // SLOTS, lax.rem(slot, SLOTS)] = tail[:, block * BLOCK : (block + 1) * BLOCK]


def pack_tiles(info, block_map, block_owner, tail):
    smem = pl.BlockSpec(memory_space=pltpu.SMEM)
    vmem = pl.BlockSpec(memory_space=pltpu.VMEM)
    return pl.pallas_call(
        pack_kernel,
        out_shape=jax.ShapeDtypeStruct((FRONT, SLOTS, BLOCK, BLOCK), jnp.bfloat16),
        in_specs=[smem, smem, smem, vmem],
        out_specs=vmem,
        compiler_params=pltpu.CompilerParams(vmem_limit_bytes=8 * MIB),
        name="pack",
    )(info, block_map, block_owner, tail)


def update_kernel(layout, info, sizes, block_map, block_owner, tiles, *refs):
    count = len(layout)
    bundles = refs[:count]
    out = refs[count]
    factor, chosen, staged, blank, taken, column, load_sems, store_sems, blank_sem = refs[
        count + 1 :
    ]
    parent, front, child = info[0], info[1], info[2]
    live = sizes[child]
    part = BLOCK // 2
    loads = []
    for bundle, places in zip(bundles, layout, strict=True):
        for half, at, dx, dz in places:
            row = pl.multiple_of(place_of(front, dx, dz) * BLOCK + half * part, part)
            copy = pltpu.make_async_copy(
                bundle.at[pl.ds(at, part), :],
                factor.at[pl.ds(row, part), :],
                load_sems.at[len(loads)],
            )
            copy.start()
            loads.append(copy)
    blank[...] = jnp.zeros_like(blank)
    for slot in range(SLOTS):
        column[slot] = -1

    @pl.loop(0, 2 * FRONT)
    def _(block):
        taken[block] = 0

    @pl.loop(0, FRONT)
    def _(block):
        into = block_map[child, block]
        taken[into] = 1
        slot = block_owner[parent, into]

        @pl.when(slot // SLOTS == front)
        def _():
            column[lax.rem(slot, SLOTS)] = block

    def blank_copy(block):
        row = pl.multiple_of(block * BLOCK, BLOCK)
        return pltpu.make_async_copy(blank, out.at[pl.ds(row, BLOCK), :], blank_sem)

    @pl.loop(0, 2 * FRONT)
    def _(block):
        @pl.when(taken[block] == 0)
        def _():
            blank_copy(block).start()

    for copy in loads:
        copy.wait()
    for slot in range(SLOTS):
        row = pl.multiple_of(jnp.maximum(column[slot], 0) * BLOCK, BLOCK)
        chosen[slot * BLOCK : (slot + 1) * BLOCK, :] = factor[pl.ds(row, BLOCK), :]

    def store(block):
        row = pl.multiple_of(block_map[child, block] * BLOCK, BLOCK)
        return pltpu.make_async_copy(
            staged.at[block], out.at[pl.ds(row, BLOCK), :], store_sems.at[block]
        )

    lane = lax.broadcasted_iota(jnp.int32, (BLOCK, BLOCK), 1)
    line = lax.broadcasted_iota(jnp.int32, (BLOCK, BLOCK), 0)

    @pl.loop(0, FRONT // 2)
    def _(pair):
        top = pl.multiple_of(pair * 2 * BLOCK, 2 * BLOCK)
        product = dot_nt(factor[pl.ds(top, 2 * BLOCK), :], chosen[...])
        for low in range(2):
            block = pair * 2 + low
            for slot in range(SLOTS):
                first = column[slot]
                keep = (
                    (line + block * BLOCK < live)
                    & (lane + first * BLOCK < live)
                    & (lane * 0 + first >= 0)
                )
                schur = (
                    tiles[block, slot].astype(jnp.float32)
                    - product[low * BLOCK : (low + 1) * BLOCK, slot * BLOCK : (slot + 1) * BLOCK]
                )
                staged[block, :, slot * BLOCK : (slot + 1) * BLOCK] = (
                    jnp.where(keep, schur, 0.0).astype(jnp.bfloat16).astype(jnp.float32)
                )
            store(block).start()

    for block in range(FRONT):
        store(block).wait()

    @pl.loop(0, FRONT)
    def _(block):
        blank_copy(0).wait()


def update_parent(info, sizes, block_map, block_owner, tiles, bundles, layout):
    smem = pl.BlockSpec(memory_space=pltpu.SMEM)
    vmem = pl.BlockSpec(memory_space=pltpu.VMEM)
    held = pl.BlockSpec(memory_space=pl.ANY)
    return pl.pallas_call(
        functools.partial(update_kernel, layout),
        out_shape=jax.ShapeDtypeStruct((2 * CONTRIB, SLOTS * BLOCK), jnp.float32),
        in_specs=[smem, smem, smem, smem, vmem] + [held] * len(bundles),
        out_specs=held,
        scratch_shapes=[
            pltpu.VMEM((CONTRIB, 2 * PANEL), jnp.bfloat16),
            pltpu.VMEM((SLOTS * BLOCK, 2 * PANEL), jnp.bfloat16),
            pltpu.VMEM((FRONT, BLOCK, SLOTS * BLOCK), jnp.float32),
            pltpu.VMEM((BLOCK, SLOTS * BLOCK), jnp.float32),
            pltpu.SMEM((2 * FRONT,), jnp.int32),
            pltpu.SMEM((SLOTS,), jnp.int32),
            pltpu.SemaphoreType.DMA((2 * FRONT,)),
            pltpu.SemaphoreType.DMA((FRONT,)),
            pltpu.SemaphoreType.DMA,
        ],
        compiler_params=pltpu.CompilerParams(vmem_limit_bytes=32 * MIB),
        cost_estimate=pl.CostEstimate(
            flops=2 * CONTRIB * SLOTS * BLOCK * 2 * PANEL,
            bytes_accessed=16 * MIB,
            transcendentals=0,
        ),
        name="update",
    )(info, sizes, block_map, block_owner, tiles, *bundles)


def per_device(inv_factors, panel_rows, border, tail, front_sizes, block_map, block_owner):
    groups = lax.axis_size("leaf")
    group = lax.axis_index("leaf")
    front = lax.axis_index("front")
    info = jnp.stack([group, front, (group + groups // 2) % groups]).astype(jnp.int32)

    tail_here = to_parent(tail[0])
    packed = pack_tiles(info, block_map, block_owner, tail_here)
    tiles = lax.all_to_all(packed, "front", split_axis=0, concat_axis=0, tiled=True)

    part = ROWS // 2
    own = jnp.concatenate([inv_factors[0], panel_rows], axis=0)
    top = own[:, :part].reshape(3 * part, PANEL)
    bottom = own[:, part:].reshape(3 * part, PANEL)
    bundles, layout = gather_pieces(top, bottom)
    link_local, factor_local = eliminate(info, border[0], bundles, layout)

    child_rows = to_parent(factor_local)
    bundles, layout = gather_pieces(child_rows[: BLOCK // 2], child_rows[BLOCK // 2 :])
    update = update_parent(info, front_sizes, block_map, block_owner, tiles, bundles, layout)
    return link_local[None], factor_local[None], update[None]


def solution(mesh):
    return jax.shard_map(
        per_device,
        mesh=mesh,
        in_specs=(
            P("leaf", None, "front", None),
            P("leaf", "front", None),
            P("leaf", "front", None),
            P("leaf", "front", None),
            P(),
            P(),
            P(),
        ),
        out_specs=(P("leaf", "front", None), P("leaf", "front", None), P("leaf", None, "front")),
        check_vma=False,
    )
```

time: 321 us -> 176 us (0.55)
  waiting for transfers between devices: 241 us -> 64.8 us
  starting transfers between devices: 3.17 us -> 58.8 us
  Pallas kernels: 0 us -> 30 us
  blocking collectives: 27.6 us -> 0 us
  matrix products: 18.1 us -> 0 us
  between operations: 13.9 us -> 1.06 us
  local copies, waits for them, and re-layouts: 14.5 us -> 19.7 us
    all_gather x4 -> x0, waiting for transfers between devices: 207 us -> none  [the longest x1 67.8 us: per_device(): lax.all_gather(factor_local, 'front', axis=0, tiled=True)]
    ppermute x1 -> x34, starting transfers between devices: 3.01 us -> 53.6 us  [the longest x32 47.1 us: shift(): return lax.ppermute(value, 'front', pairs)]
    ppermute x1 -> x34, waiting for transfers between devices: 33.3 us -> 64 us  [the longest x32 56.3 us: shift(): return lax.ppermute(value, 'front', pairs)]
    pallas_call x0 -> x3, Pallas kernels: none -> 30 us  [the longest x1 16 us: eliminate(): pl.pallas_call(functools.partial(panel_kernel, layout), out_shape=(jax.Sh...]
    all_to_all x1 -> x0, blocking collectives: 27.6 us -> none  [per_device(): lax.all_to_all(routed, 'front', split_axis=0, concat_axis=0, tiled=True)]
    dot_general x5 -> x0, matrix products: 18.1 us -> none  [the longest x3 12.6 us: dot_rows(): lax.dot_general(left_rows, right_rows, (((1,), (1,)), ((), ())), preferre...]
    slice x3 -> x17, local copies, waits for them, and re-layouts: 2.43 us -> 10.7 us  [the longest x4 5.34 us: gather_half(): far_low = shift(left_bundle[:2 * rows], second_axis, 1)]
    unnamed x11 -> x32, local copies, waits for them, and re-layouts: 0.14 us -> 7.65 us
  transfers between devices with their start and end apart: 5 -> 35, of which waited for: 5 -> 14; matrix products, arithmetic and copies ran while one was open for 2% -> 9% of each run, Pallas kernels for 0% -> 1%
where the time goes in v1:
time: 176 us; the launch traced here: 175 us
  waiting for transfers between devices  64.8 us (37%)
  starting transfers between devices  58.8 us (33%)
  Pallas kernels  30 us (17%)
  local copies, waits for them, and re-layouts  19.7 us (11%)
    ppermute x32, waiting for transfers between devices, shift(): return lax.ppermute(value, 'front', pairs)  56.3 us
    ppermute x32, starting transfers between devices, shift(): return lax.ppermute(value, 'front', pairs)  47.1 us
    pallas_call x1, Pallas kernels, eliminate(): pl.pallas_call(functools.partial(panel_kernel, layout), out_shape=(jax.Sh...  16 us
    pallas_call x1, Pallas kernels, update_parent(): pl.pallas_call(functools.partial(update_kernel, layout), out_shape=jax.Sh...  12 us
    ppermute x2, waiting for transfers between devices, to_parent(): lax.ppermute(value, 'leaf', [(g, (g + groups // 2) % groups) for g in ran...  7.7 us
    unnamed x32, local copies, waits for them, and re-layouts  7.65 us
    ppermute x2, starting transfers between devices, to_parent(): lax.ppermute(value, 'leaf', [(g, (g + groups // 2) % groups) for g in ran...  6.46 us
    slice x4, local copies, waits for them, and re-layouts, gather_half(): far_low = shift(left_bundle[:2 * rows], second_axis, 1)  5.34 us
  transfers between devices with their start and end apart: 35, of which 14 were waited for; matrix products, arithmetic and copies ran while one was open for 9% of the time, Pallas kernels for 1%

profile of v1, /device:TPU:0, one launch (start us, length us, event | category | flops | bytes accessed | tf_op | source)
XLA Modules:
  0.0 175.5 jit_solution(6590816953586884772)
XLA Ops:
  1.7 2.9 %collective-permute-start.1 = (bf16[96,1024]{1,0:T(8,128)(2,1)S(1)}, bf16[96,1024]{1,0:T(8,128)(2,1)S(1)}, u32[]{:S(2)}, u32[]{:S(2)}) collective-permute-start(bf16[96,1024]{1,0:T(8,128)(2,1)S(1)} %bitcast.16), channel_id=1, source_target_pairs={{0,12},{1,13},{2,14},{3,15},{4,0},{5,1},{6,2},{7,3},{8,4},{9,5},{1... | collective-permute-start | bytes 589832 | tf_op jit(solution)/shard_map/ppermute | solution.py:33
  4.6 4.0 %collective-permute-start.9 = (bf16[96,1024]{1,0:T(8,128)(2,1)S(1)}, bf16[96,1024]{1,0:T(8,128)(2,1)S(1)}, u32[]{:S(2)}, u32[]{:S(2)}) collective-permute-start(bf16[96,1024]{1,0:T(8,128)(2,1)S(1)} %bitcast.13), channel_id=1, source_target_pairs={{0,3},{1,0},{2,1},{3,2},{4,7},{5,4},{6,5},{7,6},{8,11},{9,8},{10,9... | collective-permute-start | bytes 589832 | tf_op jit(solution)/shard_map/ppermute | solution.py:33
  8.8 3.8 %collective-permute-start.3 = (bf16[48,1024]{1,0:T(8,128)(2,1)S(1)}, bf16[48,1024]{1,0:T(8,128)(2,1)S(1)}, u32[]{:S(2)}, u32[]{:S(2)}) collective-permute-start(bf16[48,1024]{1,0:T(8,128)(2,1)S(1)} %slice.83), channel_id=1, source_target_pairs={{0,12},{1,13},{2,14},{3,15},{4,0},{5,1},{6,2},{7,3},{8,4},{9,5},{1... | collective-permute-start | bytes 294920 | tf_op jit(solution)/shard_map/ppermute | solution.py:33
  12.7 4.1 %collective-permute-start.11 = (bf16[48,1024]{1,0:T(8,128)(2,1)S(1)}, bf16[48,1024]{1,0:T(8,128)(2,1)S(1)}, u32[]{:S(2)}, u32[]{:S(2)}) collective-permute-start(bf16[48,1024]{1,0:T(8,128)(2,1)S(1)} %slice.87), channel_id=1, source_target_pairs={{0,3},{1,0},{2,1},{3,2},{4,7},{5,4},{6,5},{7,6},{8,11},{9,8},{10,9... | collective-permute-start | bytes 294920 | tf_op jit(solution)/shard_map/ppermute | solution.py:33
  17.0 5.7 %collective-permute-done.10 = bf16[48,1024]{1,0:T(8,128)(2,1)S(1)} collective-permute-done((bf16[48,1024]{1,0:T(8,128)(2,1)S(1)}, bf16[48,1024]{1,0:T(8,128)(2,1)S(1)}, u32[]{:S(2)}, u32[]{:S(2)}) %collective-permute-start.10) | collective-permute-done | bytes 98336 | tf_op jit(solution)/shard_map/ppermute | solution.py:33
  22.7 3.3 %collective-permute-start.13 = (bf16[384,1024]{1,0:T(8,128)(2,1)S(1)}, bf16[384,1024]{1,0:T(8,128)(2,1)S(1)}, u32[]{:S(2)}, u32[]{:S(2)}) collective-permute-start(bf16[384,1024]{1,0:T(8,128)(2,1)S(1)} %constant_dynamic-update-slice_fusion.5.refs_5_), channel_id=1, source_target_pairs={{0,12},{1,13},{2,14},{3,15},{4,0},{5,1},{6,2},{7,3},{8,4},{9,5},{1... | collective-permute-start | bytes 2359304 | tf_op jit(solution)/shard_map/ppermute | solution.py:33
  26.2 2.0 %collective-permute-start.4 = (bf16[384,1024]{1,0:T(8,128)(2,1)S(1)}, bf16[384,1024]{1,0:T(8,128)(2,1)S(1)}, u32[]{:S(2)}, u32[]{:S(2)}) collective-permute-start(bf16[384,1024]{1,0:T(8,128)(2,1)S(1)} %constant_dynamic-update-slice_fusion.refs_0_), channel_id=1, source_target_pairs={{0,1},{1,2},{2,3},{3,0},{4,5},{5,6},{6,7},{7,4},{8,9},{9,10},{10,1... | collective-permute-start | bytes 2359304 | tf_op jit(solution)/shard_map/ppermute | solution.py:33
  28.2 11.8 %collective-permute-done.13.refs_7_ = bf16[384,1024]{1,0:T(8,128)(2,1)S(1)} collective-permute-done((bf16[384,1024]{1,0:T(8,128)(2,1)S(1)}, bf16[384,1024]{1,0:T(8,128)(2,1)S(1)}, u32[]{:S(2)}, u32[]{:S(2)}) %collective-permute-start.13) | collective-permute-done | bytes 786464 | tf_op jit(solution)/shard_map/ppermute | solution.py:33
  40.7 3.7 %collective-permute-start.15 = (bf16[192,1024]{1,0:T(8,128)(2,1)}, bf16[192,1024]{1,0:T(8,128)(2,1)S(1)}, u32[]{:S(2)}, u32[]{:S(2)}) collective-permute-start(bf16[192,1024]{1,0:T(8,128)(2,1)} %slice.89), channel_id=1, source_target_pairs={{0,12},{1,13},{2,14},{3,15},{4,0},{5,1},{6,2},{7,3},{8,4},{9,5},{1... | collective-permute-start | bytes 1179656 | tf_op jit(solution)/shard_map/ppermute | solution.py:33
  46.9 1.9 %collective-permute-start.6 = (bf16[192,1024]{1,0:T(8,128)(2,1)}, bf16[192,1024]{1,0:T(8,128)(2,1)}, u32[]{:S(2)}, u32[]{:S(2)}) collective-permute-start(bf16[192,1024]{1,0:T(8,128)(2,1)} %slice.84), channel_id=1, source_target_pairs={{0,1},{1,2},{2,3},{3,0},{4,5},{5,6},{6,7},{7,4},{8,9},{9,10},{10,1... | collective-permute-start | bytes 1179656 | tf_op jit(solution)/shard_map/ppermute | solution.py:33
  50.0 4.5 %collective-permute-done.14.refs_8_ = bf16[192,1024]{1,0:T(8,128)(2,1)} collective-permute-done((bf16[192,1024]{1,0:T(8,128)(2,1)}, bf16[192,1024]{1,0:T(8,128)(2,1)}, u32[]{:S(2)}, u32[]{:S(2)}) %collective-permute-start.14) | collective-permute-done | bytes 393248 | tf_op jit(solution)/shard_map/ppermute | solution.py:33
  59.5 16.0 %panels.1 = (bf16[64,1024]{1,0:T(8,128)(2,1)}, bf16[128,2048]{1,0:T(8,128)(2,1)}) custom-call(s32[3]{0:T(128)S(1)} %pad_add_fusion.info, bf16[128,2048]{1,0:T(8,128)(2,1)S(1)} %bitcast.11, bf16[384,1024]{1,0:T(8,128)(2,1)S(1)} %copy-done.3, bf16[384,1024]{1,0:T(8,128)(2,1)S(1)} %collective-permute-done.4.refs_1_, ...), custom_call_target="tpu_custom_call" | custom-call | flops 2952790016 | bytes 8388608 | tf_op jit(solution)/shard_map/panels/pallas_call | solution.py:142
  75.6 3.3 %collective-permute-start.17 = (bf16[128,2048]{1,0:T(8,128)(2,1)}, bf16[128,2048]{1,0:T(8,128)(2,1)S(1)}, u32[]{:S(2)}, u32[]{:S(2)}) collective-permute-start(bf16[128,2048]{1,0:T(8,128)(2,1)} %get-tuple-element.6), channel_id=1, source_target_pairs={{0,64},{16,80},{32,96},{48,112},{64,0},{80,16},{96,32},{112,48},{1... | collective-permute-start | bytes 1572872 | tf_op jit(solution)/shard_map/ppermute | solution.py:38
  78.8 7.7 %collective-permute-done.17 = bf16[128,2048]{1,0:T(8,128)(2,1)S(1)} collective-permute-done((bf16[128,2048]{1,0:T(8,128)(2,1)}, bf16[128,2048]{1,0:T(8,128)(2,1)S(1)}, u32[]{:S(2)}, u32[]{:S(2)}) %collective-permute-start.17) | collective-permute-done | bytes 524320 | tf_op jit(solution)/shard_map/ppermute | solution.py:38
  87.5 2.0 %collective-permute-start.26 = (bf16[64,2048]{1,0:T(8,128)(2,1)S(1)}, bf16[64,2048]{1,0:T(8,128)(2,1)S(1)}, u32[]{:S(2)}, u32[]{:S(2)}) collective-permute-start(bf16[64,2048]{1,0:T(8,128)(2,1)S(1)} %get-tuple-element.7), channel_id=1, source_target_pairs={{0,1},{1,2},{2,3},{3,0},{4,5},{5,6},{6,7},{7,4},{8,9},{9,10},{10,1... | collective-permute-start | bytes 786440 | tf_op jit(solution)/shard_map/ppermute | solution.py:33
  89.5 3.3 %collective-permute-start.19 = (bf16[64,2048]{1,0:T(8,128)(2,1)S(1)}, bf16[64,2048]{1,0:T(8,128)(2,1)S(1)}, u32[]{:S(2)}, u32[]{:S(2)}) collective-permute-start(bf16[64,2048]{1,0:T(8,128)(2,1)S(1)} %get-tuple-element.10), channel_id=1, source_target_pairs={{0,12},{1,13},{2,14},{3,15},{4,0},{5,1},{6,2},{7,3},{8,4},{9,5},{1... | collective-permute-start | bytes 786440 | tf_op jit(solution)/shard_map/ppermute | solution.py:33
  92.8 3.2 %collective-permute-start.16 = (bf16[128,2048]{1,0:T(8,128)(2,1)S(1)}, bf16[128,2048]{1,0:T(8,128)(2,1)S(1)}, u32[]{:S(2)}, u32[]{:S(2)}) collective-permute-start(bf16[128,2048]{1,0:T(8,128)(2,1)S(1)} %bitcast.20), channel_id=1, source_target_pairs={{0,64},{16,80},{32,96},{48,112},{64,0},{80,16},{96,32},{112,48},{1... | collective-permute-start | bytes 1572872 | tf_op jit(solution)/shard_map/ppermute | solution.py:38
  98.3 3.3 %collective-permute-start.21 = (bf16[32,2048]{1,0:T(8,128)(2,1)S(1)}, bf16[32,2048]{1,0:T(8,128)(2,1)S(1)}, u32[]{:S(2)}, u32[]{:S(2)}) collective-permute-start(bf16[32,2048]{1,0:T(8,128)(2,1)S(1)} %slice.92), channel_id=1, source_target_pairs={{0,12},{1,13},{2,14},{3,15},{4,0},{5,1},{6,2},{7,3},{8,4},{9,5},{1... | collective-permute-start | bytes 393224 | tf_op jit(solution)/shard_map/ppermute | solution.py:33
  104.7 3.3 %collective-permute-done.20 = bf16[32,2048]{1,0:T(8,128)(2,1)S(1)} collective-permute-done((bf16[32,2048]{1,0:T(8,128)(2,1)S(1)}, bf16[32,2048]{1,0:T(8,128)(2,1)S(1)}, u32[]{:S(2)}, u32[]{:S(2)}) %collective-permute-start.20) | collective-permute-done | bytes 131104 | tf_op jit(solution)/shard_map/ppermute | solution.py:33
  109.2 2.4 %collective-permute-start.23 = (bf16[256,2048]{1,0:T(8,128)(2,1)}, bf16[256,2048]{1,0:T(8,128)(2,1)S(1)}, u32[]{:S(2)}, u32[]{:S(2)}) collective-permute-start(bf16[256,2048]{1,0:T(8,128)(2,1)} %constant_dynamic-update-slice_fusion.10.refs_0_), channel_id=1, source_target_pairs={{0,3},{1,0},{2,1},{3,2},{4,7},{5,4},{6,5},{7,6},{8,11},{9,8},{10,9... | collective-permute-start | bytes 3145736 | tf_op jit(solution)/shard_map/ppermute | solution.py:33
  113.0 2.0 %collective-permute-start.30 = (bf16[256,2048]{1,0:T(8,128)(2,1)}, bf16[256,2048]{1,0:T(8,128)(2,1)}, u32[]{:S(2)}, u32[]{:S(2)}) collective-permute-start(bf16[256,2048]{1,0:T(8,128)(2,1)} %constant_dynamic-update-slice_fusion.15.refs_5_), channel_id=1, source_target_pairs={{0,4},{1,5},{2,6},{3,7},{4,8},{5,9},{6,10},{7,11},{8,12},{9,13},{1... | collective-permute-start | bytes 3145736 | tf_op jit(solution)/shard_map/ppermute | solution.py:33
  115.0 2.0 %pack.1 = bf16[16,3,128,128]{3,2,1,0:T(8,128)(2,1)} custom-call(s32[3]{0:T(128)S(1)} %pad_add_fusion.info, s32[8,16]{1,0:T(8,128)S(1)} %copy-done.4, s32[8,32]{1,0:T(8,128)S(1)} %copy-done.5, bf16[128,2048]{1,0:T(8,128)(2,1)S(1)} %collective-permute-done.16.tail), custom_call_target="tpu_custom_call" | custom-call | tf_op jit(solution)/shard_map/pack/pallas_call | solution.py:177
  117.1 5.3 %all-to-all-start = ((bf16[16,3,128,128]{3,2,1,0:T(8,128)(2,1)}), bf16[16,3,128,128]{3,2,1,0:T(8,128)(2,1)S(1)}, u32[]{:S(2)}, u32[]{:S(2)}) async-start(bf16[16,3,128,128]{3,2,1,0:T(8,128)(2,1)} %pack.1), calls=%async_computation | async-start | bytes 3145728 | tf_op jit(solution)/shard_map/all_to_all | solution.py:319
  122.3 19.1 %collective-permute-done.23.refs_2_ = bf16[256,2048]{1,0:T(8,128)(2,1)S(1)} collective-permute-done((bf16[256,2048]{1,0:T(8,128)(2,1)}, bf16[256,2048]{1,0:T(8,128)(2,1)S(1)}, u32[]{:S(2)}, u32[]{:S(2)}) %collective-permute-start.23) | collective-permute-done | bytes 1048608 | tf_op jit(solution)/shard_map/ppermute | solution.py:33
  142.3 3.6 %collective-permute-start.25 = (bf16[128,2048]{1,0:T(8,128)(2,1)}, bf16[128,2048]{1,0:T(8,128)(2,1)S(1)}, u32[]{:S(2)}, u32[]{:S(2)}) collective-permute-start(bf16[128,2048]{1,0:T(8,128)(2,1)} %slice.94), channel_id=1, source_target_pairs={{0,3},{1,0},{2,1},{3,2},{4,7},{5,4},{6,5},{7,6},{8,11},{9,8},{10,9... | collective-permute-start | bytes 1572872 | tf_op jit(solution)/shard_map/ppermute | solution.py:33
  146.9 1.9 %slice.93 = bf16[128,2048]{1,0:T(8,128)(2,1)} slice(bf16[256,2048]{1,0:T(8,128)(2,1)} %collective-permute-done.22.refs_1_), slice={[0:128], [0:2048]} | slice | bytes 1048576 | tf_op jit(solution)/shard_map/slice | solution.py:56
  148.8 1.9 %slice.99 = bf16[128,2048]{1,0:T(8,128)(2,1)} slice(bf16[256,2048]{1,0:T(8,128)(2,1)} %collective-permute-done.31.refs_7_), slice={[128:256], [0:2048]} | slice | bytes 1048576 | tf_op jit(solution)/shard_map/slice | solution.py:57
  150.7 1.9 %slice.98 = bf16[128,2048]{1,0:T(8,128)(2,1)} slice(bf16[256,2048]{1,0:T(8,128)(2,1)} %collective-permute-done.30.refs_6_), slice={[0:128], [0:2048]} | slice | bytes 1048576 | tf_op jit(solution)/shard_map/slice | solution.py:56
  152.6 2.0 %collective-permute-start.32 = (bf16[128,2048]{1,0:T(8,128)(2,1)}, bf16[128,2048]{1,0:T(8,128)(2,1)}, u32[]{:S(2)}, u32[]{:S(2)}) collective-permute-start(bf16[128,2048]{1,0:T(8,128)(2,1)} %slice.98), channel_id=1, source_target_pairs={{0,4},{1,5},{2,6},{3,7},{4,8},{5,9},{6,10},{7,11},{8,12},{9,13},{1... | collective-permute-start | bytes 1572872 | tf_op jit(solution)/shard_map/ppermute | solution.py:33
  157.1 4.0 %collective-permute-done.24.refs_3_ = bf16[128,2048]{1,0:T(8,128)(2,1)} collective-permute-done((bf16[128,2048]{1,0:T(8,128)(2,1)}, bf16[128,2048]{1,0:T(8,128)(2,1)}, u32[]{:S(2)}, u32[]{:S(2)}) %collective-permute-start.24) | collective-permute-done | bytes 524320 | tf_op jit(solution)/shard_map/ppermute | solution.py:33
  161.1 2.3 %collective-permute-done.32.refs_8_ = bf16[128,2048]{1,0:T(8,128)(2,1)} collective-permute-done((bf16[128,2048]{1,0:T(8,128)(2,1)}, bf16[128,2048]{1,0:T(8,128)(2,1)}, u32[]{:S(2)}, u32[]{:S(2)}) %collective-permute-start.32) | collective-permute-done | bytes 524320 | tf_op jit(solution)/shard_map/ppermute | solution.py:33
  163.3 12.0 %update.1 = f32[4096,384]{1,0:T(8,128)} custom-call(s32[3]{0:T(128)S(1)} %pad_add_fusion.info, s32[8]{0:T(128)S(1)} %copy-done.6, s32[8,16]{1,0:T(8,128)S(1)} %copy-done.4, s32[8,32]{1,0:T(8,128)S(1)} %copy-done.5, bf16[16,3,128,128]{3,2,1,0:T(8,128)(2,1)S(1)} %all-to-all-done.tiles, bf16[256,2048]{1,0:T(8,128)(2,1)} %constant_dynamic-update-slice_fusion.10.refs_0_, ...), custom_call_target="tpu_custom_call" | custom-call | flops 3221225472 | bytes 16777216 | tf_op jit(solution)/shard_map/update/pallas_call | solution.py:285
  (96 shorter events, 24.4 us)
Async XLA Ops:
  4.6 7.9 %collective-permute-start = (bf16[96,1024]{1,0:T(8,128)(2,1)S(1)}, bf16[96,1024]{1,0:T(8,128)(2,1)S(1)}, u32[]{:S(2)}, u32[]{:S(2)}) collective-permute-start(bf16[96,1024]{1,0:T(8,128)(2,1)S(1)} %bitcast.17), channel_id=1, source_target_pairs={{0,4},{1,5},{2,6},{3,7},{4,8},{5,9},{6,10},{7,11},{8,12},{9,13},{1... | collective-permute-start | bytes 589832 | tf_op jit(solution)/shard_map/ppermute | solution.py:33
  4.6 8.0 %collective-permute-start.9 = (bf16[96,1024]{1,0:T(8,128)(2,1)S(1)}, bf16[96,1024]{1,0:T(8,128)(2,1)S(1)}, u32[]{:S(2)}, u32[]{:S(2)}) collective-permute-start(bf16[96,1024]{1,0:T(8,128)(2,1)S(1)} %bitcast.13), channel_id=1, source_target_pairs={{0,3},{1,0},{2,1},{3,2},{4,7},{5,4},{6,5},{7,6},{8,11},{9,8},{10,9... | collective-permute-start | bytes 589832 | tf_op jit(solution)/shard_map/ppermute | solution.py:33
  8.7 8.1 %collective-permute-start.8 = (bf16[96,1024]{1,0:T(8,128)(2,1)S(1)}, bf16[96,1024]{1,0:T(8,128)(2,1)S(1)}, u32[]{:S(2)}, u32[]{:S(2)}) collective-permute-start(bf16[96,1024]{1,0:T(8,128)(2,1)S(1)} %bitcast.14), channel_id=1, source_target_pairs={{0,1},{1,2},{2,3},{3,0},{4,5},{5,6},{6,7},{7,4},{8,9},{9,10},{10,1... | collective-permute-start | bytes 589832 | tf_op jit(solution)/shard_map/ppermute | solution.py:33
  8.8 17.3 %collective-permute-start.3 = (bf16[48,1024]{1,0:T(8,128)(2,1)S(1)}, bf16[48,1024]{1,0:T(8,128)(2,1)S(1)}, u32[]{:S(2)}, u32[]{:S(2)}) collective-permute-start(bf16[48,1024]{1,0:T(8,128)(2,1)S(1)} %slice.83), channel_id=1, source_target_pairs={{0,12},{1,13},{2,14},{3,15},{4,0},{5,1},{6,2},{7,3},{8,4},{9,5},{1... | collective-permute-start | bytes 294920 | tf_op jit(solution)/shard_map/ppermute | solution.py:33
  12.6 13.5 %collective-permute-start.2 = (bf16[48,1024]{1,0:T(8,128)(2,1)S(1)}, bf16[48,1024]{1,0:T(8,128)(2,1)S(1)}, u32[]{:S(2)}, u32[]{:S(2)}) collective-permute-start(bf16[48,1024]{1,0:T(8,128)(2,1)S(1)} %slice.82), channel_id=1, source_target_pairs={{0,4},{1,5},{2,6},{3,7},{4,8},{5,9},{6,10},{7,11},{8,12},{9,13},{1... | collective-permute-start | bytes 294920 | tf_op jit(solution)/shard_map/ppermute | solution.py:33
  12.7 10.0 %collective-permute-start.11 = (bf16[48,1024]{1,0:T(8,128)(2,1)S(1)}, bf16[48,1024]{1,0:T(8,128)(2,1)S(1)}, u32[]{:S(2)}, u32[]{:S(2)}) collective-permute-start(bf16[48,1024]{1,0:T(8,128)(2,1)S(1)} %slice.87), channel_id=1, source_target_pairs={{0,3},{1,0},{2,1},{3,2},{4,7},{5,4},{6,5},{7,6},{8,11},{9,8},{10,9... | collective-permute-start | bytes 294920 | tf_op jit(solution)/shard_map/ppermute | solution.py:33
  22.7 17.2 %collective-permute-start.13 = (bf16[384,1024]{1,0:T(8,128)(2,1)S(1)}, bf16[384,1024]{1,0:T(8,128)(2,1)S(1)}, u32[]{:S(2)}, u32[]{:S(2)}) collective-permute-start(bf16[384,1024]{1,0:T(8,128)(2,1)S(1)} %constant_dynamic-update-slice_fusion.5.refs_5_), channel_id=1, source_target_pairs={{0,12},{1,13},{2,14},{3,15},{4,0},{5,1},{6,2},{7,3},{8,4},{9,5},{1... | collective-permute-start | bytes 2359304 | tf_op jit(solution)/shard_map/ppermute | solution.py:33
  26.0 18.4 %collective-permute-start.12 = (bf16[384,1024]{1,0:T(8,128)(2,1)S(1)}, bf16[384,1024]{1,0:T(8,128)(2,1)S(1)}, u32[]{:S(2)}, u32[]{:S(2)}) collective-permute-start(bf16[384,1024]{1,0:T(8,128)(2,1)S(1)} %constant_dynamic-update-slice_fusion.5.refs_5_), channel_id=1, source_target_pairs={{0,4},{1,5},{2,6},{3,7},{4,8},{5,9},{6,10},{7,11},{8,12},{9,13},{1... | collective-permute-start | bytes 2359304 | tf_op jit(solution)/shard_map/ppermute | solution.py:33
  26.1 19.1 %collective-permute-start.5 = (bf16[384,1024]{1,0:T(8,128)(2,1)S(1)}, bf16[384,1024]{1,0:T(8,128)(2,1)S(1)}, u32[]{:S(2)}, u32[]{:S(2)}) collective-permute-start(bf16[384,1024]{1,0:T(8,128)(2,1)S(1)} %constant_dynamic-update-slice_fusion.refs_0_), channel_id=1, source_target_pairs={{0,3},{1,0},{2,1},{3,2},{4,7},{5,4},{6,5},{7,6},{8,11},{9,8},{10,9... | collective-permute-start | bytes 2359304 | tf_op jit(solution)/shard_map/ppermute | solution.py:33
  26.2 20.0 %collective-permute-start.4 = (bf16[384,1024]{1,0:T(8,128)(2,1)S(1)}, bf16[384,1024]{1,0:T(8,128)(2,1)S(1)}, u32[]{:S(2)}, u32[]{:S(2)}) collective-permute-start(bf16[384,1024]{1,0:T(8,128)(2,1)S(1)} %constant_dynamic-update-slice_fusion.refs_0_), channel_id=1, source_target_pairs={{0,1},{1,2},{2,3},{3,0},{4,5},{5,6},{6,7},{7,4},{8,9},{9,10},{10,1... | collective-permute-start | bytes 2359304 | tf_op jit(solution)/shard_map/ppermute | solution.py:33
  40.7 9.3 %collective-permute-start.15 = (bf16[192,1024]{1,0:T(8,128)(2,1)}, bf16[192,1024]{1,0:T(8,128)(2,1)S(1)}, u32[]{:S(2)}, u32[]{:S(2)}) collective-permute-start(bf16[192,1024]{1,0:T(8,128)(2,1)} %slice.89), channel_id=1, source_target_pairs={{0,12},{1,13},{2,14},{3,15},{4,0},{5,1},{6,2},{7,3},{8,4},{9,5},{1... | collective-permute-start | bytes 1179656 | tf_op jit(solution)/shard_map/ppermute | solution.py:33
  45.2 9.3 %collective-permute-start.14 = (bf16[192,1024]{1,0:T(8,128)(2,1)}, bf16[192,1024]{1,0:T(8,128)(2,1)}, u32[]{:S(2)}, u32[]{:S(2)}) collective-permute-start(bf16[192,1024]{1,0:T(8,128)(2,1)} %slice.88), channel_id=1, source_target_pairs={{0,4},{1,5},{2,6},{3,7},{4,8},{5,9},{6,10},{7,11},{8,12},{9,13},{1... | collective-permute-start | bytes 1179656 | tf_op jit(solution)/shard_map/ppermute | solution.py:33
  46.0 8.5 %collective-permute-start.7 = (bf16[192,1024]{1,0:T(8,128)(2,1)}, bf16[192,1024]{1,0:T(8,128)(2,1)}, u32[]{:S(2)}, u32[]{:S(2)}) collective-permute-start(bf16[192,1024]{1,0:T(8,128)(2,1)} %slice.85), channel_id=1, source_target_pairs={{0,3},{1,0},{2,1},{3,2},{4,7},{5,4},{6,5},{7,6},{8,11},{9,8},{10,9... | collective-permute-start | bytes 1179656 | tf_op jit(solution)/shard_map/ppermute | solution.py:33
  46.9 9.3 %collective-permute-start.6 = (bf16[192,1024]{1,0:T(8,128)(2,1)}, bf16[192,1024]{1,0:T(8,128)(2,1)}, u32[]{:S(2)}, u32[]{:S(2)}) collective-permute-start(bf16[192,1024]{1,0:T(8,128)(2,1)} %slice.84), channel_id=1, source_target_pairs={{0,1},{1,2},{2,3},{3,0},{4,5},{5,6},{6,7},{7,4},{8,9},{9,10},{10,1... | collective-permute-start | bytes 1179656 | tf_op jit(solution)/shard_map/ppermute | solution.py:33
  75.6 11.0 %collective-permute-start.17 = (bf16[128,2048]{1,0:T(8,128)(2,1)}, bf16[128,2048]{1,0:T(8,128)(2,1)S(1)}, u32[]{:S(2)}, u32[]{:S(2)}) collective-permute-start(bf16[128,2048]{1,0:T(8,128)(2,1)} %get-tuple-element.6), channel_id=1, source_target_pairs={{0,64},{16,80},{32,96},{48,112},{64,0},{80,16},{96,32},{112,48},{1... | collective-permute-start | bytes 1572872 | tf_op jit(solution)/shard_map/ppermute | solution.py:38
  87.5 8.5 %collective-permute-start.27 = (bf16[64,2048]{1,0:T(8,128)(2,1)S(1)}, bf16[64,2048]{1,0:T(8,128)(2,1)S(1)}, u32[]{:S(2)}, u32[]{:S(2)}) collective-permute-start(bf16[64,2048]{1,0:T(8,128)(2,1)S(1)} %get-tuple-element.7), channel_id=1, source_target_pairs={{0,3},{1,0},{2,1},{3,2},{4,7},{5,4},{6,5},{7,6},{8,11},{9,8},{10,9... | collective-permute-start | bytes 786440 | tf_op jit(solution)/shard_map/ppermute | solution.py:33
  87.5 9.9 %collective-permute-start.26 = (bf16[64,2048]{1,0:T(8,128)(2,1)S(1)}, bf16[64,2048]{1,0:T(8,128)(2,1)S(1)}, u32[]{:S(2)}, u32[]{:S(2)}) collective-permute-start(bf16[64,2048]{1,0:T(8,128)(2,1)S(1)} %get-tuple-element.7), channel_id=1, source_target_pairs={{0,1},{1,2},{2,3},{3,0},{4,5},{5,6},{6,7},{7,4},{8,9},{9,10},{10,1... | collective-permute-start | bytes 786440 | tf_op jit(solution)/shard_map/ppermute | solution.py:33
  89.5 8.8 %collective-permute-start.19 = (bf16[64,2048]{1,0:T(8,128)(2,1)S(1)}, bf16[64,2048]{1,0:T(8,128)(2,1)S(1)}, u32[]{:S(2)}, u32[]{:S(2)}) collective-permute-start(bf16[64,2048]{1,0:T(8,128)(2,1)S(1)} %get-tuple-element.10), channel_id=1, source_target_pairs={{0,12},{1,13},{2,14},{3,15},{4,0},{5,1},{6,2},{7,3},{8,4},{9,5},{1... | collective-permute-start | bytes 786440 | tf_op jit(solution)/shard_map/ppermute | solution.py:33
  92.8 8.9 %collective-permute-start.18 = (bf16[64,2048]{1,0:T(8,128)(2,1)S(1)}, bf16[64,2048]{1,0:T(8,128)(2,1)S(1)}, u32[]{:S(2)}, u32[]{:S(2)}) collective-permute-start(bf16[64,2048]{1,0:T(8,128)(2,1)S(1)} %get-tuple-element.10), channel_id=1, source_target_pairs={{0,4},{1,5},{2,6},{3,7},{4,8},{5,9},{6,10},{7,11},{8,12},{9,13},{1... | collective-permute-start | bytes 786440 | tf_op jit(solution)/shard_map/ppermute | solution.py:33
  92.8 22.3 %collective-permute-start.16 = (bf16[128,2048]{1,0:T(8,128)(2,1)S(1)}, bf16[128,2048]{1,0:T(8,128)(2,1)S(1)}, u32[]{:S(2)}, u32[]{:S(2)}) collective-permute-start(bf16[128,2048]{1,0:T(8,128)(2,1)S(1)} %bitcast.20), channel_id=1, source_target_pairs={{0,64},{16,80},{32,96},{48,112},{64,0},{80,16},{96,32},{112,48},{1... | collective-permute-start | bytes 1572872 | tf_op jit(solution)/shard_map/ppermute | solution.py:38
  96.0 16.4 %collective-permute-start.29 = (bf16[32,2048]{1,0:T(8,128)(2,1)S(1)}, bf16[32,2048]{1,0:T(8,128)(2,1)S(1)}, u32[]{:S(2)}, u32[]{:S(2)}) collective-permute-start(bf16[32,2048]{1,0:T(8,128)(2,1)S(1)} %slice.97), channel_id=1, source_target_pairs={{0,3},{1,0},{2,1},{3,2},{4,7},{5,4},{6,5},{7,6},{8,11},{9,8},{10,9... | collective-permute-start | bytes 393224 | tf_op jit(solution)/shard_map/ppermute | solution.py:33
  97.4 14.2 %collective-permute-start.28 = (bf16[32,2048]{1,0:T(8,128)(2,1)S(1)}, bf16[32,2048]{1,0:T(8,128)(2,1)S(1)}, u32[]{:S(2)}, u32[]{:S(2)}) collective-permute-start(bf16[32,2048]{1,0:T(8,128)(2,1)S(1)} %slice.96), channel_id=1, source_target_pairs={{0,1},{1,2},{2,3},{3,0},{4,5},{5,6},{6,7},{7,4},{8,9},{9,10},{10,1... | collective-permute-start | bytes 393224 | tf_op jit(solution)/shard_map/ppermute | solution.py:33
  98.3 10.2 %collective-permute-start.21 = (bf16[32,2048]{1,0:T(8,128)(2,1)S(1)}, bf16[32,2048]{1,0:T(8,128)(2,1)S(1)}, u32[]{:S(2)}, u32[]{:S(2)}) collective-permute-start(bf16[32,2048]{1,0:T(8,128)(2,1)S(1)} %slice.92), channel_id=1, source_target_pairs={{0,12},{1,13},{2,14},{3,15},{4,0},{5,1},{6,2},{7,3},{8,4},{9,5},{1... | collective-permute-start | bytes 393224 | tf_op jit(solution)/shard_map/ppermute | solution.py:33
  109.2 32.2 %collective-permute-start.23 = (bf16[256,2048]{1,0:T(8,128)(2,1)}, bf16[256,2048]{1,0:T(8,128)(2,1)S(1)}, u32[]{:S(2)}, u32[]{:S(2)}) collective-permute-start(bf16[256,2048]{1,0:T(8,128)(2,1)} %constant_dynamic-update-slice_fusion.10.refs_0_), channel_id=1, source_target_pairs={{0,3},{1,0},{2,1},{3,2},{4,7},{5,4},{6,5},{7,6},{8,11},{9,8},{10,9... | collective-permute-start | bytes 3145736 | tf_op jit(solution)/shard_map/ppermute | solution.py:33
  111.7 35.2 %collective-permute-start.22 = (bf16[256,2048]{1,0:T(8,128)(2,1)}, bf16[256,2048]{1,0:T(8,128)(2,1)}, u32[]{:S(2)}, u32[]{:S(2)}) collective-permute-start(bf16[256,2048]{1,0:T(8,128)(2,1)} %constant_dynamic-update-slice_fusion.10.refs_0_), channel_id=1, source_target_pairs={{0,1},{1,2},{2,3},{3,0},{4,5},{5,6},{6,7},{7,4},{8,9},{9,10},{10,1... | collective-permute-start | bytes 3145736 | tf_op jit(solution)/shard_map/ppermute | solution.py:33
  113.0 35.8 %collective-permute-start.31 = (bf16[256,2048]{1,0:T(8,128)(2,1)}, bf16[256,2048]{1,0:T(8,128)(2,1)}, u32[]{:S(2)}, u32[]{:S(2)}) collective-permute-start(bf16[256,2048]{1,0:T(8,128)(2,1)} %constant_dynamic-update-slice_fusion.15.refs_5_), channel_id=1, source_target_pairs={{0,12},{1,13},{2,14},{3,15},{4,0},{5,1},{6,2},{7,3},{8,4},{9,5},{1... | collective-permute-start | bytes 3145736 | tf_op jit(solution)/shard_map/ppermute | solution.py:33
  113.0 37.7 %collective-permute-start.30 = (bf16[256,2048]{1,0:T(8,128)(2,1)}, bf16[256,2048]{1,0:T(8,128)(2,1)}, u32[]{:S(2)}, u32[]{:S(2)}) collective-permute-start(bf16[256,2048]{1,0:T(8,128)(2,1)} %constant_dynamic-update-slice_fusion.15.refs_5_), channel_id=1, source_target_pairs={{0,4},{1,5},{2,6},{3,7},{4,8},{5,9},{6,10},{7,11},{8,12},{9,13},{1... | collective-permute-start | bytes 3145736 | tf_op jit(solution)/shard_map/ppermute | solution.py:33
  117.1 38.4 %all-to-all-start = ((bf16[16,3,128,128]{3,2,1,0:T(8,128)(2,1)}), bf16[16,3,128,128]{3,2,1,0:T(8,128)(2,1)S(1)}, u32[]{:S(2)}, u32[]{:S(2)}) async-start(bf16[16,3,128,128]{3,2,1,0:T(8,128)(2,1)} %pack.1), calls=%async_computation | async-start | bytes 3145728 | tf_op jit(solution)/shard_map/all_to_all | solution.py:319
  142.3 14.8 %collective-permute-start.25 = (bf16[128,2048]{1,0:T(8,128)(2,1)}, bf16[128,2048]{1,0:T(8,128)(2,1)S(1)}, u32[]{:S(2)}, u32[]{:S(2)}) collective-permute-start(bf16[128,2048]{1,0:T(8,128)(2,1)} %slice.94), channel_id=1, source_target_pairs={{0,3},{1,0},{2,1},{3,2},{4,7},{5,4},{6,5},{7,6},{8,11},{9,8},{10,9... | collective-permute-start | bytes 1572872 | tf_op jit(solution)/shard_map/ppermute | solution.py:33
  148.8 12.3 %collective-permute-start.24 = (bf16[128,2048]{1,0:T(8,128)(2,1)}, bf16[128,2048]{1,0:T(8,128)(2,1)}, u32[]{:S(2)}, u32[]{:S(2)}) collective-permute-start(bf16[128,2048]{1,0:T(8,128)(2,1)} %slice.93), channel_id=1, source_target_pairs={{0,1},{1,2},{2,3},{3,0},{4,5},{5,6},{6,7},{7,4},{8,9},{9,10},{10,1... | collective-permute-start | bytes 1572872 | tf_op jit(solution)/shard_map/ppermute | solution.py:33
  150.7 10.4 %collective-permute-start.33 = (bf16[128,2048]{1,0:T(8,128)(2,1)}, bf16[128,2048]{1,0:T(8,128)(2,1)}, u32[]{:S(2)}, u32[]{:S(2)}) collective-permute-start(bf16[128,2048]{1,0:T(8,128)(2,1)} %slice.99), channel_id=1, source_target_pairs={{0,12},{1,13},{2,14},{3,15},{4,0},{5,1},{6,2},{7,3},{8,4},{9,5},{1... | collective-permute-start | bytes 1572872 | tf_op jit(solution)/shard_map/ppermute | solution.py:33
  152.6 10.7 %collective-permute-start.32 = (bf16[128,2048]{1,0:T(8,128)(2,1)}, bf16[128,2048]{1,0:T(8,128)(2,1)}, u32[]{:S(2)}, u32[]{:S(2)}) collective-permute-start(bf16[128,2048]{1,0:T(8,128)(2,1)} %slice.98), channel_id=1, source_target_pairs={{0,4},{1,5},{2,6},{3,7},{4,8},{5,9},{6,10},{7,11},{8,12},{9,13},{1... | collective-permute-start | bytes 1572872 | tf_op jit(solution)/shard_map/ppermute | solution.py:33
  (12 other events, 132.4 us)

commit v2 on v0

v2 whole, which is shorter than its diff:
```python
import functools

import jax
import jax.numpy as jnp
from jax import lax
from jax.experimental import pallas as pl
from jax.experimental.pallas import tpu as pltpu
from jax.sharding import PartitionSpec as P

PANEL = 1024
BLOCK = 128
SLOTS = 3
SIDE = 4
FRONT = SIDE * SIDE
CONTRIB = BLOCK * FRONT
ROWS = PANEL // FRONT
MIB = 1024 * 1024


def dot_nt(left, right):
    return lax.dot_general(
        left, right, (((1,), (1,)), ((), ())), preferred_element_type=jnp.float32
    )


def shift(value, axis, by):
    dx, dz = (by, 0) if axis == "x" else (0, by)
    pairs = [
        (x * SIDE + z, (x + dx) % SIDE * SIDE + (z + dz) % SIDE)
        for x in range(SIDE)
        for z in range(SIDE)
    ]
    return lax.ppermute(value, "front", pairs)


def to_parent(value):
    groups = lax.axis_size("leaf")
    return lax.ppermute(
        value, "leaf", [(g, (g + groups // 2) % groups) for g in range(groups)]
    )


RING = (0, -1, 1, 2)


def bundle_of(own, axis):
    half = own.shape[0] // 2
    from_left = shift(own, axis, 1)
    from_right = shift(own, axis, -1)
    far_top = shift(from_left[:half], axis, 1)
    far_bottom = shift(from_right[half:], axis, -1)
    return jnp.concatenate([own, from_left, from_right, far_top, far_bottom], axis=0)


def spread(bundle, axis):
    half = bundle.shape[0] // 2
    left = shift(bundle, axis, 1)
    right = shift(bundle, axis, -1)
    far_low = shift(left[:half], axis, 1)
    far_high = shift(right[half:], axis, -1)
    return [bundle, left, right, far_low, far_high]


def places(x_first):
    found = []
    for part, second in ((RING, 0), (RING, -1), (RING, 1), (RING[:2], 2), (RING[2:], 2)):
        found.append([(first, second) if x_first else (second, first) for first in part])
    return found


X_FIRST, Z_FIRST = places(True), places(False)


def place_of(front, dx, dz):
    x, z = front // SIDE, front % SIDE
    return lax.rem(x + dx + SIDE, SIDE) * SIDE + lax.rem(z + dz + SIDE, SIDE)


def family():
    groups = lax.axis_size("leaf")
    parent = lax.axis_index("leaf")
    return parent, lax.rem(parent + groups // 2, groups), lax.axis_index("front")


def unpack(front, bundles, which, mat):
    part = ROWS // 2
    for half, layout in enumerate((X_FIRST, Z_FIRST)):
        for bundle, blocks in zip(bundles[half * 5 : half * 5 + 5], layout, strict=True):
            for at, (dx, dz) in enumerate(blocks):
                row = pl.multiple_of(place_of(front, dx, dz) * ROWS + half * part, part)
                top = (at * 3 + which) * part
                mat[pl.ds(row, part), :] = bundle[top : top + part, :]


WIDE = 256


def project(rows, inverse, keep):
    for at in range(0, PANEL, WIDE):
        upto = at + WIDE
        keep(at, dot_nt(rows[:, :upto], inverse[at:upto, :upto]))


def first_kernel(border, *refs):
    bundles, (first, inverse) = refs[:10], refs[10:]
    unpack(lax.axis_index("front"), bundles, 0, inverse)

    def keep(at, value):
        first[:, at : at + WIDE] = value.astype(jnp.bfloat16)

    project(border, inverse, keep)


def second_kernel(border, first, *refs):
    bundles, (link_out, factor) = refs[:10], refs[10:12]
    mats, link, updated = refs[12:]
    front = lax.axis_index("front")
    for which in range(3):
        unpack(front, bundles, which, mats.at[which])
    factor[:, :PANEL] = first[...]

    def keep_link(at, value):
        link[:, at : at + WIDE] = value.astype(jnp.bfloat16)

    def keep_second(at, value):
        factor[:, PANEL + at : PANEL + at + WIDE] = value.astype(jnp.bfloat16)

    project(mats.at[2], mats.at[0], keep_link)
    link_out[...] = link[pl.ds(pl.multiple_of(front * ROWS, ROWS), ROWS), :]
    for at in range(0, PANEL, WIDE):
        coupled = dot_nt(first[...], link[at : at + WIDE, :])
        updated[:, at : at + WIDE] = (
            border[:, PANEL + at : PANEL + at + WIDE].astype(jnp.float32) - coupled
        ).astype(jnp.bfloat16)
    project(updated, mats.at[1], keep_second)


VMEM_SPEC = pl.BlockSpec(memory_space=pltpu.VMEM)
SMEM_SPEC = pl.BlockSpec(memory_space=pltpu.SMEM)


def first_columns(border, bundles):
    return pl.pallas_call(
        first_kernel,
        out_shape=jax.ShapeDtypeStruct((BLOCK, PANEL), jnp.bfloat16),
        in_specs=[VMEM_SPEC] * 11,
        out_specs=VMEM_SPEC,
        scratch_shapes=[pltpu.VMEM((PANEL, PANEL), jnp.bfloat16)],
        compiler_params=pltpu.CompilerParams(vmem_limit_bytes=8 * MIB),
        cost_estimate=pl.CostEstimate(
            flops=2 * BLOCK * PANEL**2, bytes_accessed=3 * MIB, transcendentals=0
        ),
        name="first",
    )(border, *bundles)


def second_columns(border, first, bundles):
    return pl.pallas_call(
        second_kernel,
        out_shape=(
            jax.ShapeDtypeStruct((ROWS, PANEL), jnp.bfloat16),
            jax.ShapeDtypeStruct((BLOCK, 2 * PANEL), jnp.bfloat16),
        ),
        in_specs=[VMEM_SPEC] * 12,
        out_specs=(VMEM_SPEC,) * 2,
        scratch_shapes=[
            pltpu.VMEM((3, PANEL, PANEL), jnp.bfloat16),
            pltpu.VMEM((PANEL, PANEL), jnp.bfloat16),
            pltpu.VMEM((BLOCK, PANEL), jnp.bfloat16),
        ],
        compiler_params=pltpu.CompilerParams(vmem_limit_bytes=16 * MIB),
        cost_estimate=pl.CostEstimate(
            flops=2 * PANEL**3 + 4 * BLOCK * PANEL**2,
            bytes_accessed=8 * MIB,
            transcendentals=0,
        ),
        name="second",
    )(border, first, *bundles)


def tail_kernel(tail, *outs):
    z = lax.rem(lax.axis_index("front"), SIDE)
    for step, out in enumerate(outs):
        to = lax.rem(z + step, SIDE)
        for x in range(SIDE):
            at = pl.multiple_of((x * SIDE + to) * BLOCK, BLOCK)
            out[:, x * BLOCK : (x + 1) * BLOCK] = tail[:, pl.ds(at, BLOCK)]


LINE = SIDE * BLOCK


def split_tail(tail):
    return pl.pallas_call(
        tail_kernel,
        out_shape=(jax.ShapeDtypeStruct((BLOCK, LINE), jnp.bfloat16),) * SIDE,
        in_specs=[VMEM_SPEC],
        out_specs=(VMEM_SPEC,) * SIDE,
        compiler_params=pltpu.CompilerParams(vmem_limit_bytes=4 * MIB),
        cost_estimate=pl.CostEstimate(flops=0, bytes_accessed=MIB, transcendentals=0),
        name="tail",
    )(tail)


def tile_kernel(sizes, rows_z, rows_x, *refs):
    tails, outs, (product,) = refs[:SIDE], refs[SIDE : SIDE + 2], refs[SIDE + 2 :]
    front = lax.axis_index("front")
    live = sizes[lax.axis_index("leaf")]
    x, z = front // SIDE, lax.rem(front, SIDE)
    lane = lax.broadcasted_iota(jnp.int32, (BLOCK, BLOCK), 1)
    line = lax.broadcasted_iota(jnp.int32, (BLOCK, BLOCK), 0)
    for at in range(0, LINE, WIDE):
        product[:, at : at + WIDE] = dot_nt(rows_z[...], rows_x[at : at + WIDE, :])
    for up, dz in enumerate(RING):
        row_z = lax.rem(z + dz + SIDE, SIDE)
        for across, dx in enumerate(RING):
            col_x = lax.rem(x + dx + SIDE, SIDE)
            columns = slice(across * BLOCK, (across + 1) * BLOCK)
            keep = (line + (x * SIDE + row_z) * BLOCK < live) & (
                lane + (col_x * SIDE + z) * BLOCK < live
            )
            old = tails[-dz % SIDE][:, pl.ds(pl.multiple_of(col_x * BLOCK, BLOCK), BLOCK)]
            schur = old.astype(jnp.float32) - product[up * BLOCK : (up + 1) * BLOCK, columns]
            value = jnp.where(keep, schur, 0.0).astype(jnp.bfloat16)
            for chunk, out in enumerate(outs):

                @pl.when(row_z // 2 == chunk)
                def _():
                    row = pl.multiple_of(lax.rem(row_z, 2) * BLOCK, BLOCK)
                    out[pl.ds(row, BLOCK), columns] = value


def make_tile(sizes, rows_z, rows_x, tails):
    return pl.pallas_call(
        tile_kernel,
        out_shape=(jax.ShapeDtypeStruct((LINE // 2, LINE), jnp.bfloat16),) * 2,
        in_specs=[SMEM_SPEC] + [VMEM_SPEC] * (2 + SIDE),
        out_specs=(VMEM_SPEC,) * 2,
        scratch_shapes=[pltpu.VMEM((LINE, LINE), jnp.float32)],
        compiler_params=pltpu.CompilerParams(vmem_limit_bytes=8 * MIB),
        cost_estimate=pl.CostEstimate(
            flops=4 * LINE * LINE * PANEL, bytes_accessed=6 * MIB, transcendentals=0
        ),
        name="tile",
    )(sizes, rows_z, rows_x, *tails)


def pack_kernel(block_map, block_owner, line, *outs):
    parent, child, front = family()
    x, z = front // SIDE, lax.rem(front, SIDE)
    rows = LINE // 2
    for up, dz in enumerate(RING):
        for across, dx in enumerate(RING):
            block = place_of(front, dx, dz)
            slot = block_owner[parent, block_map[child, block]]
            owner = slot // SLOTS
            for step, out in enumerate(outs):

                @pl.when(
                    (lax.rem(owner, SIDE) == z)
                    & (lax.rem(owner // SIDE - x + SIDE, SIDE) == step)
                )
                def _():
                    out[lax.rem(slot, SLOTS)] = line[
                        up * rows : (up + 1) * rows, across * BLOCK : (across + 1) * BLOCK
                    ]


def pack_tiles(block_map, block_owner, line):
    shape = jax.ShapeDtypeStruct((SLOTS, LINE // 2, BLOCK), jnp.bfloat16)
    return pl.pallas_call(
        pack_kernel,
        out_shape=(shape,) * SIDE,
        in_specs=[SMEM_SPEC, SMEM_SPEC, VMEM_SPEC],
        out_specs=(VMEM_SPEC,) * SIDE,
        compiler_params=pltpu.CompilerParams(vmem_limit_bytes=4 * MIB),
        cost_estimate=pl.CostEstimate(flops=0, bytes_accessed=2 * MIB, transcendentals=0),
        name="pack",
    )(block_map, block_owner, line)


def blank_kernel(block_map, out, blank, taken, sem):
    _, child, _ = family()
    blank[...] = jnp.zeros_like(blank)

    @pl.loop(0, 2 * FRONT)
    def _(block):
        taken[block] = 0

    @pl.loop(0, FRONT)
    def _(block):
        taken[block_map[child, block]] = 1

    def copy(block):
        row = pl.multiple_of(block * BLOCK, BLOCK)
        return pltpu.make_async_copy(blank, out.at[pl.ds(row, BLOCK), :], sem)

    @pl.loop(0, 2 * FRONT)
    def _(block):
        @pl.when(taken[block] == 0)
        def _():
            copy(block).start()

    @pl.loop(0, FRONT)
    def _(block):
        copy(0).wait()


PARENT = jax.ShapeDtypeStruct((2 * CONTRIB, SLOTS * BLOCK), jnp.float32)
HELD = pl.BlockSpec(memory_space=pl.ANY)


def blank_rows(block_map):
    return pl.pallas_call(
        blank_kernel,
        out_shape=PARENT,
        in_specs=[SMEM_SPEC],
        out_specs=HELD,
        scratch_shapes=[
            pltpu.VMEM((BLOCK, SLOTS * BLOCK), jnp.float32),
            pltpu.SMEM((2 * FRONT,), jnp.int32),
            pltpu.SemaphoreType.DMA,
        ],
        compiler_params=pltpu.CompilerParams(vmem_limit_bytes=2 * MIB),
        cost_estimate=pl.CostEstimate(flops=0, bytes_accessed=3 * MIB, transcendentals=0),
        name="blank",
    )(block_map)


def place_kernel(chunk, block_map, block_owner, *refs):
    tiles, (out, staged, held, sems) = refs[:SIDE], refs[SIDE + 1 :]
    parent, child, front = family()
    for slot in range(SLOTS):
        held[slot] = 0

    @pl.loop(0, FRONT)
    def _(block):
        slot = block_owner[parent, block_map[child, block]]

        @pl.when(slot // SLOTS == front)
        def _():
            held[lax.rem(slot, SLOTS)] = 1

    none = lax.broadcasted_iota(jnp.int32, (BLOCK, BLOCK), 0) * 0
    copies = []
    for step, tile in enumerate(tiles):
        x = lax.rem(front // SIDE - step + SIDE, SIDE)
        for up in range(2):
            block = x * SIDE + chunk * 2 + up
            here = len(copies)
            for slot in range(SLOTS):
                value = tile[slot, up * BLOCK : (up + 1) * BLOCK, :].astype(jnp.float32)
                staged[here, :, slot * BLOCK : (slot + 1) * BLOCK] = jnp.where(
                    none + held[slot] > 0, value, 0.0
                )
            row = pl.multiple_of(block_map[child, block] * BLOCK, BLOCK)
            copy = pltpu.make_async_copy(
                staged.at[here], out.at[pl.ds(row, BLOCK), :], sems.at[here]
            )
            copy.start()
            copies.append(copy)
    for copy in copies:
        copy.wait()


def place_tiles(chunk, block_map, block_owner, tiles, parent_rows):
    return pl.pallas_call(
        functools.partial(place_kernel, chunk),
        out_shape=PARENT,
        in_specs=[SMEM_SPEC] * 2 + [VMEM_SPEC] * SIDE + [HELD],
        out_specs=HELD,
        scratch_shapes=[
            pltpu.VMEM((2 * SIDE, BLOCK, SLOTS * BLOCK), jnp.float32),
            pltpu.SMEM((SLOTS,), jnp.int32),
            pltpu.SemaphoreType.DMA((2 * SIDE,)),
        ],
        input_output_aliases={2 + SIDE: 0},
        compiler_params=pltpu.CompilerParams(vmem_limit_bytes=6 * MIB),
        cost_estimate=pl.CostEstimate(flops=0, bytes_accessed=3 * MIB, transcendentals=0),
        name="place",
    )(block_map, block_owner, *tiles, parent_rows)


def per_device(inv_factors, panel_rows, border, tail, front_sizes, block_map, block_owner):
    tails = split_tail(tail[0])
    tails = [tails[0]] + [shift(tails[step], "z", step) for step in range(1, SIDE)]

    part = ROWS // 2
    own = jnp.concatenate([inv_factors[0], panel_rows], axis=0)
    top = bundle_of(own[:, :part].reshape(3 * part, PANEL), "x")
    bottom = bundle_of(own[:, part:].reshape(3 * part, PANEL), "z")
    bundles = spread(top, "z") + spread(bottom, "x")
    tails, bundles = lax.optimization_barrier((tails, bundles))
    first = first_columns(border[0], bundles)
    link_local, factor_local = second_columns(border[0], first, bundles)

    chunks = make_tile(
        front_sizes, bundle_of(factor_local, "z"), bundle_of(factor_local, "x"), tails
    )

    update = blank_rows(block_map)
    for chunk, rows in enumerate(chunks):
        line = bundle_of(to_parent(rows), "z")
        packed = pack_tiles(block_map, block_owner, line)
        tiles = [packed[0]] + [shift(packed[step], "x", step) for step in range(1, SIDE)]
        update = place_tiles(chunk, block_map, block_owner, tiles, update)
    return link_local[None], factor_local[None], update[None]


def solution(mesh):
    return jax.shard_map(
        per_device,
        mesh=mesh,
        in_specs=(
            P("leaf", None, "front", None),
            P("leaf", "front", None),
            P("leaf", "front", None),
            P("leaf", "front", None),
            P(),
            P(),
            P(),
        ),
        out_specs=(P("leaf", "front", None), P("leaf", "front", None), P("leaf", None, "front")),
        check_vma=False,
    )
```

time: 321 us -> 133 us (0.41)
  waiting for transfers between devices: 241 us -> 47.6 us
  starting transfers between devices: 3.17 us -> 63.3 us
  blocking collectives: 27.6 us -> 0 us
  matrix products: 18.1 us -> 0 us
  Pallas kernels: 0 us -> 17.1 us
  between operations: 13.9 us -> 1.45 us
  local copies, waits for them, and re-layouts: 14.5 us -> 2.15 us
    all_gather x4 -> x0, waiting for transfers between devices: 207 us -> none  [the longest x1 67.8 us: per_device(): lax.all_gather(factor_local, 'front', axis=0, tiled=True)]
    ppermute x1 -> x43, starting transfers between devices: 3.01 us -> 63.3 us  [the longest x41 59.7 us: shift(): return lax.ppermute(value, 'front', pairs)]
    all_to_all x1 -> x0, blocking collectives: 27.6 us -> none  [per_device(): lax.all_to_all(routed, 'front', split_axis=0, concat_axis=0, tiled=True)]
    dot_general x5 -> x0, matrix products: 18.1 us -> none  [the longest x3 12.6 us: dot_rows(): lax.dot_general(left_rows, right_rows, (((1,), (1,)), ((), ())), preferre...]
    pallas_call x0 -> x9, Pallas kernels: none -> 17.1 us  [the longest x2 4.52 us: place_tiles(): pl.pallas_call(functools.partial(place_kernel, chunk), out_shape=PARENT,...]
    ppermute x1 -> x43, waiting for transfers between devices: 33.3 us -> 47.6 us  [the longest x41 43.3 us: shift(): return lax.ppermute(value, 'front', pairs)]
    another operation x1 -> x0, local copies, waits for them, and re-layouts: 6.14 us -> none  [per_device(): return (link_local[None], factor_local[None], merged[None])]
  transfers between devices with their start and end apart: 5 -> 43, of which waited for: 5 -> 14; matrix products, arithmetic and copies ran while one was open for 2% -> 2% of each run, Pallas kernels for 0% -> 6%
where the time goes in v2:
time: 133 us
  starting transfers between devices  63.3 us (48%)
  waiting for transfers between devices  47.6 us (36%)
  Pallas kernels  17.1 us (13%)
  local copies, waits for them, and re-layouts  2.15 us (2%)
  between operations  1.45 us (1%)
    ppermute x41, starting transfers between devices, shift(): return lax.ppermute(value, 'front', pairs)  59.7 us
    ppermute x41, waiting for transfers between devices, shift(): return lax.ppermute(value, 'front', pairs)  43.3 us
    pallas_call x2, Pallas kernels, place_tiles(): pl.pallas_call(functools.partial(place_kernel, chunk), out_shape=PARENT,...  4.52 us
    ppermute x2, waiting for transfers between devices, to_parent(): lax.ppermute(value, 'leaf', [(g, (g + groups // 2) % groups) for g in ran...  4.35 us
    pallas_call x1, Pallas kernels, second_columns(): pl.pallas_call(second_kernel, out_shape=(jax.ShapeDtypeStruct((ROWS, PANE...  3.79 us
    ppermute x2, starting transfers between devices, to_parent(): lax.ppermute(value, 'leaf', [(g, (g + groups // 2) % groups) for g in ran...  3.61 us
    pallas_call x2, Pallas kernels, pack_tiles(): pl.pallas_call(pack_kernel, out_shape=(shape,) * SIDE, in_specs=[SMEM_SPE...  3.22 us
  transfers between devices with their start and end apart: 43, of which 14 were waited for; matrix products, arithmetic and copies ran while one was open for 2% of the time, Pallas kernels for 6%

profile of v2, /device:TPU:0, one launch (start us, length us, event | category | flops | bytes accessed | tf_op | source)
XLA Modules:
  0.0 132.7 jit_solution(13384392492688707129)
XLA Ops:
  1.7 2.1 %collective-permute-start.11 = (bf16[96,1024]{1,0:T(8,128)(2,1)S(1)}, bf16[96,1024]{1,0:T(8,128)(2,1)S(1)}, u32[]{:S(2)}, u32[]{:S(2)}) collective-permute-start(bf16[96,1024]{1,0:T(8,128)(2,1)S(1)} %bitcast.15), channel_id=1, source_target_pairs={{0,1},{1,2},{2,3},{3,0},{4,5},{5,6},{6,7},{7,4},{8,9},{9,10},{10,1... | collective-permute-start | bytes 589832 | tf_op jit(solution)/shard_map/ppermute | solution.py:33
  3.8 2.2 %collective-permute-start.12 = (bf16[96,1024]{1,0:T(8,128)(2,1)S(1)}, bf16[96,1024]{1,0:T(8,128)(2,1)S(1)}, u32[]{:S(2)}, u32[]{:S(2)}) collective-permute-start(bf16[96,1024]{1,0:T(8,128)(2,1)S(1)} %bitcast.16), channel_id=1, source_target_pairs={{0,3},{1,0},{2,1},{3,2},{4,7},{5,4},{6,5},{7,6},{8,11},{9,8},{10,9... | collective-permute-start | bytes 589832 | tf_op jit(solution)/shard_map/ppermute | solution.py:33
  7.5 1.7 %collective-permute-start.4 = (bf16[96,1024]{1,0:T(8,128)(2,1)S(1)}, bf16[96,1024]{1,0:T(8,128)(2,1)S(1)}, u32[]{:S(2)}, u32[]{:S(2)}) collective-permute-start(bf16[96,1024]{1,0:T(8,128)(2,1)S(1)} %bitcast.13), channel_id=1, source_target_pairs={{0,12},{1,13},{2,14},{3,15},{4,0},{5,1},{6,2},{7,3},{8,4},{9,5},{1... | collective-permute-start | bytes 589832 | tf_op jit(solution)/shard_map/ppermute | solution.py:33
  10.9 3.3 %collective-permute-start.14 = (bf16[48,1024]{1,0:T(8,128)(2,1)S(1)}, bf16[48,1024]{1,0:T(8,128)(2,1)S(1)}, u32[]{:S(2)}, u32[]{:S(2)}) collective-permute-start(bf16[48,1024]{1,0:T(8,128)(2,1)S(1)} %slice.79), channel_id=1, source_target_pairs={{0,3},{1,0},{2,1},{3,2},{4,7},{5,4},{6,5},{7,6},{8,11},{9,8},{10,9... | collective-permute-start | bytes 294920 | tf_op jit(solution)/shard_map/ppermute | solution.py:33
  15.8 1.8 %collective-permute-start.6 = (bf16[48,1024]{1,0:T(8,128)(2,1)S(1)}, bf16[48,1024]{1,0:T(8,128)(2,1)S(1)}, u32[]{:S(2)}, u32[]{:S(2)}) collective-permute-start(bf16[48,1024]{1,0:T(8,128)(2,1)S(1)} %slice.75), channel_id=1, source_target_pairs={{0,12},{1,13},{2,14},{3,15},{4,0},{5,1},{6,2},{7,3},{8,4},{9,5},{1... | collective-permute-start | bytes 294920 | tf_op jit(solution)/shard_map/ppermute | solution.py:33
  18.3 2.7 %collective-permute-start.16 = (bf16[384,1024]{1,0:T(8,128)(2,1)S(1)}, bf16[384,1024]{1,0:T(8,128)(2,1)S(1)}, u32[]{:S(2)}, u32[]{:S(2)}) collective-permute-start(bf16[384,1024]{1,0:T(8,128)(2,1)S(1)} %constant_dynamic-update-slice_fusion.5.refs_5_), channel_id=1, source_target_pairs={{0,12},{1,13},{2,14},{3,15},{4,0},{5,1},{6,2},{7,3},{8,4},{9,5},{1... | collective-permute-start | bytes 2359304 | tf_op jit(solution)/shard_map/ppermute | solution.py:33
  21.5 2.0 %collective-permute-start.8 = (bf16[384,1024]{1,0:T(8,128)(2,1)S(1)}, bf16[384,1024]{1,0:T(8,128)(2,1)S(1)}, u32[]{:S(2)}, u32[]{:S(2)}) collective-permute-start(bf16[384,1024]{1,0:T(8,128)(2,1)S(1)} %constant_dynamic-update-slice_fusion.refs_0_), channel_id=1, source_target_pairs={{0,3},{1,0},{2,1},{3,2},{4,7},{5,4},{6,5},{7,6},{8,11},{9,8},{10,9... | collective-permute-start | bytes 2359304 | tf_op jit(solution)/shard_map/ppermute | solution.py:33
  23.8 13.2 %collective-permute-done.15.refs_6_ = bf16[384,1024]{1,0:T(8,128)(2,1)S(1)} collective-permute-done((bf16[384,1024]{1,0:T(8,128)(2,1)S(1)}, bf16[384,1024]{1,0:T(8,128)(2,1)S(1)}, u32[]{:S(2)}, u32[]{:S(2)}) %collective-permute-start.15) | collective-permute-done | bytes 786464 | tf_op jit(solution)/shard_map/ppermute | solution.py:33
  37.1 3.3 %collective-permute-start.18 = (bf16[192,1024]{1,0:T(8,128)(2,1)S(1)}, bf16[192,1024]{1,0:T(8,128)(2,1)S(1)}, u32[]{:S(2)}, u32[]{:S(2)}) collective-permute-start(bf16[192,1024]{1,0:T(8,128)(2,1)S(1)} %slice.81), channel_id=1, source_target_pairs={{0,12},{1,13},{2,14},{3,15},{4,0},{5,1},{6,2},{7,3},{8,4},{9,5},{1... | collective-permute-start | bytes 1179656 | tf_op jit(solution)/shard_map/ppermute | solution.py:33
  43.0 2.7 %collective-permute-done.refs_1_ = bf16[128,512]{1,0:T(8,128)(2,1)S(1)} collective-permute-done((bf16[128,512]{1,0:T(8,128)(2,1)S(1)}, bf16[128,512]{1,0:T(8,128)(2,1)S(1)}, u32[]{:S(2)}, u32[]{:S(2)}) %collective-permute-start) | collective-permute-done | bytes 131104 | tf_op jit(solution)/shard_map/ppermute | solution.py:33
  45.7 8.2 %collective-permute-done.1.refs_2_ = bf16[128,512]{1,0:T(8,128)(2,1)S(1)} collective-permute-done((bf16[128,512]{1,0:T(8,128)(2,1)S(1)}, bf16[128,512]{1,0:T(8,128)(2,1)S(1)}, u32[]{:S(2)}, u32[]{:S(2)}) %collective-permute-start.1) | collective-permute-done | bytes 131104 | tf_op jit(solution)/shard_map/ppermute | solution.py:33
  54.4 4.5 %collective-permute-done.2.refs_3_ = bf16[128,512]{1,0:T(8,128)(2,1)S(1)} collective-permute-done((bf16[128,512]{1,0:T(8,128)(2,1)S(1)}, bf16[128,512]{1,0:T(8,128)(2,1)S(1)}, u32[]{:S(2)}, u32[]{:S(2)}) %collective-permute-start.2) | collective-permute-done | bytes 131104 | tf_op jit(solution)/shard_map/ppermute | solution.py:33
  59.6 3.8 %second.1 = (bf16[64,1024]{1,0:T(8,128)(2,1)}, bf16[128,2048]{1,0:T(8,128)(2,1)}) custom-call(bf16[128,2048]{1,0:T(8,128)(2,1)S(1)} %bitcast.9, bf16[128,1024]{1,0:T(8,128)(2,1)S(1)} %first.1, bf16[384,1024]{1,0:T(8,128)(2,1)S(1)} %constant_dynamic-update-slice_fusion.refs_0_, bf16[384,1024]{1,0:T(8,128)(2,1)S(1)} %collective-permute-done.7.refs_1_, ...), custom_call_target="tpu_custom_call" | custom-call | flops 2684354560 | bytes 8388608 | tf_op jit(solution)/shard_map/second/pallas_call | solution.py:158
  63.7 3.0 %collective-permute-start.24 = (bf16[128,2048]{1,0:T(8,128)(2,1)}, bf16[128,2048]{1,0:T(8,128)(2,1)S(1)}, u32[]{:S(2)}, u32[]{:S(2)}) collective-permute-start(bf16[128,2048]{1,0:T(8,128)(2,1)} %get-tuple-element.48), channel_id=1, source_target_pairs={{0,12},{1,13},{2,14},{3,15},{4,0},{5,1},{6,2},{7,3},{8,4},{9,5},{1... | collective-permute-start | bytes 1572872 | tf_op jit(solution)/shard_map/ppermute | solution.py:33
  66.6 3.2 %collective-permute-start.20 = (bf16[128,2048]{1,0:T(8,128)(2,1)}, bf16[128,2048]{1,0:T(8,128)(2,1)S(1)}, u32[]{:S(2)}, u32[]{:S(2)}) collective-permute-start(bf16[128,2048]{1,0:T(8,128)(2,1)} %get-tuple-element.48), channel_id=1, source_target_pairs={{0,3},{1,0},{2,1},{3,2},{4,7},{5,4},{6,5},{7,6},{8,11},{9,8},{10,9... | collective-permute-start | bytes 1572872 | tf_op jit(solution)/shard_map/ppermute | solution.py:33
  71.2 4.4 %collective-permute-done.23 = bf16[128,2048]{1,0:T(8,128)(2,1)S(1)} collective-permute-done((bf16[128,2048]{1,0:T(8,128)(2,1)}, bf16[128,2048]{1,0:T(8,128)(2,1)S(1)}, u32[]{:S(2)}, u32[]{:S(2)}) %collective-permute-start.23) | collective-permute-done | bytes 524320 | tf_op jit(solution)/shard_map/ppermute | solution.py:33
  75.7 3.3 %collective-permute-start.26 = (bf16[64,2048]{1,0:T(8,128)(2,1)S(1)}, bf16[64,2048]{1,0:T(8,128)(2,1)S(1)}, u32[]{:S(2)}, u32[]{:S(2)}) collective-permute-start(bf16[64,2048]{1,0:T(8,128)(2,1)S(1)} %slice.85), channel_id=1, source_target_pairs={{0,12},{1,13},{2,14},{3,15},{4,0},{5,1},{6,2},{7,3},{8,4},{9,5},{1... | collective-permute-start | bytes 786440 | tf_op jit(solution)/shard_map/ppermute | solution.py:33
  79.2 3.3 %collective-permute-start.22 = (bf16[64,2048]{1,0:T(8,128)(2,1)S(1)}, bf16[64,2048]{1,0:T(8,128)(2,1)S(1)}, u32[]{:S(2)}, u32[]{:S(2)}) collective-permute-start(bf16[64,2048]{1,0:T(8,128)(2,1)S(1)} %slice.83), channel_id=1, source_target_pairs={{0,3},{1,0},{2,1},{3,2},{4,7},{5,4},{6,5},{7,6},{8,11},{9,8},{10,9... | collective-permute-start | bytes 786440 | tf_op jit(solution)/shard_map/ppermute | solution.py:33
  83.3 3.4 %collective-permute-done.21 = bf16[64,2048]{1,0:T(8,128)(2,1)S(1)} collective-permute-done((bf16[64,2048]{1,0:T(8,128)(2,1)S(1)}, bf16[64,2048]{1,0:T(8,128)(2,1)S(1)}, u32[]{:S(2)}, u32[]{:S(2)}) %collective-permute-start.21) | collective-permute-done | bytes 262176 | tf_op jit(solution)/shard_map/ppermute | solution.py:33
  86.8 2.2 %tile.1 = (bf16[256,512]{1,0:T(8,128)(2,1)S(1)}, bf16[256,512]{1,0:T(8,128)(2,1)S(1)}) custom-call(s32[8]{0:T(128)S(1)} %copy-done.4, bf16[512,2048]{1,0:T(8,128)(2,1)S(1)} %constant_dynamic-update-slice_fusion.10.rows_z, bf16[512,2048]{1,0:T(8,128)(2,1)S(1)} %constant_dynamic-update-slice_fusion.15.rows_x, bf16[128,512]{1,0:T(8,128)(2,1)S(1)} %get-tuple-element.49.refs_0_, ...), custom_call_target="tpu_custom_call" | custom-call | flops 1073741824 | bytes 6291456 | tf_op jit(solution)/shard_map/tile/pallas_call | solution.py:234
  89.0 3.3 %collective-permute-start.35 = (bf16[256,512]{1,0:T(8,128)(2,1)S(1)}, bf16[256,512]{1,0:T(8,128)(2,1)S(1)}, u32[]{:S(2)}, u32[]{:S(2)}) collective-permute-start(bf16[256,512]{1,0:T(8,128)(2,1)S(1)} %get-tuple-element.58), channel_id=1, source_target_pairs={{0,64},{16,80},{32,96},{48,112},{64,0},{80,16},{96,32},{112,48},{1... | collective-permute-start | bytes 786440 | tf_op jit(solution)/shard_map/ppermute | solution.py:38
  92.6 4.3 %collective-permute-done.35 = bf16[256,512]{1,0:T(8,128)(2,1)S(1)} collective-permute-done((bf16[256,512]{1,0:T(8,128)(2,1)S(1)}, bf16[256,512]{1,0:T(8,128)(2,1)S(1)}, u32[]{:S(2)}, u32[]{:S(2)}) %collective-permute-start.35) | collective-permute-done | bytes 262176 | tf_op jit(solution)/shard_map/ppermute | solution.py:38
  98.1 2.1 %collective-permute-start.37 = (bf16[256,512]{1,0:T(8,128)(2,1)S(1)}, bf16[256,512]{1,0:T(8,128)(2,1)S(1)}, u32[]{:S(2)}, u32[]{:S(2)}) collective-permute-start(bf16[256,512]{1,0:T(8,128)(2,1)S(1)} %collective-permute-done.35), channel_id=1, source_target_pairs={{0,3},{1,0},{2,1},{3,2},{4,7},{5,4},{6,5},{7,6},{8,11},{9,8},{10,9... | collective-permute-start | bytes 786440 | tf_op jit(solution)/shard_map/ppermute | solution.py:33
  101.3 2.1 %collective-permute-start.29 = (bf16[256,512]{1,0:T(8,128)(2,1)S(1)}, bf16[256,512]{1,0:T(8,128)(2,1)S(1)}, u32[]{:S(2)}, u32[]{:S(2)}) collective-permute-start(bf16[256,512]{1,0:T(8,128)(2,1)S(1)} %collective-permute-done.27), channel_id=1, source_target_pairs={{0,3},{1,0},{2,1},{3,2},{4,7},{5,4},{6,5},{7,6},{8,11},{9,8},{10,9... | collective-permute-start | bytes 786440 | tf_op jit(solution)/shard_map/ppermute | solution.py:33
  103.5 2.4 %collective-permute-done.36 = bf16[256,512]{1,0:T(8,128)(2,1)S(1)} collective-permute-done((bf16[256,512]{1,0:T(8,128)(2,1)S(1)}, bf16[256,512]{1,0:T(8,128)(2,1)S(1)}, u32[]{:S(2)}, u32[]{:S(2)}) %collective-permute-start.36) | collective-permute-done | bytes 262176 | tf_op jit(solution)/shard_map/ppermute | solution.py:33
  106.1 3.3 %collective-permute-start.39 = (bf16[128,512]{1,0:T(8,128)(2,1)S(1)}, bf16[128,512]{1,0:T(8,128)(2,1)S(1)}, u32[]{:S(2)}, u32[]{:S(2)}) collective-permute-start(bf16[128,512]{1,0:T(8,128)(2,1)S(1)} %slice.89), channel_id=1, source_target_pairs={{0,3},{1,0},{2,1},{3,2},{4,7},{5,4},{6,5},{7,6},{8,11},{9,8},{10,9... | collective-permute-start | bytes 393224 | tf_op jit(solution)/shard_map/ppermute | solution.py:33
  109.5 3.3 %collective-permute-start.31 = (bf16[128,512]{1,0:T(8,128)(2,1)S(1)}, bf16[128,512]{1,0:T(8,128)(2,1)S(1)}, u32[]{:S(2)}, u32[]{:S(2)}) collective-permute-start(bf16[128,512]{1,0:T(8,128)(2,1)S(1)} %slice.87), channel_id=1, source_target_pairs={{0,3},{1,0},{2,1},{3,2},{4,7},{5,4},{6,5},{7,6},{8,11},{9,8},{10,9... | collective-permute-start | bytes 393224 | tf_op jit(solution)/shard_map/ppermute | solution.py:33
  116.2 2.5 %collective-permute-start.42 = (bf16[3,256,128]{2,1,0:T(8,128)(2,1)S(1)}, bf16[3,256,128]{2,1,0:T(8,128)(2,1)S(1)}, u32[]{:S(2)}, u32[]{:S(2)}) collective-permute-start(bf16[3,256,128]{2,1,0:T(8,128)(2,1)S(1)} %get-tuple-element.62), channel_id=1, source_target_pairs={{0,12},{1,13},{2,14},{3,15},{4,0},{5,1},{6,2},{7,3},{8,4},{9,5},{1... | collective-permute-start | bytes 589832 | tf_op jit(solution)/shard_map/ppermute | solution.py:33
  120.5 2.1 %collective-permute-start.33 = (bf16[3,256,128]{2,1,0:T(8,128)(2,1)S(1)}, bf16[3,256,128]{2,1,0:T(8,128)(2,1)S(1)}, u32[]{:S(2)}, u32[]{:S(2)}) collective-permute-start(bf16[3,256,128]{2,1,0:T(8,128)(2,1)S(1)} %get-tuple-element.56), channel_id=1, source_target_pairs={{0,8},{1,9},{2,10},{3,11},{4,12},{5,13},{6,14},{7,15},{8,0},{9,1},... | collective-permute-start | bytes 589832 | tf_op jit(solution)/shard_map/ppermute | solution.py:33
  125.2 2.6 %blank.1.refs_4_ = f32[4096,384]{1,0:T(8,128)} custom-call(s32[8,16]{1,0:T(8,128)S(1)} %copy-done.2), custom_call_target="tpu_custom_call" | custom-call | bytes 3145728 | tf_op jit(solution)/shard_map/blank/pallas_call | solution.py:314
  127.8 2.3 %place.2.refs_4_ = f32[4096,384]{1,0:T(8,128)} custom-call(s32[8,16]{1,0:T(8,128)S(1)} %copy-done.2, s32[8,32]{1,0:T(8,128)S(1)} %copy-done.3, bf16[3,256,128]{2,1,0:T(8,128)(2,1)S(1)} %get-tuple-element.59.refs_0_, bf16[3,256,128]{2,1,0:T(8,128)(2,1)S(1)} %collective-permute-done.40.refs_1_, ...), custom_call_target="tpu_custom_call", output_to_operand_aliasing={{}: (6, {})} | custom-call | bytes 3145728 | tf_op jit(solution)/shard_map/place/pallas_call | solution.py:367
  130.3 2.3 %place.3 = f32[4096,384]{1,0:T(8,128)} custom-call(s32[8,16]{1,0:T(8,128)S(1)} %copy-done.2, s32[8,32]{1,0:T(8,128)S(1)} %copy-done.3, bf16[3,256,128]{2,1,0:T(8,128)(2,1)S(1)} %get-tuple-element.54.refs_0_, bf16[3,256,128]{2,1,0:T(8,128)(2,1)S(1)} %collective-permute-done.32.refs_1_, ...), custom_call_target="tpu_custom_call", output_to_operand_aliasing={{}: (6, {})} | custom-call | bytes 3145728 | tf_op jit(solution)/shard_map/place/pallas_call | solution.py:367
  (120 shorter events, 24.5 us)
Async XLA Ops:
  1.7 9.1 %collective-permute-start.11 = (bf16[96,1024]{1,0:T(8,128)(2,1)S(1)}, bf16[96,1024]{1,0:T(8,128)(2,1)S(1)}, u32[]{:S(2)}, u32[]{:S(2)}) collective-permute-start(bf16[96,1024]{1,0:T(8,128)(2,1)S(1)} %bitcast.15), channel_id=1, source_target_pairs={{0,1},{1,2},{2,3},{3,0},{4,5},{5,6},{6,7},{7,4},{8,9},{9,10},{10,1... | collective-permute-start | bytes 589832 | tf_op jit(solution)/shard_map/ppermute | solution.py:33
  6.0 8.2 %collective-permute-start.3 = (bf16[96,1024]{1,0:T(8,128)(2,1)S(1)}, bf16[96,1024]{1,0:T(8,128)(2,1)S(1)}, u32[]{:S(2)}, u32[]{:S(2)}) collective-permute-start(bf16[96,1024]{1,0:T(8,128)(2,1)S(1)} %bitcast.12), channel_id=1, source_target_pairs={{0,4},{1,5},{2,6},{3,7},{4,8},{5,9},{6,10},{7,11},{8,12},{9,13},{1... | collective-permute-start | bytes 589832 | tf_op jit(solution)/shard_map/ppermute | solution.py:33
  7.5 8.3 %collective-permute-start.4 = (bf16[96,1024]{1,0:T(8,128)(2,1)S(1)}, bf16[96,1024]{1,0:T(8,128)(2,1)S(1)}, u32[]{:S(2)}, u32[]{:S(2)}) collective-permute-start(bf16[96,1024]{1,0:T(8,128)(2,1)S(1)} %bitcast.13), channel_id=1, source_target_pairs={{0,12},{1,13},{2,14},{3,15},{4,0},{5,1},{6,2},{7,3},{8,4},{9,5},{1... | collective-permute-start | bytes 589832 | tf_op jit(solution)/shard_map/ppermute | solution.py:33
  17.8 19.2 %collective-permute-start.15 = (bf16[384,1024]{1,0:T(8,128)(2,1)S(1)}, bf16[384,1024]{1,0:T(8,128)(2,1)S(1)}, u32[]{:S(2)}, u32[]{:S(2)}) collective-permute-start(bf16[384,1024]{1,0:T(8,128)(2,1)S(1)} %constant_dynamic-update-slice_fusion.5.refs_5_), channel_id=1, source_target_pairs={{0,4},{1,5},{2,6},{3,7},{4,8},{5,9},{6,10},{7,11},{8,12},{9,13},{1... | collective-permute-start | bytes 2359304 | tf_op jit(solution)/shard_map/ppermute | solution.py:33
  18.3 18.8 %collective-permute-start.16 = (bf16[384,1024]{1,0:T(8,128)(2,1)S(1)}, bf16[384,1024]{1,0:T(8,128)(2,1)S(1)}, u32[]{:S(2)}, u32[]{:S(2)}) collective-permute-start(bf16[384,1024]{1,0:T(8,128)(2,1)S(1)} %constant_dynamic-update-slice_fusion.5.refs_5_), channel_id=1, source_target_pairs={{0,12},{1,13},{2,14},{3,15},{4,0},{5,1},{6,2},{7,3},{8,4},{9,5},{1... | collective-permute-start | bytes 2359304 | tf_op jit(solution)/shard_map/ppermute | solution.py:33
  21.5 18.9 %collective-permute-start.8 = (bf16[384,1024]{1,0:T(8,128)(2,1)S(1)}, bf16[384,1024]{1,0:T(8,128)(2,1)S(1)}, u32[]{:S(2)}, u32[]{:S(2)}) collective-permute-start(bf16[384,1024]{1,0:T(8,128)(2,1)S(1)} %constant_dynamic-update-slice_fusion.refs_0_), channel_id=1, source_target_pairs={{0,3},{1,0},{2,1},{3,2},{4,7},{5,4},{6,5},{7,6},{8,11},{9,8},{10,9... | collective-permute-start | bytes 2359304 | tf_op jit(solution)/shard_map/ppermute | solution.py:33
  23.5 19.4 %collective-permute-start.7 = (bf16[384,1024]{1,0:T(8,128)(2,1)S(1)}, bf16[384,1024]{1,0:T(8,128)(2,1)S(1)}, u32[]{:S(2)}, u32[]{:S(2)}) collective-permute-start(bf16[384,1024]{1,0:T(8,128)(2,1)S(1)} %constant_dynamic-update-slice_fusion.refs_0_), channel_id=1, source_target_pairs={{0,1},{1,2},{2,3},{3,0},{4,5},{5,6},{6,7},{7,4},{8,9},{9,10},{10,1... | collective-permute-start | bytes 2359304 | tf_op jit(solution)/shard_map/ppermute | solution.py:33
  23.7 21.9 %collective-permute-start = (bf16[128,512]{1,0:T(8,128)(2,1)S(1)}, bf16[128,512]{1,0:T(8,128)(2,1)S(1)}, u32[]{:S(2)}, u32[]{:S(2)}) collective-permute-start(bf16[128,512]{1,0:T(8,128)(2,1)S(1)} %get-tuple-element.34), channel_id=1, source_target_pairs={{0,1},{1,2},{2,3},{3,0},{4,5},{5,6},{6,7},{7,4},{8,9},{9,10},{10,1... | collective-permute-start | bytes 393224 | tf_op jit(solution)/shard_map/ppermute | solution.py:33
  37.0 21.8 %collective-permute-start.17 = (bf16[192,1024]{1,0:T(8,128)(2,1)S(1)}, bf16[192,1024]{1,0:T(8,128)(2,1)S(1)}, u32[]{:S(2)}, u32[]{:S(2)}) collective-permute-start(bf16[192,1024]{1,0:T(8,128)(2,1)S(1)} %slice.80), channel_id=1, source_target_pairs={{0,4},{1,5},{2,6},{3,7},{4,8},{5,9},{6,10},{7,11},{8,12},{9,13},{1... | collective-permute-start | bytes 1179656 | tf_op jit(solution)/shard_map/ppermute | solution.py:33
  37.1 21.7 %collective-permute-start.18 = (bf16[192,1024]{1,0:T(8,128)(2,1)S(1)}, bf16[192,1024]{1,0:T(8,128)(2,1)S(1)}, u32[]{:S(2)}, u32[]{:S(2)}) collective-permute-start(bf16[192,1024]{1,0:T(8,128)(2,1)S(1)} %slice.81), channel_id=1, source_target_pairs={{0,12},{1,13},{2,14},{3,15},{4,0},{5,1},{6,2},{7,3},{8,4},{9,5},{1... | collective-permute-start | bytes 1179656 | tf_op jit(solution)/shard_map/ppermute | solution.py:33
  40.4 18.4 %collective-permute-start.10 = (bf16[192,1024]{1,0:T(8,128)(2,1)S(1)}, bf16[192,1024]{1,0:T(8,128)(2,1)S(1)}, u32[]{:S(2)}, u32[]{:S(2)}) collective-permute-start(bf16[192,1024]{1,0:T(8,128)(2,1)S(1)} %slice.77), channel_id=1, source_target_pairs={{0,3},{1,0},{2,1},{3,2},{4,7},{5,4},{6,5},{7,6},{8,11},{9,8},{10,9... | collective-permute-start | bytes 1179656 | tf_op jit(solution)/shard_map/ppermute | solution.py:33
  42.9 16.0 %collective-permute-start.9 = (bf16[192,1024]{1,0:T(8,128)(2,1)S(1)}, bf16[192,1024]{1,0:T(8,128)(2,1)S(1)}, u32[]{:S(2)}, u32[]{:S(2)}) collective-permute-start(bf16[192,1024]{1,0:T(8,128)(2,1)S(1)} %slice.76), channel_id=1, source_target_pairs={{0,1},{1,2},{2,3},{3,0},{4,5},{5,6},{6,7},{7,4},{8,9},{9,10},{10,1... | collective-permute-start | bytes 1179656 | tf_op jit(solution)/shard_map/ppermute | solution.py:33
  45.7 8.2 %collective-permute-start.1 = (bf16[128,512]{1,0:T(8,128)(2,1)S(1)}, bf16[128,512]{1,0:T(8,128)(2,1)S(1)}, u32[]{:S(2)}, u32[]{:S(2)}) collective-permute-start(bf16[128,512]{1,0:T(8,128)(2,1)S(1)} %get-tuple-element.35), channel_id=1, source_target_pairs={{0,2},{1,3},{2,0},{3,1},{4,6},{5,7},{6,4},{7,5},{8,10},{9,11},{10,... | collective-permute-start | bytes 393224 | tf_op jit(solution)/shard_map/ppermute | solution.py:33
  63.4 12.2 %collective-permute-start.23 = (bf16[128,2048]{1,0:T(8,128)(2,1)}, bf16[128,2048]{1,0:T(8,128)(2,1)S(1)}, u32[]{:S(2)}, u32[]{:S(2)}) collective-permute-start(bf16[128,2048]{1,0:T(8,128)(2,1)} %get-tuple-element.48), channel_id=1, source_target_pairs={{0,4},{1,5},{2,6},{3,7},{4,8},{5,9},{6,10},{7,11},{8,12},{9,13},{1... | collective-permute-start | bytes 1572872 | tf_op jit(solution)/shard_map/ppermute | solution.py:33
  63.7 12.0 %collective-permute-start.24 = (bf16[128,2048]{1,0:T(8,128)(2,1)}, bf16[128,2048]{1,0:T(8,128)(2,1)S(1)}, u32[]{:S(2)}, u32[]{:S(2)}) collective-permute-start(bf16[128,2048]{1,0:T(8,128)(2,1)} %get-tuple-element.48), channel_id=1, source_target_pairs={{0,12},{1,13},{2,14},{3,15},{4,0},{5,1},{6,2},{7,3},{8,4},{9,5},{1... | collective-permute-start | bytes 1572872 | tf_op jit(solution)/shard_map/ppermute | solution.py:33
  66.6 12.4 %collective-permute-start.19 = (bf16[128,2048]{1,0:T(8,128)(2,1)}, bf16[128,2048]{1,0:T(8,128)(2,1)S(1)}, u32[]{:S(2)}, u32[]{:S(2)}) collective-permute-start(bf16[128,2048]{1,0:T(8,128)(2,1)} %get-tuple-element.48), channel_id=1, source_target_pairs={{0,1},{1,2},{2,3},{3,0},{4,5},{5,6},{6,7},{7,4},{8,9},{9,10},{10,1... | collective-permute-start | bytes 1572872 | tf_op jit(solution)/shard_map/ppermute | solution.py:33
  66.6 12.5 %collective-permute-start.20 = (bf16[128,2048]{1,0:T(8,128)(2,1)}, bf16[128,2048]{1,0:T(8,128)(2,1)S(1)}, u32[]{:S(2)}, u32[]{:S(2)}) collective-permute-start(bf16[128,2048]{1,0:T(8,128)(2,1)} %get-tuple-element.48), channel_id=1, source_target_pairs={{0,3},{1,0},{2,1},{3,2},{4,7},{5,4},{6,5},{7,6},{8,11},{9,8},{10,9... | collective-permute-start | bytes 1572872 | tf_op jit(solution)/shard_map/ppermute | solution.py:33
  75.6 7.7 %collective-permute-start.25 = (bf16[64,2048]{1,0:T(8,128)(2,1)S(1)}, bf16[64,2048]{1,0:T(8,128)(2,1)S(1)}, u32[]{:S(2)}, u32[]{:S(2)}) collective-permute-start(bf16[64,2048]{1,0:T(8,128)(2,1)S(1)} %slice.84), channel_id=1, source_target_pairs={{0,4},{1,5},{2,6},{3,7},{4,8},{5,9},{6,10},{7,11},{8,12},{9,13},{1... | collective-permute-start | bytes 786440 | tf_op jit(solution)/shard_map/ppermute | solution.py:33
  79.1 7.7 %collective-permute-start.21 = (bf16[64,2048]{1,0:T(8,128)(2,1)S(1)}, bf16[64,2048]{1,0:T(8,128)(2,1)S(1)}, u32[]{:S(2)}, u32[]{:S(2)}) collective-permute-start(bf16[64,2048]{1,0:T(8,128)(2,1)S(1)} %slice.82), channel_id=1, source_target_pairs={{0,1},{1,2},{2,3},{3,0},{4,5},{5,6},{6,7},{7,4},{8,9},{9,10},{10,1... | collective-permute-start | bytes 786440 | tf_op jit(solution)/shard_map/ppermute | solution.py:33
  89.0 8.0 %collective-permute-start.35 = (bf16[256,512]{1,0:T(8,128)(2,1)S(1)}, bf16[256,512]{1,0:T(8,128)(2,1)S(1)}, u32[]{:S(2)}, u32[]{:S(2)}) collective-permute-start(bf16[256,512]{1,0:T(8,128)(2,1)S(1)} %get-tuple-element.58), channel_id=1, source_target_pairs={{0,64},{16,80},{32,96},{48,112},{64,0},{80,16},{96,32},{112,48},{1... | collective-permute-start | bytes 786440 | tf_op jit(solution)/shard_map/ppermute | solution.py:38
  92.2 8.0 %collective-permute-start.27 = (bf16[256,512]{1,0:T(8,128)(2,1)S(1)}, bf16[256,512]{1,0:T(8,128)(2,1)S(1)}, u32[]{:S(2)}, u32[]{:S(2)}) collective-permute-start(bf16[256,512]{1,0:T(8,128)(2,1)S(1)} %get-tuple-element.53), channel_id=1, source_target_pairs={{0,64},{16,80},{32,96},{48,112},{64,0},{80,16},{96,32},{112,48},{1... | collective-permute-start | bytes 786440 | tf_op jit(solution)/shard_map/ppermute | solution.py:38
  96.9 9.1 %collective-permute-start.36 = (bf16[256,512]{1,0:T(8,128)(2,1)S(1)}, bf16[256,512]{1,0:T(8,128)(2,1)S(1)}, u32[]{:S(2)}, u32[]{:S(2)}) collective-permute-start(bf16[256,512]{1,0:T(8,128)(2,1)S(1)} %collective-permute-done.35), channel_id=1, source_target_pairs={{0,1},{1,2},{2,3},{3,0},{4,5},{5,6},{6,7},{7,4},{8,9},{9,10},{10,1... | collective-permute-start | bytes 786440 | tf_op jit(solution)/shard_map/ppermute | solution.py:33
  98.1 7.9 %collective-permute-start.37 = (bf16[256,512]{1,0:T(8,128)(2,1)S(1)}, bf16[256,512]{1,0:T(8,128)(2,1)S(1)}, u32[]{:S(2)}, u32[]{:S(2)}) collective-permute-start(bf16[256,512]{1,0:T(8,128)(2,1)S(1)} %collective-permute-done.35), channel_id=1, source_target_pairs={{0,3},{1,0},{2,1},{3,2},{4,7},{5,4},{6,5},{7,6},{8,11},{9,8},{10,9... | collective-permute-start | bytes 786440 | tf_op jit(solution)/shard_map/ppermute | solution.py:33
  100.2 9.2 %collective-permute-start.28 = (bf16[256,512]{1,0:T(8,128)(2,1)S(1)}, bf16[256,512]{1,0:T(8,128)(2,1)S(1)}, u32[]{:S(2)}, u32[]{:S(2)}) collective-permute-start(bf16[256,512]{1,0:T(8,128)(2,1)S(1)} %collective-permute-done.27), channel_id=1, source_target_pairs={{0,1},{1,2},{2,3},{3,0},{4,5},{5,6},{6,7},{7,4},{8,9},{9,10},{10,1... | collective-permute-start | bytes 786440 | tf_op jit(solution)/shard_map/ppermute | solution.py:33
  101.3 8.2 %collective-permute-start.29 = (bf16[256,512]{1,0:T(8,128)(2,1)S(1)}, bf16[256,512]{1,0:T(8,128)(2,1)S(1)}, u32[]{:S(2)}, u32[]{:S(2)}) collective-permute-start(bf16[256,512]{1,0:T(8,128)(2,1)S(1)} %collective-permute-done.27), channel_id=1, source_target_pairs={{0,3},{1,0},{2,1},{3,2},{4,7},{5,4},{6,5},{7,6},{8,11},{9,8},{10,9... | collective-permute-start | bytes 786440 | tf_op jit(solution)/shard_map/ppermute | solution.py:33
  109.4 9.4 %collective-permute-start.30 = (bf16[128,512]{1,0:T(8,128)(2,1)S(1)}, bf16[128,512]{1,0:T(8,128)(2,1)S(1)}, u32[]{:S(2)}, u32[]{:S(2)}) collective-permute-start(bf16[128,512]{1,0:T(8,128)(2,1)S(1)} %slice.86), channel_id=1, source_target_pairs={{0,1},{1,2},{2,3},{3,0},{4,5},{5,6},{6,7},{7,4},{8,9},{9,10},{10,1... | collective-permute-start | bytes 393224 | tf_op jit(solution)/shard_map/ppermute | solution.py:33
  109.5 9.3 %collective-permute-start.31 = (bf16[128,512]{1,0:T(8,128)(2,1)S(1)}, bf16[128,512]{1,0:T(8,128)(2,1)S(1)}, u32[]{:S(2)}, u32[]{:S(2)}) collective-permute-start(bf16[128,512]{1,0:T(8,128)(2,1)S(1)} %slice.87), channel_id=1, source_target_pairs={{0,3},{1,0},{2,1},{3,2},{4,7},{5,4},{6,5},{7,6},{8,11},{9,8},{10,9... | collective-permute-start | bytes 393224 | tf_op jit(solution)/shard_map/ppermute | solution.py:33
  114.6 9.1 %collective-permute-start.40 = (bf16[3,256,128]{2,1,0:T(8,128)(2,1)S(1)}, bf16[3,256,128]{2,1,0:T(8,128)(2,1)S(1)}, u32[]{:S(2)}, u32[]{:S(2)}) collective-permute-start(bf16[3,256,128]{2,1,0:T(8,128)(2,1)S(1)} %get-tuple-element.60), channel_id=1, source_target_pairs={{0,4},{1,5},{2,6},{3,7},{4,8},{5,9},{6,10},{7,11},{8,12},{9,13},{1... | collective-permute-start | bytes 589832 | tf_op jit(solution)/shard_map/ppermute | solution.py:33
  114.7 13.1 %collective-permute-start.41 = (bf16[3,256,128]{2,1,0:T(8,128)(2,1)S(1)}, bf16[3,256,128]{2,1,0:T(8,128)(2,1)S(1)}, u32[]{:S(2)}, u32[]{:S(2)}) collective-permute-start(bf16[3,256,128]{2,1,0:T(8,128)(2,1)S(1)} %get-tuple-element.61), channel_id=1, source_target_pairs={{0,8},{1,9},{2,10},{3,11},{4,12},{5,13},{6,14},{7,15},{8,0},{9,1},... | collective-permute-start | bytes 589832 | tf_op jit(solution)/shard_map/ppermute | solution.py:33
  116.2 11.6 %collective-permute-start.42 = (bf16[3,256,128]{2,1,0:T(8,128)(2,1)S(1)}, bf16[3,256,128]{2,1,0:T(8,128)(2,1)S(1)}, u32[]{:S(2)}, u32[]{:S(2)}) collective-permute-start(bf16[3,256,128]{2,1,0:T(8,128)(2,1)S(1)} %get-tuple-element.62), channel_id=1, source_target_pairs={{0,12},{1,13},{2,14},{3,15},{4,0},{5,1},{6,2},{7,3},{8,4},{9,5},{1... | collective-permute-start | bytes 589832 | tf_op jit(solution)/shard_map/ppermute | solution.py:33
  120.4 9.6 %collective-permute-start.32 = (bf16[3,256,128]{2,1,0:T(8,128)(2,1)S(1)}, bf16[3,256,128]{2,1,0:T(8,128)(2,1)S(1)}, u32[]{:S(2)}, u32[]{:S(2)}) collective-permute-start(bf16[3,256,128]{2,1,0:T(8,128)(2,1)S(1)} %get-tuple-element.55), channel_id=1, source_target_pairs={{0,4},{1,5},{2,6},{3,7},{4,8},{5,9},{6,10},{7,11},{8,12},{9,13},{1... | collective-permute-start | bytes 589832 | tf_op jit(solution)/shard_map/ppermute | solution.py:33
  120.5 9.6 %collective-permute-start.33 = (bf16[3,256,128]{2,1,0:T(8,128)(2,1)S(1)}, bf16[3,256,128]{2,1,0:T(8,128)(2,1)S(1)}, u32[]{:S(2)}, u32[]{:S(2)}) collective-permute-start(bf16[3,256,128]{2,1,0:T(8,128)(2,1)S(1)} %get-tuple-element.56), channel_id=1, source_target_pairs={{0,8},{1,9},{2,10},{3,11},{4,12},{5,13},{6,14},{7,15},{8,0},{9,1},... | collective-permute-start | bytes 589832 | tf_op jit(solution)/shard_map/ppermute | solution.py:33
  (16 other events, 160.0 us)

commit v3 on v2

v3 whole, which is shorter than its diff:
```python
import functools

import jax
import jax.numpy as jnp
from jax import lax
from jax.experimental import pallas as pl
from jax.experimental.pallas import tpu as pltpu
from jax.sharding import PartitionSpec as P

PANEL = 1024
BLOCK = 128
SLOTS = 3
SIDE = 4
FRONT = SIDE * SIDE
CONTRIB = BLOCK * FRONT
ROWS = PANEL // FRONT
MIB = 1024 * 1024


def dot_nt(left, right):
    return lax.dot_general(
        left, right, (((1,), (1,)), ((), ())), preferred_element_type=jnp.float32
    )


def shift(value, axis, by):
    dx, dz = (by, 0) if axis == "x" else (0, by)
    pairs = [
        (x * SIDE + z, (x + dx) % SIDE * SIDE + (z + dz) % SIDE)
        for x in range(SIDE)
        for z in range(SIDE)
    ]
    return lax.ppermute(value, "front", pairs)


def to_parent(value):
    groups = lax.axis_size("leaf")
    return lax.ppermute(
        value, "leaf", [(g, (g + groups // 2) % groups) for g in range(groups)]
    )


RING = (0, -1, 1, 2)


def bundle_of(own, axis):
    half = own.shape[0] // 2
    from_left = shift(own, axis, 1)
    from_right = shift(own, axis, -1)
    far_top = shift(from_left[:half], axis, 1)
    far_bottom = shift(from_right[half:], axis, -1)
    return jnp.concatenate([own, from_left, from_right, far_top, far_bottom], axis=0)


def spread(bundle, axis):
    half = bundle.shape[0] // 2
    left = shift(bundle, axis, 1)
    right = shift(bundle, axis, -1)
    far_low = shift(left[:half], axis, 1)
    far_high = shift(right[half:], axis, -1)
    return [bundle, left, right, far_low, far_high]


def places(x_first):
    found = []
    for part, second in ((RING, 0), (RING, -1), (RING, 1), (RING[:2], 2), (RING[2:], 2)):
        found.append([(first, second) if x_first else (second, first) for first in part])
    return found


X_FIRST, Z_FIRST = places(True), places(False)


def place_of(front, dx, dz):
    x, z = front // SIDE, front % SIDE
    return lax.rem(x + dx + SIDE, SIDE) * SIDE + lax.rem(z + dz + SIDE, SIDE)


def family():
    groups = lax.axis_size("leaf")
    parent = lax.axis_index("leaf")
    return parent, lax.rem(parent + groups // 2, groups), lax.axis_index("front")


def unpack_inverses(front, bundles, mats):
    z = lax.rem(front, SIDE)
    for bundle, dz, start in zip(bundles, (0, -1, 1, 2, 2), (0, 0, 0, 0, CHUNKS // 2), strict=True):
        place = lax.rem(z + dz + SIDE, SIDE) * ROWS
        for at in range(bundle.shape[0] // (2 * ROWS)):
            x, chunk = LOWER[start + at]
            row = pl.multiple_of(place + x * SIDE * ROWS, ROWS)
            for which in range(2):
                top = (at * 2 + which) * ROWS
                mats[which, pl.ds(row, ROWS), chunk * WIDE : (chunk + 1) * WIDE] = bundle[
                    top : top + ROWS, :
                ]


def unpack_panel(front, bundles, mat):
    for bundle, blocks in zip(bundles, Z_FIRST, strict=True):
        for at, (dx, dz) in enumerate(blocks):
            row = pl.multiple_of(place_of(front, dx, dz) * ROWS, ROWS)
            mat[pl.ds(row, ROWS), :] = bundle[at * ROWS : (at + 1) * ROWS, :]


WIDE = SIDE * ROWS
LOWER = [(x, chunk) for x in range(SIDE) for chunk in range(x + 1)]
CHUNKS = len(LOWER)


def project(rows, inverse, keep):
    for at in range(0, PANEL, WIDE):
        upto = at + WIDE
        keep(at, dot_nt(rows[:, :upto], inverse[at:upto, :upto]))


def lower_kernel(*refs):
    sources, out = refs[:5], refs[5]
    x = lax.axis_index("front") // SIDE
    blocks = [(sources[0], 0, 0), (sources[1], 0, -1), (sources[2], 0, 1)]
    blocks += [(sources[3], 0, 2), (sources[4], 1, 2)]
    for source, first, dx in blocks:
        from_x = lax.rem(x + dx + SIDE, SIDE)
        start = (from_x * (from_x + 1)) // 2
        for chunk in range(SIDE):

            @pl.when(chunk <= from_x)
            def _():
                row = pl.multiple_of((start + chunk) * 2 * ROWS + first * ROWS, ROWS)
                out[pl.ds(row, source.shape[0]), :] = source[:, chunk * WIDE : (chunk + 1) * WIDE]


def lower_chunks(own, left, right, far_first, far_second):
    return pl.pallas_call(
        lower_kernel,
        out_shape=jax.ShapeDtypeStruct((CHUNKS * 2 * ROWS, WIDE), jnp.bfloat16),
        in_specs=[VMEM_SPEC] * 5,
        out_specs=VMEM_SPEC,
        compiler_params=pltpu.CompilerParams(vmem_limit_bytes=4 * MIB),
        cost_estimate=pl.CostEstimate(flops=0, bytes_accessed=MIB, transcendentals=0),
        name="lower",
    )(own, left, right, far_first, far_second)


def panel_kernel(border, *refs):
    inverses, panels, (link_out, factor) = refs[:5], refs[5:10], refs[10:12]
    mats, panel, link, updated = refs[12:]
    front = lax.axis_index("front")
    unpack_inverses(front, inverses, mats)

    def keep_first(at, value):
        factor[:, at : at + WIDE] = value.astype(jnp.bfloat16)

    def keep_link(at, value):
        link[:, at : at + WIDE] = value.astype(jnp.bfloat16)

    def keep_second(at, value):
        factor[:, PANEL + at : PANEL + at + WIDE] = value.astype(jnp.bfloat16)

    project(border, mats.at[0], keep_first)
    unpack_panel(front, panels, panel)
    project(panel, mats.at[0], keep_link)
    link_out[...] = link[pl.ds(pl.multiple_of(front * ROWS, ROWS), ROWS), :]
    for at in range(0, PANEL, WIDE):
        coupled = dot_nt(factor[:, :PANEL], link[at : at + WIDE, :])
        updated[:, at : at + WIDE] = (
            border[:, PANEL + at : PANEL + at + WIDE].astype(jnp.float32) - coupled
        ).astype(jnp.bfloat16)
    project(updated, mats.at[1], keep_second)


VMEM_SPEC = pl.BlockSpec(memory_space=pltpu.VMEM)
SMEM_SPEC = pl.BlockSpec(memory_space=pltpu.SMEM)


def eliminate(border, inverses, panels):
    return pl.pallas_call(
        panel_kernel,
        out_shape=(
            jax.ShapeDtypeStruct((ROWS, PANEL), jnp.bfloat16),
            jax.ShapeDtypeStruct((BLOCK, 2 * PANEL), jnp.bfloat16),
        ),
        in_specs=[VMEM_SPEC] * 11,
        out_specs=(VMEM_SPEC,) * 2,
        scratch_shapes=[
            pltpu.VMEM((2, PANEL, PANEL), jnp.bfloat16),
            pltpu.VMEM((PANEL, PANEL), jnp.bfloat16),
            pltpu.VMEM((PANEL, PANEL), jnp.bfloat16),
            pltpu.VMEM((BLOCK, PANEL), jnp.bfloat16),
        ],
        compiler_params=pltpu.CompilerParams(vmem_limit_bytes=16 * MIB),
        cost_estimate=pl.CostEstimate(
            flops=2 * PANEL**3 + 6 * BLOCK * PANEL**2,
            bytes_accessed=8 * MIB,
            transcendentals=0,
        ),
        name="panels",
    )(border, *inverses, *panels)


LINE = SIDE * BLOCK
CHUNKS_OF_ROWS = ((0, 1), (2, 3))
HALF = ROWS // 2
TAIL_AT, PANEL_AT, ON_AT, MESSAGE = 0, ROWS, 2 * ROWS - HALF, 2 * ROWS + HALF


def message_kernel(tail, panel, up, down, kept):
    z = lax.rem(lax.axis_index("front"), SIDE)

    def columns(step, x):
        at = pl.multiple_of((x * SIDE + lax.rem(z + step, SIDE)) * BLOCK, BLOCK)
        return tail[:, pl.ds(at, BLOCK)]

    for x in range(SIDE):
        here = slice(x * BLOCK, (x + 1) * BLOCK)
        there = slice(LINE + x * BLOCK, LINE + (x + 1) * BLOCK)
        kept[:, here] = columns(0, x)
        for step, out in ((1, up), (SIDE - 1, down)):
            block = columns(step, x)
            out[:ROWS, here] = block[:ROWS]
            out[:ROWS, there] = block[ROWS:]
        block = columns(2, x)
        for part, out in enumerate((up, down)):
            first = part * ROWS
            out[2 * ROWS :, here] = block[first : first + HALF]
            out[2 * ROWS :, there] = block[first + HALF : first + ROWS]
    up[ROWS : ROWS + HALF] = panel[HALF:]
    up[ROWS + HALF : 2 * ROWS] = panel[:HALF]
    down[ROWS : ROWS + HALF] = panel[:HALF]
    down[ROWS + HALF : 2 * ROWS] = panel[HALF:]


def make_messages(tail, panel):
    message = jax.ShapeDtypeStruct((MESSAGE, PANEL), jnp.bfloat16)
    return pl.pallas_call(
        message_kernel,
        out_shape=(message, message, jax.ShapeDtypeStruct((BLOCK, LINE), jnp.bfloat16)),
        in_specs=[VMEM_SPEC] * 2,
        out_specs=(VMEM_SPEC,) * 3,
        compiler_params=pltpu.CompilerParams(vmem_limit_bytes=4 * MIB),
        cost_estimate=pl.CostEstimate(flops=0, bytes_accessed=2 * MIB, transcendentals=0),
        name="messages",
    )(tail, panel)


def tile_kernel(chunk, sizes, rows_z, rows_x, *refs):
    (kept, low, high, far_low, far_high), (out, product, tails, rows) = refs[:5], refs[5:]
    front = lax.axis_index("front")
    live = sizes[lax.axis_index("leaf")]
    x, z = front // SIDE, lax.rem(front, SIDE)
    lane = lax.broadcasted_iota(jnp.int32, (BLOCK, BLOCK), 1)
    line = lax.broadcasted_iota(jnp.int32, (BLOCK, BLOCK), 0)
    tails[0] = kept[...]
    for step, source in ((1, low), (SIDE - 1, high)):
        tails[step, :ROWS] = source[:ROWS, :LINE]
        tails[step, ROWS:] = source[:ROWS, LINE:]
    for part, source in enumerate((far_low, far_high)):
        first = part * ROWS
        tails[2, first : first + HALF] = source[HALF:, :LINE]
        tails[2, first + HALF : first + ROWS] = source[HALF:, LINE:]
    for up, row_z in enumerate(chunk):
        away = lax.rem(row_z - z + SIDE, SIDE)
        at = jnp.where(away == 0, 0, jnp.where(away == SIDE - 1, 1, away + 1))
        at = pl.multiple_of(at * BLOCK, BLOCK)
        rows[up * BLOCK : (up + 1) * BLOCK, :] = rows_z[pl.ds(at, BLOCK), :]
    for at in range(0, LINE, WIDE):
        product[:, at : at + WIDE] = dot_nt(rows[...], rows_x[at : at + WIDE, :])
    for up, row_z in enumerate(chunk):
        step = lax.rem(z - row_z + SIDE, SIDE)
        for across, dx in enumerate(RING):
            col_x = lax.rem(x + dx + SIDE, SIDE)
            columns = slice(across * BLOCK, (across + 1) * BLOCK)
            keep = (line + (x * SIDE + row_z) * BLOCK < live) & (
                lane + (col_x * SIDE + z) * BLOCK < live
            )
            old = tails[step, :, pl.ds(pl.multiple_of(col_x * BLOCK, BLOCK), BLOCK)]
            schur = old.astype(jnp.float32) - product[up * BLOCK : (up + 1) * BLOCK, columns]
            out[up * BLOCK : (up + 1) * BLOCK, columns] = jnp.where(keep, schur, 0.0).astype(
                jnp.bfloat16
            )


def make_tile(chunk, sizes, rows_z, rows_x, tails):
    rows = len(chunk) * BLOCK
    return pl.pallas_call(
        functools.partial(tile_kernel, chunk),
        out_shape=jax.ShapeDtypeStruct((rows, LINE), jnp.bfloat16),
        in_specs=[SMEM_SPEC] + [VMEM_SPEC] * 7,
        out_specs=VMEM_SPEC,
        scratch_shapes=[
            pltpu.VMEM((rows, LINE), jnp.float32),
            pltpu.VMEM((SIDE, BLOCK, LINE), jnp.bfloat16),
            pltpu.VMEM((rows, 2 * PANEL), jnp.bfloat16),
        ],
        compiler_params=pltpu.CompilerParams(vmem_limit_bytes=8 * MIB),
        cost_estimate=pl.CostEstimate(
            flops=4 * rows * LINE * PANEL, bytes_accessed=5 * MIB, transcendentals=0
        ),
        name="tile",
    )(sizes, rows_z, rows_x, *tails)


def pack_kernel(block_map, block_owner, line, out):
    parent, child, front = family()
    x, z = front // SIDE, lax.rem(front, SIDE)
    rows = line.shape[0] // SIDE
    for up, dz in enumerate(RING):
        for across, dx in enumerate(RING):
            block = place_of(front, dx, dz)
            slot = block_owner[parent, block_map[child, block]]
            owner = slot // SLOTS

            @pl.when(lax.rem(owner, SIDE) == z)
            def _():
                step = lax.rem(owner // SIDE - x + SIDE, SIDE)
                out[step, lax.rem(slot, SLOTS)] = line[
                    up * rows : (up + 1) * rows, across * BLOCK : (across + 1) * BLOCK
                ]


def pack_tiles(block_map, block_owner, line):
    return pl.pallas_call(
        pack_kernel,
        out_shape=jax.ShapeDtypeStruct(
            (SIDE, SLOTS, line.shape[0] // SIDE, BLOCK), jnp.bfloat16
        ),
        in_specs=[SMEM_SPEC, SMEM_SPEC, VMEM_SPEC],
        out_specs=VMEM_SPEC,
        compiler_params=pltpu.CompilerParams(vmem_limit_bytes=4 * MIB),
        cost_estimate=pl.CostEstimate(flops=0, bytes_accessed=2 * MIB, transcendentals=0),
        name="pack",
    )(block_map, block_owner, line)


def blank_kernel(block_map, out, blank, taken, sem):
    _, child, _ = family()
    blank[...] = jnp.zeros_like(blank)

    @pl.loop(0, 2 * FRONT)
    def _(block):
        taken[block] = 0

    @pl.loop(0, FRONT)
    def _(block):
        taken[block_map[child, block]] = 1

    def copy(block):
        row = pl.multiple_of(block * BLOCK, BLOCK)
        return pltpu.make_async_copy(blank, out.at[pl.ds(row, BLOCK), :], sem)

    @pl.loop(0, 2 * FRONT)
    def _(block):
        @pl.when(taken[block] == 0)
        def _():
            copy(block).start()

    @pl.loop(0, FRONT)
    def _(block):
        copy(0).wait()


PARENT = jax.ShapeDtypeStruct((2 * CONTRIB, SLOTS * BLOCK), jnp.float32)
HELD = pl.BlockSpec(memory_space=pl.ANY)


def blank_rows(block_map):
    return pl.pallas_call(
        blank_kernel,
        out_shape=PARENT,
        in_specs=[SMEM_SPEC],
        out_specs=HELD,
        scratch_shapes=[
            pltpu.VMEM((BLOCK, SLOTS * BLOCK), jnp.float32),
            pltpu.SMEM((2 * FRONT,), jnp.int32),
            pltpu.SemaphoreType.DMA,
        ],
        compiler_params=pltpu.CompilerParams(vmem_limit_bytes=2 * MIB),
        cost_estimate=pl.CostEstimate(flops=0, bytes_accessed=3 * MIB, transcendentals=0),
        name="blank",
    )(block_map)


def place_kernel(chunk, block_map, block_owner, *refs):
    tiles, (out, staged, held, sems) = refs[:SIDE], refs[SIDE + 1 :]
    parent, child, front = family()
    for slot in range(SLOTS):
        held[slot] = 0

    @pl.loop(0, FRONT)
    def _(block):
        slot = block_owner[parent, block_map[child, block]]

        @pl.when(slot // SLOTS == front)
        def _():
            held[lax.rem(slot, SLOTS)] = 1

    none = lax.broadcasted_iota(jnp.int32, (BLOCK, BLOCK), 0) * 0
    copies = []
    for step, tile in enumerate(tiles):
        x = lax.rem(front // SIDE - step + SIDE, SIDE)
        for up, row_z in enumerate(chunk):
            block = x * SIDE + row_z
            here = len(copies)
            for slot in range(SLOTS):
                value = tile[slot, up * BLOCK : (up + 1) * BLOCK, :].astype(jnp.float32)
                staged[here, :, slot * BLOCK : (slot + 1) * BLOCK] = jnp.where(
                    none + held[slot] > 0, value, 0.0
                )
            row = pl.multiple_of(block_map[child, block] * BLOCK, BLOCK)
            copy = pltpu.make_async_copy(
                staged.at[here], out.at[pl.ds(row, BLOCK), :], sems.at[here]
            )
            copy.start()
            copies.append(copy)
    for copy in copies:
        copy.wait()


def place_tiles(chunk, block_map, block_owner, tiles, parent_rows):
    return pl.pallas_call(
        functools.partial(place_kernel, chunk),
        out_shape=PARENT,
        in_specs=[SMEM_SPEC] * 2 + [VMEM_SPEC] * SIDE + [HELD],
        out_specs=HELD,
        scratch_shapes=[
            pltpu.VMEM((len(chunk) * SIDE, BLOCK, SLOTS * BLOCK), jnp.float32),
            pltpu.SMEM((SLOTS,), jnp.int32),
            pltpu.SemaphoreType.DMA((len(chunk) * SIDE,)),
        ],
        input_output_aliases={2 + SIDE: 0},
        compiler_params=pltpu.CompilerParams(vmem_limit_bytes=6 * MIB),
        cost_estimate=pl.CostEstimate(flops=0, bytes_accessed=3 * MIB, transcendentals=0),
        name="place",
    )(block_map, block_owner, *tiles, parent_rows)


def per_device(inv_factors, panel_rows, border, tail, front_sizes, block_map, block_owner):
    inverses = inv_factors[0].reshape(2 * ROWS, PANEL)
    left, right = shift(inverses, "x", 1), shift(inverses, "x", -1)
    up, down, kept = make_messages(tail[0], panel_rows[0])
    low, high = shift(up, "z", 1), shift(down, "z", -1)
    far_first = shift(left[:ROWS], "x", 1)
    far_second = shift(right[ROWS:], "x", -1)
    far_low = shift(low[ON_AT:], "z", 1)
    far_high = shift(high[ON_AT:], "z", -1)

    chunks = spread(lower_chunks(inverses, left, right, far_first, far_second), "z")
    middle = slice(PANEL_AT, ON_AT)
    last = slice(ON_AT, 2 * ROWS)
    panels = [panel_rows[0], low[last], low[middle], high[middle], high[last]]
    panels = spread(jnp.concatenate(panels + [far_low[:HALF], far_high[:HALF]], axis=0), "x")
    blanked = blank_rows(block_map)
    chunks, blanked = lax.optimization_barrier((chunks, blanked))
    link_local, factor_local = eliminate(border[0], chunks, panels)

    rows_z, rows_x = bundle_of(factor_local, "z"), bundle_of(factor_local, "x")
    tails = (kept, low, high, far_low, far_high)

    update = blanked
    for chunk in CHUNKS_OF_ROWS:
        rows = make_tile(chunk, front_sizes, rows_z, rows_x, tails)
        line = bundle_of(to_parent(rows), "z")
        packed = pack_tiles(block_map, block_owner, line)
        tiles = [packed[0]] + [shift(packed[step], "x", step) for step in range(1, SIDE)]
        update = place_tiles(chunk, block_map, block_owner, tiles, update)
    return link_local[None], factor_local[None], update[None]


def solution(mesh):
    return jax.shard_map(
        per_device,
        mesh=mesh,
        in_specs=(
            P("leaf", None, "front", None),
            P("leaf", "front", None),
            P("leaf", "front", None),
            P("leaf", "front", None),
            P(),
            P(),
            P(),
        ),
        out_specs=(P("leaf", "front", None), P("leaf", "front", None), P("leaf", None, "front")),
        check_vma=False,
    )
```

time: 133 us -> 125 us (0.940)
  waiting for transfers between devices: 47.6 us -> 34.2 us
  starting transfers between devices: 63.3 us -> 67.2 us
  local copies, waits for them, and re-layouts: 2.15 us -> 4.98 us
    ppermute x41 -> x38, waiting for transfers between devices: 43.3 us -> 29.9 us  [shift(): return lax.ppermute(value, 'front', pairs)]
    ppermute x41 -> x38, starting transfers between devices: 59.7 us -> 63.6 us  [shift(): return lax.ppermute(value, 'front', pairs)]
    unnamed x34, local copies, waits for them, and re-layouts: 1.82 us -> 4.56 us
    pallas_call x6 -> x7, Pallas kernels: 10 us -> 9.84 us  [the longest x1 4.51 us: eliminate(): pl.pallas_call(panel_kernel, out_shape=(jax.ShapeDtypeStruct((ROWS, PANEL...]
  transfers between devices with their start and end apart: 43 -> 40, of which waited for: 14 -> 16; matrix products, arithmetic and copies ran while one was open for 2% -> 2% of each run, Pallas kernels for 6% -> 6%
where the time goes in v3:
time: 125 us
  starting transfers between devices  67.2 us (54%)
  waiting for transfers between devices  34.2 us (27%)
  Pallas kernels  16.9 us (14%)
  local copies, waits for them, and re-layouts  4.98 us (4%)
  between operations  1.32 us (1%)
    ppermute x38, starting transfers between devices, shift(): return lax.ppermute(value, 'front', pairs)  63.6 us
    ppermute x38, waiting for transfers between devices, shift(): return lax.ppermute(value, 'front', pairs)  29.9 us
    unnamed x34, local copies, waits for them, and re-layouts  4.56 us
    pallas_call x2, Pallas kernels, place_tiles(): pl.pallas_call(functools.partial(place_kernel, chunk), out_shape=PARENT,...  4.52 us
    pallas_call x1, Pallas kernels, eliminate(): pl.pallas_call(panel_kernel, out_shape=(jax.ShapeDtypeStruct((ROWS, PANEL...  4.51 us
    ppermute x2, waiting for transfers between devices, to_parent(): lax.ppermute(value, 'leaf', [(g, (g + groups // 2) % groups) for g in ran...  4.3 us
    ppermute x2, starting transfers between devices, to_parent(): lax.ppermute(value, 'leaf', [(g, (g + groups // 2) % groups) for g in ran...  3.69 us
    pallas_call x2, Pallas kernels, make_tile(): pl.pallas_call(functools.partial(tile_kernel, chunk), out_shape=jax.Shape...  2.58 us
  transfers between devices with their start and end apart: 40, of which 16 were waited for; matrix products, arithmetic and copies ran while one was open for 2% of the time, Pallas kernels for 6%

profile of v3, /device:TPU:0, one launch (start us, length us, event | category | flops | bytes accessed | tf_op | source)
XLA Modules:
  0.0 124.7 jit_solution(9806014257693559055)
XLA Ops:
  2.7 2.1 %collective-permute-start.8 = (bf16[160,1024]{1,0:T(8,128)(2,1)S(1)}, bf16[160,1024]{1,0:T(8,128)(2,1)S(1)}, u32[]{:S(2)}, u32[]{:S(2)}) collective-permute-start(bf16[160,1024]{1,0:T(8,128)(2,1)S(1)} %get-tuple-element.19), channel_id=1, source_target_pairs={{0,1},{1,2},{2,3},{3,0},{4,5},{5,6},{6,7},{7,4},{8,9},{9,10},{10,1... | collective-permute-start | bytes 983048 | tf_op jit(solution)/shard_map/ppermute | solution.py:33
  4.8 1.5 %collective-permute-start = (bf16[128,1024]{1,0:T(8,128)(2,1)}, bf16[128,1024]{1,0:T(8,128)(2,1)S(1)}, u32[]{:S(2)}, u32[]{:S(2)}) collective-permute-start(bf16[128,1024]{1,0:T(8,128)(2,1)} %bitcast.26), channel_id=1, source_target_pairs={{0,4},{1,5},{2,6},{3,7},{4,8},{5,9},{6,10},{7,11},{8,12},{9,13},{1... | collective-permute-start | bytes 786440 | tf_op jit(solution)/shard_map/ppermute | solution.py:33
  6.3 1.7 %collective-permute-start.1 = (bf16[128,1024]{1,0:T(8,128)(2,1)}, bf16[128,1024]{1,0:T(8,128)(2,1)S(1)}, u32[]{:S(2)}, u32[]{:S(2)}) collective-permute-start(bf16[128,1024]{1,0:T(8,128)(2,1)} %bitcast.27), channel_id=1, source_target_pairs={{0,12},{1,13},{2,14},{3,15},{4,0},{5,1},{6,2},{7,3},{8,4},{9,5},{1... | collective-permute-start | bytes 786440 | tf_op jit(solution)/shard_map/ppermute | solution.py:33
  8.0 2.2 %collective-permute-start.9 = (bf16[160,1024]{1,0:T(8,128)(2,1)S(1)}, bf16[160,1024]{1,0:T(8,128)(2,1)S(1)}, u32[]{:S(2)}, u32[]{:S(2)}) collective-permute-start(bf16[160,1024]{1,0:T(8,128)(2,1)S(1)} %get-tuple-element.20), channel_id=1, source_target_pairs={{0,3},{1,0},{2,1},{3,2},{4,7},{5,4},{6,5},{7,6},{8,11},{9,8},{10,9... | collective-permute-start | bytes 983048 | tf_op jit(solution)/shard_map/ppermute | solution.py:33
  11.2 2.8 %collective-permute-done.refs_1_ = bf16[128,1024]{1,0:T(8,128)(2,1)S(1)} collective-permute-done((bf16[128,1024]{1,0:T(8,128)(2,1)}, bf16[128,1024]{1,0:T(8,128)(2,1)S(1)}, u32[]{:S(2)}, u32[]{:S(2)}) %collective-permute-start) | collective-permute-done | bytes 262176 | tf_op jit(solution)/shard_map/ppermute | solution.py:33
  14.4 3.0 %collective-permute-start.3 = (bf16[64,1024]{1,0:T(8,128)(2,1)S(1)}, bf16[64,1024]{1,0:T(8,128)(2,1)S(1)}, u32[]{:S(2)}, u32[]{:S(2)}) collective-permute-start(bf16[64,1024]{1,0:T(8,128)(2,1)S(1)} %slice.119), channel_id=1, source_target_pairs={{0,12},{1,13},{2,14},{3,15},{4,0},{5,1},{6,2},{7,3},{8,4},{9,5},{1... | collective-permute-start | bytes 393224 | tf_op jit(solution)/shard_map/ppermute | solution.py:33
  17.4 2.0 %collective-permute-start.10 = (bf16[64,1024]{1,0:T(8,128)(2,1)S(1)}, bf16[64,1024]{1,0:T(8,128)(2,1)S(1)}, u32[]{:S(2)}, u32[]{:S(2)}) collective-permute-start(bf16[64,1024]{1,0:T(8,128)(2,1)S(1)} %slice.125), channel_id=1, source_target_pairs={{0,1},{1,2},{2,3},{3,0},{4,5},{5,6},{6,7},{7,4},{8,9},{9,10},{10,1... | collective-permute-start | bytes 393224 | tf_op jit(solution)/shard_map/ppermute | solution.py:33
  22.4 1.9 %collective-permute-start.5 = (bf16[1280,256]{1,0:T(8,128)(2,1)S(1)}, bf16[1280,256]{1,0:T(8,128)(2,1)S(1)}, u32[]{:S(2)}, u32[]{:S(2)}) collective-permute-start(bf16[1280,256]{1,0:T(8,128)(2,1)S(1)} %lower.1.refs_0_), channel_id=1, source_target_pairs={{0,3},{1,0},{2,1},{3,2},{4,7},{5,4},{6,5},{7,6},{8,11},{9,8},{10,9... | collective-permute-start | bytes 1966088 | tf_op jit(solution)/shard_map/ppermute | solution.py:33
  25.9 3.2 %collective-permute-start.13 = (bf16[256,1024]{1,0:T(8,128)(2,1)S(1)}, bf16[256,1024]{1,0:T(8,128)(2,1)S(1)}, u32[]{:S(2)}, u32[]{:S(2)}) collective-permute-start(bf16[256,1024]{1,0:T(8,128)(2,1)S(1)} %slice_dynamic-update-slice_fusion.1.refs_5_), channel_id=1, source_target_pairs={{0,12},{1,13},{2,14},{3,15},{4,0},{5,1},{6,2},{7,3},{8,4},{9,5},{1... | collective-permute-start | bytes 1572872 | tf_op jit(solution)/shard_map/ppermute | solution.py:33
  29.1 8.6 %collective-permute-done.4.refs_1_ = bf16[1280,256]{1,0:T(8,128)(2,1)S(1)} collective-permute-done((bf16[1280,256]{1,0:T(8,128)(2,1)S(1)}, bf16[1280,256]{1,0:T(8,128)(2,1)S(1)}, u32[]{:S(2)}, u32[]{:S(2)}) %collective-permute-start.4) | collective-permute-done | bytes 655392 | tf_op jit(solution)/shard_map/ppermute | solution.py:33
  38.1 3.1 %collective-permute-start.7 = (bf16[640,256]{1,0:T(8,128)(2,1)S(1)}, bf16[640,256]{1,0:T(8,128)(2,1)S(1)}, u32[]{:S(2)}, u32[]{:S(2)}) collective-permute-start(bf16[640,256]{1,0:T(8,128)(2,1)S(1)} %slice.121), channel_id=1, source_target_pairs={{0,3},{1,0},{2,1},{3,2},{4,7},{5,4},{6,5},{7,6},{8,11},{9,8},{10,9... | collective-permute-start | bytes 983048 | tf_op jit(solution)/shard_map/ppermute | solution.py:33
  41.3 3.3 %collective-permute-start.15 = (bf16[128,1024]{1,0:T(8,128)(2,1)S(1)}, bf16[128,1024]{1,0:T(8,128)(2,1)S(1)}, u32[]{:S(2)}, u32[]{:S(2)}) collective-permute-start(bf16[128,1024]{1,0:T(8,128)(2,1)S(1)} %slice.130), channel_id=1, source_target_pairs={{0,12},{1,13},{2,14},{3,15},{4,0},{5,1},{6,2},{7,3},{8,4},{9,5},{1... | collective-permute-start | bytes 786440 | tf_op jit(solution)/shard_map/ppermute | solution.py:33
  44.6 2.6 %blank.1.refs_4_ = f32[4096,384]{1,0:T(8,128)} custom-call(s32[8,16]{1,0:T(8,128)S(1)} %copy-done.3), custom_call_target="tpu_custom_call" | custom-call | bytes 3145728 | tf_op jit(solution)/shard_map/blank/pallas_call | solution.py:367
  47.2 1.6 %collective-permute-done.14.refs_8_ = bf16[128,1024]{1,0:T(8,128)(2,1)S(1)} collective-permute-done((bf16[128,1024]{1,0:T(8,128)(2,1)S(1)}, bf16[128,1024]{1,0:T(8,128)(2,1)S(1)}, u32[]{:S(2)}, u32[]{:S(2)}) %collective-permute-start.14) | collective-permute-done | bytes 262176 | tf_op jit(solution)/shard_map/ppermute | solution.py:33
  48.8 4.5 %panels.1 = (bf16[64,1024]{1,0:T(8,128)(2,1)}, bf16[128,2048]{1,0:T(8,128)(2,1)}) custom-call(bf16[128,2048]{1,0:T(8,128)(2,1)S(1)} %bitcast.29, bf16[1280,256]{1,0:T(8,128)(2,1)S(1)} %lower.1.refs_0_, bf16[1280,256]{1,0:T(8,128)(2,1)S(1)} %collective-permute-done.4.refs_1_, bf16[1280,256]{1,0:T(8,128)(2,1)S(1)} %collective-permute-done.5.refs_2_, ...), custom_call_target="tpu_custom_call" | custom-call | flops 2952790016 | bytes 8388608 | tf_op jit(solution)/shard_map/panels/pallas_call | solution.py:177
  53.3 3.2 %collective-permute-start.17 = (bf16[128,2048]{1,0:T(8,128)(2,1)}, bf16[128,2048]{1,0:T(8,128)(2,1)S(1)}, u32[]{:S(2)}, u32[]{:S(2)}) collective-permute-start(bf16[128,2048]{1,0:T(8,128)(2,1)} %get-tuple-element.22), channel_id=1, source_target_pairs={{0,3},{1,0},{2,1},{3,2},{4,7},{5,4},{6,5},{7,6},{8,11},{9,8},{10,9... | collective-permute-start | bytes 1572872 | tf_op jit(solution)/shard_map/ppermute | solution.py:33
  56.9 3.0 %collective-permute-start.21 = (bf16[128,2048]{1,0:T(8,128)(2,1)}, bf16[128,2048]{1,0:T(8,128)(2,1)S(1)}, u32[]{:S(2)}, u32[]{:S(2)}) collective-permute-start(bf16[128,2048]{1,0:T(8,128)(2,1)} %get-tuple-element.22), channel_id=1, source_target_pairs={{0,12},{1,13},{2,14},{3,15},{4,0},{5,1},{6,2},{7,3},{8,4},{9,5},{1... | collective-permute-start | bytes 1572872 | tf_op jit(solution)/shard_map/ppermute | solution.py:33
  61.3 4.3 %collective-permute-done.16 = bf16[128,2048]{1,0:T(8,128)(2,1)S(1)} collective-permute-done((bf16[128,2048]{1,0:T(8,128)(2,1)}, bf16[128,2048]{1,0:T(8,128)(2,1)S(1)}, u32[]{:S(2)}, u32[]{:S(2)}) %collective-permute-start.16) | collective-permute-done | bytes 524320 | tf_op jit(solution)/shard_map/ppermute | solution.py:33
  65.7 3.5 %collective-permute-start.19 = (bf16[64,2048]{1,0:T(8,128)(2,1)S(1)}, bf16[64,2048]{1,0:T(8,128)(2,1)S(1)}, u32[]{:S(2)}, u32[]{:S(2)}) collective-permute-start(bf16[64,2048]{1,0:T(8,128)(2,1)S(1)} %slice.132), channel_id=1, source_target_pairs={{0,3},{1,0},{2,1},{3,2},{4,7},{5,4},{6,5},{7,6},{8,11},{9,8},{10,9... | collective-permute-start | bytes 786440 | tf_op jit(solution)/shard_map/ppermute | solution.py:33
  69.6 3.1 %collective-permute-start.23 = (bf16[64,2048]{1,0:T(8,128)(2,1)S(1)}, bf16[64,2048]{1,0:T(8,128)(2,1)S(1)}, u32[]{:S(2)}, u32[]{:S(2)}) collective-permute-start(bf16[64,2048]{1,0:T(8,128)(2,1)S(1)} %slice.134), channel_id=1, source_target_pairs={{0,12},{1,13},{2,14},{3,15},{4,0},{5,1},{6,2},{7,3},{8,4},{9,5},{1... | collective-permute-start | bytes 786440 | tf_op jit(solution)/shard_map/ppermute | solution.py:33
  73.3 3.7 %collective-permute-done.22 = bf16[64,2048]{1,0:T(8,128)(2,1)S(1)} collective-permute-done((bf16[64,2048]{1,0:T(8,128)(2,1)S(1)}, bf16[64,2048]{1,0:T(8,128)(2,1)S(1)}, u32[]{:S(2)}, u32[]{:S(2)}) %collective-permute-start.22) | collective-permute-done | bytes 262176 | tf_op jit(solution)/shard_map/ppermute | solution.py:33
  78.3 3.3 %collective-permute-start.24 = (bf16[256,512]{1,0:T(8,128)(2,1)S(1)}, bf16[256,512]{1,0:T(8,128)(2,1)S(1)}, u32[]{:S(2)}, u32[]{:S(2)}) collective-permute-start(bf16[256,512]{1,0:T(8,128)(2,1)S(1)} %tile.2), channel_id=1, source_target_pairs={{0,64},{16,80},{32,96},{48,112},{64,0},{80,16},{96,32},{112,48},{1... | collective-permute-start | bytes 786440 | tf_op jit(solution)/shard_map/ppermute | solution.py:38
  83.3 3.1 %collective-permute-done.24 = bf16[256,512]{1,0:T(8,128)(2,1)S(1)} collective-permute-done((bf16[256,512]{1,0:T(8,128)(2,1)S(1)}, bf16[256,512]{1,0:T(8,128)(2,1)S(1)}, u32[]{:S(2)}, u32[]{:S(2)}) %collective-permute-start.24) | collective-permute-done | bytes 262176 | tf_op jit(solution)/shard_map/ppermute | solution.py:38
  86.4 3.2 %collective-permute-start.26 = (bf16[256,512]{1,0:T(8,128)(2,1)S(1)}, bf16[256,512]{1,0:T(8,128)(2,1)S(1)}, u32[]{:S(2)}, u32[]{:S(2)}) collective-permute-start(bf16[256,512]{1,0:T(8,128)(2,1)S(1)} %collective-permute-done.24), channel_id=1, source_target_pairs={{0,3},{1,0},{2,1},{3,2},{4,7},{5,4},{6,5},{7,6},{8,11},{9,8},{10,9... | collective-permute-start | bytes 786440 | tf_op jit(solution)/shard_map/ppermute | solution.py:33
  90.8 3.2 %collective-permute-start.34 = (bf16[256,512]{1,0:T(8,128)(2,1)S(1)}, bf16[256,512]{1,0:T(8,128)(2,1)S(1)}, u32[]{:S(2)}, u32[]{:S(2)}) collective-permute-start(bf16[256,512]{1,0:T(8,128)(2,1)S(1)} %collective-permute-done.32), channel_id=1, source_target_pairs={{0,3},{1,0},{2,1},{3,2},{4,7},{5,4},{6,5},{7,6},{8,11},{9,8},{10,9... | collective-permute-start | bytes 786440 | tf_op jit(solution)/shard_map/ppermute | solution.py:33
  94.9 3.3 %collective-permute-start.28 = (bf16[128,512]{1,0:T(8,128)(2,1)S(1)}, bf16[128,512]{1,0:T(8,128)(2,1)S(1)}, u32[]{:S(2)}, u32[]{:S(2)}) collective-permute-start(bf16[128,512]{1,0:T(8,128)(2,1)S(1)} %slice.136), channel_id=1, source_target_pairs={{0,3},{1,0},{2,1},{3,2},{4,7},{5,4},{6,5},{7,6},{8,11},{9,8},{10,9... | collective-permute-start | bytes 393224 | tf_op jit(solution)/shard_map/ppermute | solution.py:33
  98.9 3.3 %collective-permute-start.36 = (bf16[128,512]{1,0:T(8,128)(2,1)S(1)}, bf16[128,512]{1,0:T(8,128)(2,1)S(1)}, u32[]{:S(2)}, u32[]{:S(2)}) collective-permute-start(bf16[128,512]{1,0:T(8,128)(2,1)S(1)} %slice.142), channel_id=1, source_target_pairs={{0,3},{1,0},{2,1},{3,2},{4,7},{5,4},{6,5},{7,6},{8,11},{9,8},{10,9... | collective-permute-start | bytes 393224 | tf_op jit(solution)/shard_map/ppermute | solution.py:33
  107.5 3.3 %collective-permute-start.38 = (bf16[3,256,128]{2,1,0:T(8,128)(2,1)S(1)}, bf16[3,256,128]{2,1,0:T(8,128)(2,1)S(1)}, u32[]{:S(2)}, u32[]{:S(2)}) collective-permute-start(bf16[3,256,128]{2,1,0:T(8,128)(2,1)S(1)} %get-tuple-element.26), channel_id=1, source_target_pairs={{0,8},{1,9},{2,10},{3,11},{4,12},{5,13},{6,14},{7,15},{8,0},{9,1},... | collective-permute-start | bytes 589832 | tf_op jit(solution)/shard_map/ppermute | solution.py:33
  113.9 1.8 %collective-permute-start.31 = (bf16[3,256,128]{2,1,0:T(8,128)(2,1)S(1)}, bf16[3,256,128]{2,1,0:T(8,128)(2,1)S(1)}, u32[]{:S(2)}, u32[]{:S(2)}) collective-permute-start(bf16[3,256,128]{2,1,0:T(8,128)(2,1)S(1)} %get-tuple-element.29), channel_id=1, source_target_pairs={{0,12},{1,13},{2,14},{3,15},{4,0},{5,1},{6,2},{7,3},{8,4},{9,5},{1... | collective-permute-start | bytes 589832 | tf_op jit(solution)/shard_map/ppermute | solution.py:33
  116.6 2.3 %place.2.refs_4_ = f32[4096,384]{1,0:T(8,128)} custom-call(s32[8,16]{1,0:T(8,128)S(1)} %copy-done.3, s32[8,32]{1,0:T(8,128)S(1)} %copy-done.4, bf16[3,256,128]{2,1,0:T(8,128)(2,1)S(1)} %get-tuple-element.28.refs_0_, bf16[3,256,128]{2,1,0:T(8,128)(2,1)S(1)} %collective-permute-done.37.refs_1_, ...), custom_call_target="tpu_custom_call", output_to_operand_aliasing={{}: (6, {})} | custom-call | bytes 3145728 | tf_op jit(solution)/shard_map/place/pallas_call | solution.py:420
  118.9 2.4 %collective-permute-done.29.refs_1_ = bf16[3,256,128]{2,1,0:T(8,128)(2,1)S(1)} collective-permute-done((bf16[3,256,128]{2,1,0:T(8,128)(2,1)S(1)}, bf16[3,256,128]{2,1,0:T(8,128)(2,1)S(1)}, u32[]{:S(2)}, u32[]{:S(2)}) %collective-permute-start.29) | collective-permute-done | bytes 196640 | tf_op jit(solution)/shard_map/ppermute | solution.py:33
  122.2 2.3 %place.3 = f32[4096,384]{1,0:T(8,128)} custom-call(s32[8,16]{1,0:T(8,128)S(1)} %copy-done.3, s32[8,32]{1,0:T(8,128)S(1)} %copy-done.4, bf16[3,256,128]{2,1,0:T(8,128)(2,1)S(1)} %get-tuple-element.32.refs_0_, bf16[3,256,128]{2,1,0:T(8,128)(2,1)S(1)} %collective-permute-done.29.refs_1_, ...), custom_call_target="tpu_custom_call", output_to_operand_aliasing={{}: (6, {})} | custom-call | bytes 3145728 | tf_op jit(solution)/shard_map/place/pallas_call | solution.py:420
  (115 shorter events, 27.0 us)
Async XLA Ops:
  2.7 14.7 %collective-permute-start.8 = (bf16[160,1024]{1,0:T(8,128)(2,1)S(1)}, bf16[160,1024]{1,0:T(8,128)(2,1)S(1)}, u32[]{:S(2)}, u32[]{:S(2)}) collective-permute-start(bf16[160,1024]{1,0:T(8,128)(2,1)S(1)} %get-tuple-element.19), channel_id=1, source_target_pairs={{0,1},{1,2},{2,3},{3,0},{4,5},{5,6},{6,7},{7,4},{8,9},{9,10},{10,1... | collective-permute-start | bytes 983048 | tf_op jit(solution)/shard_map/ppermute | solution.py:33
  4.8 9.2 %collective-permute-start = (bf16[128,1024]{1,0:T(8,128)(2,1)}, bf16[128,1024]{1,0:T(8,128)(2,1)S(1)}, u32[]{:S(2)}, u32[]{:S(2)}) collective-permute-start(bf16[128,1024]{1,0:T(8,128)(2,1)} %bitcast.26), channel_id=1, source_target_pairs={{0,4},{1,5},{2,6},{3,7},{4,8},{5,9},{6,10},{7,11},{8,12},{9,13},{1... | collective-permute-start | bytes 786440 | tf_op jit(solution)/shard_map/ppermute | solution.py:33
  6.3 8.1 %collective-permute-start.1 = (bf16[128,1024]{1,0:T(8,128)(2,1)}, bf16[128,1024]{1,0:T(8,128)(2,1)S(1)}, u32[]{:S(2)}, u32[]{:S(2)}) collective-permute-start(bf16[128,1024]{1,0:T(8,128)(2,1)} %bitcast.27), channel_id=1, source_target_pairs={{0,12},{1,13},{2,14},{3,15},{4,0},{5,1},{6,2},{7,3},{8,4},{9,5},{1... | collective-permute-start | bytes 786440 | tf_op jit(solution)/shard_map/ppermute | solution.py:33
  8.0 11.4 %collective-permute-start.9 = (bf16[160,1024]{1,0:T(8,128)(2,1)S(1)}, bf16[160,1024]{1,0:T(8,128)(2,1)S(1)}, u32[]{:S(2)}, u32[]{:S(2)}) collective-permute-start(bf16[160,1024]{1,0:T(8,128)(2,1)S(1)} %get-tuple-element.20), channel_id=1, source_target_pairs={{0,3},{1,0},{2,1},{3,2},{4,7},{5,4},{6,5},{7,6},{8,11},{9,8},{10,9... | collective-permute-start | bytes 983048 | tf_op jit(solution)/shard_map/ppermute | solution.py:33
  21.1 16.7 %collective-permute-start.4 = (bf16[1280,256]{1,0:T(8,128)(2,1)S(1)}, bf16[1280,256]{1,0:T(8,128)(2,1)S(1)}, u32[]{:S(2)}, u32[]{:S(2)}) collective-permute-start(bf16[1280,256]{1,0:T(8,128)(2,1)S(1)} %lower.1.refs_0_), channel_id=1, source_target_pairs={{0,1},{1,2},{2,3},{3,0},{4,5},{5,6},{6,7},{7,4},{8,9},{9,10},{10,1... | collective-permute-start | bytes 1966088 | tf_op jit(solution)/shard_map/ppermute | solution.py:33
  22.4 15.6 %collective-permute-start.5 = (bf16[1280,256]{1,0:T(8,128)(2,1)S(1)}, bf16[1280,256]{1,0:T(8,128)(2,1)S(1)}, u32[]{:S(2)}, u32[]{:S(2)}) collective-permute-start(bf16[1280,256]{1,0:T(8,128)(2,1)S(1)} %lower.1.refs_0_), channel_id=1, source_target_pairs={{0,3},{1,0},{2,1},{3,2},{4,7},{5,4},{6,5},{7,6},{8,11},{9,8},{10,9... | collective-permute-start | bytes 1966088 | tf_op jit(solution)/shard_map/ppermute | solution.py:33
  25.9 15.3 %collective-permute-start.12 = (bf16[256,1024]{1,0:T(8,128)(2,1)S(1)}, bf16[256,1024]{1,0:T(8,128)(2,1)S(1)}, u32[]{:S(2)}, u32[]{:S(2)}) collective-permute-start(bf16[256,1024]{1,0:T(8,128)(2,1)S(1)} %slice_dynamic-update-slice_fusion.1.refs_5_), channel_id=1, source_target_pairs={{0,4},{1,5},{2,6},{3,7},{4,8},{5,9},{6,10},{7,11},{8,12},{9,13},{1... | collective-permute-start | bytes 1572872 | tf_op jit(solution)/shard_map/ppermute | solution.py:33
  25.9 15.3 %collective-permute-start.13 = (bf16[256,1024]{1,0:T(8,128)(2,1)S(1)}, bf16[256,1024]{1,0:T(8,128)(2,1)S(1)}, u32[]{:S(2)}, u32[]{:S(2)}) collective-permute-start(bf16[256,1024]{1,0:T(8,128)(2,1)S(1)} %slice_dynamic-update-slice_fusion.1.refs_5_), channel_id=1, source_target_pairs={{0,12},{1,13},{2,14},{3,15},{4,0},{5,1},{6,2},{7,3},{8,4},{9,5},{1... | collective-permute-start | bytes 1572872 | tf_op jit(solution)/shard_map/ppermute | solution.py:33
  37.7 9.4 %collective-permute-start.6 = (bf16[640,256]{1,0:T(8,128)(2,1)S(1)}, bf16[640,256]{1,0:T(8,128)(2,1)S(1)}, u32[]{:S(2)}, u32[]{:S(2)}) collective-permute-start(bf16[640,256]{1,0:T(8,128)(2,1)S(1)} %slice.120), channel_id=1, source_target_pairs={{0,1},{1,2},{2,3},{3,0},{4,5},{5,6},{6,7},{7,4},{8,9},{9,10},{10,1... | collective-permute-start | bytes 983048 | tf_op jit(solution)/shard_map/ppermute | solution.py:33
  38.1 9.1 %collective-permute-start.7 = (bf16[640,256]{1,0:T(8,128)(2,1)S(1)}, bf16[640,256]{1,0:T(8,128)(2,1)S(1)}, u32[]{:S(2)}, u32[]{:S(2)}) collective-permute-start(bf16[640,256]{1,0:T(8,128)(2,1)S(1)} %slice.121), channel_id=1, source_target_pairs={{0,3},{1,0},{2,1},{3,2},{4,7},{5,4},{6,5},{7,6},{8,11},{9,8},{10,9... | collective-permute-start | bytes 983048 | tf_op jit(solution)/shard_map/ppermute | solution.py:33
  41.2 7.7 %collective-permute-start.14 = (bf16[128,1024]{1,0:T(8,128)(2,1)S(1)}, bf16[128,1024]{1,0:T(8,128)(2,1)S(1)}, u32[]{:S(2)}, u32[]{:S(2)}) collective-permute-start(bf16[128,1024]{1,0:T(8,128)(2,1)S(1)} %slice.129), channel_id=1, source_target_pairs={{0,4},{1,5},{2,6},{3,7},{4,8},{5,9},{6,10},{7,11},{8,12},{9,13},{1... | collective-permute-start | bytes 786440 | tf_op jit(solution)/shard_map/ppermute | solution.py:33
  41.3 7.5 %collective-permute-start.15 = (bf16[128,1024]{1,0:T(8,128)(2,1)S(1)}, bf16[128,1024]{1,0:T(8,128)(2,1)S(1)}, u32[]{:S(2)}, u32[]{:S(2)}) collective-permute-start(bf16[128,1024]{1,0:T(8,128)(2,1)S(1)} %slice.130), channel_id=1, source_target_pairs={{0,12},{1,13},{2,14},{3,15},{4,0},{5,1},{6,2},{7,3},{8,4},{9,5},{1... | collective-permute-start | bytes 786440 | tf_op jit(solution)/shard_map/ppermute | solution.py:33
  53.3 12.2 %collective-permute-start.16 = (bf16[128,2048]{1,0:T(8,128)(2,1)}, bf16[128,2048]{1,0:T(8,128)(2,1)S(1)}, u32[]{:S(2)}, u32[]{:S(2)}) collective-permute-start(bf16[128,2048]{1,0:T(8,128)(2,1)} %get-tuple-element.22), channel_id=1, source_target_pairs={{0,1},{1,2},{2,3},{3,0},{4,5},{5,6},{6,7},{7,4},{8,9},{9,10},{10,1... | collective-permute-start | bytes 1572872 | tf_op jit(solution)/shard_map/ppermute | solution.py:33
  53.3 12.3 %collective-permute-start.17 = (bf16[128,2048]{1,0:T(8,128)(2,1)}, bf16[128,2048]{1,0:T(8,128)(2,1)S(1)}, u32[]{:S(2)}, u32[]{:S(2)}) collective-permute-start(bf16[128,2048]{1,0:T(8,128)(2,1)} %get-tuple-element.22), channel_id=1, source_target_pairs={{0,3},{1,0},{2,1},{3,2},{4,7},{5,4},{6,5},{7,6},{8,11},{9,8},{10,9... | collective-permute-start | bytes 1572872 | tf_op jit(solution)/shard_map/ppermute | solution.py:33
  56.6 12.6 %collective-permute-start.20 = (bf16[128,2048]{1,0:T(8,128)(2,1)}, bf16[128,2048]{1,0:T(8,128)(2,1)S(1)}, u32[]{:S(2)}, u32[]{:S(2)}) collective-permute-start(bf16[128,2048]{1,0:T(8,128)(2,1)} %get-tuple-element.22), channel_id=1, source_target_pairs={{0,4},{1,5},{2,6},{3,7},{4,8},{5,9},{6,10},{7,11},{8,12},{9,13},{1... | collective-permute-start | bytes 1572872 | tf_op jit(solution)/shard_map/ppermute | solution.py:33
  56.9 12.7 %collective-permute-start.21 = (bf16[128,2048]{1,0:T(8,128)(2,1)}, bf16[128,2048]{1,0:T(8,128)(2,1)S(1)}, u32[]{:S(2)}, u32[]{:S(2)}) collective-permute-start(bf16[128,2048]{1,0:T(8,128)(2,1)} %get-tuple-element.22), channel_id=1, source_target_pairs={{0,12},{1,13},{2,14},{3,15},{4,0},{5,1},{6,2},{7,3},{8,4},{9,5},{1... | collective-permute-start | bytes 1572872 | tf_op jit(solution)/shard_map/ppermute | solution.py:33
  65.6 7.7 %collective-permute-start.18 = (bf16[64,2048]{1,0:T(8,128)(2,1)S(1)}, bf16[64,2048]{1,0:T(8,128)(2,1)S(1)}, u32[]{:S(2)}, u32[]{:S(2)}) collective-permute-start(bf16[64,2048]{1,0:T(8,128)(2,1)S(1)} %slice.131), channel_id=1, source_target_pairs={{0,1},{1,2},{2,3},{3,0},{4,5},{5,6},{6,7},{7,4},{8,9},{9,10},{10,1... | collective-permute-start | bytes 786440 | tf_op jit(solution)/shard_map/ppermute | solution.py:33
  65.7 7.6 %collective-permute-start.19 = (bf16[64,2048]{1,0:T(8,128)(2,1)S(1)}, bf16[64,2048]{1,0:T(8,128)(2,1)S(1)}, u32[]{:S(2)}, u32[]{:S(2)}) collective-permute-start(bf16[64,2048]{1,0:T(8,128)(2,1)S(1)} %slice.132), channel_id=1, source_target_pairs={{0,3},{1,0},{2,1},{3,2},{4,7},{5,4},{6,5},{7,6},{8,11},{9,8},{10,9... | collective-permute-start | bytes 786440 | tf_op jit(solution)/shard_map/ppermute | solution.py:33
  69.2 7.8 %collective-permute-start.22 = (bf16[64,2048]{1,0:T(8,128)(2,1)S(1)}, bf16[64,2048]{1,0:T(8,128)(2,1)S(1)}, u32[]{:S(2)}, u32[]{:S(2)}) collective-permute-start(bf16[64,2048]{1,0:T(8,128)(2,1)S(1)} %slice.133), channel_id=1, source_target_pairs={{0,4},{1,5},{2,6},{3,7},{4,8},{5,9},{6,10},{7,11},{8,12},{9,13},{1... | collective-permute-start | bytes 786440 | tf_op jit(solution)/shard_map/ppermute | solution.py:33
  78.3 8.1 %collective-permute-start.24 = (bf16[256,512]{1,0:T(8,128)(2,1)S(1)}, bf16[256,512]{1,0:T(8,128)(2,1)S(1)}, u32[]{:S(2)}, u32[]{:S(2)}) collective-permute-start(bf16[256,512]{1,0:T(8,128)(2,1)S(1)} %tile.2), channel_id=1, source_target_pairs={{0,64},{16,80},{32,96},{48,112},{64,0},{80,16},{96,32},{112,48},{1... | collective-permute-start | bytes 786440 | tf_op jit(solution)/shard_map/ppermute | solution.py:38
  82.9 8.0 %collective-permute-start.32 = (bf16[256,512]{1,0:T(8,128)(2,1)S(1)}, bf16[256,512]{1,0:T(8,128)(2,1)S(1)}, u32[]{:S(2)}, u32[]{:S(2)}) collective-permute-start(bf16[256,512]{1,0:T(8,128)(2,1)S(1)} %tile.3), channel_id=1, source_target_pairs={{0,64},{16,80},{32,96},{48,112},{64,0},{80,16},{96,32},{112,48},{1... | collective-permute-start | bytes 786440 | tf_op jit(solution)/shard_map/ppermute | solution.py:38
  86.4 8.4 %collective-permute-start.25 = (bf16[256,512]{1,0:T(8,128)(2,1)S(1)}, bf16[256,512]{1,0:T(8,128)(2,1)S(1)}, u32[]{:S(2)}, u32[]{:S(2)}) collective-permute-start(bf16[256,512]{1,0:T(8,128)(2,1)S(1)} %collective-permute-done.24), channel_id=1, source_target_pairs={{0,1},{1,2},{2,3},{3,0},{4,5},{5,6},{6,7},{7,4},{8,9},{9,10},{10,1... | collective-permute-start | bytes 786440 | tf_op jit(solution)/shard_map/ppermute | solution.py:33
  86.4 8.5 %collective-permute-start.26 = (bf16[256,512]{1,0:T(8,128)(2,1)S(1)}, bf16[256,512]{1,0:T(8,128)(2,1)S(1)}, u32[]{:S(2)}, u32[]{:S(2)}) collective-permute-start(bf16[256,512]{1,0:T(8,128)(2,1)S(1)} %collective-permute-done.24), channel_id=1, source_target_pairs={{0,3},{1,0},{2,1},{3,2},{4,7},{5,4},{6,5},{7,6},{8,11},{9,8},{10,9... | collective-permute-start | bytes 786440 | tf_op jit(solution)/shard_map/ppermute | solution.py:33
  90.8 8.0 %collective-permute-start.33 = (bf16[256,512]{1,0:T(8,128)(2,1)S(1)}, bf16[256,512]{1,0:T(8,128)(2,1)S(1)}, u32[]{:S(2)}, u32[]{:S(2)}) collective-permute-start(bf16[256,512]{1,0:T(8,128)(2,1)S(1)} %collective-permute-done.32), channel_id=1, source_target_pairs={{0,1},{1,2},{2,3},{3,0},{4,5},{5,6},{6,7},{7,4},{8,9},{9,10},{10,1... | collective-permute-start | bytes 786440 | tf_op jit(solution)/shard_map/ppermute | solution.py:33
  90.8 8.1 %collective-permute-start.34 = (bf16[256,512]{1,0:T(8,128)(2,1)S(1)}, bf16[256,512]{1,0:T(8,128)(2,1)S(1)}, u32[]{:S(2)}, u32[]{:S(2)}) collective-permute-start(bf16[256,512]{1,0:T(8,128)(2,1)S(1)} %collective-permute-done.32), channel_id=1, source_target_pairs={{0,3},{1,0},{2,1},{3,2},{4,7},{5,4},{6,5},{7,6},{8,11},{9,8},{10,9... | collective-permute-start | bytes 786440 | tf_op jit(solution)/shard_map/ppermute | solution.py:33
  94.8 7.5 %collective-permute-start.27 = (bf16[128,512]{1,0:T(8,128)(2,1)S(1)}, bf16[128,512]{1,0:T(8,128)(2,1)S(1)}, u32[]{:S(2)}, u32[]{:S(2)}) collective-permute-start(bf16[128,512]{1,0:T(8,128)(2,1)S(1)} %slice.135), channel_id=1, source_target_pairs={{0,1},{1,2},{2,3},{3,0},{4,5},{5,6},{6,7},{7,4},{8,9},{9,10},{10,1... | collective-permute-start | bytes 393224 | tf_op jit(solution)/shard_map/ppermute | solution.py:33
  94.9 7.5 %collective-permute-start.28 = (bf16[128,512]{1,0:T(8,128)(2,1)S(1)}, bf16[128,512]{1,0:T(8,128)(2,1)S(1)}, u32[]{:S(2)}, u32[]{:S(2)}) collective-permute-start(bf16[128,512]{1,0:T(8,128)(2,1)S(1)} %slice.136), channel_id=1, source_target_pairs={{0,3},{1,0},{2,1},{3,2},{4,7},{5,4},{6,5},{7,6},{8,11},{9,8},{10,9... | collective-permute-start | bytes 393224 | tf_op jit(solution)/shard_map/ppermute | solution.py:33
  106.4 7.5 %collective-permute-start.37 = (bf16[3,256,128]{2,1,0:T(8,128)(2,1)S(1)}, bf16[3,256,128]{2,1,0:T(8,128)(2,1)S(1)}, u32[]{:S(2)}, u32[]{:S(2)}) collective-permute-start(bf16[3,256,128]{2,1,0:T(8,128)(2,1)S(1)} %get-tuple-element.27), channel_id=1, source_target_pairs={{0,4},{1,5},{2,6},{3,7},{4,8},{5,9},{6,10},{7,11},{8,12},{9,13},{1... | collective-permute-start | bytes 589832 | tf_op jit(solution)/shard_map/ppermute | solution.py:33
  107.5 9.0 %collective-permute-start.38 = (bf16[3,256,128]{2,1,0:T(8,128)(2,1)S(1)}, bf16[3,256,128]{2,1,0:T(8,128)(2,1)S(1)}, u32[]{:S(2)}, u32[]{:S(2)}) collective-permute-start(bf16[3,256,128]{2,1,0:T(8,128)(2,1)S(1)} %get-tuple-element.26), channel_id=1, source_target_pairs={{0,8},{1,9},{2,10},{3,11},{4,12},{5,13},{6,14},{7,15},{8,0},{9,1},... | collective-permute-start | bytes 589832 | tf_op jit(solution)/shard_map/ppermute | solution.py:33
  112.4 9.0 %collective-permute-start.29 = (bf16[3,256,128]{2,1,0:T(8,128)(2,1)S(1)}, bf16[3,256,128]{2,1,0:T(8,128)(2,1)S(1)}, u32[]{:S(2)}, u32[]{:S(2)}) collective-permute-start(bf16[3,256,128]{2,1,0:T(8,128)(2,1)S(1)} %get-tuple-element.31), channel_id=1, source_target_pairs={{0,4},{1,5},{2,6},{3,7},{4,8},{5,9},{6,10},{7,11},{8,12},{9,13},{1... | collective-permute-start | bytes 589832 | tf_op jit(solution)/shard_map/ppermute | solution.py:33
  113.0 8.4 %collective-permute-start.30 = (bf16[3,256,128]{2,1,0:T(8,128)(2,1)S(1)}, bf16[3,256,128]{2,1,0:T(8,128)(2,1)S(1)}, u32[]{:S(2)}, u32[]{:S(2)}) collective-permute-start(bf16[3,256,128]{2,1,0:T(8,128)(2,1)S(1)} %get-tuple-element.30), channel_id=1, source_target_pairs={{0,8},{1,9},{2,10},{3,11},{4,12},{5,13},{6,14},{7,15},{8,0},{9,1},... | collective-permute-start | bytes 589832 | tf_op jit(solution)/shard_map/ppermute | solution.py:33
  113.9 8.3 %collective-permute-start.31 = (bf16[3,256,128]{2,1,0:T(8,128)(2,1)S(1)}, bf16[3,256,128]{2,1,0:T(8,128)(2,1)S(1)}, u32[]{:S(2)}, u32[]{:S(2)}) collective-permute-start(bf16[3,256,128]{2,1,0:T(8,128)(2,1)S(1)} %get-tuple-element.29), channel_id=1, source_target_pairs={{0,12},{1,13},{2,14},{3,15},{4,0},{5,1},{6,2},{7,3},{8,4},{9,5},{1... | collective-permute-start | bytes 589832 | tf_op jit(solution)/shard_map/ppermute | solution.py:33
  (15 other events, 118.0 us)

commit v4 on v3

v4 whole, which is shorter than its diff:
```python
import functools

import jax
import jax.numpy as jnp
from jax import lax
from jax.experimental import pallas as pl
from jax.experimental.pallas import tpu as pltpu
from jax.sharding import PartitionSpec as P

PANEL = 1024
BLOCK = 128
SLOTS = 3
SIDE = 4
FRONT = SIDE * SIDE
CONTRIB = BLOCK * FRONT
ROWS = PANEL // FRONT
MIB = 1024 * 1024


def dot_nt(left, right):
    return lax.dot_general(
        left, right, (((1,), (1,)), ((), ())), preferred_element_type=jnp.float32
    )


def shift(value, axis, by):
    dx, dz = (by, 0) if axis == "x" else (0, by)
    pairs = [
        (x * SIDE + z, (x + dx) % SIDE * SIDE + (z + dz) % SIDE)
        for x in range(SIDE)
        for z in range(SIDE)
    ]
    return lax.ppermute(value, "front", pairs)


def to_parent(value):
    groups = lax.axis_size("leaf")
    return lax.ppermute(
        value, "leaf", [(g, (g + groups // 2) % groups) for g in range(groups)]
    )


RING = (0, -1, 1, 2)


def bundle_of(own, axis):
    half = own.shape[0] // 2
    from_left = shift(own, axis, 1)
    from_right = shift(own, axis, -1)
    far_top = shift(from_left[:half], axis, 1)
    far_bottom = shift(from_right[half:], axis, -1)
    return jnp.concatenate([own, from_left, from_right, far_top, far_bottom], axis=0)


def spread(bundle, axis, *meanwhile):
    half = bundle.shape[0] // 2
    left = shift(bundle, axis, 1)
    right = shift(bundle, axis, -1)
    left, right, meanwhile = lax.optimization_barrier((left, right, meanwhile))
    far_low = shift(left[:half], axis, 1)
    far_high = shift(right[half:], axis, -1)
    return [bundle, left, right, far_low, far_high], *meanwhile


def places(x_first):
    found = []
    for part, second in ((RING, 0), (RING, -1), (RING, 1), (RING[:2], 2), (RING[2:], 2)):
        found.append([(first, second) if x_first else (second, first) for first in part])
    return found


X_FIRST, Z_FIRST = places(True), places(False)


def place_of(front, dx, dz):
    x, z = front // SIDE, front % SIDE
    return lax.rem(x + dx + SIDE, SIDE) * SIDE + lax.rem(z + dz + SIDE, SIDE)


def family():
    groups = lax.axis_size("leaf")
    parent = lax.axis_index("leaf")
    return parent, lax.rem(parent + groups // 2, groups), lax.axis_index("front")


def unpack_inverses(front, bundles, mats):
    z = lax.rem(front, SIDE)
    for bundle, dz, start in zip(bundles, (0, -1, 1, 2, 2), (0, 0, 0, 0, CHUNKS // 2), strict=True):
        place = lax.rem(z + dz + SIDE, SIDE) * ROWS
        for at in range(bundle.shape[0] // (2 * ROWS)):
            x, chunk = LOWER[start + at]
            row = pl.multiple_of(place + x * SIDE * ROWS, ROWS)
            for which in range(2):
                top = (at * 2 + which) * ROWS
                mats[which, pl.ds(row, ROWS), chunk * WIDE : (chunk + 1) * WIDE] = bundle[
                    top : top + ROWS, :
                ]


def unpack_panel(front, sources, mat):
    own, left, right, ahead, behind = sources
    half = 2 * ROWS
    parts = [(own, MIDDLE, 0, 0), (own, ON_AT, 1, 0), (left, ON_AT, 0, -1), (left, MIDDLE, 1, -1)]
    parts += [(right, MIDDLE, 0, 1), (right, ON_AT, 1, 1), (ahead, 0, 0, 2), (behind, 0, 1, 2)]
    for source, top, part, dx in parts:
        for at, dz in enumerate(RING[part * 2 : part * 2 + 2]):
            row = pl.multiple_of(place_of(front, dx, dz) * ROWS, ROWS)
            first = top + at * half // 2
            mat[pl.ds(row, ROWS), :] = source[first : first + ROWS, :]


WIDE = SIDE * ROWS
LOWER = [(x, chunk) for x in range(SIDE) for chunk in range(x + 1)]
CHUNKS = len(LOWER)


def project(rows, inverse, keep):
    for at in range(0, PANEL, WIDE):
        upto = at + WIDE
        keep(at, dot_nt(rows[:, :upto], inverse[at:upto, :upto]))


def lower_kernel(*refs):
    sources, out = refs[:5], refs[5]
    x = lax.axis_index("front") // SIDE
    blocks = [(sources[0], 0, 0), (sources[1], 0, -1), (sources[2], 0, 1)]
    blocks += [(sources[3], 0, 2), (sources[4], 1, 2)]
    for source, first, dx in blocks:
        from_x = lax.rem(x + dx + SIDE, SIDE)
        start = (from_x * (from_x + 1)) // 2
        for chunk in range(SIDE):

            @pl.when(chunk <= from_x)
            def _():
                row = pl.multiple_of((start + chunk) * 2 * ROWS + first * ROWS, ROWS)
                out[pl.ds(row, source.shape[0]), :] = source[:, chunk * WIDE : (chunk + 1) * WIDE]


def lower_chunks(own, left, right, far_first, far_second):
    return pl.pallas_call(
        lower_kernel,
        out_shape=jax.ShapeDtypeStruct((CHUNKS * 2 * ROWS, WIDE), jnp.bfloat16),
        in_specs=[VMEM_SPEC] * 5,
        out_specs=VMEM_SPEC,
        compiler_params=pltpu.CompilerParams(vmem_limit_bytes=4 * MIB),
        cost_estimate=pl.CostEstimate(flops=0, bytes_accessed=MIB, transcendentals=0),
        name="lower",
    )(own, left, right, far_first, far_second)


def panel_kernel(border, *refs):
    inverses, panels, (link_out, factor) = refs[:5], refs[5:10], refs[10:12]
    mats, panel, link, updated = refs[12:]
    front = lax.axis_index("front")
    unpack_inverses(front, inverses, mats)

    def keep_first(at, value):
        factor[:, at : at + WIDE] = value.astype(jnp.bfloat16)

    def keep_link(at, value):
        link[:, at : at + WIDE] = value.astype(jnp.bfloat16)

    def keep_second(at, value):
        factor[:, PANEL + at : PANEL + at + WIDE] = value.astype(jnp.bfloat16)

    project(border, mats.at[0], keep_first)
    unpack_panel(front, panels, panel)
    project(panel, mats.at[0], keep_link)
    link_out[...] = link[pl.ds(pl.multiple_of(front * ROWS, ROWS), ROWS), :]
    for at in range(0, PANEL, WIDE):
        coupled = dot_nt(factor[:, :PANEL], link[at : at + WIDE, :])
        updated[:, at : at + WIDE] = (
            border[:, PANEL + at : PANEL + at + WIDE].astype(jnp.float32) - coupled
        ).astype(jnp.bfloat16)
    project(updated, mats.at[1], keep_second)


VMEM_SPEC = pl.BlockSpec(memory_space=pltpu.VMEM)
SMEM_SPEC = pl.BlockSpec(memory_space=pltpu.SMEM)
HELD = pl.BlockSpec(memory_space=pl.ANY)


def eliminate(border, inverses, panels):
    return pl.pallas_call(
        panel_kernel,
        out_shape=(
            jax.ShapeDtypeStruct((ROWS, PANEL), jnp.bfloat16),
            jax.ShapeDtypeStruct((BLOCK, 2 * PANEL), jnp.bfloat16),
        ),
        in_specs=[VMEM_SPEC] * 11,
        out_specs=(VMEM_SPEC,) * 2,
        scratch_shapes=[
            pltpu.VMEM((2, PANEL, PANEL), jnp.bfloat16),
            pltpu.VMEM((PANEL, PANEL), jnp.bfloat16),
            pltpu.VMEM((PANEL, PANEL), jnp.bfloat16),
            pltpu.VMEM((BLOCK, PANEL), jnp.bfloat16),
        ],
        compiler_params=pltpu.CompilerParams(vmem_limit_bytes=16 * MIB),
        cost_estimate=pl.CostEstimate(
            flops=2 * PANEL**3 + 6 * BLOCK * PANEL**2,
            bytes_accessed=8 * MIB,
            transcendentals=0,
        ),
        name="panels",
    )(border, *inverses, *panels)


LINE = SIDE * BLOCK
CHUNKS_OF_ROWS = ((0, 1), (2, 3))
FIRST, SECOND = CHUNKS_OF_ROWS
GROUPS = (
    [(FIRST, step) for step in range(SIDE)] + [(SECOND, 0)],
    [(SECOND, step) for step in range(1, SIDE)],
)
HALF = ROWS // 2
MIDDLE, ON_AT, LAST, MESSAGE = ROWS, 3 * ROWS, 5 * ROWS, 5 * ROWS + HALF


FOLDED = ((0, 0, ROWS), (1, 0, ROWS), (SIDE - 1, 0, ROWS), (2, 0, HALF), (2, ROWS, HALF))


def fold_kernel(tail, panel_in, inverses_in, folded, panel, inverses):
    x = lax.axis_index("front") // SIDE
    top = 0
    for step, first, height in FOLDED:
        at = pl.multiple_of(lax.rem(x + step, SIDE) * LINE, LINE)
        folded[top : top + height, :LINE] = tail[first : first + height, pl.ds(at, LINE)]
        first += height
        folded[top : top + height, LINE:] = tail[first : first + height, pl.ds(at, LINE)]
        top += height
    panel[...] = panel_in[...]
    inverses[...] = inverses_in[...]


def fold_tail(tail, panel, inverses):
    return pl.pallas_call(
        fold_kernel,
        out_shape=(
            jax.ShapeDtypeStruct((SIDE * ROWS, PANEL), jnp.bfloat16),
            jax.ShapeDtypeStruct(panel.shape, jnp.bfloat16),
            jax.ShapeDtypeStruct(inverses.shape, jnp.bfloat16),
        ),
        in_specs=[VMEM_SPEC] * 3,
        out_specs=(VMEM_SPEC,) * 3,
        compiler_params=pltpu.CompilerParams(vmem_limit_bytes=6 * MIB),
        cost_estimate=pl.CostEstimate(flops=0, bytes_accessed=2 * MIB, transcendentals=0),
        name="fold",
    )(tail, panel, inverses)


def message_kernel(folded, panel, low, high, far_low, far_high, up, down):
    for part, out in enumerate((up, down)):
        first = (part + 1) * ROWS
        out[:ROWS] = folded[first : first + ROWS]
        first = 3 * ROWS + part * HALF
        out[LAST:] = folded[first : first + HALF]
    for out, first, second in ((up, ON_AT, MIDDLE), (down, MIDDLE, ON_AT)):
        out[first : first + ROWS] = panel[...]
        out[first + ROWS : first + 2 * ROWS] = low[...]
        out[second : second + ROWS] = high[...]
        out[second + ROWS : second + ROWS + HALF] = far_low[...]
        out[second + ROWS + HALF : second + 2 * ROWS] = far_high[...]


def make_messages(folded, panels):
    message = jax.ShapeDtypeStruct((MESSAGE, PANEL), jnp.bfloat16)
    return pl.pallas_call(
        message_kernel,
        out_shape=(message, message),
        in_specs=[VMEM_SPEC] * 6,
        out_specs=(VMEM_SPEC,) * 2,
        compiler_params=pltpu.CompilerParams(vmem_limit_bytes=6 * MIB),
        cost_estimate=pl.CostEstimate(flops=0, bytes_accessed=2 * MIB, transcendentals=0),
        name="messages",
    )(folded, *panels)


def tile_kernel(chunk, sizes, rows_x, rows_z, *refs):
    (kept, left, right, ahead, behind), (out, product, tails, rows) = refs[:5], refs[5:]
    front = lax.axis_index("front")
    live = sizes[lax.axis_index("leaf")]
    x, z = front // SIDE, lax.rem(front, SIDE)
    lane = lax.broadcasted_iota(jnp.int32, (BLOCK, BLOCK), 1)
    line = lax.broadcasted_iota(jnp.int32, (BLOCK, BLOCK), 0)
    for step, source in ((0, kept), (1, left), (SIDE - 1, right)):
        tails[step, :ROWS] = source[:ROWS, :LINE]
        tails[step, ROWS:] = source[:ROWS, LINE:]
    for part, source in enumerate((ahead, behind)):
        first = part * ROWS
        tails[2, first : first + HALF] = source[2 * ROWS :, :LINE]
        tails[2, first + HALF : first + ROWS] = source[2 * ROWS :, LINE:]
    for up, row_x in enumerate(chunk):
        away = lax.rem(row_x - x + SIDE, SIDE)
        at = jnp.where(away == 0, 0, jnp.where(away == SIDE - 1, 1, away + 1))
        at = pl.multiple_of(at * BLOCK, BLOCK)
        rows[up * BLOCK : (up + 1) * BLOCK, :] = rows_x[pl.ds(at, BLOCK), :]
    for at in range(0, LINE, WIDE):
        product[:, at : at + WIDE] = dot_nt(rows[...], rows_z[at : at + WIDE, :])
    for up, row_x in enumerate(chunk):
        step = lax.rem(x - row_x + SIDE, SIDE)
        for across, dz in enumerate(RING):
            col_z = lax.rem(z + dz + SIDE, SIDE)
            columns = slice(across * BLOCK, (across + 1) * BLOCK)
            keep = (line + (row_x * SIDE + z) * BLOCK < live) & (
                lane + (x * SIDE + col_z) * BLOCK < live
            )
            old = tails[step, :, pl.ds(pl.multiple_of(col_z * BLOCK, BLOCK), BLOCK)]
            schur = old.astype(jnp.float32) - product[up * BLOCK : (up + 1) * BLOCK, columns]
            out[up * BLOCK : (up + 1) * BLOCK, columns] = jnp.where(keep, schur, 0.0).astype(
                jnp.bfloat16
            )


def make_tile(chunk, sizes, rows_x, rows_z, tails):
    rows = len(chunk) * BLOCK
    return pl.pallas_call(
        functools.partial(tile_kernel, chunk),
        out_shape=jax.ShapeDtypeStruct((rows, LINE), jnp.bfloat16),
        in_specs=[SMEM_SPEC] + [VMEM_SPEC] * 7,
        out_specs=VMEM_SPEC,
        scratch_shapes=[
            pltpu.VMEM((rows, LINE), jnp.float32),
            pltpu.VMEM((SIDE, BLOCK, LINE), jnp.bfloat16),
            pltpu.VMEM((rows, 2 * PANEL), jnp.bfloat16),
        ],
        compiler_params=pltpu.CompilerParams(vmem_limit_bytes=8 * MIB),
        cost_estimate=pl.CostEstimate(
            flops=4 * rows * LINE * PANEL, bytes_accessed=5 * MIB, transcendentals=0
        ),
        name="tile",
    )(sizes, rows_x, rows_z, *tails)


def pack_kernel(plan, line, out):
    rows = line.shape[0] // SIDE
    for at in range(FRONT):

        @pl.when(plan[at] >= 0)
        def _():
            up, across = at // SIDE, at % SIDE
            out[plan[at]] = line[
                up * rows : (up + 1) * rows, across * BLOCK : (across + 1) * BLOCK
            ]


def pack_tiles(plan, line):
    rows = line.shape[0] // SIDE
    return pl.pallas_call(
        pack_kernel,
        out_shape=jax.ShapeDtypeStruct((SIDE * SLOTS, rows, BLOCK), jnp.bfloat16),
        in_specs=[SMEM_SPEC, VMEM_SPEC],
        out_specs=VMEM_SPEC,
        compiler_params=pltpu.CompilerParams(vmem_limit_bytes=4 * MIB),
        cost_estimate=pl.CostEstimate(flops=0, bytes_accessed=6 * MIB, transcendentals=0),
        name="pack",
    )(plan, line)


def blank_kernel(block_map, block_owner, out, plan, blank, taken, sem):
    parent, child, front = family()
    x, z = front // SIDE, lax.rem(front, SIDE)
    blank[...] = jnp.zeros_like(blank)

    @pl.loop(0, 2 * FRONT)
    def _(block):
        taken[block] = 0
        plan[block] = 0

    @pl.loop(0, FRONT)
    def _(block):
        into = block_map[child, block]
        taken[into] = 1
        slot = block_owner[parent, into]

        @pl.when(slot // SLOTS == front)
        def _():
            plan[FRONT + lax.rem(slot, SLOTS)] = 1

    def copy(block):
        row = pl.multiple_of(block * BLOCK, BLOCK)
        return pltpu.make_async_copy(blank, out.at[pl.ds(row, BLOCK), :], sem)

    @pl.loop(0, 2 * FRONT)
    def _(block):
        @pl.when(taken[block] == 0)
        def _():
            copy(block).start()

    for up, dx in enumerate(RING):
        for across, dz in enumerate(RING):
            slot = block_owner[parent, block_map[child, place_of(front, dx, dz)]]
            owner = slot // SLOTS
            step = lax.rem(lax.rem(owner, SIDE) - z + SIDE, SIDE)
            plan[up * SIDE + across] = jnp.where(
                owner // SIDE == x, step * SLOTS + lax.rem(slot, SLOTS), -1
            )

    @pl.loop(0, FRONT)
    def _(block):
        copy(0).wait()


PARENT = jax.ShapeDtypeStruct((2 * CONTRIB, SLOTS * BLOCK), jnp.float32)


def blank_rows(block_map, block_owner):
    return pl.pallas_call(
        blank_kernel,
        out_shape=(PARENT, jax.ShapeDtypeStruct((2 * FRONT,), jnp.int32)),
        in_specs=[SMEM_SPEC] * 2,
        out_specs=(HELD, SMEM_SPEC),
        scratch_shapes=[
            pltpu.VMEM((BLOCK, SLOTS * BLOCK), jnp.float32),
            pltpu.SMEM((2 * FRONT,), jnp.int32),
            pltpu.SemaphoreType.DMA,
        ],
        compiler_params=pltpu.CompilerParams(vmem_limit_bytes=2 * MIB),
        cost_estimate=pl.CostEstimate(flops=0, bytes_accessed=3 * MIB, transcendentals=0),
        name="blank",
    )(block_map, block_owner)


def place_kernel(parts, block_map, plan, *refs):
    tiles, (out, staged, sems) = refs[: len(parts)], refs[len(parts) + 1 :]
    _, child, front = family()
    none = lax.broadcasted_iota(jnp.int32, (BLOCK, BLOCK), 0) * 0
    copies = []
    for (chunk, step), tile in zip(parts, tiles, strict=True):
        z = lax.rem(lax.rem(front, SIDE) - step + SIDE, SIDE)
        for up, row_x in enumerate(chunk):
            here = len(copies)
            for slot in range(SLOTS):
                value = tile[slot, up * BLOCK : (up + 1) * BLOCK, :].astype(jnp.float32)
                staged[here, :, slot * BLOCK : (slot + 1) * BLOCK] = jnp.where(
                    none + plan[FRONT + slot] > 0, value, 0.0
                )
            row = pl.multiple_of(block_map[child, row_x * SIDE + z] * BLOCK, BLOCK)
            copy = pltpu.make_async_copy(
                staged.at[here], out.at[pl.ds(row, BLOCK), :], sems.at[here]
            )
            copy.start()
            copies.append(copy)
    for copy in copies:
        copy.wait()


def place_tiles(block_map, plan, parent_rows, tiles):
    blocks = sum(len(chunk) for chunk, _ in tiles)
    return pl.pallas_call(
        functools.partial(place_kernel, list(tiles)),
        out_shape=PARENT,
        in_specs=[SMEM_SPEC] * 2 + [VMEM_SPEC] * len(tiles) + [HELD],
        out_specs=HELD,
        scratch_shapes=[
            pltpu.VMEM((blocks, BLOCK, SLOTS * BLOCK), jnp.float32),
            pltpu.SemaphoreType.DMA((blocks,)),
        ],
        input_output_aliases={2 + len(tiles): 0},
        compiler_params=pltpu.CompilerParams(vmem_limit_bytes=6 * MIB),
        cost_estimate=pl.CostEstimate(flops=0, bytes_accessed=MIB, transcendentals=0),
        name="place",
    )(block_map, plan, *tiles.values(), parent_rows)


def per_device(inv_factors, panel_rows, border, tail, front_sizes, block_map, block_owner):
    inverses, panel = inv_factors[0].reshape(2 * ROWS, PANEL), panel_rows[0]
    left, right = shift(inverses, "x", 1), shift(inverses, "x", -1)
    low, high = shift(panel, "z", 1), shift(panel, "z", -1)
    folded, panel, inverses = fold_tail(tail[0], panel, inverses)
    low, high, folded, panel, inverses = lax.optimization_barrier(
        (low, high, folded, panel, inverses)
    )
    far_first = shift(left[:ROWS], "x", 1)
    far_second = shift(right[ROWS:], "x", -1)
    far_low = shift(low[:HALF], "z", 1)
    far_high = shift(high[HALF:], "z", -1)

    chunks = lower_chunks(inverses, left, right, far_first, far_second)
    chunks, update, plan = spread(chunks, "z", *blank_rows(block_map, block_owner))
    up, down = make_messages(folded, (panel, low, high, far_low, far_high))
    from_left, from_right = shift(up, "x", 1), shift(down, "x", -1)
    ahead = shift(from_left[ON_AT:], "x", 1)
    behind = shift(from_right[ON_AT:], "x", -1)
    panels = (down, from_left, from_right, ahead, behind)
    link_local, factor_local = eliminate(border[0], chunks, panels)

    rows_x, rows_z = bundle_of(factor_local, "x"), bundle_of(factor_local, "z")
    tails = (folded, from_left, from_right, ahead, behind)

    tiles = {}
    for chunk in CHUNKS_OF_ROWS:
        rows = make_tile(chunk, front_sizes, rows_x, rows_z, tails)
        packed = pack_tiles(plan, bundle_of(to_parent(rows), "x"))
        for step in range(SIDE):
            tile = packed[step * SLOTS : (step + 1) * SLOTS]
            tiles[chunk, step] = shift(tile, "z", step) if step else tile
    for group in GROUPS:
        update = place_tiles(block_map, plan, update, {key: tiles[key] for key in group})
    return link_local[None], factor_local[None], update[None]


def solution(mesh):
    return jax.shard_map(
        per_device,
        mesh=mesh,
        in_specs=(
            P("leaf", None, "front", None),
            P("leaf", "front", None),
            P("leaf", "front", None),
            P("leaf", "front", None),
            P(),
            P(),
            P(),
        ),
        out_specs=(P("leaf", "front", None), P("leaf", "front", None), P("leaf", None, "front")),
        check_vma=False,
    )
```

time: 125 us -> 124 us (level)
    pallas_call x6 -> x7, Pallas kernels: 9.66 us -> 8.72 us  [the longest x2 3.65 us: place_tiles(): pl.pallas_call(functools.partial(place_kernel, list(tiles)), out_shape=PA...]
    unnamed x34 -> x30, local copies, waits for them, and re-layouts: 4.56 us -> 4.57 us
where the time goes in v4:
time: 124 us; the launch traced here: 123 us
  starting transfers between devices  67.5 us (54%)
  waiting for transfers between devices  33.2 us (27%)
  Pallas kernels  15.9 us (13%)
  local copies, waits for them, and re-layouts  4.97 us (4%)
  between operations  1.25 us (1%)
    ppermute x38, starting transfers between devices, shift(): return lax.ppermute(value, 'front', pairs)  63.8 us
    ppermute x38, waiting for transfers between devices, shift(): return lax.ppermute(value, 'front', pairs)  28.9 us
    unnamed x30, local copies, waits for them, and re-layouts  4.57 us
    pallas_call x1, Pallas kernels, eliminate(): pl.pallas_call(panel_kernel, out_shape=(jax.ShapeDtypeStruct((ROWS, PANEL...  4.49 us
    ppermute x2, waiting for transfers between devices, to_parent(): lax.ppermute(value, 'leaf', [(g, (g + groups // 2) % groups) for g in ran...  4.3 us
    ppermute x2, starting transfers between devices, to_parent(): lax.ppermute(value, 'leaf', [(g, (g + groups // 2) % groups) for g in ran...  3.69 us
    pallas_call x2, Pallas kernels, place_tiles(): pl.pallas_call(functools.partial(place_kernel, list(tiles)), out_shape=PA...  3.65 us
    pallas_call x1, Pallas kernels, blank_rows(): pl.pallas_call(blank_kernel, out_shape=(PARENT, jax.ShapeDtypeStruct((2 *...  3.51 us
  transfers between devices with their start and end apart: 40, of which 16 were waited for; matrix products, arithmetic and copies ran while one was open for 2% of the time, Pallas kernels for 6%

profile of v4, /device:TPU:0, one launch (start us, length us, event | category | flops | bytes accessed | tf_op | source)
XLA Modules:
  0.0 122.8 jit_solution(1644443248970626132)
XLA Ops:
  2.3 1.7 %collective-permute-start.3 = (bf16[128,1024]{1,0:T(8,128)(2,1)}, bf16[128,1024]{1,0:T(8,128)(2,1)S(1)}, u32[]{:S(2)}, u32[]{:S(2)}) collective-permute-start(bf16[128,1024]{1,0:T(8,128)(2,1)} %bitcast.9), channel_id=1, source_target_pairs={{0,12},{1,13},{2,14},{3,15},{4,0},{5,1},{6,2},{7,3},{8,4},{9,5},{1... | collective-permute-start | bytes 786440 | tf_op jit(solution)/shard_map/ppermute | solution.py:33
  3.9 2.0 %collective-permute-start = (bf16[64,1024]{1,0:T(8,128)(2,1)}, bf16[64,1024]{1,0:T(8,128)(2,1)S(1)}, u32[]{:S(2)}, u32[]{:S(2)}) collective-permute-start(bf16[64,1024]{1,0:T(8,128)(2,1)} %bitcast.11), channel_id=1, source_target_pairs={{0,1},{1,2},{2,3},{3,0},{4,5},{5,6},{6,7},{7,4},{8,9},{9,10},{10,1... | collective-permute-start | bytes 393224 | tf_op jit(solution)/shard_map/ppermute | solution.py:33
  5.9 2.1 %collective-permute-start.1 = (bf16[64,1024]{1,0:T(8,128)(2,1)}, bf16[64,1024]{1,0:T(8,128)(2,1)S(1)}, u32[]{:S(2)}, u32[]{:S(2)}) collective-permute-start(bf16[64,1024]{1,0:T(8,128)(2,1)} %bitcast.12), channel_id=1, source_target_pairs={{0,3},{1,0},{2,1},{3,2},{4,7},{5,4},{6,5},{7,6},{8,11},{9,8},{10,9... | collective-permute-start | bytes 393224 | tf_op jit(solution)/shard_map/ppermute | solution.py:33
  11.2 1.8 %collective-permute-start.10 = (bf16[32,1024]{1,0:T(8,128)(2,1)S(1)}, bf16[32,1024]{1,0:T(8,128)(2,1)S(1)}, u32[]{:S(2)}, u32[]{:S(2)}) collective-permute-start(bf16[32,1024]{1,0:T(8,128)(2,1)S(1)} %slice.76), channel_id=1, source_target_pairs={{0,1},{1,2},{2,3},{3,0},{4,5},{5,6},{6,7},{7,4},{8,9},{9,10},{10,1... | collective-permute-start | bytes 196616 | tf_op jit(solution)/shard_map/ppermute | solution.py:33
  14.9 3.0 %collective-permute-start.5 = (bf16[64,1024]{1,0:T(8,128)(2,1)S(1)}, bf16[64,1024]{1,0:T(8,128)(2,1)S(1)}, u32[]{:S(2)}, u32[]{:S(2)}) collective-permute-start(bf16[64,1024]{1,0:T(8,128)(2,1)S(1)} %slice.97), channel_id=1, source_target_pairs={{0,12},{1,13},{2,14},{3,15},{4,0},{5,1},{6,2},{7,3},{8,4},{9,5},{1... | collective-permute-start | bytes 393224 | tf_op jit(solution)/shard_map/ppermute | solution.py:33
  18.2 3.2 %collective-permute-start.13 = (bf16[352,1024]{1,0:T(8,128)(2,1)S(1)}, bf16[352,1024]{1,0:T(8,128)(2,1)S(1)}, u32[]{:S(2)}, u32[]{:S(2)}) collective-permute-start(bf16[352,1024]{1,0:T(8,128)(2,1)S(1)} %get-tuple-element.33.refs_5_), channel_id=1, source_target_pairs={{0,12},{1,13},{2,14},{3,15},{4,0},{5,1},{6,2},{7,3},{8,4},{9,5},{1... | collective-permute-start | bytes 2162696 | tf_op jit(solution)/shard_map/ppermute | solution.py:33
  23.0 2.5 %collective-permute-start.7 = (bf16[1280,256]{1,0:T(8,128)(2,1)S(1)}, bf16[1280,256]{1,0:T(8,128)(2,1)S(1)}, u32[]{:S(2)}, u32[]{:S(2)}) collective-permute-start(bf16[1280,256]{1,0:T(8,128)(2,1)S(1)} %lower.1.refs_0_), channel_id=1, source_target_pairs={{0,3},{1,0},{2,1},{3,2},{4,7},{5,4},{6,5},{7,6},{8,11},{9,8},{10,9... | collective-permute-start | bytes 1966088 | tf_op jit(solution)/shard_map/ppermute | solution.py:33
  25.5 3.5 %blank.1 = (f32[4096,384]{1,0:T(8,128)}, s32[32]{0:T(128)S(1)}) custom-call(s32[8,16]{1,0:T(8,128)S(1)} %copy-done.3, s32[8,32]{1,0:T(8,128)S(1)} %copy-done.4), custom_call_target="tpu_custom_call" | custom-call | bytes 3145728 | tf_op jit(solution)/shard_map/blank/pallas_call | solution.py:407
  29.0 7.3 %collective-permute-done.12.refs_6_.refs_1_ = bf16[352,1024]{1,0:T(8,128)(2,1)S(1)} collective-permute-done((bf16[352,1024]{1,0:T(8,128)(2,1)S(1)}, bf16[352,1024]{1,0:T(8,128)(2,1)S(1)}, u32[]{:S(2)}, u32[]{:S(2)}) %collective-permute-start.12) | collective-permute-done | bytes 720928 | tf_op jit(solution)/shard_map/ppermute | solution.py:33
  36.4 3.3 %collective-permute-start.15 = (bf16[160,1024]{1,0:T(8,128)(2,1)S(1)}, bf16[160,1024]{1,0:T(8,128)(2,1)S(1)}, u32[]{:S(2)}, u32[]{:S(2)}) collective-permute-start(bf16[160,1024]{1,0:T(8,128)(2,1)S(1)} %slice.99), channel_id=1, source_target_pairs={{0,12},{1,13},{2,14},{3,15},{4,0},{5,1},{6,2},{7,3},{8,4},{9,5},{1... | collective-permute-start | bytes 983048 | tf_op jit(solution)/shard_map/ppermute | solution.py:33
  40.0 3.1 %collective-permute-start.9 = (bf16[640,256]{1,0:T(8,128)(2,1)S(1)}, bf16[640,256]{1,0:T(8,128)(2,1)S(1)}, u32[]{:S(2)}, u32[]{:S(2)}) collective-permute-start(bf16[640,256]{1,0:T(8,128)(2,1)S(1)} %slice.75), channel_id=1, source_target_pairs={{0,3},{1,0},{2,1},{3,2},{4,7},{5,4},{6,5},{7,6},{8,11},{9,8},{10,9... | collective-permute-start | bytes 983048 | tf_op jit(solution)/shard_map/ppermute | solution.py:33
  43.1 2.0 %collective-permute-done.14.refs_8_.refs_3_ = bf16[160,1024]{1,0:T(8,128)(2,1)S(1)} collective-permute-done((bf16[160,1024]{1,0:T(8,128)(2,1)S(1)}, bf16[160,1024]{1,0:T(8,128)(2,1)S(1)}, u32[]{:S(2)}, u32[]{:S(2)}) %collective-permute-start.14) | collective-permute-done | bytes 327712 | tf_op jit(solution)/shard_map/ppermute | solution.py:33
  45.1 3.0 %collective-permute-done.8.refs_3_ = bf16[640,256]{1,0:T(8,128)(2,1)S(1)} collective-permute-done((bf16[640,256]{1,0:T(8,128)(2,1)S(1)}, bf16[640,256]{1,0:T(8,128)(2,1)S(1)}, u32[]{:S(2)}, u32[]{:S(2)}) %collective-permute-start.8) | collective-permute-done | bytes 327712 | tf_op jit(solution)/shard_map/ppermute | solution.py:33
  48.1 4.5 %panels.1 = (bf16[64,1024]{1,0:T(8,128)(2,1)}, bf16[128,2048]{1,0:T(8,128)(2,1)}) custom-call(bf16[128,2048]{1,0:T(8,128)(2,1)S(1)} %bitcast.14, bf16[1280,256]{1,0:T(8,128)(2,1)S(1)} %lower.1.refs_0_, bf16[1280,256]{1,0:T(8,128)(2,1)S(1)} %collective-permute-done.6.refs_1_, bf16[1280,256]{1,0:T(8,128)(2,1)S(1)} %collective-permute-done.7.refs_2_, ...), custom_call_target="tpu_custom_call" | custom-call | flops 2952790016 | bytes 8388608 | tf_op jit(solution)/shard_map/panels/pallas_call | solution.py:184
  52.6 3.2 %collective-permute-start.17 = (bf16[128,2048]{1,0:T(8,128)(2,1)}, bf16[128,2048]{1,0:T(8,128)(2,1)S(1)}, u32[]{:S(2)}, u32[]{:S(2)}) collective-permute-start(bf16[128,2048]{1,0:T(8,128)(2,1)} %get-tuple-element.36), channel_id=1, source_target_pairs={{0,12},{1,13},{2,14},{3,15},{4,0},{5,1},{6,2},{7,3},{8,4},{9,5},{1... | collective-permute-start | bytes 1572872 | tf_op jit(solution)/shard_map/ppermute | solution.py:33
  56.4 2.7 %collective-permute-start.21 = (bf16[128,2048]{1,0:T(8,128)(2,1)}, bf16[128,2048]{1,0:T(8,128)(2,1)S(1)}, u32[]{:S(2)}, u32[]{:S(2)}) collective-permute-start(bf16[128,2048]{1,0:T(8,128)(2,1)} %get-tuple-element.36), channel_id=1, source_target_pairs={{0,3},{1,0},{2,1},{3,2},{4,7},{5,4},{6,5},{7,6},{8,11},{9,8},{10,9... | collective-permute-start | bytes 1572872 | tf_op jit(solution)/shard_map/ppermute | solution.py:33
  60.5 4.3 %collective-permute-done.16 = bf16[128,2048]{1,0:T(8,128)(2,1)S(1)} collective-permute-done((bf16[128,2048]{1,0:T(8,128)(2,1)}, bf16[128,2048]{1,0:T(8,128)(2,1)S(1)}, u32[]{:S(2)}, u32[]{:S(2)}) %collective-permute-start.16) | collective-permute-done | bytes 524320 | tf_op jit(solution)/shard_map/ppermute | solution.py:33
  64.9 3.5 %collective-permute-start.19 = (bf16[64,2048]{1,0:T(8,128)(2,1)S(1)}, bf16[64,2048]{1,0:T(8,128)(2,1)S(1)}, u32[]{:S(2)}, u32[]{:S(2)}) collective-permute-start(bf16[64,2048]{1,0:T(8,128)(2,1)S(1)} %slice.101), channel_id=1, source_target_pairs={{0,12},{1,13},{2,14},{3,15},{4,0},{5,1},{6,2},{7,3},{8,4},{9,5},{1... | collective-permute-start | bytes 786440 | tf_op jit(solution)/shard_map/ppermute | solution.py:33
  69.1 2.8 %collective-permute-start.23 = (bf16[64,2048]{1,0:T(8,128)(2,1)S(1)}, bf16[64,2048]{1,0:T(8,128)(2,1)S(1)}, u32[]{:S(2)}, u32[]{:S(2)}) collective-permute-start(bf16[64,2048]{1,0:T(8,128)(2,1)S(1)} %slice.103), channel_id=1, source_target_pairs={{0,3},{1,0},{2,1},{3,2},{4,7},{5,4},{6,5},{7,6},{8,11},{9,8},{10,9... | collective-permute-start | bytes 786440 | tf_op jit(solution)/shard_map/ppermute | solution.py:33
  72.5 3.6 %collective-permute-done.22 = bf16[64,2048]{1,0:T(8,128)(2,1)S(1)} collective-permute-done((bf16[64,2048]{1,0:T(8,128)(2,1)S(1)}, bf16[64,2048]{1,0:T(8,128)(2,1)S(1)}, u32[]{:S(2)}, u32[]{:S(2)}) %collective-permute-start.22) | collective-permute-done | bytes 262176 | tf_op jit(solution)/shard_map/ppermute | solution.py:33
  77.5 3.3 %collective-permute-start.24 = (bf16[256,512]{1,0:T(8,128)(2,1)S(1)}, bf16[256,512]{1,0:T(8,128)(2,1)S(1)}, u32[]{:S(2)}, u32[]{:S(2)}) collective-permute-start(bf16[256,512]{1,0:T(8,128)(2,1)S(1)} %tile.2), channel_id=1, source_target_pairs={{0,64},{16,80},{32,96},{48,112},{64,0},{80,16},{96,32},{112,48},{1... | collective-permute-start | bytes 786440 | tf_op jit(solution)/shard_map/ppermute | solution.py:38
  82.5 3.0 %collective-permute-done.24 = bf16[256,512]{1,0:T(8,128)(2,1)S(1)} collective-permute-done((bf16[256,512]{1,0:T(8,128)(2,1)S(1)}, bf16[256,512]{1,0:T(8,128)(2,1)S(1)}, u32[]{:S(2)}, u32[]{:S(2)}) %collective-permute-start.24) | collective-permute-done | bytes 262176 | tf_op jit(solution)/shard_map/ppermute | solution.py:38
  85.5 3.2 %collective-permute-start.26 = (bf16[256,512]{1,0:T(8,128)(2,1)S(1)}, bf16[256,512]{1,0:T(8,128)(2,1)S(1)}, u32[]{:S(2)}, u32[]{:S(2)}) collective-permute-start(bf16[256,512]{1,0:T(8,128)(2,1)S(1)} %collective-permute-done.24), channel_id=1, source_target_pairs={{0,12},{1,13},{2,14},{3,15},{4,0},{5,1},{6,2},{7,3},{8,4},{9,5},{1... | collective-permute-start | bytes 786440 | tf_op jit(solution)/shard_map/ppermute | solution.py:33
  90.0 3.2 %collective-permute-start.34 = (bf16[256,512]{1,0:T(8,128)(2,1)S(1)}, bf16[256,512]{1,0:T(8,128)(2,1)S(1)}, u32[]{:S(2)}, u32[]{:S(2)}) collective-permute-start(bf16[256,512]{1,0:T(8,128)(2,1)S(1)} %collective-permute-done.32), channel_id=1, source_target_pairs={{0,12},{1,13},{2,14},{3,15},{4,0},{5,1},{6,2},{7,3},{8,4},{9,5},{1... | collective-permute-start | bytes 786440 | tf_op jit(solution)/shard_map/ppermute | solution.py:33
  93.6 3.3 %collective-permute-start.28 = (bf16[128,512]{1,0:T(8,128)(2,1)S(1)}, bf16[128,512]{1,0:T(8,128)(2,1)S(1)}, u32[]{:S(2)}, u32[]{:S(2)}) collective-permute-start(bf16[128,512]{1,0:T(8,128)(2,1)S(1)} %slice.105), channel_id=1, source_target_pairs={{0,12},{1,13},{2,14},{3,15},{4,0},{5,1},{6,2},{7,3},{8,4},{9,5},{1... | collective-permute-start | bytes 393224 | tf_op jit(solution)/shard_map/ppermute | solution.py:33
  97.8 3.3 %collective-permute-start.36 = (bf16[128,512]{1,0:T(8,128)(2,1)S(1)}, bf16[128,512]{1,0:T(8,128)(2,1)S(1)}, u32[]{:S(2)}, u32[]{:S(2)}) collective-permute-start(bf16[128,512]{1,0:T(8,128)(2,1)S(1)} %slice.110), channel_id=1, source_target_pairs={{0,12},{1,13},{2,14},{3,15},{4,0},{5,1},{6,2},{7,3},{8,4},{9,5},{1... | collective-permute-start | bytes 393224 | tf_op jit(solution)/shard_map/ppermute | solution.py:33
  101.9 2.0 %collective-permute-done.35 = bf16[128,512]{1,0:T(8,128)(2,1)S(1)} collective-permute-done((bf16[128,512]{1,0:T(8,128)(2,1)S(1)}, bf16[128,512]{1,0:T(8,128)(2,1)S(1)}, u32[]{:S(2)}, u32[]{:S(2)}) %collective-permute-start.35) | collective-permute-done | bytes 131104 | tf_op jit(solution)/shard_map/ppermute | solution.py:33
  106.3 3.3 %collective-permute-start.38 = (bf16[3,256,128]{2,1,0:T(8,128)(2,1)S(1)}, bf16[3,256,128]{2,1,0:T(8,128)(2,1)S(1)}, u32[]{:S(2)}, u32[]{:S(2)}) collective-permute-start(bf16[3,256,128]{2,1,0:T(8,128)(2,1)S(1)} %get-tuple-element.44), channel_id=1, source_target_pairs={{0,2},{1,3},{2,0},{3,1},{4,6},{5,7},{6,4},{7,5},{8,10},{9,11},{10,... | collective-permute-start | bytes 589832 | tf_op jit(solution)/shard_map/ppermute | solution.py:33
  112.6 1.8 %collective-permute-start.31 = (bf16[3,256,128]{2,1,0:T(8,128)(2,1)S(1)}, bf16[3,256,128]{2,1,0:T(8,128)(2,1)S(1)}, u32[]{:S(2)}, u32[]{:S(2)}) collective-permute-start(bf16[3,256,128]{2,1,0:T(8,128)(2,1)S(1)} %get-tuple-element.40), channel_id=1, source_target_pairs={{0,3},{1,0},{2,1},{3,2},{4,7},{5,4},{6,5},{7,6},{8,11},{9,8},{10,9... | collective-permute-start | bytes 589832 | tf_op jit(solution)/shard_map/ppermute | solution.py:33
  115.3 2.0 %place.2.refs_3_ = f32[4096,384]{1,0:T(8,128)} custom-call(s32[8,16]{1,0:T(8,128)S(1)} %copy-done.3, s32[32]{0:T(128)S(1)} %get-tuple-element.37.plan, bf16[3,256,128]{2,1,0:T(8,128)(2,1)S(1)} %get-tuple-element.46.refs_0_, bf16[3,256,128]{2,1,0:T(8,128)(2,1)S(1)} %collective-permute-done.37.refs_1_, ...), custom_call_target="tpu_custom_call", output_to_operand_aliasing={{}: (7, {})} | custom-call | bytes 1048576 | tf_op jit(solution)/shard_map/place/pallas_call | solution.py:449
  117.3 2.7 %collective-permute-done.29.refs_0_ = bf16[3,256,128]{2,1,0:T(8,128)(2,1)S(1)} collective-permute-done((bf16[3,256,128]{2,1,0:T(8,128)(2,1)S(1)}, bf16[3,256,128]{2,1,0:T(8,128)(2,1)S(1)}, u32[]{:S(2)}, u32[]{:S(2)}) %collective-permute-start.29) | collective-permute-done | bytes 196640 | tf_op jit(solution)/shard_map/ppermute | solution.py:33
  121.0 1.7 %place.3 = f32[4096,384]{1,0:T(8,128)} custom-call(s32[8,16]{1,0:T(8,128)S(1)} %copy-done.3, s32[32]{0:T(128)S(1)} %get-tuple-element.37.plan, bf16[3,256,128]{2,1,0:T(8,128)(2,1)S(1)} %collective-permute-done.29.refs_0_, bf16[3,256,128]{2,1,0:T(8,128)(2,1)S(1)} %collective-permute-done.30.refs_1_, ...), custom_call_target="tpu_custom_call", output_to_operand_aliasing={{}: (5, {})} | custom-call | bytes 1048576 | tf_op jit(solution)/shard_map/place/pallas_call | solution.py:449
  (111 shorter events, 25.7 us)
Async XLA Ops:
  0.6 13.9 %collective-permute-start.2 = (bf16[128,1024]{1,0:T(8,128)(2,1)}, bf16[128,1024]{1,0:T(8,128)(2,1)S(1)}, u32[]{:S(2)}, u32[]{:S(2)}) collective-permute-start(bf16[128,1024]{1,0:T(8,128)(2,1)} %bitcast.8), channel_id=1, source_target_pairs={{0,4},{1,5},{2,6},{3,7},{4,8},{5,9},{6,10},{7,11},{8,12},{9,13},{1... | collective-permute-start | bytes 786440 | tf_op jit(solution)/shard_map/ppermute | solution.py:33
  2.3 12.6 %collective-permute-start.3 = (bf16[128,1024]{1,0:T(8,128)(2,1)}, bf16[128,1024]{1,0:T(8,128)(2,1)S(1)}, u32[]{:S(2)}, u32[]{:S(2)}) collective-permute-start(bf16[128,1024]{1,0:T(8,128)(2,1)} %bitcast.9), channel_id=1, source_target_pairs={{0,12},{1,13},{2,14},{3,15},{4,0},{5,1},{6,2},{7,3},{8,4},{9,5},{1... | collective-permute-start | bytes 786440 | tf_op jit(solution)/shard_map/ppermute | solution.py:33
  3.9 7.3 %collective-permute-start = (bf16[64,1024]{1,0:T(8,128)(2,1)}, bf16[64,1024]{1,0:T(8,128)(2,1)S(1)}, u32[]{:S(2)}, u32[]{:S(2)}) collective-permute-start(bf16[64,1024]{1,0:T(8,128)(2,1)} %bitcast.11), channel_id=1, source_target_pairs={{0,1},{1,2},{2,3},{3,0},{4,5},{5,6},{6,7},{7,4},{8,9},{9,10},{10,1... | collective-permute-start | bytes 393224 | tf_op jit(solution)/shard_map/ppermute | solution.py:33
  14.6 7.4 %collective-permute-start.4 = (bf16[64,1024]{1,0:T(8,128)(2,1)S(1)}, bf16[64,1024]{1,0:T(8,128)(2,1)S(1)}, u32[]{:S(2)}, u32[]{:S(2)}) collective-permute-start(bf16[64,1024]{1,0:T(8,128)(2,1)S(1)} %slice.96), channel_id=1, source_target_pairs={{0,4},{1,5},{2,6},{3,7},{4,8},{5,9},{6,10},{7,11},{8,12},{9,13},{1... | collective-permute-start | bytes 393224 | tf_op jit(solution)/shard_map/ppermute | solution.py:33
  18.1 18.2 %collective-permute-start.12 = (bf16[352,1024]{1,0:T(8,128)(2,1)S(1)}, bf16[352,1024]{1,0:T(8,128)(2,1)S(1)}, u32[]{:S(2)}, u32[]{:S(2)}) collective-permute-start(bf16[352,1024]{1,0:T(8,128)(2,1)S(1)} %get-tuple-element.34), channel_id=1, source_target_pairs={{0,4},{1,5},{2,6},{3,7},{4,8},{5,9},{6,10},{7,11},{8,12},{9,13},{1... | collective-permute-start | bytes 2162696 | tf_op jit(solution)/shard_map/ppermute | solution.py:33
  18.2 18.2 %collective-permute-start.13 = (bf16[352,1024]{1,0:T(8,128)(2,1)S(1)}, bf16[352,1024]{1,0:T(8,128)(2,1)S(1)}, u32[]{:S(2)}, u32[]{:S(2)}) collective-permute-start(bf16[352,1024]{1,0:T(8,128)(2,1)S(1)} %get-tuple-element.33.refs_5_), channel_id=1, source_target_pairs={{0,12},{1,13},{2,14},{3,15},{4,0},{5,1},{6,2},{7,3},{8,4},{9,5},{1... | collective-permute-start | bytes 2162696 | tf_op jit(solution)/shard_map/ppermute | solution.py:33
  22.2 17.5 %collective-permute-start.6 = (bf16[1280,256]{1,0:T(8,128)(2,1)S(1)}, bf16[1280,256]{1,0:T(8,128)(2,1)S(1)}, u32[]{:S(2)}, u32[]{:S(2)}) collective-permute-start(bf16[1280,256]{1,0:T(8,128)(2,1)S(1)} %lower.1.refs_0_), channel_id=1, source_target_pairs={{0,1},{1,2},{2,3},{3,0},{4,5},{5,6},{6,7},{7,4},{8,9},{9,10},{10,1... | collective-permute-start | bytes 1966088 | tf_op jit(solution)/shard_map/ppermute | solution.py:33
  23.0 16.7 %collective-permute-start.7 = (bf16[1280,256]{1,0:T(8,128)(2,1)S(1)}, bf16[1280,256]{1,0:T(8,128)(2,1)S(1)}, u32[]{:S(2)}, u32[]{:S(2)}) collective-permute-start(bf16[1280,256]{1,0:T(8,128)(2,1)S(1)} %lower.1.refs_0_), channel_id=1, source_target_pairs={{0,3},{1,0},{2,1},{3,2},{4,7},{5,4},{6,5},{7,6},{8,11},{9,8},{10,9... | collective-permute-start | bytes 1966088 | tf_op jit(solution)/shard_map/ppermute | solution.py:33
  36.3 8.8 %collective-permute-start.14 = (bf16[160,1024]{1,0:T(8,128)(2,1)S(1)}, bf16[160,1024]{1,0:T(8,128)(2,1)S(1)}, u32[]{:S(2)}, u32[]{:S(2)}) collective-permute-start(bf16[160,1024]{1,0:T(8,128)(2,1)S(1)} %slice.98), channel_id=1, source_target_pairs={{0,4},{1,5},{2,6},{3,7},{4,8},{5,9},{6,10},{7,11},{8,12},{9,13},{1... | collective-permute-start | bytes 983048 | tf_op jit(solution)/shard_map/ppermute | solution.py:33
  36.4 8.7 %collective-permute-start.15 = (bf16[160,1024]{1,0:T(8,128)(2,1)S(1)}, bf16[160,1024]{1,0:T(8,128)(2,1)S(1)}, u32[]{:S(2)}, u32[]{:S(2)}) collective-permute-start(bf16[160,1024]{1,0:T(8,128)(2,1)S(1)} %slice.99), channel_id=1, source_target_pairs={{0,12},{1,13},{2,14},{3,15},{4,0},{5,1},{6,2},{7,3},{8,4},{9,5},{1... | collective-permute-start | bytes 983048 | tf_op jit(solution)/shard_map/ppermute | solution.py:33
  39.7 8.4 %collective-permute-start.8 = (bf16[640,256]{1,0:T(8,128)(2,1)S(1)}, bf16[640,256]{1,0:T(8,128)(2,1)S(1)}, u32[]{:S(2)}, u32[]{:S(2)}) collective-permute-start(bf16[640,256]{1,0:T(8,128)(2,1)S(1)} %slice.74), channel_id=1, source_target_pairs={{0,1},{1,2},{2,3},{3,0},{4,5},{5,6},{6,7},{7,4},{8,9},{9,10},{10,1... | collective-permute-start | bytes 983048 | tf_op jit(solution)/shard_map/ppermute | solution.py:33
  40.0 8.1 %collective-permute-start.9 = (bf16[640,256]{1,0:T(8,128)(2,1)S(1)}, bf16[640,256]{1,0:T(8,128)(2,1)S(1)}, u32[]{:S(2)}, u32[]{:S(2)}) collective-permute-start(bf16[640,256]{1,0:T(8,128)(2,1)S(1)} %slice.75), channel_id=1, source_target_pairs={{0,3},{1,0},{2,1},{3,2},{4,7},{5,4},{6,5},{7,6},{8,11},{9,8},{10,9... | collective-permute-start | bytes 983048 | tf_op jit(solution)/shard_map/ppermute | solution.py:33
  52.6 12.2 %collective-permute-start.16 = (bf16[128,2048]{1,0:T(8,128)(2,1)}, bf16[128,2048]{1,0:T(8,128)(2,1)S(1)}, u32[]{:S(2)}, u32[]{:S(2)}) collective-permute-start(bf16[128,2048]{1,0:T(8,128)(2,1)} %get-tuple-element.36), channel_id=1, source_target_pairs={{0,4},{1,5},{2,6},{3,7},{4,8},{5,9},{6,10},{7,11},{8,12},{9,13},{1... | collective-permute-start | bytes 1572872 | tf_op jit(solution)/shard_map/ppermute | solution.py:33
  52.6 12.3 %collective-permute-start.17 = (bf16[128,2048]{1,0:T(8,128)(2,1)}, bf16[128,2048]{1,0:T(8,128)(2,1)S(1)}, u32[]{:S(2)}, u32[]{:S(2)}) collective-permute-start(bf16[128,2048]{1,0:T(8,128)(2,1)} %get-tuple-element.36), channel_id=1, source_target_pairs={{0,12},{1,13},{2,14},{3,15},{4,0},{5,1},{6,2},{7,3},{8,4},{9,5},{1... | collective-permute-start | bytes 1572872 | tf_op jit(solution)/shard_map/ppermute | solution.py:33
  55.8 12.6 %collective-permute-start.20 = (bf16[128,2048]{1,0:T(8,128)(2,1)}, bf16[128,2048]{1,0:T(8,128)(2,1)S(1)}, u32[]{:S(2)}, u32[]{:S(2)}) collective-permute-start(bf16[128,2048]{1,0:T(8,128)(2,1)} %get-tuple-element.36), channel_id=1, source_target_pairs={{0,1},{1,2},{2,3},{3,0},{4,5},{5,6},{6,7},{7,4},{8,9},{9,10},{10,1... | collective-permute-start | bytes 1572872 | tf_op jit(solution)/shard_map/ppermute | solution.py:33
  56.4 12.7 %collective-permute-start.21 = (bf16[128,2048]{1,0:T(8,128)(2,1)}, bf16[128,2048]{1,0:T(8,128)(2,1)S(1)}, u32[]{:S(2)}, u32[]{:S(2)}) collective-permute-start(bf16[128,2048]{1,0:T(8,128)(2,1)} %get-tuple-element.36), channel_id=1, source_target_pairs={{0,3},{1,0},{2,1},{3,2},{4,7},{5,4},{6,5},{7,6},{8,11},{9,8},{10,9... | collective-permute-start | bytes 1572872 | tf_op jit(solution)/shard_map/ppermute | solution.py:33
  64.8 7.7 %collective-permute-start.18 = (bf16[64,2048]{1,0:T(8,128)(2,1)S(1)}, bf16[64,2048]{1,0:T(8,128)(2,1)S(1)}, u32[]{:S(2)}, u32[]{:S(2)}) collective-permute-start(bf16[64,2048]{1,0:T(8,128)(2,1)S(1)} %slice.100), channel_id=1, source_target_pairs={{0,4},{1,5},{2,6},{3,7},{4,8},{5,9},{6,10},{7,11},{8,12},{9,13},{1... | collective-permute-start | bytes 786440 | tf_op jit(solution)/shard_map/ppermute | solution.py:33
  64.9 7.6 %collective-permute-start.19 = (bf16[64,2048]{1,0:T(8,128)(2,1)S(1)}, bf16[64,2048]{1,0:T(8,128)(2,1)S(1)}, u32[]{:S(2)}, u32[]{:S(2)}) collective-permute-start(bf16[64,2048]{1,0:T(8,128)(2,1)S(1)} %slice.101), channel_id=1, source_target_pairs={{0,12},{1,13},{2,14},{3,15},{4,0},{5,1},{6,2},{7,3},{8,4},{9,5},{1... | collective-permute-start | bytes 786440 | tf_op jit(solution)/shard_map/ppermute | solution.py:33
  68.4 7.7 %collective-permute-start.22 = (bf16[64,2048]{1,0:T(8,128)(2,1)S(1)}, bf16[64,2048]{1,0:T(8,128)(2,1)S(1)}, u32[]{:S(2)}, u32[]{:S(2)}) collective-permute-start(bf16[64,2048]{1,0:T(8,128)(2,1)S(1)} %slice.102), channel_id=1, source_target_pairs={{0,1},{1,2},{2,3},{3,0},{4,5},{5,6},{6,7},{7,4},{8,9},{9,10},{10,1... | collective-permute-start | bytes 786440 | tf_op jit(solution)/shard_map/ppermute | solution.py:33
  77.5 8.0 %collective-permute-start.24 = (bf16[256,512]{1,0:T(8,128)(2,1)S(1)}, bf16[256,512]{1,0:T(8,128)(2,1)S(1)}, u32[]{:S(2)}, u32[]{:S(2)}) collective-permute-start(bf16[256,512]{1,0:T(8,128)(2,1)S(1)} %tile.2), channel_id=1, source_target_pairs={{0,64},{16,80},{32,96},{48,112},{64,0},{80,16},{96,32},{112,48},{1... | collective-permute-start | bytes 786440 | tf_op jit(solution)/shard_map/ppermute | solution.py:38
  82.1 8.0 %collective-permute-start.32 = (bf16[256,512]{1,0:T(8,128)(2,1)S(1)}, bf16[256,512]{1,0:T(8,128)(2,1)S(1)}, u32[]{:S(2)}, u32[]{:S(2)}) collective-permute-start(bf16[256,512]{1,0:T(8,128)(2,1)S(1)} %tile.3), channel_id=1, source_target_pairs={{0,64},{16,80},{32,96},{48,112},{64,0},{80,16},{96,32},{112,48},{1... | collective-permute-start | bytes 786440 | tf_op jit(solution)/shard_map/ppermute | solution.py:38
  85.5 8.0 %collective-permute-start.25 = (bf16[256,512]{1,0:T(8,128)(2,1)S(1)}, bf16[256,512]{1,0:T(8,128)(2,1)S(1)}, u32[]{:S(2)}, u32[]{:S(2)}) collective-permute-start(bf16[256,512]{1,0:T(8,128)(2,1)S(1)} %collective-permute-done.24), channel_id=1, source_target_pairs={{0,4},{1,5},{2,6},{3,7},{4,8},{5,9},{6,10},{7,11},{8,12},{9,13},{1... | collective-permute-start | bytes 786440 | tf_op jit(solution)/shard_map/ppermute | solution.py:33
  85.5 8.1 %collective-permute-start.26 = (bf16[256,512]{1,0:T(8,128)(2,1)S(1)}, bf16[256,512]{1,0:T(8,128)(2,1)S(1)}, u32[]{:S(2)}, u32[]{:S(2)}) collective-permute-start(bf16[256,512]{1,0:T(8,128)(2,1)S(1)} %collective-permute-done.24), channel_id=1, source_target_pairs={{0,12},{1,13},{2,14},{3,15},{4,0},{5,1},{6,2},{7,3},{8,4},{9,5},{1... | collective-permute-start | bytes 786440 | tf_op jit(solution)/shard_map/ppermute | solution.py:33
  90.0 7.6 %collective-permute-start.33 = (bf16[256,512]{1,0:T(8,128)(2,1)S(1)}, bf16[256,512]{1,0:T(8,128)(2,1)S(1)}, u32[]{:S(2)}, u32[]{:S(2)}) collective-permute-start(bf16[256,512]{1,0:T(8,128)(2,1)S(1)} %collective-permute-done.32), channel_id=1, source_target_pairs={{0,4},{1,5},{2,6},{3,7},{4,8},{5,9},{6,10},{7,11},{8,12},{9,13},{1... | collective-permute-start | bytes 786440 | tf_op jit(solution)/shard_map/ppermute | solution.py:33
  90.0 7.7 %collective-permute-start.34 = (bf16[256,512]{1,0:T(8,128)(2,1)S(1)}, bf16[256,512]{1,0:T(8,128)(2,1)S(1)}, u32[]{:S(2)}, u32[]{:S(2)}) collective-permute-start(bf16[256,512]{1,0:T(8,128)(2,1)S(1)} %collective-permute-done.32), channel_id=1, source_target_pairs={{0,12},{1,13},{2,14},{3,15},{4,0},{5,1},{6,2},{7,3},{8,4},{9,5},{1... | collective-permute-start | bytes 786440 | tf_op jit(solution)/shard_map/ppermute | solution.py:33
  93.5 7.6 %collective-permute-start.27 = (bf16[128,512]{1,0:T(8,128)(2,1)S(1)}, bf16[128,512]{1,0:T(8,128)(2,1)S(1)}, u32[]{:S(2)}, u32[]{:S(2)}) collective-permute-start(bf16[128,512]{1,0:T(8,128)(2,1)S(1)} %slice.104), channel_id=1, source_target_pairs={{0,4},{1,5},{2,6},{3,7},{4,8},{5,9},{6,10},{7,11},{8,12},{9,13},{1... | collective-permute-start | bytes 393224 | tf_op jit(solution)/shard_map/ppermute | solution.py:33
  93.6 7.5 %collective-permute-start.28 = (bf16[128,512]{1,0:T(8,128)(2,1)S(1)}, bf16[128,512]{1,0:T(8,128)(2,1)S(1)}, u32[]{:S(2)}, u32[]{:S(2)}) collective-permute-start(bf16[128,512]{1,0:T(8,128)(2,1)S(1)} %slice.105), channel_id=1, source_target_pairs={{0,12},{1,13},{2,14},{3,15},{4,0},{5,1},{6,2},{7,3},{8,4},{9,5},{1... | collective-permute-start | bytes 393224 | tf_op jit(solution)/shard_map/ppermute | solution.py:33
  104.7 7.9 %collective-permute-start.37 = (bf16[3,256,128]{2,1,0:T(8,128)(2,1)S(1)}, bf16[3,256,128]{2,1,0:T(8,128)(2,1)S(1)}, u32[]{:S(2)}, u32[]{:S(2)}) collective-permute-start(bf16[3,256,128]{2,1,0:T(8,128)(2,1)S(1)} %get-tuple-element.45), channel_id=1, source_target_pairs={{0,1},{1,2},{2,3},{3,0},{4,5},{5,6},{6,7},{7,4},{8,9},{9,10},{10,1... | collective-permute-start | bytes 589832 | tf_op jit(solution)/shard_map/ppermute | solution.py:33
  106.3 9.0 %collective-permute-start.38 = (bf16[3,256,128]{2,1,0:T(8,128)(2,1)S(1)}, bf16[3,256,128]{2,1,0:T(8,128)(2,1)S(1)}, u32[]{:S(2)}, u32[]{:S(2)}) collective-permute-start(bf16[3,256,128]{2,1,0:T(8,128)(2,1)S(1)} %get-tuple-element.44), channel_id=1, source_target_pairs={{0,2},{1,3},{2,0},{3,1},{4,6},{5,7},{6,4},{7,5},{8,10},{9,11},{10,... | collective-permute-start | bytes 589832 | tf_op jit(solution)/shard_map/ppermute | solution.py:33
  111.1 9.0 %collective-permute-start.29 = (bf16[3,256,128]{2,1,0:T(8,128)(2,1)S(1)}, bf16[3,256,128]{2,1,0:T(8,128)(2,1)S(1)}, u32[]{:S(2)}, u32[]{:S(2)}) collective-permute-start(bf16[3,256,128]{2,1,0:T(8,128)(2,1)S(1)} %get-tuple-element.42), channel_id=1, source_target_pairs={{0,1},{1,2},{2,3},{3,0},{4,5},{5,6},{6,7},{7,4},{8,9},{9,10},{10,1... | collective-permute-start | bytes 589832 | tf_op jit(solution)/shard_map/ppermute | solution.py:33
  111.7 8.4 %collective-permute-start.30 = (bf16[3,256,128]{2,1,0:T(8,128)(2,1)S(1)}, bf16[3,256,128]{2,1,0:T(8,128)(2,1)S(1)}, u32[]{:S(2)}, u32[]{:S(2)}) collective-permute-start(bf16[3,256,128]{2,1,0:T(8,128)(2,1)S(1)} %get-tuple-element.41), channel_id=1, source_target_pairs={{0,2},{1,3},{2,0},{3,1},{4,6},{5,7},{6,4},{7,5},{8,10},{9,11},{10,... | collective-permute-start | bytes 589832 | tf_op jit(solution)/shard_map/ppermute | solution.py:33
  112.6 8.3 %collective-permute-start.31 = (bf16[3,256,128]{2,1,0:T(8,128)(2,1)S(1)}, bf16[3,256,128]{2,1,0:T(8,128)(2,1)S(1)}, u32[]{:S(2)}, u32[]{:S(2)}) collective-permute-start(bf16[3,256,128]{2,1,0:T(8,128)(2,1)S(1)} %get-tuple-element.40), channel_id=1, source_target_pairs={{0,3},{1,0},{2,1},{3,2},{4,7},{5,4},{6,5},{7,6},{8,11},{9,8},{10,9... | collective-permute-start | bytes 589832 | tf_op jit(solution)/shard_map/ppermute | solution.py:33
  (15 other events, 115.3 us)

commit v5 on v4

--- a/solution.py
+++ b/solution.py
@@ -110,6 +110,7 @@
 
 
 WIDE = SIDE * ROWS
+TALL = 576
 LOWER = [(x, chunk) for x in range(SIDE) for chunk in range(x + 1)]
 CHUNKS = len(LOWER)
 
@@ -150,22 +151,28 @@
 
 def panel_kernel(border, *refs):
     inverses, panels, (link_out, factor) = refs[:5], refs[5:10], refs[10:12]
-    mats, panel, link, updated = refs[12:]
+    mats, both, link, updated = refs[12:]
     front = lax.axis_index("front")
     unpack_inverses(front, inverses, mats)
 
-    def keep_first(at, value):
-        factor[:, at : at + WIDE] = value.astype(jnp.bfloat16)
-
-    def keep_link(at, value):
-        link[:, at : at + WIDE] = value.astype(jnp.bfloat16)
+    both[:BLOCK] = border[:, :PANEL]
+    unpack_panel(front, panels, both.at[BLOCK:])
+
+    def keep_both(up):
+        def keep(at, value):
+            if up == 0:
+                factor[:, at : at + WIDE] = value[:BLOCK].astype(jnp.bfloat16)
+                value = value[BLOCK:]
+            first = max(up - BLOCK, 0)
+            link[first : first + value.shape[0], at : at + WIDE] = value.astype(jnp.bfloat16)
+
+        return keep
 
     def keep_second(at, value):
         factor[:, PANEL + at : PANEL + at + WIDE] = value.astype(jnp.bfloat16)
 
-    project(border, mats.at[0], keep_first)
-    unpack_panel(front, panels, panel)
-    project(panel, mats.at[0], keep_link)
+    for up in range(0, BLOCK + PANEL, TALL):
+        project(both.at[up : up + TALL], mats.at[0], keep_both(up))
     link_out[...] = link[pl.ds(pl.multiple_of(front * ROWS, ROWS), ROWS), :]
     for at in range(0, PANEL, WIDE):
         coupled = dot_nt(factor[:, :PANEL], link[at : at + WIDE, :])
@@ -191,7 +198,7 @@
         out_specs=(VMEM_SPEC,) * 2,
         scratch_shapes=[
             pltpu.VMEM((2, PANEL, PANEL), jnp.bfloat16),
-            pltpu.VMEM((PANEL, PANEL), jnp.bfloat16),
+            pltpu.VMEM((BLOCK + PANEL, PANEL), jnp.bfloat16),
             pltpu.VMEM((PANEL, PANEL), jnp.bfloat16),
             pltpu.VMEM((BLOCK, PANEL), jnp.bfloat16),
         ],
@@ -485,12 +492,17 @@
     link_local, factor_local = eliminate(border[0], chunks, panels)
 
     rows_x, rows_z = bundle_of(factor_local, "x"), bundle_of(factor_local, "z")
+    rows_x, rows_z = lax.optimization_barrier((rows_x, rows_z))
+    factor_local = rows_z[:BLOCK]
     tails = (folded, from_left, from_right, ahead, behind)
 
     tiles = {}
     for chunk in CHUNKS_OF_ROWS:
         rows = make_tile(chunk, front_sizes, rows_x, rows_z, tails)
-        packed = pack_tiles(plan, bundle_of(to_parent(rows), "x"))
+        there = to_parent(rows)
+        if chunk is FIRST:
+            there, factor_local = lax.optimization_barrier((there, factor_local))
+        packed = pack_tiles(plan, bundle_of(there, "x"))
         for step in range(SIDE):
             tile = packed[step * SLOTS : (step + 1) * SLOTS]
             tiles[chunk, step] = shift(tile, "z", step) if step else tile

time: 124 us -> 122 us (0.984)
  transfers between devices with their start and end apart: 40 -> 40, of which waited for: 16 -> 16; matrix products, arithmetic and copies ran while one was open for 2% -> 1% of each run, Pallas kernels for 6% -> 6%
where the time goes in v5:
time: 122 us; the launch traced here: 121 us
  starting transfers between devices  67.5 us (55%)
  waiting for transfers between devices  33.2 us (27%)
  Pallas kernels  14.8 us (12%)
  local copies, waits for them, and re-layouts  4.73 us (4%)
  between operations  1.26 us (1%)
    ppermute x38, starting transfers between devices, shift(): return lax.ppermute(value, 'front', pairs)  63.8 us
    ppermute x38, waiting for transfers between devices, shift(): return lax.ppermute(value, 'front', pairs)  29.7 us
    ppermute x2, starting transfers between devices, to_parent(): lax.ppermute(value, 'leaf', [(g, (g + groups // 2) % groups) for g in ran...  3.69 us
    pallas_call x2, Pallas kernels, place_tiles(): pl.pallas_call(functools.partial(place_kernel, list(tiles)), out_shape=PA...  3.65 us
    pallas_call x1, Pallas kernels, blank_rows(): pl.pallas_call(blank_kernel, out_shape=(PARENT, jax.ShapeDtypeStruct((2 *...  3.51 us
    unnamed x30, local copies, waits for them, and re-layouts  3.5 us
    ppermute x2, waiting for transfers between devices, to_parent(): lax.ppermute(value, 'leaf', [(g, (g + groups // 2) % groups) for g in ran...  3.48 us
    pallas_call x1, Pallas kernels, eliminate(): pl.pallas_call(panel_kernel, out_shape=(jax.ShapeDtypeStruct((ROWS, PANEL...  3.33 us
  transfers between devices with their start and end apart: 40, of which 16 were waited for; matrix products, arithmetic and copies ran while one was open for 1% of the time, Pallas kernels for 6%

profile of v5, /device:TPU:0, one launch (start us, length us, event | category | flops | bytes accessed | tf_op | source)
XLA Modules:
  0.0 121.5 jit_solution(11139325547072557012)
XLA Ops:
  2.3 1.7 %collective-permute-start.3 = (bf16[128,1024]{1,0:T(8,128)(2,1)}, bf16[128,1024]{1,0:T(8,128)(2,1)S(1)}, u32[]{:S(2)}, u32[]{:S(2)}) collective-permute-start(bf16[128,1024]{1,0:T(8,128)(2,1)} %bitcast.9), channel_id=1, source_target_pairs={{0,12},{1,13},{2,14},{3,15},{4,0},{5,1},{6,2},{7,3},{8,4},{9,5},{1... | collective-permute-start | bytes 786440 | tf_op jit(solution)/shard_map/ppermute | solution.py:33
  3.9 2.0 %collective-permute-start = (bf16[64,1024]{1,0:T(8,128)(2,1)}, bf16[64,1024]{1,0:T(8,128)(2,1)S(1)}, u32[]{:S(2)}, u32[]{:S(2)}) collective-permute-start(bf16[64,1024]{1,0:T(8,128)(2,1)} %bitcast.11), channel_id=1, source_target_pairs={{0,1},{1,2},{2,3},{3,0},{4,5},{5,6},{6,7},{7,4},{8,9},{9,10},{10,1... | collective-permute-start | bytes 393224 | tf_op jit(solution)/shard_map/ppermute | solution.py:33
  5.9 2.1 %collective-permute-start.1 = (bf16[64,1024]{1,0:T(8,128)(2,1)}, bf16[64,1024]{1,0:T(8,128)(2,1)S(1)}, u32[]{:S(2)}, u32[]{:S(2)}) collective-permute-start(bf16[64,1024]{1,0:T(8,128)(2,1)} %bitcast.12), channel_id=1, source_target_pairs={{0,3},{1,0},{2,1},{3,2},{4,7},{5,4},{6,5},{7,6},{8,11},{9,8},{10,9... | collective-permute-start | bytes 393224 | tf_op jit(solution)/shard_map/ppermute | solution.py:33
  11.2 1.8 %collective-permute-start.10 = (bf16[32,1024]{1,0:T(8,128)(2,1)S(1)}, bf16[32,1024]{1,0:T(8,128)(2,1)S(1)}, u32[]{:S(2)}, u32[]{:S(2)}) collective-permute-start(bf16[32,1024]{1,0:T(8,128)(2,1)S(1)} %slice.79), channel_id=1, source_target_pairs={{0,1},{1,2},{2,3},{3,0},{4,5},{5,6},{6,7},{7,4},{8,9},{9,10},{10,1... | collective-permute-start | bytes 196616 | tf_op jit(solution)/shard_map/ppermute | solution.py:33
  14.9 3.0 %collective-permute-start.5 = (bf16[64,1024]{1,0:T(8,128)(2,1)S(1)}, bf16[64,1024]{1,0:T(8,128)(2,1)S(1)}, u32[]{:S(2)}, u32[]{:S(2)}) collective-permute-start(bf16[64,1024]{1,0:T(8,128)(2,1)S(1)} %slice.101), channel_id=1, source_target_pairs={{0,12},{1,13},{2,14},{3,15},{4,0},{5,1},{6,2},{7,3},{8,4},{9,5},{1... | collective-permute-start | bytes 393224 | tf_op jit(solution)/shard_map/ppermute | solution.py:33
  18.2 3.2 %collective-permute-start.13 = (bf16[352,1024]{1,0:T(8,128)(2,1)S(1)}, bf16[352,1024]{1,0:T(8,128)(2,1)S(1)}, u32[]{:S(2)}, u32[]{:S(2)}) collective-permute-start(bf16[352,1024]{1,0:T(8,128)(2,1)S(1)} %get-tuple-element.37.refs_5_), channel_id=1, source_target_pairs={{0,12},{1,13},{2,14},{3,15},{4,0},{5,1},{6,2},{7,3},{8,4},{9,5},{1... | collective-permute-start | bytes 2162696 | tf_op jit(solution)/shard_map/ppermute | solution.py:33
  23.0 2.5 %collective-permute-start.7 = (bf16[1280,256]{1,0:T(8,128)(2,1)S(1)}, bf16[1280,256]{1,0:T(8,128)(2,1)S(1)}, u32[]{:S(2)}, u32[]{:S(2)}) collective-permute-start(bf16[1280,256]{1,0:T(8,128)(2,1)S(1)} %lower.1.refs_0_), channel_id=1, source_target_pairs={{0,3},{1,0},{2,1},{3,2},{4,7},{5,4},{6,5},{7,6},{8,11},{9,8},{10,9... | collective-permute-start | bytes 1966088 | tf_op jit(solution)/shard_map/ppermute | solution.py:33
  25.5 3.5 %blank.1 = (f32[4096,384]{1,0:T(8,128)}, s32[32]{0:T(128)S(1)}) custom-call(s32[8,16]{1,0:T(8,128)S(1)} %copy-done.3, s32[8,32]{1,0:T(8,128)S(1)} %copy-done.4), custom_call_target="tpu_custom_call" | custom-call | bytes 3145728 | tf_op jit(solution)/shard_map/blank/pallas_call | solution.py:414
  29.0 7.3 %collective-permute-done.12.refs_6_.refs_1_ = bf16[352,1024]{1,0:T(8,128)(2,1)S(1)} collective-permute-done((bf16[352,1024]{1,0:T(8,128)(2,1)S(1)}, bf16[352,1024]{1,0:T(8,128)(2,1)S(1)}, u32[]{:S(2)}, u32[]{:S(2)}) %collective-permute-start.12) | collective-permute-done | bytes 720928 | tf_op jit(solution)/shard_map/ppermute | solution.py:33
  36.4 3.3 %collective-permute-start.15 = (bf16[160,1024]{1,0:T(8,128)(2,1)S(1)}, bf16[160,1024]{1,0:T(8,128)(2,1)S(1)}, u32[]{:S(2)}, u32[]{:S(2)}) collective-permute-start(bf16[160,1024]{1,0:T(8,128)(2,1)S(1)} %slice.103), channel_id=1, source_target_pairs={{0,12},{1,13},{2,14},{3,15},{4,0},{5,1},{6,2},{7,3},{8,4},{9,5},{1... | collective-permute-start | bytes 983048 | tf_op jit(solution)/shard_map/ppermute | solution.py:33
  40.0 3.1 %collective-permute-start.9 = (bf16[640,256]{1,0:T(8,128)(2,1)S(1)}, bf16[640,256]{1,0:T(8,128)(2,1)S(1)}, u32[]{:S(2)}, u32[]{:S(2)}) collective-permute-start(bf16[640,256]{1,0:T(8,128)(2,1)S(1)} %slice.78), channel_id=1, source_target_pairs={{0,3},{1,0},{2,1},{3,2},{4,7},{5,4},{6,5},{7,6},{8,11},{9,8},{10,9... | collective-permute-start | bytes 983048 | tf_op jit(solution)/shard_map/ppermute | solution.py:33
  43.1 2.0 %collective-permute-done.14.refs_8_.refs_3_ = bf16[160,1024]{1,0:T(8,128)(2,1)S(1)} collective-permute-done((bf16[160,1024]{1,0:T(8,128)(2,1)S(1)}, bf16[160,1024]{1,0:T(8,128)(2,1)S(1)}, u32[]{:S(2)}, u32[]{:S(2)}) %collective-permute-start.14) | collective-permute-done | bytes 327712 | tf_op jit(solution)/shard_map/ppermute | solution.py:33
  45.1 3.0 %collective-permute-done.8.refs_3_ = bf16[640,256]{1,0:T(8,128)(2,1)S(1)} collective-permute-done((bf16[640,256]{1,0:T(8,128)(2,1)S(1)}, bf16[640,256]{1,0:T(8,128)(2,1)S(1)}, u32[]{:S(2)}, u32[]{:S(2)}) %collective-permute-start.8) | collective-permute-done | bytes 327712 | tf_op jit(solution)/shard_map/ppermute | solution.py:33
  48.1 3.3 %panels.1 = (bf16[64,1024]{1,0:T(8,128)(2,1)}, bf16[128,2048]{1,0:T(8,128)(2,1)S(1)}) custom-call(bf16[128,2048]{1,0:T(8,128)(2,1)S(1)} %bitcast.14, bf16[1280,256]{1,0:T(8,128)(2,1)S(1)} %lower.1.refs_0_, bf16[1280,256]{1,0:T(8,128)(2,1)S(1)} %collective-permute-done.6.refs_1_, bf16[1280,256]{1,0:T(8,128)(2,1)S(1)} %collective-permute-done.7.refs_2_, ...), custom_call_target="tpu_custom_call" | custom-call | flops 2952790016 | bytes 8388608 | tf_op jit(solution)/shard_map/panels/pallas_call | solution.py:191
  51.4 3.2 %collective-permute-start.17 = (bf16[128,2048]{1,0:T(8,128)(2,1)S(1)}, bf16[128,2048]{1,0:T(8,128)(2,1)S(1)}, u32[]{:S(2)}, u32[]{:S(2)}) collective-permute-start(bf16[128,2048]{1,0:T(8,128)(2,1)S(1)} %get-tuple-element.40), channel_id=1, source_target_pairs={{0,12},{1,13},{2,14},{3,15},{4,0},{5,1},{6,2},{7,3},{8,4},{9,5},{1... | collective-permute-start | bytes 1572872 | tf_op jit(solution)/shard_map/ppermute | solution.py:33
  55.2 2.7 %collective-permute-start.21 = (bf16[128,2048]{1,0:T(8,128)(2,1)S(1)}, bf16[128,2048]{1,0:T(8,128)(2,1)S(1)}, u32[]{:S(2)}, u32[]{:S(2)}) collective-permute-start(bf16[128,2048]{1,0:T(8,128)(2,1)S(1)} %get-tuple-element.40), channel_id=1, source_target_pairs={{0,3},{1,0},{2,1},{3,2},{4,7},{5,4},{6,5},{7,6},{8,11},{9,8},{10,9... | collective-permute-start | bytes 1572872 | tf_op jit(solution)/shard_map/ppermute | solution.py:33
  58.3 5.1 %collective-permute-done.16 = bf16[128,2048]{1,0:T(8,128)(2,1)S(1)} collective-permute-done((bf16[128,2048]{1,0:T(8,128)(2,1)S(1)}, bf16[128,2048]{1,0:T(8,128)(2,1)S(1)}, u32[]{:S(2)}, u32[]{:S(2)}) %collective-permute-start.16) | collective-permute-done | bytes 524320 | tf_op jit(solution)/shard_map/ppermute | solution.py:33
  63.6 3.5 %collective-permute-start.19 = (bf16[64,2048]{1,0:T(8,128)(2,1)S(1)}, bf16[64,2048]{1,0:T(8,128)(2,1)S(1)}, u32[]{:S(2)}, u32[]{:S(2)}) collective-permute-start(bf16[64,2048]{1,0:T(8,128)(2,1)S(1)} %slice.105), channel_id=1, source_target_pairs={{0,12},{1,13},{2,14},{3,15},{4,0},{5,1},{6,2},{7,3},{8,4},{9,5},{1... | collective-permute-start | bytes 786440 | tf_op jit(solution)/shard_map/ppermute | solution.py:33
  67.7 2.8 %collective-permute-start.23 = (bf16[64,2048]{1,0:T(8,128)(2,1)S(1)}, bf16[64,2048]{1,0:T(8,128)(2,1)S(1)}, u32[]{:S(2)}, u32[]{:S(2)}) collective-permute-start(bf16[64,2048]{1,0:T(8,128)(2,1)S(1)} %slice.107), channel_id=1, source_target_pairs={{0,3},{1,0},{2,1},{3,2},{4,7},{5,4},{6,5},{7,6},{8,11},{9,8},{10,9... | collective-permute-start | bytes 786440 | tf_op jit(solution)/shard_map/ppermute | solution.py:33
  71.2 3.6 %collective-permute-done.22 = bf16[64,2048]{1,0:T(8,128)(2,1)S(1)} collective-permute-done((bf16[64,2048]{1,0:T(8,128)(2,1)S(1)}, bf16[64,2048]{1,0:T(8,128)(2,1)S(1)}, u32[]{:S(2)}, u32[]{:S(2)}) %collective-permute-start.22) | collective-permute-done | bytes 262176 | tf_op jit(solution)/shard_map/ppermute | solution.py:33
  76.2 3.3 %collective-permute-start.25 = (bf16[256,512]{1,0:T(8,128)(2,1)S(1)}, bf16[256,512]{1,0:T(8,128)(2,1)S(1)}, u32[]{:S(2)}, u32[]{:S(2)}) collective-permute-start(bf16[256,512]{1,0:T(8,128)(2,1)S(1)} %tile.3), channel_id=1, source_target_pairs={{0,64},{16,80},{32,96},{48,112},{64,0},{80,16},{96,32},{112,48},{1... | collective-permute-start | bytes 786440 | tf_op jit(solution)/shard_map/ppermute | solution.py:38
  82.0 2.2 %collective-permute-done.25 = bf16[256,512]{1,0:T(8,128)(2,1)S(1)} collective-permute-done((bf16[256,512]{1,0:T(8,128)(2,1)S(1)}, bf16[256,512]{1,0:T(8,128)(2,1)S(1)}, u32[]{:S(2)}, u32[]{:S(2)}) %collective-permute-start.25) | collective-permute-done | bytes 262176 | tf_op jit(solution)/shard_map/ppermute | solution.py:38
  84.1 3.2 %collective-permute-start.27 = (bf16[256,512]{1,0:T(8,128)(2,1)S(1)}, bf16[256,512]{1,0:T(8,128)(2,1)S(1)}, u32[]{:S(2)}, u32[]{:S(2)}) collective-permute-start(bf16[256,512]{1,0:T(8,128)(2,1)S(1)} %collective-permute-done.25), channel_id=1, source_target_pairs={{0,12},{1,13},{2,14},{3,15},{4,0},{5,1},{6,2},{7,3},{8,4},{9,5},{1... | collective-permute-start | bytes 786440 | tf_op jit(solution)/shard_map/ppermute | solution.py:33
  88.7 3.2 %collective-permute-start.34 = (bf16[256,512]{1,0:T(8,128)(2,1)S(1)}, bf16[256,512]{1,0:T(8,128)(2,1)S(1)}, u32[]{:S(2)}, u32[]{:S(2)}) collective-permute-start(bf16[256,512]{1,0:T(8,128)(2,1)S(1)} %collective-permute-done.24), channel_id=1, source_target_pairs={{0,12},{1,13},{2,14},{3,15},{4,0},{5,1},{6,2},{7,3},{8,4},{9,5},{1... | collective-permute-start | bytes 786440 | tf_op jit(solution)/shard_map/ppermute | solution.py:33
  92.3 3.3 %collective-permute-start.29 = (bf16[128,512]{1,0:T(8,128)(2,1)S(1)}, bf16[128,512]{1,0:T(8,128)(2,1)S(1)}, u32[]{:S(2)}, u32[]{:S(2)}) collective-permute-start(bf16[128,512]{1,0:T(8,128)(2,1)S(1)} %slice.109), channel_id=1, source_target_pairs={{0,12},{1,13},{2,14},{3,15},{4,0},{5,1},{6,2},{7,3},{8,4},{9,5},{1... | collective-permute-start | bytes 393224 | tf_op jit(solution)/shard_map/ppermute | solution.py:33
  96.4 3.3 %collective-permute-start.36 = (bf16[128,512]{1,0:T(8,128)(2,1)S(1)}, bf16[128,512]{1,0:T(8,128)(2,1)S(1)}, u32[]{:S(2)}, u32[]{:S(2)}) collective-permute-start(bf16[128,512]{1,0:T(8,128)(2,1)S(1)} %slice.114), channel_id=1, source_target_pairs={{0,12},{1,13},{2,14},{3,15},{4,0},{5,1},{6,2},{7,3},{8,4},{9,5},{1... | collective-permute-start | bytes 393224 | tf_op jit(solution)/shard_map/ppermute | solution.py:33
  100.6 2.0 %collective-permute-done.35 = bf16[128,512]{1,0:T(8,128)(2,1)S(1)} collective-permute-done((bf16[128,512]{1,0:T(8,128)(2,1)S(1)}, bf16[128,512]{1,0:T(8,128)(2,1)S(1)}, u32[]{:S(2)}, u32[]{:S(2)}) %collective-permute-start.35) | collective-permute-done | bytes 131104 | tf_op jit(solution)/shard_map/ppermute | solution.py:33
  104.9 3.3 %collective-permute-start.38 = (bf16[3,256,128]{2,1,0:T(8,128)(2,1)S(1)}, bf16[3,256,128]{2,1,0:T(8,128)(2,1)S(1)}, u32[]{:S(2)}, u32[]{:S(2)}) collective-permute-start(bf16[3,256,128]{2,1,0:T(8,128)(2,1)S(1)} %get-tuple-element.52), channel_id=1, source_target_pairs={{0,2},{1,3},{2,0},{3,1},{4,6},{5,7},{6,4},{7,5},{8,10},{9,11},{10,... | collective-permute-start | bytes 589832 | tf_op jit(solution)/shard_map/ppermute | solution.py:33
  111.3 1.8 %collective-permute-start.32 = (bf16[3,256,128]{2,1,0:T(8,128)(2,1)S(1)}, bf16[3,256,128]{2,1,0:T(8,128)(2,1)S(1)}, u32[]{:S(2)}, u32[]{:S(2)}) collective-permute-start(bf16[3,256,128]{2,1,0:T(8,128)(2,1)S(1)} %get-tuple-element.48), channel_id=1, source_target_pairs={{0,3},{1,0},{2,1},{3,2},{4,7},{5,4},{6,5},{7,6},{8,11},{9,8},{10,9... | collective-permute-start | bytes 589832 | tf_op jit(solution)/shard_map/ppermute | solution.py:33
  114.0 2.0 %place.2.refs_3_ = f32[4096,384]{1,0:T(8,128)} custom-call(s32[8,16]{1,0:T(8,128)S(1)} %copy-done.3, s32[32]{0:T(128)S(1)} %get-tuple-element.44.plan, bf16[3,256,128]{2,1,0:T(8,128)(2,1)S(1)} %get-tuple-element.54.refs_0_, bf16[3,256,128]{2,1,0:T(8,128)(2,1)S(1)} %collective-permute-done.37.refs_1_, ...), custom_call_target="tpu_custom_call", output_to_operand_aliasing={{}: (7, {})} | custom-call | bytes 1048576 | tf_op jit(solution)/shard_map/place/pallas_call | solution.py:456
  116.0 2.7 %collective-permute-done.30.refs_0_ = bf16[3,256,128]{2,1,0:T(8,128)(2,1)S(1)} collective-permute-done((bf16[3,256,128]{2,1,0:T(8,128)(2,1)S(1)}, bf16[3,256,128]{2,1,0:T(8,128)(2,1)S(1)}, u32[]{:S(2)}, u32[]{:S(2)}) %collective-permute-start.30) | collective-permute-done | bytes 196640 | tf_op jit(solution)/shard_map/ppermute | solution.py:33
  119.6 1.7 %place.3 = f32[4096,384]{1,0:T(8,128)} custom-call(s32[8,16]{1,0:T(8,128)S(1)} %copy-done.3, s32[32]{0:T(128)S(1)} %get-tuple-element.44.plan, bf16[3,256,128]{2,1,0:T(8,128)(2,1)S(1)} %collective-permute-done.30.refs_0_, bf16[3,256,128]{2,1,0:T(8,128)(2,1)S(1)} %collective-permute-done.31.refs_1_, ...), custom_call_target="tpu_custom_call", output_to_operand_aliasing={{}: (5, {})} | custom-call | bytes 1048576 | tf_op jit(solution)/shard_map/place/pallas_call | solution.py:456
  (112 shorter events, 25.5 us)
Async XLA Ops:
  0.6 13.9 %collective-permute-start.2 = (bf16[128,1024]{1,0:T(8,128)(2,1)}, bf16[128,1024]{1,0:T(8,128)(2,1)S(1)}, u32[]{:S(2)}, u32[]{:S(2)}) collective-permute-start(bf16[128,1024]{1,0:T(8,128)(2,1)} %bitcast.8), channel_id=1, source_target_pairs={{0,4},{1,5},{2,6},{3,7},{4,8},{5,9},{6,10},{7,11},{8,12},{9,13},{1... | collective-permute-start | bytes 786440 | tf_op jit(solution)/shard_map/ppermute | solution.py:33
  2.3 12.6 %collective-permute-start.3 = (bf16[128,1024]{1,0:T(8,128)(2,1)}, bf16[128,1024]{1,0:T(8,128)(2,1)S(1)}, u32[]{:S(2)}, u32[]{:S(2)}) collective-permute-start(bf16[128,1024]{1,0:T(8,128)(2,1)} %bitcast.9), channel_id=1, source_target_pairs={{0,12},{1,13},{2,14},{3,15},{4,0},{5,1},{6,2},{7,3},{8,4},{9,5},{1... | collective-permute-start | bytes 786440 | tf_op jit(solution)/shard_map/ppermute | solution.py:33
  3.9 7.3 %collective-permute-start = (bf16[64,1024]{1,0:T(8,128)(2,1)}, bf16[64,1024]{1,0:T(8,128)(2,1)S(1)}, u32[]{:S(2)}, u32[]{:S(2)}) collective-permute-start(bf16[64,1024]{1,0:T(8,128)(2,1)} %bitcast.11), channel_id=1, source_target_pairs={{0,1},{1,2},{2,3},{3,0},{4,5},{5,6},{6,7},{7,4},{8,9},{9,10},{10,1... | collective-permute-start | bytes 393224 | tf_op jit(solution)/shard_map/ppermute | solution.py:33
  14.6 7.4 %collective-permute-start.4 = (bf16[64,1024]{1,0:T(8,128)(2,1)S(1)}, bf16[64,1024]{1,0:T(8,128)(2,1)S(1)}, u32[]{:S(2)}, u32[]{:S(2)}) collective-permute-start(bf16[64,1024]{1,0:T(8,128)(2,1)S(1)} %slice.100), channel_id=1, source_target_pairs={{0,4},{1,5},{2,6},{3,7},{4,8},{5,9},{6,10},{7,11},{8,12},{9,13},{1... | collective-permute-start | bytes 393224 | tf_op jit(solution)/shard_map/ppermute | solution.py:33
  18.1 18.2 %collective-permute-start.12 = (bf16[352,1024]{1,0:T(8,128)(2,1)S(1)}, bf16[352,1024]{1,0:T(8,128)(2,1)S(1)}, u32[]{:S(2)}, u32[]{:S(2)}) collective-permute-start(bf16[352,1024]{1,0:T(8,128)(2,1)S(1)} %get-tuple-element.38), channel_id=1, source_target_pairs={{0,4},{1,5},{2,6},{3,7},{4,8},{5,9},{6,10},{7,11},{8,12},{9,13},{1... | collective-permute-start | bytes 2162696 | tf_op jit(solution)/shard_map/ppermute | solution.py:33
  18.2 18.2 %collective-permute-start.13 = (bf16[352,1024]{1,0:T(8,128)(2,1)S(1)}, bf16[352,1024]{1,0:T(8,128)(2,1)S(1)}, u32[]{:S(2)}, u32[]{:S(2)}) collective-permute-start(bf16[352,1024]{1,0:T(8,128)(2,1)S(1)} %get-tuple-element.37.refs_5_), channel_id=1, source_target_pairs={{0,12},{1,13},{2,14},{3,15},{4,0},{5,1},{6,2},{7,3},{8,4},{9,5},{1... | collective-permute-start | bytes 2162696 | tf_op jit(solution)/shard_map/ppermute | solution.py:33
  22.2 17.5 %collective-permute-start.6 = (bf16[1280,256]{1,0:T(8,128)(2,1)S(1)}, bf16[1280,256]{1,0:T(8,128)(2,1)S(1)}, u32[]{:S(2)}, u32[]{:S(2)}) collective-permute-start(bf16[1280,256]{1,0:T(8,128)(2,1)S(1)} %lower.1.refs_0_), channel_id=1, source_target_pairs={{0,1},{1,2},{2,3},{3,0},{4,5},{5,6},{6,7},{7,4},{8,9},{9,10},{10,1... | collective-permute-start | bytes 1966088 | tf_op jit(solution)/shard_map/ppermute | solution.py:33
  23.0 16.7 %collective-permute-start.7 = (bf16[1280,256]{1,0:T(8,128)(2,1)S(1)}, bf16[1280,256]{1,0:T(8,128)(2,1)S(1)}, u32[]{:S(2)}, u32[]{:S(2)}) collective-permute-start(bf16[1280,256]{1,0:T(8,128)(2,1)S(1)} %lower.1.refs_0_), channel_id=1, source_target_pairs={{0,3},{1,0},{2,1},{3,2},{4,7},{5,4},{6,5},{7,6},{8,11},{9,8},{10,9... | collective-permute-start | bytes 1966088 | tf_op jit(solution)/shard_map/ppermute | solution.py:33
  36.3 8.8 %collective-permute-start.14 = (bf16[160,1024]{1,0:T(8,128)(2,1)S(1)}, bf16[160,1024]{1,0:T(8,128)(2,1)S(1)}, u32[]{:S(2)}, u32[]{:S(2)}) collective-permute-start(bf16[160,1024]{1,0:T(8,128)(2,1)S(1)} %slice.102), channel_id=1, source_target_pairs={{0,4},{1,5},{2,6},{3,7},{4,8},{5,9},{6,10},{7,11},{8,12},{9,13},{1... | collective-permute-start | bytes 983048 | tf_op jit(solution)/shard_map/ppermute | solution.py:33
  36.4 8.7 %collective-permute-start.15 = (bf16[160,1024]{1,0:T(8,128)(2,1)S(1)}, bf16[160,1024]{1,0:T(8,128)(2,1)S(1)}, u32[]{:S(2)}, u32[]{:S(2)}) collective-permute-start(bf16[160,1024]{1,0:T(8,128)(2,1)S(1)} %slice.103), channel_id=1, source_target_pairs={{0,12},{1,13},{2,14},{3,15},{4,0},{5,1},{6,2},{7,3},{8,4},{9,5},{1... | collective-permute-start | bytes 983048 | tf_op jit(solution)/shard_map/ppermute | solution.py:33
  39.7 8.4 %collective-permute-start.8 = (bf16[640,256]{1,0:T(8,128)(2,1)S(1)}, bf16[640,256]{1,0:T(8,128)(2,1)S(1)}, u32[]{:S(2)}, u32[]{:S(2)}) collective-permute-start(bf16[640,256]{1,0:T(8,128)(2,1)S(1)} %slice.77), channel_id=1, source_target_pairs={{0,1},{1,2},{2,3},{3,0},{4,5},{5,6},{6,7},{7,4},{8,9},{9,10},{10,1... | collective-permute-start | bytes 983048 | tf_op jit(solution)/shard_map/ppermute | solution.py:33
  40.0 8.1 %collective-permute-start.9 = (bf16[640,256]{1,0:T(8,128)(2,1)S(1)}, bf16[640,256]{1,0:T(8,128)(2,1)S(1)}, u32[]{:S(2)}, u32[]{:S(2)}) collective-permute-start(bf16[640,256]{1,0:T(8,128)(2,1)S(1)} %slice.78), channel_id=1, source_target_pairs={{0,3},{1,0},{2,1},{3,2},{4,7},{5,4},{6,5},{7,6},{8,11},{9,8},{10,9... | collective-permute-start | bytes 983048 | tf_op jit(solution)/shard_map/ppermute | solution.py:33
  51.4 12.0 %collective-permute-start.16 = (bf16[128,2048]{1,0:T(8,128)(2,1)S(1)}, bf16[128,2048]{1,0:T(8,128)(2,1)S(1)}, u32[]{:S(2)}, u32[]{:S(2)}) collective-permute-start(bf16[128,2048]{1,0:T(8,128)(2,1)S(1)} %get-tuple-element.40), channel_id=1, source_target_pairs={{0,4},{1,5},{2,6},{3,7},{4,8},{5,9},{6,10},{7,11},{8,12},{9,13},{1... | collective-permute-start | bytes 1572872 | tf_op jit(solution)/shard_map/ppermute | solution.py:33
  51.4 12.1 %collective-permute-start.17 = (bf16[128,2048]{1,0:T(8,128)(2,1)S(1)}, bf16[128,2048]{1,0:T(8,128)(2,1)S(1)}, u32[]{:S(2)}, u32[]{:S(2)}) collective-permute-start(bf16[128,2048]{1,0:T(8,128)(2,1)S(1)} %get-tuple-element.40), channel_id=1, source_target_pairs={{0,12},{1,13},{2,14},{3,15},{4,0},{5,1},{6,2},{7,3},{8,4},{9,5},{1... | collective-permute-start | bytes 1572872 | tf_op jit(solution)/shard_map/ppermute | solution.py:33
  54.7 12.4 %collective-permute-start.20 = (bf16[128,2048]{1,0:T(8,128)(2,1)S(1)}, bf16[128,2048]{1,0:T(8,128)(2,1)S(1)}, u32[]{:S(2)}, u32[]{:S(2)}) collective-permute-start(bf16[128,2048]{1,0:T(8,128)(2,1)S(1)} %get-tuple-element.40), channel_id=1, source_target_pairs={{0,1},{1,2},{2,3},{3,0},{4,5},{5,6},{6,7},{7,4},{8,9},{9,10},{10,1... | collective-permute-start | bytes 1572872 | tf_op jit(solution)/shard_map/ppermute | solution.py:33
  55.2 12.5 %collective-permute-start.21 = (bf16[128,2048]{1,0:T(8,128)(2,1)S(1)}, bf16[128,2048]{1,0:T(8,128)(2,1)S(1)}, u32[]{:S(2)}, u32[]{:S(2)}) collective-permute-start(bf16[128,2048]{1,0:T(8,128)(2,1)S(1)} %get-tuple-element.40), channel_id=1, source_target_pairs={{0,3},{1,0},{2,1},{3,2},{4,7},{5,4},{6,5},{7,6},{8,11},{9,8},{10,9... | collective-permute-start | bytes 1572872 | tf_op jit(solution)/shard_map/ppermute | solution.py:33
  63.5 7.7 %collective-permute-start.18 = (bf16[64,2048]{1,0:T(8,128)(2,1)S(1)}, bf16[64,2048]{1,0:T(8,128)(2,1)S(1)}, u32[]{:S(2)}, u32[]{:S(2)}) collective-permute-start(bf16[64,2048]{1,0:T(8,128)(2,1)S(1)} %slice.104), channel_id=1, source_target_pairs={{0,4},{1,5},{2,6},{3,7},{4,8},{5,9},{6,10},{7,11},{8,12},{9,13},{1... | collective-permute-start | bytes 786440 | tf_op jit(solution)/shard_map/ppermute | solution.py:33
  63.6 7.6 %collective-permute-start.19 = (bf16[64,2048]{1,0:T(8,128)(2,1)S(1)}, bf16[64,2048]{1,0:T(8,128)(2,1)S(1)}, u32[]{:S(2)}, u32[]{:S(2)}) collective-permute-start(bf16[64,2048]{1,0:T(8,128)(2,1)S(1)} %slice.105), channel_id=1, source_target_pairs={{0,12},{1,13},{2,14},{3,15},{4,0},{5,1},{6,2},{7,3},{8,4},{9,5},{1... | collective-permute-start | bytes 786440 | tf_op jit(solution)/shard_map/ppermute | solution.py:33
  67.1 7.7 %collective-permute-start.22 = (bf16[64,2048]{1,0:T(8,128)(2,1)S(1)}, bf16[64,2048]{1,0:T(8,128)(2,1)S(1)}, u32[]{:S(2)}, u32[]{:S(2)}) collective-permute-start(bf16[64,2048]{1,0:T(8,128)(2,1)S(1)} %slice.106), channel_id=1, source_target_pairs={{0,1},{1,2},{2,3},{3,0},{4,5},{5,6},{6,7},{7,4},{8,9},{9,10},{10,1... | collective-permute-start | bytes 786440 | tf_op jit(solution)/shard_map/ppermute | solution.py:33
  76.2 8.0 %collective-permute-start.25 = (bf16[256,512]{1,0:T(8,128)(2,1)S(1)}, bf16[256,512]{1,0:T(8,128)(2,1)S(1)}, u32[]{:S(2)}, u32[]{:S(2)}) collective-permute-start(bf16[256,512]{1,0:T(8,128)(2,1)S(1)} %tile.3), channel_id=1, source_target_pairs={{0,64},{16,80},{32,96},{48,112},{64,0},{80,16},{96,32},{112,48},{1... | collective-permute-start | bytes 786440 | tf_op jit(solution)/shard_map/ppermute | solution.py:38
  80.7 8.0 %collective-permute-start.24 = (bf16[256,512]{1,0:T(8,128)(2,1)S(1)}, bf16[256,512]{1,0:T(8,128)(2,1)S(1)}, u32[]{:S(2)}, u32[]{:S(2)}) collective-permute-start(bf16[256,512]{1,0:T(8,128)(2,1)S(1)} %tile.2), channel_id=1, source_target_pairs={{0,64},{16,80},{32,96},{48,112},{64,0},{80,16},{96,32},{112,48},{1... | collective-permute-start | bytes 786440 | tf_op jit(solution)/shard_map/ppermute | solution.py:38
  84.1 8.0 %collective-permute-start.26 = (bf16[256,512]{1,0:T(8,128)(2,1)S(1)}, bf16[256,512]{1,0:T(8,128)(2,1)S(1)}, u32[]{:S(2)}, u32[]{:S(2)}) collective-permute-start(bf16[256,512]{1,0:T(8,128)(2,1)S(1)} %collective-permute-done.25), channel_id=1, source_target_pairs={{0,4},{1,5},{2,6},{3,7},{4,8},{5,9},{6,10},{7,11},{8,12},{9,13},{1... | collective-permute-start | bytes 786440 | tf_op jit(solution)/shard_map/ppermute | solution.py:33
  84.1 8.1 %collective-permute-start.27 = (bf16[256,512]{1,0:T(8,128)(2,1)S(1)}, bf16[256,512]{1,0:T(8,128)(2,1)S(1)}, u32[]{:S(2)}, u32[]{:S(2)}) collective-permute-start(bf16[256,512]{1,0:T(8,128)(2,1)S(1)} %collective-permute-done.25), channel_id=1, source_target_pairs={{0,12},{1,13},{2,14},{3,15},{4,0},{5,1},{6,2},{7,3},{8,4},{9,5},{1... | collective-permute-start | bytes 786440 | tf_op jit(solution)/shard_map/ppermute | solution.py:33
  88.7 7.6 %collective-permute-start.33 = (bf16[256,512]{1,0:T(8,128)(2,1)S(1)}, bf16[256,512]{1,0:T(8,128)(2,1)S(1)}, u32[]{:S(2)}, u32[]{:S(2)}) collective-permute-start(bf16[256,512]{1,0:T(8,128)(2,1)S(1)} %collective-permute-done.24), channel_id=1, source_target_pairs={{0,4},{1,5},{2,6},{3,7},{4,8},{5,9},{6,10},{7,11},{8,12},{9,13},{1... | collective-permute-start | bytes 786440 | tf_op jit(solution)/shard_map/ppermute | solution.py:33
  88.7 7.7 %collective-permute-start.34 = (bf16[256,512]{1,0:T(8,128)(2,1)S(1)}, bf16[256,512]{1,0:T(8,128)(2,1)S(1)}, u32[]{:S(2)}, u32[]{:S(2)}) collective-permute-start(bf16[256,512]{1,0:T(8,128)(2,1)S(1)} %collective-permute-done.24), channel_id=1, source_target_pairs={{0,12},{1,13},{2,14},{3,15},{4,0},{5,1},{6,2},{7,3},{8,4},{9,5},{1... | collective-permute-start | bytes 786440 | tf_op jit(solution)/shard_map/ppermute | solution.py:33
  92.2 7.6 %collective-permute-start.28 = (bf16[128,512]{1,0:T(8,128)(2,1)S(1)}, bf16[128,512]{1,0:T(8,128)(2,1)S(1)}, u32[]{:S(2)}, u32[]{:S(2)}) collective-permute-start(bf16[128,512]{1,0:T(8,128)(2,1)S(1)} %slice.108), channel_id=1, source_target_pairs={{0,4},{1,5},{2,6},{3,7},{4,8},{5,9},{6,10},{7,11},{8,12},{9,13},{1... | collective-permute-start | bytes 393224 | tf_op jit(solution)/shard_map/ppermute | solution.py:33
  92.3 7.5 %collective-permute-start.29 = (bf16[128,512]{1,0:T(8,128)(2,1)S(1)}, bf16[128,512]{1,0:T(8,128)(2,1)S(1)}, u32[]{:S(2)}, u32[]{:S(2)}) collective-permute-start(bf16[128,512]{1,0:T(8,128)(2,1)S(1)} %slice.109), channel_id=1, source_target_pairs={{0,12},{1,13},{2,14},{3,15},{4,0},{5,1},{6,2},{7,3},{8,4},{9,5},{1... | collective-permute-start | bytes 393224 | tf_op jit(solution)/shard_map/ppermute | solution.py:33
  103.4 7.9 %collective-permute-start.37 = (bf16[3,256,128]{2,1,0:T(8,128)(2,1)S(1)}, bf16[3,256,128]{2,1,0:T(8,128)(2,1)S(1)}, u32[]{:S(2)}, u32[]{:S(2)}) collective-permute-start(bf16[3,256,128]{2,1,0:T(8,128)(2,1)S(1)} %get-tuple-element.53), channel_id=1, source_target_pairs={{0,1},{1,2},{2,3},{3,0},{4,5},{5,6},{6,7},{7,4},{8,9},{9,10},{10,1... | collective-permute-start | bytes 589832 | tf_op jit(solution)/shard_map/ppermute | solution.py:33
  104.9 9.0 %collective-permute-start.38 = (bf16[3,256,128]{2,1,0:T(8,128)(2,1)S(1)}, bf16[3,256,128]{2,1,0:T(8,128)(2,1)S(1)}, u32[]{:S(2)}, u32[]{:S(2)}) collective-permute-start(bf16[3,256,128]{2,1,0:T(8,128)(2,1)S(1)} %get-tuple-element.52), channel_id=1, source_target_pairs={{0,2},{1,3},{2,0},{3,1},{4,6},{5,7},{6,4},{7,5},{8,10},{9,11},{10,... | collective-permute-start | bytes 589832 | tf_op jit(solution)/shard_map/ppermute | solution.py:33
  109.7 9.0 %collective-permute-start.30 = (bf16[3,256,128]{2,1,0:T(8,128)(2,1)S(1)}, bf16[3,256,128]{2,1,0:T(8,128)(2,1)S(1)}, u32[]{:S(2)}, u32[]{:S(2)}) collective-permute-start(bf16[3,256,128]{2,1,0:T(8,128)(2,1)S(1)} %get-tuple-element.50), channel_id=1, source_target_pairs={{0,1},{1,2},{2,3},{3,0},{4,5},{5,6},{6,7},{7,4},{8,9},{9,10},{10,1... | collective-permute-start | bytes 589832 | tf_op jit(solution)/shard_map/ppermute | solution.py:33
  110.4 8.4 %collective-permute-start.31 = (bf16[3,256,128]{2,1,0:T(8,128)(2,1)S(1)}, bf16[3,256,128]{2,1,0:T(8,128)(2,1)S(1)}, u32[]{:S(2)}, u32[]{:S(2)}) collective-permute-start(bf16[3,256,128]{2,1,0:T(8,128)(2,1)S(1)} %get-tuple-element.49), channel_id=1, source_target_pairs={{0,2},{1,3},{2,0},{3,1},{4,6},{5,7},{6,4},{7,5},{8,10},{9,11},{10,... | collective-permute-start | bytes 589832 | tf_op jit(solution)/shard_map/ppermute | solution.py:33
  111.3 8.3 %collective-permute-start.32 = (bf16[3,256,128]{2,1,0:T(8,128)(2,1)S(1)}, bf16[3,256,128]{2,1,0:T(8,128)(2,1)S(1)}, u32[]{:S(2)}, u32[]{:S(2)}) collective-permute-start(bf16[3,256,128]{2,1,0:T(8,128)(2,1)S(1)} %get-tuple-element.48), channel_id=1, source_target_pairs={{0,3},{1,0},{2,1},{3,2},{4,7},{5,4},{6,5},{7,6},{8,11},{9,8},{10,9... | collective-permute-start | bytes 589832 | tf_op jit(solution)/shard_map/ppermute | solution.py:33
  (15 other events, 115.3 us)

commit v6 on v5

--- a/solution.py
+++ b/solution.py
@@ -255,7 +255,7 @@
     )(tail, panel, inverses)
 
 
-def message_kernel(folded, panel, low, high, far_low, far_high, up, down):
+def message_kernel(folded, panel, low, high, far, up, down):
     for part, out in enumerate((up, down)):
         first = (part + 1) * ROWS
         out[:ROWS] = folded[first : first + ROWS]
@@ -265,8 +265,7 @@
         out[first : first + ROWS] = panel[...]
         out[first + ROWS : first + 2 * ROWS] = low[...]
         out[second : second + ROWS] = high[...]
-        out[second + ROWS : second + ROWS + HALF] = far_low[...]
-        out[second + ROWS + HALF : second + 2 * ROWS] = far_high[...]
+        out[second + ROWS : second + 2 * ROWS] = far[...]
 
 
 def make_messages(folded, panels):
@@ -274,7 +273,7 @@
     return pl.pallas_call(
         message_kernel,
         out_shape=(message, message),
-        in_specs=[VMEM_SPEC] * 6,
+        in_specs=[VMEM_SPEC] * 5,
         out_specs=(VMEM_SPEC,) * 2,
         compiler_params=pltpu.CompilerParams(vmem_limit_bytes=6 * MIB),
         cost_estimate=pl.CostEstimate(flops=0, bytes_accessed=2 * MIB, transcendentals=0),
@@ -472,19 +471,17 @@
 def per_device(inv_factors, panel_rows, border, tail, front_sizes, block_map, block_owner):
     inverses, panel = inv_factors[0].reshape(2 * ROWS, PANEL), panel_rows[0]
     left, right = shift(inverses, "x", 1), shift(inverses, "x", -1)
-    low, high = shift(panel, "z", 1), shift(panel, "z", -1)
+    low, high, far = (shift(panel, "z", -step) for step in RING[1:])
     folded, panel, inverses = fold_tail(tail[0], panel, inverses)
-    low, high, folded, panel, inverses = lax.optimization_barrier(
-        (low, high, folded, panel, inverses)
+    left, right, folded, panel, inverses = lax.optimization_barrier(
+        (left, right, folded, panel, inverses)
     )
     far_first = shift(left[:ROWS], "x", 1)
     far_second = shift(right[ROWS:], "x", -1)
-    far_low = shift(low[:HALF], "z", 1)
-    far_high = shift(high[HALF:], "z", -1)
 
     chunks = lower_chunks(inverses, left, right, far_first, far_second)
     chunks, update, plan = spread(chunks, "z", *blank_rows(block_map, block_owner))
-    up, down = make_messages(folded, (panel, low, high, far_low, far_high))
+    up, down = make_messages(folded, (panel, low, high, far))
     from_left, from_right = shift(up, "x", 1), shift(down, "x", -1)
     ahead = shift(from_left[ON_AT:], "x", 1)
     behind = shift(from_right[ON_AT:], "x", -1)

time: 122 us -> 121 us (level)
  starting transfers between devices: 67.5 us -> 65 us
    ppermute x38 -> x37, starting transfers between devices: 63.8 us -> 61.3 us  [shift(): return lax.ppermute(value, 'front', pairs)]
    ppermute x38 -> x37, waiting for transfers between devices: 29.7 us -> 30.5 us  [shift(): return lax.ppermute(value, 'front', pairs)]
  transfers between devices with their start and end apart: 40 -> 39, of which waited for: 16 -> 17; matrix products, arithmetic and copies ran while one was open for 1% -> 1% of each run, Pallas kernels for 6% -> 6%
where the time goes in v6:
time: 121 us; the launch traced here: 120 us
  starting transfers between devices  65 us (54%)
  waiting for transfers between devices  34 us (28%)
  Pallas kernels  14.8 us (12%)
  local copies, waits for them, and re-layouts  4.72 us (4%)
  between operations  1.27 us (1%)
    ppermute x37, starting transfers between devices, shift(): return lax.ppermute(value, 'front', pairs)  61.3 us
    ppermute x37, waiting for transfers between devices, shift(): return lax.ppermute(value, 'front', pairs)  30.5 us
    ppermute x2, starting transfers between devices, to_parent(): lax.ppermute(value, 'leaf', [(g, (g + groups // 2) % groups) for g in ran...  3.69 us
    pallas_call x2, Pallas kernels, place_tiles(): pl.pallas_call(functools.partial(place_kernel, list(tiles)), out_shape=PA...  3.65 us
    pallas_call x1, Pallas kernels, blank_rows(): pl.pallas_call(blank_kernel, out_shape=(PARENT, jax.ShapeDtypeStruct((2 *...  3.51 us
    unnamed x30, local copies, waits for them, and re-layouts  3.5 us
    ppermute x2, waiting for transfers between devices, to_parent(): lax.ppermute(value, 'leaf', [(g, (g + groups // 2) % groups) for g in ran...  3.47 us
    pallas_call x1, Pallas kernels, eliminate(): pl.pallas_call(panel_kernel, out_shape=(jax.ShapeDtypeStruct((ROWS, PANEL...  3.34 us
  transfers between devices with their start and end apart: 39, of which 17 were waited for; matrix products, arithmetic and copies ran while one was open for 1% of the time, Pallas kernels for 6%

profile of v6, /device:TPU:0, one launch (start us, length us, event | category | flops | bytes accessed | tf_op | source)
XLA Modules:
  0.0 119.8 jit_solution(8332565791011620162)
XLA Ops:
  2.3 1.7 %collective-permute-start.1 = (bf16[128,1024]{1,0:T(8,128)(2,1)}, bf16[128,1024]{1,0:T(8,128)(2,1)S(1)}, u32[]{:S(2)}, u32[]{:S(2)}) collective-permute-start(bf16[128,1024]{1,0:T(8,128)(2,1)} %bitcast.9), channel_id=1, source_target_pairs={{0,12},{1,13},{2,14},{3,15},{4,0},{5,1},{6,2},{7,3},{8,4},{9,5},{1... | collective-permute-start | bytes 786440 | tf_op jit(solution)/shard_map/ppermute | solution.py:33
  3.9 2.0 %collective-permute-start.8 = (bf16[64,1024]{1,0:T(8,128)(2,1)}, bf16[64,1024]{1,0:T(8,128)(2,1)S(1)}, u32[]{:S(2)}, u32[]{:S(2)}) collective-permute-start(bf16[64,1024]{1,0:T(8,128)(2,1)} %bitcast.11), channel_id=1, source_target_pairs={{0,1},{1,2},{2,3},{3,0},{4,5},{5,6},{6,7},{7,4},{8,9},{9,10},{10,1... | collective-permute-start | bytes 393224 | tf_op jit(solution)/shard_map/ppermute | solution.py:33
  5.9 2.1 %collective-permute-start.9 = (bf16[64,1024]{1,0:T(8,128)(2,1)}, bf16[64,1024]{1,0:T(8,128)(2,1)S(1)}, u32[]{:S(2)}, u32[]{:S(2)}) collective-permute-start(bf16[64,1024]{1,0:T(8,128)(2,1)} %bitcast.12), channel_id=1, source_target_pairs={{0,3},{1,0},{2,1},{3,2},{4,7},{5,4},{6,5},{7,6},{8,11},{9,8},{10,9... | collective-permute-start | bytes 393224 | tf_op jit(solution)/shard_map/ppermute | solution.py:33
  8.1 1.9 %collective-permute-start.10 = (bf16[64,1024]{1,0:T(8,128)(2,1)}, bf16[64,1024]{1,0:T(8,128)(2,1)S(1)}, u32[]{:S(2)}, u32[]{:S(2)}) collective-permute-start(bf16[64,1024]{1,0:T(8,128)(2,1)} %bitcast.13), channel_id=1, source_target_pairs={{0,2},{1,3},{2,0},{3,1},{4,6},{5,7},{6,4},{7,5},{8,10},{9,11},{10,... | collective-permute-start | bytes 393224 | tf_op jit(solution)/shard_map/ppermute | solution.py:33
  13.3 3.0 %collective-permute-start.3 = (bf16[64,1024]{1,0:T(8,128)(2,1)S(1)}, bf16[64,1024]{1,0:T(8,128)(2,1)S(1)}, u32[]{:S(2)}, u32[]{:S(2)}) collective-permute-start(bf16[64,1024]{1,0:T(8,128)(2,1)S(1)} %slice.70), channel_id=1, source_target_pairs={{0,12},{1,13},{2,14},{3,15},{4,0},{5,1},{6,2},{7,3},{8,4},{9,5},{1... | collective-permute-start | bytes 393224 | tf_op jit(solution)/shard_map/ppermute | solution.py:33
  16.5 3.2 %collective-permute-start.12 = (bf16[352,1024]{1,0:T(8,128)(2,1)S(1)}, bf16[352,1024]{1,0:T(8,128)(2,1)S(1)}, u32[]{:S(2)}, u32[]{:S(2)}) collective-permute-start(bf16[352,1024]{1,0:T(8,128)(2,1)S(1)} %get-tuple-element.37.refs_5_), channel_id=1, source_target_pairs={{0,12},{1,13},{2,14},{3,15},{4,0},{5,1},{6,2},{7,3},{8,4},{9,5},{1... | collective-permute-start | bytes 2162696 | tf_op jit(solution)/shard_map/ppermute | solution.py:33
  21.5 2.1 %collective-permute-start.5 = (bf16[1280,256]{1,0:T(8,128)(2,1)S(1)}, bf16[1280,256]{1,0:T(8,128)(2,1)S(1)}, u32[]{:S(2)}, u32[]{:S(2)}) collective-permute-start(bf16[1280,256]{1,0:T(8,128)(2,1)S(1)} %lower.1.refs_0_), channel_id=1, source_target_pairs={{0,3},{1,0},{2,1},{3,2},{4,7},{5,4},{6,5},{7,6},{8,11},{9,8},{10,9... | collective-permute-start | bytes 1966088 | tf_op jit(solution)/shard_map/ppermute | solution.py:33
  23.7 3.5 %blank.1 = (f32[4096,384]{1,0:T(8,128)}, s32[32]{0:T(128)S(1)}) custom-call(s32[8,16]{1,0:T(8,128)S(1)} %copy-done.3, s32[8,32]{1,0:T(8,128)S(1)} %copy-done.4), custom_call_target="tpu_custom_call" | custom-call | bytes 3145728 | tf_op jit(solution)/shard_map/blank/pallas_call | solution.py:413
  27.2 7.5 %collective-permute-done.11.refs_6_.refs_1_ = bf16[352,1024]{1,0:T(8,128)(2,1)S(1)} collective-permute-done((bf16[352,1024]{1,0:T(8,128)(2,1)S(1)}, bf16[352,1024]{1,0:T(8,128)(2,1)S(1)}, u32[]{:S(2)}, u32[]{:S(2)}) %collective-permute-start.11) | collective-permute-done | bytes 720928 | tf_op jit(solution)/shard_map/ppermute | solution.py:33
  34.8 3.3 %collective-permute-start.14 = (bf16[160,1024]{1,0:T(8,128)(2,1)S(1)}, bf16[160,1024]{1,0:T(8,128)(2,1)S(1)}, u32[]{:S(2)}, u32[]{:S(2)}) collective-permute-start(bf16[160,1024]{1,0:T(8,128)(2,1)S(1)} %slice.93), channel_id=1, source_target_pairs={{0,12},{1,13},{2,14},{3,15},{4,0},{5,1},{6,2},{7,3},{8,4},{9,5},{1... | collective-permute-start | bytes 983048 | tf_op jit(solution)/shard_map/ppermute | solution.py:33
  39.2 2.3 %collective-permute-start.7 = (bf16[640,256]{1,0:T(8,128)(2,1)S(1)}, bf16[640,256]{1,0:T(8,128)(2,1)S(1)}, u32[]{:S(2)}, u32[]{:S(2)}) collective-permute-start(bf16[640,256]{1,0:T(8,128)(2,1)S(1)} %slice.72), channel_id=1, source_target_pairs={{0,3},{1,0},{2,1},{3,2},{4,7},{5,4},{6,5},{7,6},{8,11},{9,8},{10,9... | collective-permute-start | bytes 983048 | tf_op jit(solution)/shard_map/ppermute | solution.py:33
  41.5 2.0 %collective-permute-done.13.refs_8_.refs_3_ = bf16[160,1024]{1,0:T(8,128)(2,1)S(1)} collective-permute-done((bf16[160,1024]{1,0:T(8,128)(2,1)S(1)}, bf16[160,1024]{1,0:T(8,128)(2,1)S(1)}, u32[]{:S(2)}, u32[]{:S(2)}) %collective-permute-start.13) | collective-permute-done | bytes 327712 | tf_op jit(solution)/shard_map/ppermute | solution.py:33
  43.5 3.2 %collective-permute-done.6.refs_3_ = bf16[640,256]{1,0:T(8,128)(2,1)S(1)} collective-permute-done((bf16[640,256]{1,0:T(8,128)(2,1)S(1)}, bf16[640,256]{1,0:T(8,128)(2,1)S(1)}, u32[]{:S(2)}, u32[]{:S(2)}) %collective-permute-start.6) | collective-permute-done | bytes 327712 | tf_op jit(solution)/shard_map/ppermute | solution.py:33
  46.7 3.3 %panels.1 = (bf16[64,1024]{1,0:T(8,128)(2,1)}, bf16[128,2048]{1,0:T(8,128)(2,1)S(1)}) custom-call(bf16[128,2048]{1,0:T(8,128)(2,1)S(1)} %bitcast.15, bf16[1280,256]{1,0:T(8,128)(2,1)S(1)} %lower.1.refs_0_, bf16[1280,256]{1,0:T(8,128)(2,1)S(1)} %collective-permute-done.4.refs_1_, bf16[1280,256]{1,0:T(8,128)(2,1)S(1)} %collective-permute-done.5.refs_2_, ...), custom_call_target="tpu_custom_call" | custom-call | flops 2952790016 | bytes 8388608 | tf_op jit(solution)/shard_map/panels/pallas_call | solution.py:191
  50.1 3.2 %collective-permute-start.16 = (bf16[128,2048]{1,0:T(8,128)(2,1)S(1)}, bf16[128,2048]{1,0:T(8,128)(2,1)S(1)}, u32[]{:S(2)}, u32[]{:S(2)}) collective-permute-start(bf16[128,2048]{1,0:T(8,128)(2,1)S(1)} %get-tuple-element.40), channel_id=1, source_target_pairs={{0,12},{1,13},{2,14},{3,15},{4,0},{5,1},{6,2},{7,3},{8,4},{9,5},{1... | collective-permute-start | bytes 1572872 | tf_op jit(solution)/shard_map/ppermute | solution.py:33
  53.5 3.0 %collective-permute-start.20 = (bf16[128,2048]{1,0:T(8,128)(2,1)S(1)}, bf16[128,2048]{1,0:T(8,128)(2,1)S(1)}, u32[]{:S(2)}, u32[]{:S(2)}) collective-permute-start(bf16[128,2048]{1,0:T(8,128)(2,1)S(1)} %get-tuple-element.40), channel_id=1, source_target_pairs={{0,3},{1,0},{2,1},{3,2},{4,7},{5,4},{6,5},{7,6},{8,11},{9,8},{10,9... | collective-permute-start | bytes 1572872 | tf_op jit(solution)/shard_map/ppermute | solution.py:33
  56.8 5.2 %collective-permute-done.15 = bf16[128,2048]{1,0:T(8,128)(2,1)S(1)} collective-permute-done((bf16[128,2048]{1,0:T(8,128)(2,1)S(1)}, bf16[128,2048]{1,0:T(8,128)(2,1)S(1)}, u32[]{:S(2)}, u32[]{:S(2)}) %collective-permute-start.15) | collective-permute-done | bytes 524320 | tf_op jit(solution)/shard_map/ppermute | solution.py:33
  62.2 3.3 %collective-permute-start.18 = (bf16[64,2048]{1,0:T(8,128)(2,1)S(1)}, bf16[64,2048]{1,0:T(8,128)(2,1)S(1)}, u32[]{:S(2)}, u32[]{:S(2)}) collective-permute-start(bf16[64,2048]{1,0:T(8,128)(2,1)S(1)} %slice.95), channel_id=1, source_target_pairs={{0,12},{1,13},{2,14},{3,15},{4,0},{5,1},{6,2},{7,3},{8,4},{9,5},{1... | collective-permute-start | bytes 786440 | tf_op jit(solution)/shard_map/ppermute | solution.py:33
  66.0 3.1 %collective-permute-start.22 = (bf16[64,2048]{1,0:T(8,128)(2,1)S(1)}, bf16[64,2048]{1,0:T(8,128)(2,1)S(1)}, u32[]{:S(2)}, u32[]{:S(2)}) collective-permute-start(bf16[64,2048]{1,0:T(8,128)(2,1)S(1)} %slice.97), channel_id=1, source_target_pairs={{0,3},{1,0},{2,1},{3,2},{4,7},{5,4},{6,5},{7,6},{8,11},{9,8},{10,9... | collective-permute-start | bytes 786440 | tf_op jit(solution)/shard_map/ppermute | solution.py:33
  69.8 3.5 %collective-permute-done.21 = bf16[64,2048]{1,0:T(8,128)(2,1)S(1)} collective-permute-done((bf16[64,2048]{1,0:T(8,128)(2,1)S(1)}, bf16[64,2048]{1,0:T(8,128)(2,1)S(1)}, u32[]{:S(2)}, u32[]{:S(2)}) %collective-permute-start.21) | collective-permute-done | bytes 262176 | tf_op jit(solution)/shard_map/ppermute | solution.py:33
  74.7 3.3 %collective-permute-start.24 = (bf16[256,512]{1,0:T(8,128)(2,1)S(1)}, bf16[256,512]{1,0:T(8,128)(2,1)S(1)}, u32[]{:S(2)}, u32[]{:S(2)}) collective-permute-start(bf16[256,512]{1,0:T(8,128)(2,1)S(1)} %tile.3), channel_id=1, source_target_pairs={{0,64},{16,80},{32,96},{48,112},{64,0},{80,16},{96,32},{112,48},{1... | collective-permute-start | bytes 786440 | tf_op jit(solution)/shard_map/ppermute | solution.py:38
  80.5 2.6 %collective-permute-done.24 = bf16[256,512]{1,0:T(8,128)(2,1)S(1)} collective-permute-done((bf16[256,512]{1,0:T(8,128)(2,1)S(1)}, bf16[256,512]{1,0:T(8,128)(2,1)S(1)}, u32[]{:S(2)}, u32[]{:S(2)}) %collective-permute-start.24) | collective-permute-done | bytes 262176 | tf_op jit(solution)/shard_map/ppermute | solution.py:38
  83.1 3.2 %collective-permute-start.26 = (bf16[256,512]{1,0:T(8,128)(2,1)S(1)}, bf16[256,512]{1,0:T(8,128)(2,1)S(1)}, u32[]{:S(2)}, u32[]{:S(2)}) collective-permute-start(bf16[256,512]{1,0:T(8,128)(2,1)S(1)} %collective-permute-done.24), channel_id=1, source_target_pairs={{0,12},{1,13},{2,14},{3,15},{4,0},{5,1},{6,2},{7,3},{8,4},{9,5},{1... | collective-permute-start | bytes 786440 | tf_op jit(solution)/shard_map/ppermute | solution.py:33
  87.2 3.2 %collective-permute-start.33 = (bf16[256,512]{1,0:T(8,128)(2,1)S(1)}, bf16[256,512]{1,0:T(8,128)(2,1)S(1)}, u32[]{:S(2)}, u32[]{:S(2)}) collective-permute-start(bf16[256,512]{1,0:T(8,128)(2,1)S(1)} %collective-permute-done.23), channel_id=1, source_target_pairs={{0,12},{1,13},{2,14},{3,15},{4,0},{5,1},{6,2},{7,3},{8,4},{9,5},{1... | collective-permute-start | bytes 786440 | tf_op jit(solution)/shard_map/ppermute | solution.py:33
  92.1 3.3 %collective-permute-start.28 = (bf16[128,512]{1,0:T(8,128)(2,1)S(1)}, bf16[128,512]{1,0:T(8,128)(2,1)S(1)}, u32[]{:S(2)}, u32[]{:S(2)}) collective-permute-start(bf16[128,512]{1,0:T(8,128)(2,1)S(1)} %slice.99), channel_id=1, source_target_pairs={{0,12},{1,13},{2,14},{3,15},{4,0},{5,1},{6,2},{7,3},{8,4},{9,5},{1... | collective-permute-start | bytes 393224 | tf_op jit(solution)/shard_map/ppermute | solution.py:33
  96.0 3.3 %collective-permute-start.35 = (bf16[128,512]{1,0:T(8,128)(2,1)S(1)}, bf16[128,512]{1,0:T(8,128)(2,1)S(1)}, u32[]{:S(2)}, u32[]{:S(2)}) collective-permute-start(bf16[128,512]{1,0:T(8,128)(2,1)S(1)} %slice.104), channel_id=1, source_target_pairs={{0,12},{1,13},{2,14},{3,15},{4,0},{5,1},{6,2},{7,3},{8,4},{9,5},{1... | collective-permute-start | bytes 393224 | tf_op jit(solution)/shard_map/ppermute | solution.py:33
  100.1 2.0 %collective-permute-done.34 = bf16[128,512]{1,0:T(8,128)(2,1)S(1)} collective-permute-done((bf16[128,512]{1,0:T(8,128)(2,1)S(1)}, bf16[128,512]{1,0:T(8,128)(2,1)S(1)}, u32[]{:S(2)}, u32[]{:S(2)}) %collective-permute-start.34) | collective-permute-done | bytes 131104 | tf_op jit(solution)/shard_map/ppermute | solution.py:33
  103.3 3.9 %collective-permute-start.37 = (bf16[3,256,128]{2,1,0:T(8,128)(2,1)S(1)}, bf16[3,256,128]{2,1,0:T(8,128)(2,1)S(1)}, u32[]{:S(2)}, u32[]{:S(2)}) collective-permute-start(bf16[3,256,128]{2,1,0:T(8,128)(2,1)S(1)} %get-tuple-element.52), channel_id=1, source_target_pairs={{0,2},{1,3},{2,0},{3,1},{4,6},{5,7},{6,4},{7,5},{8,10},{9,11},{10,... | collective-permute-start | bytes 589832 | tf_op jit(solution)/shard_map/ppermute | solution.py:33
  109.9 2.1 %collective-permute-start.31 = (bf16[3,256,128]{2,1,0:T(8,128)(2,1)S(1)}, bf16[3,256,128]{2,1,0:T(8,128)(2,1)S(1)}, u32[]{:S(2)}, u32[]{:S(2)}) collective-permute-start(bf16[3,256,128]{2,1,0:T(8,128)(2,1)S(1)} %get-tuple-element.48), channel_id=1, source_target_pairs={{0,3},{1,0},{2,1},{3,2},{4,7},{5,4},{6,5},{7,6},{8,11},{9,8},{10,9... | collective-permute-start | bytes 589832 | tf_op jit(solution)/shard_map/ppermute | solution.py:33
  113.0 2.0 %place.2.refs_3_ = f32[4096,384]{1,0:T(8,128)} custom-call(s32[8,16]{1,0:T(8,128)S(1)} %copy-done.3, s32[32]{0:T(128)S(1)} %get-tuple-element.44.plan, bf16[3,256,128]{2,1,0:T(8,128)(2,1)S(1)} %get-tuple-element.54.refs_0_, bf16[3,256,128]{2,1,0:T(8,128)(2,1)S(1)} %collective-permute-done.36.refs_1_, ...), custom_call_target="tpu_custom_call", output_to_operand_aliasing={{}: (7, {})} | custom-call | bytes 1048576 | tf_op jit(solution)/shard_map/place/pallas_call | solution.py:455
  115.0 2.1 %collective-permute-done.30.refs_1_ = bf16[3,256,128]{2,1,0:T(8,128)(2,1)S(1)} collective-permute-done((bf16[3,256,128]{2,1,0:T(8,128)(2,1)S(1)}, bf16[3,256,128]{2,1,0:T(8,128)(2,1)S(1)}, u32[]{:S(2)}, u32[]{:S(2)}) %collective-permute-start.30) | collective-permute-done | bytes 196640 | tf_op jit(solution)/shard_map/ppermute | solution.py:33
  117.9 1.7 %place.3 = f32[4096,384]{1,0:T(8,128)} custom-call(s32[8,16]{1,0:T(8,128)S(1)} %copy-done.3, s32[32]{0:T(128)S(1)} %get-tuple-element.44.plan, bf16[3,256,128]{2,1,0:T(8,128)(2,1)S(1)} %collective-permute-done.29.refs_0_, bf16[3,256,128]{2,1,0:T(8,128)(2,1)S(1)} %collective-permute-done.30.refs_1_, ...), custom_call_target="tpu_custom_call", output_to_operand_aliasing={{}: (5, {})} | custom-call | bytes 1048576 | tf_op jit(solution)/shard_map/place/pallas_call | solution.py:455
  (108 shorter events, 23.3 us)
Async XLA Ops:
  0.6 12.3 %collective-permute-start = (bf16[128,1024]{1,0:T(8,128)(2,1)}, bf16[128,1024]{1,0:T(8,128)(2,1)S(1)}, u32[]{:S(2)}, u32[]{:S(2)}) collective-permute-start(bf16[128,1024]{1,0:T(8,128)(2,1)} %bitcast.8), channel_id=1, source_target_pairs={{0,4},{1,5},{2,6},{3,7},{4,8},{5,9},{6,10},{7,11},{8,12},{9,13},{1... | collective-permute-start | bytes 786440 | tf_op jit(solution)/shard_map/ppermute | solution.py:33
  2.3 10.6 %collective-permute-start.1 = (bf16[128,1024]{1,0:T(8,128)(2,1)}, bf16[128,1024]{1,0:T(8,128)(2,1)S(1)}, u32[]{:S(2)}, u32[]{:S(2)}) collective-permute-start(bf16[128,1024]{1,0:T(8,128)(2,1)} %bitcast.9), channel_id=1, source_target_pairs={{0,12},{1,13},{2,14},{3,15},{4,0},{5,1},{6,2},{7,3},{8,4},{9,5},{1... | collective-permute-start | bytes 786440 | tf_op jit(solution)/shard_map/ppermute | solution.py:33
  3.9 12.4 %collective-permute-start.8 = (bf16[64,1024]{1,0:T(8,128)(2,1)}, bf16[64,1024]{1,0:T(8,128)(2,1)S(1)}, u32[]{:S(2)}, u32[]{:S(2)}) collective-permute-start(bf16[64,1024]{1,0:T(8,128)(2,1)} %bitcast.11), channel_id=1, source_target_pairs={{0,1},{1,2},{2,3},{3,0},{4,5},{5,6},{6,7},{7,4},{8,9},{9,10},{10,1... | collective-permute-start | bytes 393224 | tf_op jit(solution)/shard_map/ppermute | solution.py:33
  5.9 10.4 %collective-permute-start.9 = (bf16[64,1024]{1,0:T(8,128)(2,1)}, bf16[64,1024]{1,0:T(8,128)(2,1)S(1)}, u32[]{:S(2)}, u32[]{:S(2)}) collective-permute-start(bf16[64,1024]{1,0:T(8,128)(2,1)} %bitcast.12), channel_id=1, source_target_pairs={{0,3},{1,0},{2,1},{3,2},{4,7},{5,4},{6,5},{7,6},{8,11},{9,8},{10,9... | collective-permute-start | bytes 393224 | tf_op jit(solution)/shard_map/ppermute | solution.py:33
  8.1 8.3 %collective-permute-start.10 = (bf16[64,1024]{1,0:T(8,128)(2,1)}, bf16[64,1024]{1,0:T(8,128)(2,1)S(1)}, u32[]{:S(2)}, u32[]{:S(2)}) collective-permute-start(bf16[64,1024]{1,0:T(8,128)(2,1)} %bitcast.13), channel_id=1, source_target_pairs={{0,2},{1,3},{2,0},{3,1},{4,6},{5,7},{6,4},{7,5},{8,10},{9,11},{10,... | collective-permute-start | bytes 393224 | tf_op jit(solution)/shard_map/ppermute | solution.py:33
  16.4 18.2 %collective-permute-start.11 = (bf16[352,1024]{1,0:T(8,128)(2,1)S(1)}, bf16[352,1024]{1,0:T(8,128)(2,1)S(1)}, u32[]{:S(2)}, u32[]{:S(2)}) collective-permute-start(bf16[352,1024]{1,0:T(8,128)(2,1)S(1)} %get-tuple-element.38), channel_id=1, source_target_pairs={{0,4},{1,5},{2,6},{3,7},{4,8},{5,9},{6,10},{7,11},{8,12},{9,13},{1... | collective-permute-start | bytes 2162696 | tf_op jit(solution)/shard_map/ppermute | solution.py:33
  16.5 18.2 %collective-permute-start.12 = (bf16[352,1024]{1,0:T(8,128)(2,1)S(1)}, bf16[352,1024]{1,0:T(8,128)(2,1)S(1)}, u32[]{:S(2)}, u32[]{:S(2)}) collective-permute-start(bf16[352,1024]{1,0:T(8,128)(2,1)S(1)} %get-tuple-element.37.refs_5_), channel_id=1, source_target_pairs={{0,12},{1,13},{2,14},{3,15},{4,0},{5,1},{6,2},{7,3},{8,4},{9,5},{1... | collective-permute-start | bytes 2162696 | tf_op jit(solution)/shard_map/ppermute | solution.py:33
  20.3 17.7 %collective-permute-start.4 = (bf16[1280,256]{1,0:T(8,128)(2,1)S(1)}, bf16[1280,256]{1,0:T(8,128)(2,1)S(1)}, u32[]{:S(2)}, u32[]{:S(2)}) collective-permute-start(bf16[1280,256]{1,0:T(8,128)(2,1)S(1)} %lower.1.refs_0_), channel_id=1, source_target_pairs={{0,1},{1,2},{2,3},{3,0},{4,5},{5,6},{6,7},{7,4},{8,9},{9,10},{10,1... | collective-permute-start | bytes 1966088 | tf_op jit(solution)/shard_map/ppermute | solution.py:33
  21.5 16.5 %collective-permute-start.5 = (bf16[1280,256]{1,0:T(8,128)(2,1)S(1)}, bf16[1280,256]{1,0:T(8,128)(2,1)S(1)}, u32[]{:S(2)}, u32[]{:S(2)}) collective-permute-start(bf16[1280,256]{1,0:T(8,128)(2,1)S(1)} %lower.1.refs_0_), channel_id=1, source_target_pairs={{0,3},{1,0},{2,1},{3,2},{4,7},{5,4},{6,5},{7,6},{8,11},{9,8},{10,9... | collective-permute-start | bytes 1966088 | tf_op jit(solution)/shard_map/ppermute | solution.py:33
  34.7 8.8 %collective-permute-start.13 = (bf16[160,1024]{1,0:T(8,128)(2,1)S(1)}, bf16[160,1024]{1,0:T(8,128)(2,1)S(1)}, u32[]{:S(2)}, u32[]{:S(2)}) collective-permute-start(bf16[160,1024]{1,0:T(8,128)(2,1)S(1)} %slice.92), channel_id=1, source_target_pairs={{0,4},{1,5},{2,6},{3,7},{4,8},{5,9},{6,10},{7,11},{8,12},{9,13},{1... | collective-permute-start | bytes 983048 | tf_op jit(solution)/shard_map/ppermute | solution.py:33
  34.8 8.7 %collective-permute-start.14 = (bf16[160,1024]{1,0:T(8,128)(2,1)S(1)}, bf16[160,1024]{1,0:T(8,128)(2,1)S(1)}, u32[]{:S(2)}, u32[]{:S(2)}) collective-permute-start(bf16[160,1024]{1,0:T(8,128)(2,1)S(1)} %slice.93), channel_id=1, source_target_pairs={{0,12},{1,13},{2,14},{3,15},{4,0},{5,1},{6,2},{7,3},{8,4},{9,5},{1... | collective-permute-start | bytes 983048 | tf_op jit(solution)/shard_map/ppermute | solution.py:33
  38.1 8.6 %collective-permute-start.6 = (bf16[640,256]{1,0:T(8,128)(2,1)S(1)}, bf16[640,256]{1,0:T(8,128)(2,1)S(1)}, u32[]{:S(2)}, u32[]{:S(2)}) collective-permute-start(bf16[640,256]{1,0:T(8,128)(2,1)S(1)} %slice.71), channel_id=1, source_target_pairs={{0,1},{1,2},{2,3},{3,0},{4,5},{5,6},{6,7},{7,4},{8,9},{9,10},{10,1... | collective-permute-start | bytes 983048 | tf_op jit(solution)/shard_map/ppermute | solution.py:33
  39.2 7.5 %collective-permute-start.7 = (bf16[640,256]{1,0:T(8,128)(2,1)S(1)}, bf16[640,256]{1,0:T(8,128)(2,1)S(1)}, u32[]{:S(2)}, u32[]{:S(2)}) collective-permute-start(bf16[640,256]{1,0:T(8,128)(2,1)S(1)} %slice.72), channel_id=1, source_target_pairs={{0,3},{1,0},{2,1},{3,2},{4,7},{5,4},{6,5},{7,6},{8,11},{9,8},{10,9... | collective-permute-start | bytes 983048 | tf_op jit(solution)/shard_map/ppermute | solution.py:33
  50.1 12.0 %collective-permute-start.15 = (bf16[128,2048]{1,0:T(8,128)(2,1)S(1)}, bf16[128,2048]{1,0:T(8,128)(2,1)S(1)}, u32[]{:S(2)}, u32[]{:S(2)}) collective-permute-start(bf16[128,2048]{1,0:T(8,128)(2,1)S(1)} %get-tuple-element.40), channel_id=1, source_target_pairs={{0,4},{1,5},{2,6},{3,7},{4,8},{5,9},{6,10},{7,11},{8,12},{9,13},{1... | collective-permute-start | bytes 1572872 | tf_op jit(solution)/shard_map/ppermute | solution.py:33
  50.1 12.1 %collective-permute-start.16 = (bf16[128,2048]{1,0:T(8,128)(2,1)S(1)}, bf16[128,2048]{1,0:T(8,128)(2,1)S(1)}, u32[]{:S(2)}, u32[]{:S(2)}) collective-permute-start(bf16[128,2048]{1,0:T(8,128)(2,1)S(1)} %get-tuple-element.40), channel_id=1, source_target_pairs={{0,12},{1,13},{2,14},{3,15},{4,0},{5,1},{6,2},{7,3},{8,4},{9,5},{1... | collective-permute-start | bytes 1572872 | tf_op jit(solution)/shard_map/ppermute | solution.py:33
  53.3 12.2 %collective-permute-start.19 = (bf16[128,2048]{1,0:T(8,128)(2,1)S(1)}, bf16[128,2048]{1,0:T(8,128)(2,1)S(1)}, u32[]{:S(2)}, u32[]{:S(2)}) collective-permute-start(bf16[128,2048]{1,0:T(8,128)(2,1)S(1)} %get-tuple-element.40), channel_id=1, source_target_pairs={{0,1},{1,2},{2,3},{3,0},{4,5},{5,6},{6,7},{7,4},{8,9},{9,10},{10,1... | collective-permute-start | bytes 1572872 | tf_op jit(solution)/shard_map/ppermute | solution.py:33
  53.5 12.5 %collective-permute-start.20 = (bf16[128,2048]{1,0:T(8,128)(2,1)S(1)}, bf16[128,2048]{1,0:T(8,128)(2,1)S(1)}, u32[]{:S(2)}, u32[]{:S(2)}) collective-permute-start(bf16[128,2048]{1,0:T(8,128)(2,1)S(1)} %get-tuple-element.40), channel_id=1, source_target_pairs={{0,3},{1,0},{2,1},{3,2},{4,7},{5,4},{6,5},{7,6},{8,11},{9,8},{10,9... | collective-permute-start | bytes 1572872 | tf_op jit(solution)/shard_map/ppermute | solution.py:33
  62.1 7.7 %collective-permute-start.17 = (bf16[64,2048]{1,0:T(8,128)(2,1)S(1)}, bf16[64,2048]{1,0:T(8,128)(2,1)S(1)}, u32[]{:S(2)}, u32[]{:S(2)}) collective-permute-start(bf16[64,2048]{1,0:T(8,128)(2,1)S(1)} %slice.94), channel_id=1, source_target_pairs={{0,4},{1,5},{2,6},{3,7},{4,8},{5,9},{6,10},{7,11},{8,12},{9,13},{1... | collective-permute-start | bytes 786440 | tf_op jit(solution)/shard_map/ppermute | solution.py:33
  62.2 7.6 %collective-permute-start.18 = (bf16[64,2048]{1,0:T(8,128)(2,1)S(1)}, bf16[64,2048]{1,0:T(8,128)(2,1)S(1)}, u32[]{:S(2)}, u32[]{:S(2)}) collective-permute-start(bf16[64,2048]{1,0:T(8,128)(2,1)S(1)} %slice.95), channel_id=1, source_target_pairs={{0,12},{1,13},{2,14},{3,15},{4,0},{5,1},{6,2},{7,3},{8,4},{9,5},{1... | collective-permute-start | bytes 786440 | tf_op jit(solution)/shard_map/ppermute | solution.py:33
  65.5 7.8 %collective-permute-start.21 = (bf16[64,2048]{1,0:T(8,128)(2,1)S(1)}, bf16[64,2048]{1,0:T(8,128)(2,1)S(1)}, u32[]{:S(2)}, u32[]{:S(2)}) collective-permute-start(bf16[64,2048]{1,0:T(8,128)(2,1)S(1)} %slice.96), channel_id=1, source_target_pairs={{0,1},{1,2},{2,3},{3,0},{4,5},{5,6},{6,7},{7,4},{8,9},{9,10},{10,1... | collective-permute-start | bytes 786440 | tf_op jit(solution)/shard_map/ppermute | solution.py:33
  66.0 7.3 %collective-permute-start.22 = (bf16[64,2048]{1,0:T(8,128)(2,1)S(1)}, bf16[64,2048]{1,0:T(8,128)(2,1)S(1)}, u32[]{:S(2)}, u32[]{:S(2)}) collective-permute-start(bf16[64,2048]{1,0:T(8,128)(2,1)S(1)} %slice.97), channel_id=1, source_target_pairs={{0,3},{1,0},{2,1},{3,2},{4,7},{5,4},{6,5},{7,6},{8,11},{9,8},{10,9... | collective-permute-start | bytes 786440 | tf_op jit(solution)/shard_map/ppermute | solution.py:33
  74.7 8.4 %collective-permute-start.24 = (bf16[256,512]{1,0:T(8,128)(2,1)S(1)}, bf16[256,512]{1,0:T(8,128)(2,1)S(1)}, u32[]{:S(2)}, u32[]{:S(2)}) collective-permute-start(bf16[256,512]{1,0:T(8,128)(2,1)S(1)} %tile.3), channel_id=1, source_target_pairs={{0,64},{16,80},{32,96},{48,112},{64,0},{80,16},{96,32},{112,48},{1... | collective-permute-start | bytes 786440 | tf_op jit(solution)/shard_map/ppermute | solution.py:38
  79.3 8.0 %collective-permute-start.23 = (bf16[256,512]{1,0:T(8,128)(2,1)S(1)}, bf16[256,512]{1,0:T(8,128)(2,1)S(1)}, u32[]{:S(2)}, u32[]{:S(2)}) collective-permute-start(bf16[256,512]{1,0:T(8,128)(2,1)S(1)} %tile.2), channel_id=1, source_target_pairs={{0,64},{16,80},{32,96},{48,112},{64,0},{80,16},{96,32},{112,48},{1... | collective-permute-start | bytes 786440 | tf_op jit(solution)/shard_map/ppermute | solution.py:38
  83.1 8.9 %collective-permute-start.25 = (bf16[256,512]{1,0:T(8,128)(2,1)S(1)}, bf16[256,512]{1,0:T(8,128)(2,1)S(1)}, u32[]{:S(2)}, u32[]{:S(2)}) collective-permute-start(bf16[256,512]{1,0:T(8,128)(2,1)S(1)} %collective-permute-done.24), channel_id=1, source_target_pairs={{0,4},{1,5},{2,6},{3,7},{4,8},{5,9},{6,10},{7,11},{8,12},{9,13},{1... | collective-permute-start | bytes 786440 | tf_op jit(solution)/shard_map/ppermute | solution.py:33
  83.1 9.0 %collective-permute-start.26 = (bf16[256,512]{1,0:T(8,128)(2,1)S(1)}, bf16[256,512]{1,0:T(8,128)(2,1)S(1)}, u32[]{:S(2)}, u32[]{:S(2)}) collective-permute-start(bf16[256,512]{1,0:T(8,128)(2,1)S(1)} %collective-permute-done.24), channel_id=1, source_target_pairs={{0,12},{1,13},{2,14},{3,15},{4,0},{5,1},{6,2},{7,3},{8,4},{9,5},{1... | collective-permute-start | bytes 786440 | tf_op jit(solution)/shard_map/ppermute | solution.py:33
  87.2 8.6 %collective-permute-start.32 = (bf16[256,512]{1,0:T(8,128)(2,1)S(1)}, bf16[256,512]{1,0:T(8,128)(2,1)S(1)}, u32[]{:S(2)}, u32[]{:S(2)}) collective-permute-start(bf16[256,512]{1,0:T(8,128)(2,1)S(1)} %collective-permute-done.23), channel_id=1, source_target_pairs={{0,4},{1,5},{2,6},{3,7},{4,8},{5,9},{6,10},{7,11},{8,12},{9,13},{1... | collective-permute-start | bytes 786440 | tf_op jit(solution)/shard_map/ppermute | solution.py:33
  87.2 8.7 %collective-permute-start.33 = (bf16[256,512]{1,0:T(8,128)(2,1)S(1)}, bf16[256,512]{1,0:T(8,128)(2,1)S(1)}, u32[]{:S(2)}, u32[]{:S(2)}) collective-permute-start(bf16[256,512]{1,0:T(8,128)(2,1)S(1)} %collective-permute-done.23), channel_id=1, source_target_pairs={{0,12},{1,13},{2,14},{3,15},{4,0},{5,1},{6,2},{7,3},{8,4},{9,5},{1... | collective-permute-start | bytes 786440 | tf_op jit(solution)/shard_map/ppermute | solution.py:33
  92.0 7.4 %collective-permute-start.27 = (bf16[128,512]{1,0:T(8,128)(2,1)S(1)}, bf16[128,512]{1,0:T(8,128)(2,1)S(1)}, u32[]{:S(2)}, u32[]{:S(2)}) collective-permute-start(bf16[128,512]{1,0:T(8,128)(2,1)S(1)} %slice.98), channel_id=1, source_target_pairs={{0,4},{1,5},{2,6},{3,7},{4,8},{5,9},{6,10},{7,11},{8,12},{9,13},{1... | collective-permute-start | bytes 393224 | tf_op jit(solution)/shard_map/ppermute | solution.py:33
  92.1 7.3 %collective-permute-start.28 = (bf16[128,512]{1,0:T(8,128)(2,1)S(1)}, bf16[128,512]{1,0:T(8,128)(2,1)S(1)}, u32[]{:S(2)}, u32[]{:S(2)}) collective-permute-start(bf16[128,512]{1,0:T(8,128)(2,1)S(1)} %slice.99), channel_id=1, source_target_pairs={{0,12},{1,13},{2,14},{3,15},{4,0},{5,1},{6,2},{7,3},{8,4},{9,5},{1... | collective-permute-start | bytes 393224 | tf_op jit(solution)/shard_map/ppermute | solution.py:33
  103.3 9.7 %collective-permute-start.37 = (bf16[3,256,128]{2,1,0:T(8,128)(2,1)S(1)}, bf16[3,256,128]{2,1,0:T(8,128)(2,1)S(1)}, u32[]{:S(2)}, u32[]{:S(2)}) collective-permute-start(bf16[3,256,128]{2,1,0:T(8,128)(2,1)S(1)} %get-tuple-element.52), channel_id=1, source_target_pairs={{0,2},{1,3},{2,0},{3,1},{4,6},{5,7},{6,4},{7,5},{8,10},{9,11},{10,... | collective-permute-start | bytes 589832 | tf_op jit(solution)/shard_map/ppermute | solution.py:33
  109.3 7.8 %collective-permute-start.30 = (bf16[3,256,128]{2,1,0:T(8,128)(2,1)S(1)}, bf16[3,256,128]{2,1,0:T(8,128)(2,1)S(1)}, u32[]{:S(2)}, u32[]{:S(2)}) collective-permute-start(bf16[3,256,128]{2,1,0:T(8,128)(2,1)S(1)} %get-tuple-element.49), channel_id=1, source_target_pairs={{0,2},{1,3},{2,0},{3,1},{4,6},{5,7},{6,4},{7,5},{8,10},{9,11},{10,... | collective-permute-start | bytes 589832 | tf_op jit(solution)/shard_map/ppermute | solution.py:33
  109.9 8.1 %collective-permute-start.31 = (bf16[3,256,128]{2,1,0:T(8,128)(2,1)S(1)}, bf16[3,256,128]{2,1,0:T(8,128)(2,1)S(1)}, u32[]{:S(2)}, u32[]{:S(2)}) collective-permute-start(bf16[3,256,128]{2,1,0:T(8,128)(2,1)S(1)} %get-tuple-element.48), channel_id=1, source_target_pairs={{0,3},{1,0},{2,1},{3,2},{4,7},{5,4},{6,5},{7,6},{8,11},{9,8},{10,9... | collective-permute-start | bytes 589832 | tf_op jit(solution)/shard_map/ppermute | solution.py:33
  (14 other events, 105.2 us)

commit v7 on v6

--- a/solution.py
+++ b/solution.py
@@ -50,6 +50,10 @@
     far_top = shift(from_left[:half], axis, 1)
     far_bottom = shift(from_right[half:], axis, -1)
     return jnp.concatenate([own, from_left, from_right, far_top, far_bottom], axis=0)
+
+
+def direct_bundle(own, axis):
+    return jnp.concatenate([own] + [shift(own, axis, -step) for step in RING[1:]], axis=0)
 
 
 def spread(bundle, axis, *meanwhile):
@@ -499,7 +503,8 @@
         there = to_parent(rows)
         if chunk is FIRST:
             there, factor_local = lax.optimization_barrier((there, factor_local))
-        packed = pack_tiles(plan, bundle_of(there, "x"))
+        gather = direct_bundle if chunk is FIRST else bundle_of
+        packed = pack_tiles(plan, gather(there, "x"))
         for step in range(SIDE):
             tile = packed[step * SLOTS : (step + 1) * SLOTS]
             tiles[chunk, step] = shift(tile, "z", step) if step else tile

time: 121 us -> 118 us (0.975); the launches traced: 120 us -> 118 us
  starting transfers between devices: 65 us -> 59.2 us
  waiting for transfers between devices: 34 us -> 38.4 us
    ppermute x37 -> x36, starting transfers between devices: 61.3 us -> 55.5 us  [shift(): return lax.ppermute(value, 'front', pairs)]
    ppermute x37 -> x36, waiting for transfers between devices: 30.5 us -> 34.9 us  [shift(): return lax.ppermute(value, 'front', pairs)]
    unnamed x30 -> x26, local copies, waits for them, and re-layouts: 3.5 us -> 3.44 us
  transfers between devices with their start and end apart: 39 -> 38, of which waited for: 17 -> 14; matrix products, arithmetic and copies ran while one was open for 1% -> 1% of each run, Pallas kernels for 6% -> 7%
where the time goes in v7:
time: 118 us
  starting transfers between devices  59.2 us (50%)
  waiting for transfers between devices  38.4 us (33%)
  Pallas kernels  14.8 us (13%)
  local copies, waits for them, and re-layouts  4.63 us (4%)
  between operations  1.22 us (1%)
    ppermute x36, starting transfers between devices, shift(): return lax.ppermute(value, 'front', pairs)  55.5 us
    ppermute x36, waiting for transfers between devices, shift(): return lax.ppermute(value, 'front', pairs)  34.9 us
    ppermute x2, starting transfers between devices, to_parent(): lax.ppermute(value, 'leaf', [(g, (g + groups // 2) % groups) for g in ran...  3.69 us
    pallas_call x2, Pallas kernels, place_tiles(): pl.pallas_call(functools.partial(place_kernel, list(tiles)), out_shape=PA...  3.65 us
    pallas_call x1, Pallas kernels, blank_rows(): pl.pallas_call(blank_kernel, out_shape=(PARENT, jax.ShapeDtypeStruct((2 *...  3.53 us
    ppermute x2, waiting for transfers between devices, to_parent(): lax.ppermute(value, 'leaf', [(g, (g + groups // 2) % groups) for g in ran...  3.47 us
    unnamed x26, local copies, waits for them, and re-layouts  3.44 us
    pallas_call x1, Pallas kernels, eliminate(): pl.pallas_call(panel_kernel, out_shape=(jax.ShapeDtypeStruct((ROWS, PANEL...  3.34 us
  transfers between devices with their start and end apart: 38, of which 14 were waited for; matrix products, arithmetic and copies ran while one was open for 1% of the time, Pallas kernels for 7%

profile of v7, /device:TPU:0, one launch (start us, length us, event | category | flops | bytes accessed | tf_op | source)
XLA Modules:
  0.0 118.3 jit_solution(9077398625068938718)
XLA Ops:
  0.6 1.6 %collective-permute-start = (bf16[128,1024]{1,0:T(8,128)(2,1)}, bf16[128,1024]{1,0:T(8,128)(2,1)S(1)}, u32[]{:S(2)}, u32[]{:S(2)}) collective-permute-start(bf16[128,1024]{1,0:T(8,128)(2,1)} %bitcast.8), channel_id=1, source_target_pairs={{0,4},{1,5},{2,6},{3,7},{4,8},{5,9},{6,10},{7,11},{8,12},{9,13},{1... | collective-permute-start | bytes 786440 | tf_op jit(solution)/shard_map/ppermute | solution.py:33
  2.3 1.7 %collective-permute-start.1 = (bf16[128,1024]{1,0:T(8,128)(2,1)}, bf16[128,1024]{1,0:T(8,128)(2,1)S(1)}, u32[]{:S(2)}, u32[]{:S(2)}) collective-permute-start(bf16[128,1024]{1,0:T(8,128)(2,1)} %bitcast.9), channel_id=1, source_target_pairs={{0,12},{1,13},{2,14},{3,15},{4,0},{5,1},{6,2},{7,3},{8,4},{9,5},{1... | collective-permute-start | bytes 786440 | tf_op jit(solution)/shard_map/ppermute | solution.py:33
  3.9 2.0 %collective-permute-start.8 = (bf16[64,1024]{1,0:T(8,128)(2,1)}, bf16[64,1024]{1,0:T(8,128)(2,1)S(1)}, u32[]{:S(2)}, u32[]{:S(2)}) collective-permute-start(bf16[64,1024]{1,0:T(8,128)(2,1)} %bitcast.11), channel_id=1, source_target_pairs={{0,1},{1,2},{2,3},{3,0},{4,5},{5,6},{6,7},{7,4},{8,9},{9,10},{10,1... | collective-permute-start | bytes 393224 | tf_op jit(solution)/shard_map/ppermute | solution.py:33
  5.9 2.1 %collective-permute-start.9 = (bf16[64,1024]{1,0:T(8,128)(2,1)}, bf16[64,1024]{1,0:T(8,128)(2,1)S(1)}, u32[]{:S(2)}, u32[]{:S(2)}) collective-permute-start(bf16[64,1024]{1,0:T(8,128)(2,1)} %bitcast.12), channel_id=1, source_target_pairs={{0,3},{1,0},{2,1},{3,2},{4,7},{5,4},{6,5},{7,6},{8,11},{9,8},{10,9... | collective-permute-start | bytes 393224 | tf_op jit(solution)/shard_map/ppermute | solution.py:33
  8.1 1.9 %collective-permute-start.10 = (bf16[64,1024]{1,0:T(8,128)(2,1)}, bf16[64,1024]{1,0:T(8,128)(2,1)S(1)}, u32[]{:S(2)}, u32[]{:S(2)}) collective-permute-start(bf16[64,1024]{1,0:T(8,128)(2,1)} %bitcast.13), channel_id=1, source_target_pairs={{0,2},{1,3},{2,0},{3,1},{4,6},{5,7},{6,4},{7,5},{8,10},{9,11},{10,... | collective-permute-start | bytes 393224 | tf_op jit(solution)/shard_map/ppermute | solution.py:33
  13.3 3.0 %collective-permute-start.3 = (bf16[64,1024]{1,0:T(8,128)(2,1)S(1)}, bf16[64,1024]{1,0:T(8,128)(2,1)S(1)}, u32[]{:S(2)}, u32[]{:S(2)}) collective-permute-start(bf16[64,1024]{1,0:T(8,128)(2,1)S(1)} %slice.64), channel_id=1, source_target_pairs={{0,12},{1,13},{2,14},{3,15},{4,0},{5,1},{6,2},{7,3},{8,4},{9,5},{1... | collective-permute-start | bytes 393224 | tf_op jit(solution)/shard_map/ppermute | solution.py:33
  16.5 3.2 %collective-permute-start.12 = (bf16[352,1024]{1,0:T(8,128)(2,1)S(1)}, bf16[352,1024]{1,0:T(8,128)(2,1)S(1)}, u32[]{:S(2)}, u32[]{:S(2)}) collective-permute-start(bf16[352,1024]{1,0:T(8,128)(2,1)S(1)} %get-tuple-element.37.refs_5_), channel_id=1, source_target_pairs={{0,12},{1,13},{2,14},{3,15},{4,0},{5,1},{6,2},{7,3},{8,4},{9,5},{1... | collective-permute-start | bytes 2162696 | tf_op jit(solution)/shard_map/ppermute | solution.py:33
  21.5 2.1 %collective-permute-start.5 = (bf16[1280,256]{1,0:T(8,128)(2,1)S(1)}, bf16[1280,256]{1,0:T(8,128)(2,1)S(1)}, u32[]{:S(2)}, u32[]{:S(2)}) collective-permute-start(bf16[1280,256]{1,0:T(8,128)(2,1)S(1)} %lower.1.refs_0_), channel_id=1, source_target_pairs={{0,3},{1,0},{2,1},{3,2},{4,7},{5,4},{6,5},{7,6},{8,11},{9,8},{10,9... | collective-permute-start | bytes 1966088 | tf_op jit(solution)/shard_map/ppermute | solution.py:33
  23.7 3.5 %blank.1 = (f32[4096,384]{1,0:T(8,128)}, s32[32]{0:T(128)S(1)}) custom-call(s32[8,16]{1,0:T(8,128)S(1)} %copy-done.3, s32[8,32]{1,0:T(8,128)S(1)} %copy-done.4), custom_call_target="tpu_custom_call" | custom-call | bytes 3145728 | tf_op jit(solution)/shard_map/blank/pallas_call | solution.py:417
  27.2 7.4 %collective-permute-done.11.refs_6_.refs_1_ = bf16[352,1024]{1,0:T(8,128)(2,1)S(1)} collective-permute-done((bf16[352,1024]{1,0:T(8,128)(2,1)S(1)}, bf16[352,1024]{1,0:T(8,128)(2,1)S(1)}, u32[]{:S(2)}, u32[]{:S(2)}) %collective-permute-start.11) | collective-permute-done | bytes 720928 | tf_op jit(solution)/shard_map/ppermute | solution.py:33
  34.8 3.3 %collective-permute-start.14 = (bf16[160,1024]{1,0:T(8,128)(2,1)S(1)}, bf16[160,1024]{1,0:T(8,128)(2,1)S(1)}, u32[]{:S(2)}, u32[]{:S(2)}) collective-permute-start(bf16[160,1024]{1,0:T(8,128)(2,1)S(1)} %slice.85), channel_id=1, source_target_pairs={{0,12},{1,13},{2,14},{3,15},{4,0},{5,1},{6,2},{7,3},{8,4},{9,5},{1... | collective-permute-start | bytes 983048 | tf_op jit(solution)/shard_map/ppermute | solution.py:33
  39.2 2.3 %collective-permute-start.7 = (bf16[640,256]{1,0:T(8,128)(2,1)S(1)}, bf16[640,256]{1,0:T(8,128)(2,1)S(1)}, u32[]{:S(2)}, u32[]{:S(2)}) collective-permute-start(bf16[640,256]{1,0:T(8,128)(2,1)S(1)} %slice.66), channel_id=1, source_target_pairs={{0,3},{1,0},{2,1},{3,2},{4,7},{5,4},{6,5},{7,6},{8,11},{9,8},{10,9... | collective-permute-start | bytes 983048 | tf_op jit(solution)/shard_map/ppermute | solution.py:33
  41.5 2.0 %collective-permute-done.13.refs_8_.refs_3_ = bf16[160,1024]{1,0:T(8,128)(2,1)S(1)} collective-permute-done((bf16[160,1024]{1,0:T(8,128)(2,1)S(1)}, bf16[160,1024]{1,0:T(8,128)(2,1)S(1)}, u32[]{:S(2)}, u32[]{:S(2)}) %collective-permute-start.13) | collective-permute-done | bytes 327712 | tf_op jit(solution)/shard_map/ppermute | solution.py:33
  43.5 3.2 %collective-permute-done.6.refs_3_ = bf16[640,256]{1,0:T(8,128)(2,1)S(1)} collective-permute-done((bf16[640,256]{1,0:T(8,128)(2,1)S(1)}, bf16[640,256]{1,0:T(8,128)(2,1)S(1)}, u32[]{:S(2)}, u32[]{:S(2)}) %collective-permute-start.6) | collective-permute-done | bytes 327712 | tf_op jit(solution)/shard_map/ppermute | solution.py:33
  46.7 3.3 %panels.1 = (bf16[64,1024]{1,0:T(8,128)(2,1)}, bf16[128,2048]{1,0:T(8,128)(2,1)S(1)}) custom-call(bf16[128,2048]{1,0:T(8,128)(2,1)S(1)} %bitcast.15, bf16[1280,256]{1,0:T(8,128)(2,1)S(1)} %lower.1.refs_0_, bf16[1280,256]{1,0:T(8,128)(2,1)S(1)} %collective-permute-done.4.refs_1_, bf16[1280,256]{1,0:T(8,128)(2,1)S(1)} %collective-permute-done.5.refs_2_, ...), custom_call_target="tpu_custom_call" | custom-call | flops 2952790016 | bytes 8388608 | tf_op jit(solution)/shard_map/panels/pallas_call | solution.py:195
  50.1 3.2 %collective-permute-start.16 = (bf16[128,2048]{1,0:T(8,128)(2,1)S(1)}, bf16[128,2048]{1,0:T(8,128)(2,1)S(1)}, u32[]{:S(2)}, u32[]{:S(2)}) collective-permute-start(bf16[128,2048]{1,0:T(8,128)(2,1)S(1)} %get-tuple-element.40), channel_id=1, source_target_pairs={{0,12},{1,13},{2,14},{3,15},{4,0},{5,1},{6,2},{7,3},{8,4},{9,5},{1... | collective-permute-start | bytes 1572872 | tf_op jit(solution)/shard_map/ppermute | solution.py:33
  53.5 3.0 %collective-permute-start.20 = (bf16[128,2048]{1,0:T(8,128)(2,1)S(1)}, bf16[128,2048]{1,0:T(8,128)(2,1)S(1)}, u32[]{:S(2)}, u32[]{:S(2)}) collective-permute-start(bf16[128,2048]{1,0:T(8,128)(2,1)S(1)} %get-tuple-element.40), channel_id=1, source_target_pairs={{0,3},{1,0},{2,1},{3,2},{4,7},{5,4},{6,5},{7,6},{8,11},{9,8},{10,9... | collective-permute-start | bytes 1572872 | tf_op jit(solution)/shard_map/ppermute | solution.py:33
  56.8 5.2 %collective-permute-done.15 = bf16[128,2048]{1,0:T(8,128)(2,1)S(1)} collective-permute-done((bf16[128,2048]{1,0:T(8,128)(2,1)S(1)}, bf16[128,2048]{1,0:T(8,128)(2,1)S(1)}, u32[]{:S(2)}, u32[]{:S(2)}) %collective-permute-start.15) | collective-permute-done | bytes 524320 | tf_op jit(solution)/shard_map/ppermute | solution.py:33
  62.2 3.3 %collective-permute-start.18 = (bf16[64,2048]{1,0:T(8,128)(2,1)S(1)}, bf16[64,2048]{1,0:T(8,128)(2,1)S(1)}, u32[]{:S(2)}, u32[]{:S(2)}) collective-permute-start(bf16[64,2048]{1,0:T(8,128)(2,1)S(1)} %slice.87), channel_id=1, source_target_pairs={{0,12},{1,13},{2,14},{3,15},{4,0},{5,1},{6,2},{7,3},{8,4},{9,5},{1... | collective-permute-start | bytes 786440 | tf_op jit(solution)/shard_map/ppermute | solution.py:33
  66.0 3.1 %collective-permute-start.22 = (bf16[64,2048]{1,0:T(8,128)(2,1)S(1)}, bf16[64,2048]{1,0:T(8,128)(2,1)S(1)}, u32[]{:S(2)}, u32[]{:S(2)}) collective-permute-start(bf16[64,2048]{1,0:T(8,128)(2,1)S(1)} %slice.89), channel_id=1, source_target_pairs={{0,3},{1,0},{2,1},{3,2},{4,7},{5,4},{6,5},{7,6},{8,11},{9,8},{10,9... | collective-permute-start | bytes 786440 | tf_op jit(solution)/shard_map/ppermute | solution.py:33
  69.8 3.5 %collective-permute-done.21 = bf16[64,2048]{1,0:T(8,128)(2,1)S(1)} collective-permute-done((bf16[64,2048]{1,0:T(8,128)(2,1)S(1)}, bf16[64,2048]{1,0:T(8,128)(2,1)S(1)}, u32[]{:S(2)}, u32[]{:S(2)}) %collective-permute-start.21) | collective-permute-done | bytes 262176 | tf_op jit(solution)/shard_map/ppermute | solution.py:33
  74.7 3.3 %collective-permute-start.24 = (bf16[256,512]{1,0:T(8,128)(2,1)S(1)}, bf16[256,512]{1,0:T(8,128)(2,1)S(1)}, u32[]{:S(2)}, u32[]{:S(2)}) collective-permute-start(bf16[256,512]{1,0:T(8,128)(2,1)S(1)} %tile.3), channel_id=1, source_target_pairs={{0,64},{16,80},{32,96},{48,112},{64,0},{80,16},{96,32},{112,48},{1... | collective-permute-start | bytes 786440 | tf_op jit(solution)/shard_map/ppermute | solution.py:38
  80.5 2.6 %collective-permute-done.24 = bf16[256,512]{1,0:T(8,128)(2,1)S(1)} collective-permute-done((bf16[256,512]{1,0:T(8,128)(2,1)S(1)}, bf16[256,512]{1,0:T(8,128)(2,1)S(1)}, u32[]{:S(2)}, u32[]{:S(2)}) %collective-permute-start.24) | collective-permute-done | bytes 262176 | tf_op jit(solution)/shard_map/ppermute | solution.py:38
  83.1 3.2 %collective-permute-start.26 = (bf16[256,512]{1,0:T(8,128)(2,1)S(1)}, bf16[256,512]{1,0:T(8,128)(2,1)S(1)}, u32[]{:S(2)}, u32[]{:S(2)}) collective-permute-start(bf16[256,512]{1,0:T(8,128)(2,1)S(1)} %collective-permute-done.24), channel_id=1, source_target_pairs={{0,12},{1,13},{2,14},{3,15},{4,0},{5,1},{6,2},{7,3},{8,4},{9,5},{1... | collective-permute-start | bytes 786440 | tf_op jit(solution)/shard_map/ppermute | solution.py:33
  89.3 6.9 %collective-permute-done.25 = bf16[256,512]{1,0:T(8,128)(2,1)S(1)} collective-permute-done((bf16[256,512]{1,0:T(8,128)(2,1)S(1)}, bf16[256,512]{1,0:T(8,128)(2,1)S(1)}, u32[]{:S(2)}, u32[]{:S(2)}) %collective-permute-start.25) | collective-permute-done | bytes 262176 | tf_op jit(solution)/shard_map/ppermute | solution.py:33
  96.3 3.3 %collective-permute-start.28 = (bf16[128,512]{1,0:T(8,128)(2,1)S(1)}, bf16[128,512]{1,0:T(8,128)(2,1)S(1)}, u32[]{:S(2)}, u32[]{:S(2)}) collective-permute-start(bf16[128,512]{1,0:T(8,128)(2,1)S(1)} %slice.91), channel_id=1, source_target_pairs={{0,12},{1,13},{2,14},{3,15},{4,0},{5,1},{6,2},{7,3},{8,4},{9,5},{1... | collective-permute-start | bytes 393224 | tf_op jit(solution)/shard_map/ppermute | solution.py:33
  101.3 4.2 %collective-permute-start.36 = (bf16[3,256,128]{2,1,0:T(8,128)(2,1)S(1)}, bf16[3,256,128]{2,1,0:T(8,128)(2,1)S(1)}, u32[]{:S(2)}, u32[]{:S(2)}) collective-permute-start(bf16[3,256,128]{2,1,0:T(8,128)(2,1)S(1)} %get-tuple-element.52), channel_id=1, source_target_pairs={{0,2},{1,3},{2,0},{3,1},{4,6},{5,7},{6,4},{7,5},{8,10},{9,11},{10,... | collective-permute-start | bytes 589832 | tf_op jit(solution)/shard_map/ppermute | solution.py:33
  106.4 2.0 %collective-permute-start.29 = (bf16[3,256,128]{2,1,0:T(8,128)(2,1)S(1)}, bf16[3,256,128]{2,1,0:T(8,128)(2,1)S(1)}, u32[]{:S(2)}, u32[]{:S(2)}) collective-permute-start(bf16[3,256,128]{2,1,0:T(8,128)(2,1)S(1)} %get-tuple-element.50), channel_id=1, source_target_pairs={{0,1},{1,2},{2,3},{3,0},{4,5},{5,6},{6,7},{7,4},{8,9},{9,10},{10,1... | collective-permute-start | bytes 589832 | tf_op jit(solution)/shard_map/ppermute | solution.py:33
  108.5 1.6 %collective-permute-done.35.refs_1_ = bf16[3,256,128]{2,1,0:T(8,128)(2,1)S(1)} collective-permute-done((bf16[3,256,128]{2,1,0:T(8,128)(2,1)S(1)}, bf16[3,256,128]{2,1,0:T(8,128)(2,1)S(1)}, u32[]{:S(2)}, u32[]{:S(2)}) %collective-permute-start.35) | collective-permute-done | bytes 196640 | tf_op jit(solution)/shard_map/ppermute | solution.py:33
  112.3 2.0 %place.2.refs_3_ = f32[4096,384]{1,0:T(8,128)} custom-call(s32[8,16]{1,0:T(8,128)S(1)} %copy-done.3, s32[32]{0:T(128)S(1)} %get-tuple-element.44.plan, bf16[3,256,128]{2,1,0:T(8,128)(2,1)S(1)} %get-tuple-element.54.refs_0_, bf16[3,256,128]{2,1,0:T(8,128)(2,1)S(1)} %collective-permute-done.35.refs_1_, ...), custom_call_target="tpu_custom_call", output_to_operand_aliasing={{}: (7, {})} | custom-call | bytes 1048576 | tf_op jit(solution)/shard_map/place/pallas_call | solution.py:459
  114.3 2.1 %collective-permute-done.30.refs_1_ = bf16[3,256,128]{2,1,0:T(8,128)(2,1)S(1)} collective-permute-done((bf16[3,256,128]{2,1,0:T(8,128)(2,1)S(1)}, bf16[3,256,128]{2,1,0:T(8,128)(2,1)S(1)}, u32[]{:S(2)}, u32[]{:S(2)}) %collective-permute-start.30) | collective-permute-done | bytes 196640 | tf_op jit(solution)/shard_map/ppermute | solution.py:33
  116.4 1.7 %place.3 = f32[4096,384]{1,0:T(8,128)} custom-call(s32[8,16]{1,0:T(8,128)S(1)} %copy-done.3, s32[32]{0:T(128)S(1)} %get-tuple-element.44.plan, bf16[3,256,128]{2,1,0:T(8,128)(2,1)S(1)} %collective-permute-done.29.refs_0_, bf16[3,256,128]{2,1,0:T(8,128)(2,1)S(1)} %collective-permute-done.30.refs_1_, ...), custom_call_target="tpu_custom_call", output_to_operand_aliasing={{}: (5, {})} | custom-call | bytes 1048576 | tf_op jit(solution)/shard_map/place/pallas_call | solution.py:459
  (100 shorter events, 20.2 us)
Async XLA Ops:
  0.6 12.3 %collective-permute-start = (bf16[128,1024]{1,0:T(8,128)(2,1)}, bf16[128,1024]{1,0:T(8,128)(2,1)S(1)}, u32[]{:S(2)}, u32[]{:S(2)}) collective-permute-start(bf16[128,1024]{1,0:T(8,128)(2,1)} %bitcast.8), channel_id=1, source_target_pairs={{0,4},{1,5},{2,6},{3,7},{4,8},{5,9},{6,10},{7,11},{8,12},{9,13},{1... | collective-permute-start | bytes 786440 | tf_op jit(solution)/shard_map/ppermute | solution.py:33
  2.3 10.6 %collective-permute-start.1 = (bf16[128,1024]{1,0:T(8,128)(2,1)}, bf16[128,1024]{1,0:T(8,128)(2,1)S(1)}, u32[]{:S(2)}, u32[]{:S(2)}) collective-permute-start(bf16[128,1024]{1,0:T(8,128)(2,1)} %bitcast.9), channel_id=1, source_target_pairs={{0,12},{1,13},{2,14},{3,15},{4,0},{5,1},{6,2},{7,3},{8,4},{9,5},{1... | collective-permute-start | bytes 786440 | tf_op jit(solution)/shard_map/ppermute | solution.py:33
  3.9 12.4 %collective-permute-start.8 = (bf16[64,1024]{1,0:T(8,128)(2,1)}, bf16[64,1024]{1,0:T(8,128)(2,1)S(1)}, u32[]{:S(2)}, u32[]{:S(2)}) collective-permute-start(bf16[64,1024]{1,0:T(8,128)(2,1)} %bitcast.11), channel_id=1, source_target_pairs={{0,1},{1,2},{2,3},{3,0},{4,5},{5,6},{6,7},{7,4},{8,9},{9,10},{10,1... | collective-permute-start | bytes 393224 | tf_op jit(solution)/shard_map/ppermute | solution.py:33
  5.9 10.4 %collective-permute-start.9 = (bf16[64,1024]{1,0:T(8,128)(2,1)}, bf16[64,1024]{1,0:T(8,128)(2,1)S(1)}, u32[]{:S(2)}, u32[]{:S(2)}) collective-permute-start(bf16[64,1024]{1,0:T(8,128)(2,1)} %bitcast.12), channel_id=1, source_target_pairs={{0,3},{1,0},{2,1},{3,2},{4,7},{5,4},{6,5},{7,6},{8,11},{9,8},{10,9... | collective-permute-start | bytes 393224 | tf_op jit(solution)/shard_map/ppermute | solution.py:33
  8.1 8.3 %collective-permute-start.10 = (bf16[64,1024]{1,0:T(8,128)(2,1)}, bf16[64,1024]{1,0:T(8,128)(2,1)S(1)}, u32[]{:S(2)}, u32[]{:S(2)}) collective-permute-start(bf16[64,1024]{1,0:T(8,128)(2,1)} %bitcast.13), channel_id=1, source_target_pairs={{0,2},{1,3},{2,0},{3,1},{4,6},{5,7},{6,4},{7,5},{8,10},{9,11},{10,... | collective-permute-start | bytes 393224 | tf_op jit(solution)/shard_map/ppermute | solution.py:33
  16.4 18.2 %collective-permute-start.11 = (bf16[352,1024]{1,0:T(8,128)(2,1)S(1)}, bf16[352,1024]{1,0:T(8,128)(2,1)S(1)}, u32[]{:S(2)}, u32[]{:S(2)}) collective-permute-start(bf16[352,1024]{1,0:T(8,128)(2,1)S(1)} %get-tuple-element.38), channel_id=1, source_target_pairs={{0,4},{1,5},{2,6},{3,7},{4,8},{5,9},{6,10},{7,11},{8,12},{9,13},{1... | collective-permute-start | bytes 2162696 | tf_op jit(solution)/shard_map/ppermute | solution.py:33
  16.5 18.2 %collective-permute-start.12 = (bf16[352,1024]{1,0:T(8,128)(2,1)S(1)}, bf16[352,1024]{1,0:T(8,128)(2,1)S(1)}, u32[]{:S(2)}, u32[]{:S(2)}) collective-permute-start(bf16[352,1024]{1,0:T(8,128)(2,1)S(1)} %get-tuple-element.37.refs_5_), channel_id=1, source_target_pairs={{0,12},{1,13},{2,14},{3,15},{4,0},{5,1},{6,2},{7,3},{8,4},{9,5},{1... | collective-permute-start | bytes 2162696 | tf_op jit(solution)/shard_map/ppermute | solution.py:33
  20.3 17.7 %collective-permute-start.4 = (bf16[1280,256]{1,0:T(8,128)(2,1)S(1)}, bf16[1280,256]{1,0:T(8,128)(2,1)S(1)}, u32[]{:S(2)}, u32[]{:S(2)}) collective-permute-start(bf16[1280,256]{1,0:T(8,128)(2,1)S(1)} %lower.1.refs_0_), channel_id=1, source_target_pairs={{0,1},{1,2},{2,3},{3,0},{4,5},{5,6},{6,7},{7,4},{8,9},{9,10},{10,1... | collective-permute-start | bytes 1966088 | tf_op jit(solution)/shard_map/ppermute | solution.py:33
  21.5 16.5 %collective-permute-start.5 = (bf16[1280,256]{1,0:T(8,128)(2,1)S(1)}, bf16[1280,256]{1,0:T(8,128)(2,1)S(1)}, u32[]{:S(2)}, u32[]{:S(2)}) collective-permute-start(bf16[1280,256]{1,0:T(8,128)(2,1)S(1)} %lower.1.refs_0_), channel_id=1, source_target_pairs={{0,3},{1,0},{2,1},{3,2},{4,7},{5,4},{6,5},{7,6},{8,11},{9,8},{10,9... | collective-permute-start | bytes 1966088 | tf_op jit(solution)/shard_map/ppermute | solution.py:33
  34.7 8.8 %collective-permute-start.13 = (bf16[160,1024]{1,0:T(8,128)(2,1)S(1)}, bf16[160,1024]{1,0:T(8,128)(2,1)S(1)}, u32[]{:S(2)}, u32[]{:S(2)}) collective-permute-start(bf16[160,1024]{1,0:T(8,128)(2,1)S(1)} %slice.84), channel_id=1, source_target_pairs={{0,4},{1,5},{2,6},{3,7},{4,8},{5,9},{6,10},{7,11},{8,12},{9,13},{1... | collective-permute-start | bytes 983048 | tf_op jit(solution)/shard_map/ppermute | solution.py:33
  34.8 8.7 %collective-permute-start.14 = (bf16[160,1024]{1,0:T(8,128)(2,1)S(1)}, bf16[160,1024]{1,0:T(8,128)(2,1)S(1)}, u32[]{:S(2)}, u32[]{:S(2)}) collective-permute-start(bf16[160,1024]{1,0:T(8,128)(2,1)S(1)} %slice.85), channel_id=1, source_target_pairs={{0,12},{1,13},{2,14},{3,15},{4,0},{5,1},{6,2},{7,3},{8,4},{9,5},{1... | collective-permute-start | bytes 983048 | tf_op jit(solution)/shard_map/ppermute | solution.py:33
  38.1 8.6 %collective-permute-start.6 = (bf16[640,256]{1,0:T(8,128)(2,1)S(1)}, bf16[640,256]{1,0:T(8,128)(2,1)S(1)}, u32[]{:S(2)}, u32[]{:S(2)}) collective-permute-start(bf16[640,256]{1,0:T(8,128)(2,1)S(1)} %slice.65), channel_id=1, source_target_pairs={{0,1},{1,2},{2,3},{3,0},{4,5},{5,6},{6,7},{7,4},{8,9},{9,10},{10,1... | collective-permute-start | bytes 983048 | tf_op jit(solution)/shard_map/ppermute | solution.py:33
  50.1 12.0 %collective-permute-start.15 = (bf16[128,2048]{1,0:T(8,128)(2,1)S(1)}, bf16[128,2048]{1,0:T(8,128)(2,1)S(1)}, u32[]{:S(2)}, u32[]{:S(2)}) collective-permute-start(bf16[128,2048]{1,0:T(8,128)(2,1)S(1)} %get-tuple-element.40), channel_id=1, source_target_pairs={{0,4},{1,5},{2,6},{3,7},{4,8},{5,9},{6,10},{7,11},{8,12},{9,13},{1... | collective-permute-start | bytes 1572872 | tf_op jit(solution)/shard_map/ppermute | solution.py:33
  50.1 12.1 %collective-permute-start.16 = (bf16[128,2048]{1,0:T(8,128)(2,1)S(1)}, bf16[128,2048]{1,0:T(8,128)(2,1)S(1)}, u32[]{:S(2)}, u32[]{:S(2)}) collective-permute-start(bf16[128,2048]{1,0:T(8,128)(2,1)S(1)} %get-tuple-element.40), channel_id=1, source_target_pairs={{0,12},{1,13},{2,14},{3,15},{4,0},{5,1},{6,2},{7,3},{8,4},{9,5},{1... | collective-permute-start | bytes 1572872 | tf_op jit(solution)/shard_map/ppermute | solution.py:33
  53.3 12.2 %collective-permute-start.19 = (bf16[128,2048]{1,0:T(8,128)(2,1)S(1)}, bf16[128,2048]{1,0:T(8,128)(2,1)S(1)}, u32[]{:S(2)}, u32[]{:S(2)}) collective-permute-start(bf16[128,2048]{1,0:T(8,128)(2,1)S(1)} %get-tuple-element.40), channel_id=1, source_target_pairs={{0,1},{1,2},{2,3},{3,0},{4,5},{5,6},{6,7},{7,4},{8,9},{9,10},{10,1... | collective-permute-start | bytes 1572872 | tf_op jit(solution)/shard_map/ppermute | solution.py:33
  53.5 12.5 %collective-permute-start.20 = (bf16[128,2048]{1,0:T(8,128)(2,1)S(1)}, bf16[128,2048]{1,0:T(8,128)(2,1)S(1)}, u32[]{:S(2)}, u32[]{:S(2)}) collective-permute-start(bf16[128,2048]{1,0:T(8,128)(2,1)S(1)} %get-tuple-element.40), channel_id=1, source_target_pairs={{0,3},{1,0},{2,1},{3,2},{4,7},{5,4},{6,5},{7,6},{8,11},{9,8},{10,9... | collective-permute-start | bytes 1572872 | tf_op jit(solution)/shard_map/ppermute | solution.py:33
  62.1 7.7 %collective-permute-start.17 = (bf16[64,2048]{1,0:T(8,128)(2,1)S(1)}, bf16[64,2048]{1,0:T(8,128)(2,1)S(1)}, u32[]{:S(2)}, u32[]{:S(2)}) collective-permute-start(bf16[64,2048]{1,0:T(8,128)(2,1)S(1)} %slice.86), channel_id=1, source_target_pairs={{0,4},{1,5},{2,6},{3,7},{4,8},{5,9},{6,10},{7,11},{8,12},{9,13},{1... | collective-permute-start | bytes 786440 | tf_op jit(solution)/shard_map/ppermute | solution.py:33
  62.2 7.6 %collective-permute-start.18 = (bf16[64,2048]{1,0:T(8,128)(2,1)S(1)}, bf16[64,2048]{1,0:T(8,128)(2,1)S(1)}, u32[]{:S(2)}, u32[]{:S(2)}) collective-permute-start(bf16[64,2048]{1,0:T(8,128)(2,1)S(1)} %slice.87), channel_id=1, source_target_pairs={{0,12},{1,13},{2,14},{3,15},{4,0},{5,1},{6,2},{7,3},{8,4},{9,5},{1... | collective-permute-start | bytes 786440 | tf_op jit(solution)/shard_map/ppermute | solution.py:33
  65.5 7.8 %collective-permute-start.21 = (bf16[64,2048]{1,0:T(8,128)(2,1)S(1)}, bf16[64,2048]{1,0:T(8,128)(2,1)S(1)}, u32[]{:S(2)}, u32[]{:S(2)}) collective-permute-start(bf16[64,2048]{1,0:T(8,128)(2,1)S(1)} %slice.88), channel_id=1, source_target_pairs={{0,1},{1,2},{2,3},{3,0},{4,5},{5,6},{6,7},{7,4},{8,9},{9,10},{10,1... | collective-permute-start | bytes 786440 | tf_op jit(solution)/shard_map/ppermute | solution.py:33
  74.7 8.4 %collective-permute-start.24 = (bf16[256,512]{1,0:T(8,128)(2,1)S(1)}, bf16[256,512]{1,0:T(8,128)(2,1)S(1)}, u32[]{:S(2)}, u32[]{:S(2)}) collective-permute-start(bf16[256,512]{1,0:T(8,128)(2,1)S(1)} %tile.3), channel_id=1, source_target_pairs={{0,64},{16,80},{32,96},{48,112},{64,0},{80,16},{96,32},{112,48},{1... | collective-permute-start | bytes 786440 | tf_op jit(solution)/shard_map/ppermute | solution.py:38
  79.3 8.0 %collective-permute-start.23 = (bf16[256,512]{1,0:T(8,128)(2,1)S(1)}, bf16[256,512]{1,0:T(8,128)(2,1)S(1)}, u32[]{:S(2)}, u32[]{:S(2)}) collective-permute-start(bf16[256,512]{1,0:T(8,128)(2,1)S(1)} %tile.2), channel_id=1, source_target_pairs={{0,64},{16,80},{32,96},{48,112},{64,0},{80,16},{96,32},{112,48},{1... | collective-permute-start | bytes 786440 | tf_op jit(solution)/shard_map/ppermute | solution.py:38
  83.1 13.0 %collective-permute-start.25 = (bf16[256,512]{1,0:T(8,128)(2,1)S(1)}, bf16[256,512]{1,0:T(8,128)(2,1)S(1)}, u32[]{:S(2)}, u32[]{:S(2)}) collective-permute-start(bf16[256,512]{1,0:T(8,128)(2,1)S(1)} %collective-permute-done.24), channel_id=1, source_target_pairs={{0,4},{1,5},{2,6},{3,7},{4,8},{5,9},{6,10},{7,11},{8,12},{9,13},{1... | collective-permute-start | bytes 786440 | tf_op jit(solution)/shard_map/ppermute | solution.py:33
  83.1 13.1 %collective-permute-start.26 = (bf16[256,512]{1,0:T(8,128)(2,1)S(1)}, bf16[256,512]{1,0:T(8,128)(2,1)S(1)}, u32[]{:S(2)}, u32[]{:S(2)}) collective-permute-start(bf16[256,512]{1,0:T(8,128)(2,1)S(1)} %collective-permute-done.24), channel_id=1, source_target_pairs={{0,12},{1,13},{2,14},{3,15},{4,0},{5,1},{6,2},{7,3},{8,4},{9,5},{1... | collective-permute-start | bytes 786440 | tf_op jit(solution)/shard_map/ppermute | solution.py:33
  87.2 12.3 %collective-permute-start.34 = (bf16[256,512]{1,0:T(8,128)(2,1)S(1)}, bf16[256,512]{1,0:T(8,128)(2,1)S(1)}, u32[]{:S(2)}, u32[]{:S(2)}) collective-permute-start(bf16[256,512]{1,0:T(8,128)(2,1)S(1)} %collective-permute-done.23), channel_id=1, source_target_pairs={{0,8},{1,9},{2,10},{3,11},{4,12},{5,13},{6,14},{7,15},{8,0},{9,1},... | collective-permute-start | bytes 786440 | tf_op jit(solution)/shard_map/ppermute | solution.py:33
  87.2 12.3 %collective-permute-start.33 = (bf16[256,512]{1,0:T(8,128)(2,1)S(1)}, bf16[256,512]{1,0:T(8,128)(2,1)S(1)}, u32[]{:S(2)}, u32[]{:S(2)}) collective-permute-start(bf16[256,512]{1,0:T(8,128)(2,1)S(1)} %collective-permute-done.23), channel_id=1, source_target_pairs={{0,12},{1,13},{2,14},{3,15},{4,0},{5,1},{6,2},{7,3},{8,4},{9,5},{1... | collective-permute-start | bytes 786440 | tf_op jit(solution)/shard_map/ppermute | solution.py:33
  88.7 11.6 %collective-permute-start.32 = (bf16[256,512]{1,0:T(8,128)(2,1)S(1)}, bf16[256,512]{1,0:T(8,128)(2,1)S(1)}, u32[]{:S(2)}, u32[]{:S(2)}) collective-permute-start(bf16[256,512]{1,0:T(8,128)(2,1)S(1)} %collective-permute-done.23), channel_id=1, source_target_pairs={{0,4},{1,5},{2,6},{3,7},{4,8},{5,9},{6,10},{7,11},{8,12},{9,13},{1... | collective-permute-start | bytes 786440 | tf_op jit(solution)/shard_map/ppermute | solution.py:33
  96.1 9.5 %collective-permute-start.27 = (bf16[128,512]{1,0:T(8,128)(2,1)S(1)}, bf16[128,512]{1,0:T(8,128)(2,1)S(1)}, u32[]{:S(2)}, u32[]{:S(2)}) collective-permute-start(bf16[128,512]{1,0:T(8,128)(2,1)S(1)} %slice.90), channel_id=1, source_target_pairs={{0,4},{1,5},{2,6},{3,7},{4,8},{5,9},{6,10},{7,11},{8,12},{9,13},{1... | collective-permute-start | bytes 393224 | tf_op jit(solution)/shard_map/ppermute | solution.py:33
  96.3 9.4 %collective-permute-start.28 = (bf16[128,512]{1,0:T(8,128)(2,1)S(1)}, bf16[128,512]{1,0:T(8,128)(2,1)S(1)}, u32[]{:S(2)}, u32[]{:S(2)}) collective-permute-start(bf16[128,512]{1,0:T(8,128)(2,1)S(1)} %slice.91), channel_id=1, source_target_pairs={{0,12},{1,13},{2,14},{3,15},{4,0},{5,1},{6,2},{7,3},{8,4},{9,5},{1... | collective-permute-start | bytes 393224 | tf_op jit(solution)/shard_map/ppermute | solution.py:33
  101.2 8.9 %collective-permute-start.35 = (bf16[3,256,128]{2,1,0:T(8,128)(2,1)S(1)}, bf16[3,256,128]{2,1,0:T(8,128)(2,1)S(1)}, u32[]{:S(2)}, u32[]{:S(2)}) collective-permute-start(bf16[3,256,128]{2,1,0:T(8,128)(2,1)S(1)} %get-tuple-element.53), channel_id=1, source_target_pairs={{0,1},{1,2},{2,3},{3,0},{4,5},{5,6},{6,7},{7,4},{8,9},{9,10},{10,1... | collective-permute-start | bytes 589832 | tf_op jit(solution)/shard_map/ppermute | solution.py:33
  101.3 11.0 %collective-permute-start.36 = (bf16[3,256,128]{2,1,0:T(8,128)(2,1)S(1)}, bf16[3,256,128]{2,1,0:T(8,128)(2,1)S(1)}, u32[]{:S(2)}, u32[]{:S(2)}) collective-permute-start(bf16[3,256,128]{2,1,0:T(8,128)(2,1)S(1)} %get-tuple-element.52), channel_id=1, source_target_pairs={{0,2},{1,3},{2,0},{3,1},{4,6},{5,7},{6,4},{7,5},{8,10},{9,11},{10,... | collective-permute-start | bytes 589832 | tf_op jit(solution)/shard_map/ppermute | solution.py:33
  106.4 7.9 %collective-permute-start.29 = (bf16[3,256,128]{2,1,0:T(8,128)(2,1)S(1)}, bf16[3,256,128]{2,1,0:T(8,128)(2,1)S(1)}, u32[]{:S(2)}, u32[]{:S(2)}) collective-permute-start(bf16[3,256,128]{2,1,0:T(8,128)(2,1)S(1)} %get-tuple-element.50), channel_id=1, source_target_pairs={{0,1},{1,2},{2,3},{3,0},{4,5},{5,6},{6,7},{7,4},{8,9},{9,10},{10,1... | collective-permute-start | bytes 589832 | tf_op jit(solution)/shard_map/ppermute | solution.py:33
  108.4 8.0 %collective-permute-start.30 = (bf16[3,256,128]{2,1,0:T(8,128)(2,1)S(1)}, bf16[3,256,128]{2,1,0:T(8,128)(2,1)S(1)}, u32[]{:S(2)}, u32[]{:S(2)}) collective-permute-start(bf16[3,256,128]{2,1,0:T(8,128)(2,1)S(1)} %get-tuple-element.49), channel_id=1, source_target_pairs={{0,2},{1,3},{2,0},{3,1},{4,6},{5,7},{6,4},{7,5},{8,10},{9,11},{10,... | collective-permute-start | bytes 589832 | tf_op jit(solution)/shard_map/ppermute | solution.py:33
  (13 other events, 101.2 us)

commit v8 on v7

--- a/solution.py
+++ b/solution.py
@@ -433,17 +433,24 @@
 def place_kernel(parts, block_map, plan, *refs):
     tiles, (out, staged, sems) = refs[: len(parts)], refs[len(parts) + 1 :]
     _, child, front = family()
-    none = lax.broadcasted_iota(jnp.int32, (BLOCK, BLOCK), 0) * 0
     copies = []
     for (chunk, step), tile in zip(parts, tiles, strict=True):
         z = lax.rem(lax.rem(front, SIDE) - step + SIDE, SIDE)
         for up, row_x in enumerate(chunk):
             here = len(copies)
             for slot in range(SLOTS):
-                value = tile[slot, up * BLOCK : (up + 1) * BLOCK, :].astype(jnp.float32)
-                staged[here, :, slot * BLOCK : (slot + 1) * BLOCK] = jnp.where(
-                    none + plan[FRONT + slot] > 0, value, 0.0
-                )
+                columns = slice(slot * BLOCK, (slot + 1) * BLOCK)
+
+                @pl.when(plan[FRONT + slot] > 0)
+                def _():
+                    staged[here, :, columns] = tile[
+                        slot, up * BLOCK : (up + 1) * BLOCK, :
+                    ].astype(jnp.float32)
+
+                @pl.when(plan[FRONT + slot] <= 0)
+                def _():
+                    staged[here, :, columns] = jnp.zeros((BLOCK, BLOCK), jnp.float32)
+
             row = pl.multiple_of(block_map[child, row_x * SIDE + z] * BLOCK, BLOCK)
             copy = pltpu.make_async_copy(
                 staged.at[here], out.at[pl.ds(row, BLOCK), :], sems.at[here]

time: 118 us -> 119 us (level)
  no operation moved by 1% of the time
where the time goes in v8:
time: 119 us; the launch traced here: 118 us
  starting transfers between devices  59.2 us (50%)
  waiting for transfers between devices  38.3 us (32%)
  Pallas kernels  14.9 us (13%)
  local copies, waits for them, and re-layouts  4.63 us (4%)
  between operations  1.22 us (1%)
    ppermute x36, starting transfers between devices, shift(): return lax.ppermute(value, 'front', pairs)  55.5 us
    ppermute x36, waiting for transfers between devices, shift(): return lax.ppermute(value, 'front', pairs)  34.9 us
    pallas_call x2, Pallas kernels, place_tiles(): pl.pallas_call(functools.partial(place_kernel, list(tiles)), out_shape=PA...  3.73 us
    ppermute x2, starting transfers between devices, to_parent(): lax.ppermute(value, 'leaf', [(g, (g + groups // 2) % groups) for g in ran...  3.69 us
    pallas_call x1, Pallas kernels, blank_rows(): pl.pallas_call(blank_kernel, out_shape=(PARENT, jax.ShapeDtypeStruct((2 *...  3.51 us
    ppermute x2, waiting for transfers between devices, to_parent(): lax.ppermute(value, 'leaf', [(g, (g + groups // 2) % groups) for g in ran...  3.47 us
    unnamed x26, local copies, waits for them, and re-layouts  3.44 us
    pallas_call x1, Pallas kernels, eliminate(): pl.pallas_call(panel_kernel, out_shape=(jax.ShapeDtypeStruct((ROWS, PANEL...  3.34 us
  transfers between devices with their start and end apart: 38, of which 14 were waited for; matrix products, arithmetic and copies ran while one was open for 1% of the time, Pallas kernels for 7%

profile of v8, /device:TPU:0, one launch (start us, length us, event | category | flops | bytes accessed | tf_op | source)
XLA Modules:
  0.0 118.3 jit_solution(7646141028221404343)
XLA Ops:
  0.6 1.6 %collective-permute-start = (bf16[128,1024]{1,0:T(8,128)(2,1)}, bf16[128,1024]{1,0:T(8,128)(2,1)S(1)}, u32[]{:S(2)}, u32[]{:S(2)}) collective-permute-start(bf16[128,1024]{1,0:T(8,128)(2,1)} %bitcast.8), channel_id=1, source_target_pairs={{0,4},{1,5},{2,6},{3,7},{4,8},{5,9},{6,10},{7,11},{8,12},{9,13},{1... | collective-permute-start | bytes 786440 | tf_op jit(solution)/shard_map/ppermute | solution.py:33
  2.3 1.7 %collective-permute-start.1 = (bf16[128,1024]{1,0:T(8,128)(2,1)}, bf16[128,1024]{1,0:T(8,128)(2,1)S(1)}, u32[]{:S(2)}, u32[]{:S(2)}) collective-permute-start(bf16[128,1024]{1,0:T(8,128)(2,1)} %bitcast.9), channel_id=1, source_target_pairs={{0,12},{1,13},{2,14},{3,15},{4,0},{5,1},{6,2},{7,3},{8,4},{9,5},{1... | collective-permute-start | bytes 786440 | tf_op jit(solution)/shard_map/ppermute | solution.py:33
  3.9 2.0 %collective-permute-start.8 = (bf16[64,1024]{1,0:T(8,128)(2,1)}, bf16[64,1024]{1,0:T(8,128)(2,1)S(1)}, u32[]{:S(2)}, u32[]{:S(2)}) collective-permute-start(bf16[64,1024]{1,0:T(8,128)(2,1)} %bitcast.11), channel_id=1, source_target_pairs={{0,1},{1,2},{2,3},{3,0},{4,5},{5,6},{6,7},{7,4},{8,9},{9,10},{10,1... | collective-permute-start | bytes 393224 | tf_op jit(solution)/shard_map/ppermute | solution.py:33
  5.9 2.1 %collective-permute-start.9 = (bf16[64,1024]{1,0:T(8,128)(2,1)}, bf16[64,1024]{1,0:T(8,128)(2,1)S(1)}, u32[]{:S(2)}, u32[]{:S(2)}) collective-permute-start(bf16[64,1024]{1,0:T(8,128)(2,1)} %bitcast.12), channel_id=1, source_target_pairs={{0,3},{1,0},{2,1},{3,2},{4,7},{5,4},{6,5},{7,6},{8,11},{9,8},{10,9... | collective-permute-start | bytes 393224 | tf_op jit(solution)/shard_map/ppermute | solution.py:33
  8.1 1.9 %collective-permute-start.10 = (bf16[64,1024]{1,0:T(8,128)(2,1)}, bf16[64,1024]{1,0:T(8,128)(2,1)S(1)}, u32[]{:S(2)}, u32[]{:S(2)}) collective-permute-start(bf16[64,1024]{1,0:T(8,128)(2,1)} %bitcast.13), channel_id=1, source_target_pairs={{0,2},{1,3},{2,0},{3,1},{4,6},{5,7},{6,4},{7,5},{8,10},{9,11},{10,... | collective-permute-start | bytes 393224 | tf_op jit(solution)/shard_map/ppermute | solution.py:33
  13.3 3.0 %collective-permute-start.3 = (bf16[64,1024]{1,0:T(8,128)(2,1)S(1)}, bf16[64,1024]{1,0:T(8,128)(2,1)S(1)}, u32[]{:S(2)}, u32[]{:S(2)}) collective-permute-start(bf16[64,1024]{1,0:T(8,128)(2,1)S(1)} %slice.64), channel_id=1, source_target_pairs={{0,12},{1,13},{2,14},{3,15},{4,0},{5,1},{6,2},{7,3},{8,4},{9,5},{1... | collective-permute-start | bytes 393224 | tf_op jit(solution)/shard_map/ppermute | solution.py:33
  16.5 3.2 %collective-permute-start.12 = (bf16[352,1024]{1,0:T(8,128)(2,1)S(1)}, bf16[352,1024]{1,0:T(8,128)(2,1)S(1)}, u32[]{:S(2)}, u32[]{:S(2)}) collective-permute-start(bf16[352,1024]{1,0:T(8,128)(2,1)S(1)} %get-tuple-element.37.refs_5_), channel_id=1, source_target_pairs={{0,12},{1,13},{2,14},{3,15},{4,0},{5,1},{6,2},{7,3},{8,4},{9,5},{1... | collective-permute-start | bytes 2162696 | tf_op jit(solution)/shard_map/ppermute | solution.py:33
  21.5 2.1 %collective-permute-start.5 = (bf16[1280,256]{1,0:T(8,128)(2,1)S(1)}, bf16[1280,256]{1,0:T(8,128)(2,1)S(1)}, u32[]{:S(2)}, u32[]{:S(2)}) collective-permute-start(bf16[1280,256]{1,0:T(8,128)(2,1)S(1)} %lower.1.refs_0_), channel_id=1, source_target_pairs={{0,3},{1,0},{2,1},{3,2},{4,7},{5,4},{6,5},{7,6},{8,11},{9,8},{10,9... | collective-permute-start | bytes 1966088 | tf_op jit(solution)/shard_map/ppermute | solution.py:33
  23.7 3.5 %blank.1 = (f32[4096,384]{1,0:T(8,128)}, s32[32]{0:T(128)S(1)}) custom-call(s32[8,16]{1,0:T(8,128)S(1)} %copy-done.3, s32[8,32]{1,0:T(8,128)S(1)} %copy-done.4), custom_call_target="tpu_custom_call" | custom-call | bytes 3145728 | tf_op jit(solution)/shard_map/blank/pallas_call | solution.py:417
  27.2 7.5 %collective-permute-done.11.refs_6_.refs_1_ = bf16[352,1024]{1,0:T(8,128)(2,1)S(1)} collective-permute-done((bf16[352,1024]{1,0:T(8,128)(2,1)S(1)}, bf16[352,1024]{1,0:T(8,128)(2,1)S(1)}, u32[]{:S(2)}, u32[]{:S(2)}) %collective-permute-start.11) | collective-permute-done | bytes 720928 | tf_op jit(solution)/shard_map/ppermute | solution.py:33
  34.8 3.3 %collective-permute-start.14 = (bf16[160,1024]{1,0:T(8,128)(2,1)S(1)}, bf16[160,1024]{1,0:T(8,128)(2,1)S(1)}, u32[]{:S(2)}, u32[]{:S(2)}) collective-permute-start(bf16[160,1024]{1,0:T(8,128)(2,1)S(1)} %slice.85), channel_id=1, source_target_pairs={{0,12},{1,13},{2,14},{3,15},{4,0},{5,1},{6,2},{7,3},{8,4},{9,5},{1... | collective-permute-start | bytes 983048 | tf_op jit(solution)/shard_map/ppermute | solution.py:33
  39.2 2.3 %collective-permute-start.7 = (bf16[640,256]{1,0:T(8,128)(2,1)S(1)}, bf16[640,256]{1,0:T(8,128)(2,1)S(1)}, u32[]{:S(2)}, u32[]{:S(2)}) collective-permute-start(bf16[640,256]{1,0:T(8,128)(2,1)S(1)} %slice.66), channel_id=1, source_target_pairs={{0,3},{1,0},{2,1},{3,2},{4,7},{5,4},{6,5},{7,6},{8,11},{9,8},{10,9... | collective-permute-start | bytes 983048 | tf_op jit(solution)/shard_map/ppermute | solution.py:33
  41.5 2.0 %collective-permute-done.13.refs_8_.refs_3_ = bf16[160,1024]{1,0:T(8,128)(2,1)S(1)} collective-permute-done((bf16[160,1024]{1,0:T(8,128)(2,1)S(1)}, bf16[160,1024]{1,0:T(8,128)(2,1)S(1)}, u32[]{:S(2)}, u32[]{:S(2)}) %collective-permute-start.13) | collective-permute-done | bytes 327712 | tf_op jit(solution)/shard_map/ppermute | solution.py:33
  43.5 3.2 %collective-permute-done.6.refs_3_ = bf16[640,256]{1,0:T(8,128)(2,1)S(1)} collective-permute-done((bf16[640,256]{1,0:T(8,128)(2,1)S(1)}, bf16[640,256]{1,0:T(8,128)(2,1)S(1)}, u32[]{:S(2)}, u32[]{:S(2)}) %collective-permute-start.6) | collective-permute-done | bytes 327712 | tf_op jit(solution)/shard_map/ppermute | solution.py:33
  46.7 3.3 %panels.1 = (bf16[64,1024]{1,0:T(8,128)(2,1)}, bf16[128,2048]{1,0:T(8,128)(2,1)S(1)}) custom-call(bf16[128,2048]{1,0:T(8,128)(2,1)S(1)} %bitcast.15, bf16[1280,256]{1,0:T(8,128)(2,1)S(1)} %lower.1.refs_0_, bf16[1280,256]{1,0:T(8,128)(2,1)S(1)} %collective-permute-done.4.refs_1_, bf16[1280,256]{1,0:T(8,128)(2,1)S(1)} %collective-permute-done.5.refs_2_, ...), custom_call_target="tpu_custom_call" | custom-call | flops 2952790016 | bytes 8388608 | tf_op jit(solution)/shard_map/panels/pallas_call | solution.py:195
  50.1 3.2 %collective-permute-start.16 = (bf16[128,2048]{1,0:T(8,128)(2,1)S(1)}, bf16[128,2048]{1,0:T(8,128)(2,1)S(1)}, u32[]{:S(2)}, u32[]{:S(2)}) collective-permute-start(bf16[128,2048]{1,0:T(8,128)(2,1)S(1)} %get-tuple-element.40), channel_id=1, source_target_pairs={{0,12},{1,13},{2,14},{3,15},{4,0},{5,1},{6,2},{7,3},{8,4},{9,5},{1... | collective-permute-start | bytes 1572872 | tf_op jit(solution)/shard_map/ppermute | solution.py:33
  53.5 3.0 %collective-permute-start.20 = (bf16[128,2048]{1,0:T(8,128)(2,1)S(1)}, bf16[128,2048]{1,0:T(8,128)(2,1)S(1)}, u32[]{:S(2)}, u32[]{:S(2)}) collective-permute-start(bf16[128,2048]{1,0:T(8,128)(2,1)S(1)} %get-tuple-element.40), channel_id=1, source_target_pairs={{0,3},{1,0},{2,1},{3,2},{4,7},{5,4},{6,5},{7,6},{8,11},{9,8},{10,9... | collective-permute-start | bytes 1572872 | tf_op jit(solution)/shard_map/ppermute | solution.py:33
  56.8 5.2 %collective-permute-done.15 = bf16[128,2048]{1,0:T(8,128)(2,1)S(1)} collective-permute-done((bf16[128,2048]{1,0:T(8,128)(2,1)S(1)}, bf16[128,2048]{1,0:T(8,128)(2,1)S(1)}, u32[]{:S(2)}, u32[]{:S(2)}) %collective-permute-start.15) | collective-permute-done | bytes 524320 | tf_op jit(solution)/shard_map/ppermute | solution.py:33
  62.2 3.3 %collective-permute-start.18 = (bf16[64,2048]{1,0:T(8,128)(2,1)S(1)}, bf16[64,2048]{1,0:T(8,128)(2,1)S(1)}, u32[]{:S(2)}, u32[]{:S(2)}) collective-permute-start(bf16[64,2048]{1,0:T(8,128)(2,1)S(1)} %slice.87), channel_id=1, source_target_pairs={{0,12},{1,13},{2,14},{3,15},{4,0},{5,1},{6,2},{7,3},{8,4},{9,5},{1... | collective-permute-start | bytes 786440 | tf_op jit(solution)/shard_map/ppermute | solution.py:33
  66.0 3.1 %collective-permute-start.22 = (bf16[64,2048]{1,0:T(8,128)(2,1)S(1)}, bf16[64,2048]{1,0:T(8,128)(2,1)S(1)}, u32[]{:S(2)}, u32[]{:S(2)}) collective-permute-start(bf16[64,2048]{1,0:T(8,128)(2,1)S(1)} %slice.89), channel_id=1, source_target_pairs={{0,3},{1,0},{2,1},{3,2},{4,7},{5,4},{6,5},{7,6},{8,11},{9,8},{10,9... | collective-permute-start | bytes 786440 | tf_op jit(solution)/shard_map/ppermute | solution.py:33
  69.8 3.5 %collective-permute-done.21 = bf16[64,2048]{1,0:T(8,128)(2,1)S(1)} collective-permute-done((bf16[64,2048]{1,0:T(8,128)(2,1)S(1)}, bf16[64,2048]{1,0:T(8,128)(2,1)S(1)}, u32[]{:S(2)}, u32[]{:S(2)}) %collective-permute-start.21) | collective-permute-done | bytes 262176 | tf_op jit(solution)/shard_map/ppermute | solution.py:33
  74.7 3.3 %collective-permute-start.24 = (bf16[256,512]{1,0:T(8,128)(2,1)S(1)}, bf16[256,512]{1,0:T(8,128)(2,1)S(1)}, u32[]{:S(2)}, u32[]{:S(2)}) collective-permute-start(bf16[256,512]{1,0:T(8,128)(2,1)S(1)} %tile.3), channel_id=1, source_target_pairs={{0,64},{16,80},{32,96},{48,112},{64,0},{80,16},{96,32},{112,48},{1... | collective-permute-start | bytes 786440 | tf_op jit(solution)/shard_map/ppermute | solution.py:38
  80.5 2.6 %collective-permute-done.24 = bf16[256,512]{1,0:T(8,128)(2,1)S(1)} collective-permute-done((bf16[256,512]{1,0:T(8,128)(2,1)S(1)}, bf16[256,512]{1,0:T(8,128)(2,1)S(1)}, u32[]{:S(2)}, u32[]{:S(2)}) %collective-permute-start.24) | collective-permute-done | bytes 262176 | tf_op jit(solution)/shard_map/ppermute | solution.py:38
  83.1 3.2 %collective-permute-start.26 = (bf16[256,512]{1,0:T(8,128)(2,1)S(1)}, bf16[256,512]{1,0:T(8,128)(2,1)S(1)}, u32[]{:S(2)}, u32[]{:S(2)}) collective-permute-start(bf16[256,512]{1,0:T(8,128)(2,1)S(1)} %collective-permute-done.24), channel_id=1, source_target_pairs={{0,12},{1,13},{2,14},{3,15},{4,0},{5,1},{6,2},{7,3},{8,4},{9,5},{1... | collective-permute-start | bytes 786440 | tf_op jit(solution)/shard_map/ppermute | solution.py:33
  89.3 6.9 %collective-permute-done.25 = bf16[256,512]{1,0:T(8,128)(2,1)S(1)} collective-permute-done((bf16[256,512]{1,0:T(8,128)(2,1)S(1)}, bf16[256,512]{1,0:T(8,128)(2,1)S(1)}, u32[]{:S(2)}, u32[]{:S(2)}) %collective-permute-start.25) | collective-permute-done | bytes 262176 | tf_op jit(solution)/shard_map/ppermute | solution.py:33
  96.3 3.3 %collective-permute-start.28 = (bf16[128,512]{1,0:T(8,128)(2,1)S(1)}, bf16[128,512]{1,0:T(8,128)(2,1)S(1)}, u32[]{:S(2)}, u32[]{:S(2)}) collective-permute-start(bf16[128,512]{1,0:T(8,128)(2,1)S(1)} %slice.91), channel_id=1, source_target_pairs={{0,12},{1,13},{2,14},{3,15},{4,0},{5,1},{6,2},{7,3},{8,4},{9,5},{1... | collective-permute-start | bytes 393224 | tf_op jit(solution)/shard_map/ppermute | solution.py:33
  101.3 4.2 %collective-permute-start.36 = (bf16[3,256,128]{2,1,0:T(8,128)(2,1)S(1)}, bf16[3,256,128]{2,1,0:T(8,128)(2,1)S(1)}, u32[]{:S(2)}, u32[]{:S(2)}) collective-permute-start(bf16[3,256,128]{2,1,0:T(8,128)(2,1)S(1)} %get-tuple-element.52), channel_id=1, source_target_pairs={{0,2},{1,3},{2,0},{3,1},{4,6},{5,7},{6,4},{7,5},{8,10},{9,11},{10,... | collective-permute-start | bytes 589832 | tf_op jit(solution)/shard_map/ppermute | solution.py:33
  106.4 2.0 %collective-permute-start.29 = (bf16[3,256,128]{2,1,0:T(8,128)(2,1)S(1)}, bf16[3,256,128]{2,1,0:T(8,128)(2,1)S(1)}, u32[]{:S(2)}, u32[]{:S(2)}) collective-permute-start(bf16[3,256,128]{2,1,0:T(8,128)(2,1)S(1)} %get-tuple-element.50), channel_id=1, source_target_pairs={{0,1},{1,2},{2,3},{3,0},{4,5},{5,6},{6,7},{7,4},{8,9},{9,10},{10,1... | collective-permute-start | bytes 589832 | tf_op jit(solution)/shard_map/ppermute | solution.py:33
  108.5 1.6 %collective-permute-done.35.refs_1_ = bf16[3,256,128]{2,1,0:T(8,128)(2,1)S(1)} collective-permute-done((bf16[3,256,128]{2,1,0:T(8,128)(2,1)S(1)}, bf16[3,256,128]{2,1,0:T(8,128)(2,1)S(1)}, u32[]{:S(2)}, u32[]{:S(2)}) %collective-permute-start.35) | collective-permute-done | bytes 196640 | tf_op jit(solution)/shard_map/ppermute | solution.py:33
  112.3 2.0 %place.2.refs_3_ = f32[4096,384]{1,0:T(8,128)} custom-call(s32[8,16]{1,0:T(8,128)S(1)} %copy-done.3, s32[32]{0:T(128)S(1)} %get-tuple-element.44.plan, bf16[3,256,128]{2,1,0:T(8,128)(2,1)S(1)} %get-tuple-element.54.refs_0_, bf16[3,256,128]{2,1,0:T(8,128)(2,1)S(1)} %collective-permute-done.35.refs_1_, ...), custom_call_target="tpu_custom_call", output_to_operand_aliasing={{}: (7, {})} | custom-call | bytes 1048576 | tf_op jit(solution)/shard_map/place/pallas_call | solution.py:466
  114.3 2.1 %collective-permute-done.30.refs_1_ = bf16[3,256,128]{2,1,0:T(8,128)(2,1)S(1)} collective-permute-done((bf16[3,256,128]{2,1,0:T(8,128)(2,1)S(1)}, bf16[3,256,128]{2,1,0:T(8,128)(2,1)S(1)}, u32[]{:S(2)}, u32[]{:S(2)}) %collective-permute-start.30) | collective-permute-done | bytes 196640 | tf_op jit(solution)/shard_map/ppermute | solution.py:33
  116.4 1.7 %place.3 = f32[4096,384]{1,0:T(8,128)} custom-call(s32[8,16]{1,0:T(8,128)S(1)} %copy-done.3, s32[32]{0:T(128)S(1)} %get-tuple-element.44.plan, bf16[3,256,128]{2,1,0:T(8,128)(2,1)S(1)} %collective-permute-done.29.refs_0_, bf16[3,256,128]{2,1,0:T(8,128)(2,1)S(1)} %collective-permute-done.30.refs_1_, ...), custom_call_target="tpu_custom_call", output_to_operand_aliasing={{}: (5, {})} | custom-call | bytes 1048576 | tf_op jit(solution)/shard_map/place/pallas_call | solution.py:466
  (100 shorter events, 20.1 us)
Async XLA Ops:
  0.6 12.3 %collective-permute-start = (bf16[128,1024]{1,0:T(8,128)(2,1)}, bf16[128,1024]{1,0:T(8,128)(2,1)S(1)}, u32[]{:S(2)}, u32[]{:S(2)}) collective-permute-start(bf16[128,1024]{1,0:T(8,128)(2,1)} %bitcast.8), channel_id=1, source_target_pairs={{0,4},{1,5},{2,6},{3,7},{4,8},{5,9},{6,10},{7,11},{8,12},{9,13},{1... | collective-permute-start | bytes 786440 | tf_op jit(solution)/shard_map/ppermute | solution.py:33
  2.3 10.6 %collective-permute-start.1 = (bf16[128,1024]{1,0:T(8,128)(2,1)}, bf16[128,1024]{1,0:T(8,128)(2,1)S(1)}, u32[]{:S(2)}, u32[]{:S(2)}) collective-permute-start(bf16[128,1024]{1,0:T(8,128)(2,1)} %bitcast.9), channel_id=1, source_target_pairs={{0,12},{1,13},{2,14},{3,15},{4,0},{5,1},{6,2},{7,3},{8,4},{9,5},{1... | collective-permute-start | bytes 786440 | tf_op jit(solution)/shard_map/ppermute | solution.py:33
  3.9 12.4 %collective-permute-start.8 = (bf16[64,1024]{1,0:T(8,128)(2,1)}, bf16[64,1024]{1,0:T(8,128)(2,1)S(1)}, u32[]{:S(2)}, u32[]{:S(2)}) collective-permute-start(bf16[64,1024]{1,0:T(8,128)(2,1)} %bitcast.11), channel_id=1, source_target_pairs={{0,1},{1,2},{2,3},{3,0},{4,5},{5,6},{6,7},{7,4},{8,9},{9,10},{10,1... | collective-permute-start | bytes 393224 | tf_op jit(solution)/shard_map/ppermute | solution.py:33
  5.9 10.4 %collective-permute-start.9 = (bf16[64,1024]{1,0:T(8,128)(2,1)}, bf16[64,1024]{1,0:T(8,128)(2,1)S(1)}, u32[]{:S(2)}, u32[]{:S(2)}) collective-permute-start(bf16[64,1024]{1,0:T(8,128)(2,1)} %bitcast.12), channel_id=1, source_target_pairs={{0,3},{1,0},{2,1},{3,2},{4,7},{5,4},{6,5},{7,6},{8,11},{9,8},{10,9... | collective-permute-start | bytes 393224 | tf_op jit(solution)/shard_map/ppermute | solution.py:33
  8.1 8.3 %collective-permute-start.10 = (bf16[64,1024]{1,0:T(8,128)(2,1)}, bf16[64,1024]{1,0:T(8,128)(2,1)S(1)}, u32[]{:S(2)}, u32[]{:S(2)}) collective-permute-start(bf16[64,1024]{1,0:T(8,128)(2,1)} %bitcast.13), channel_id=1, source_target_pairs={{0,2},{1,3},{2,0},{3,1},{4,6},{5,7},{6,4},{7,5},{8,10},{9,11},{10,... | collective-permute-start | bytes 393224 | tf_op jit(solution)/shard_map/ppermute | solution.py:33
  16.4 18.2 %collective-permute-start.11 = (bf16[352,1024]{1,0:T(8,128)(2,1)S(1)}, bf16[352,1024]{1,0:T(8,128)(2,1)S(1)}, u32[]{:S(2)}, u32[]{:S(2)}) collective-permute-start(bf16[352,1024]{1,0:T(8,128)(2,1)S(1)} %get-tuple-element.38), channel_id=1, source_target_pairs={{0,4},{1,5},{2,6},{3,7},{4,8},{5,9},{6,10},{7,11},{8,12},{9,13},{1... | collective-permute-start | bytes 2162696 | tf_op jit(solution)/shard_map/ppermute | solution.py:33
  16.5 18.2 %collective-permute-start.12 = (bf16[352,1024]{1,0:T(8,128)(2,1)S(1)}, bf16[352,1024]{1,0:T(8,128)(2,1)S(1)}, u32[]{:S(2)}, u32[]{:S(2)}) collective-permute-start(bf16[352,1024]{1,0:T(8,128)(2,1)S(1)} %get-tuple-element.37.refs_5_), channel_id=1, source_target_pairs={{0,12},{1,13},{2,14},{3,15},{4,0},{5,1},{6,2},{7,3},{8,4},{9,5},{1... | collective-permute-start | bytes 2162696 | tf_op jit(solution)/shard_map/ppermute | solution.py:33
  20.3 17.7 %collective-permute-start.4 = (bf16[1280,256]{1,0:T(8,128)(2,1)S(1)}, bf16[1280,256]{1,0:T(8,128)(2,1)S(1)}, u32[]{:S(2)}, u32[]{:S(2)}) collective-permute-start(bf16[1280,256]{1,0:T(8,128)(2,1)S(1)} %lower.1.refs_0_), channel_id=1, source_target_pairs={{0,1},{1,2},{2,3},{3,0},{4,5},{5,6},{6,7},{7,4},{8,9},{9,10},{10,1... | collective-permute-start | bytes 1966088 | tf_op jit(solution)/shard_map/ppermute | solution.py:33
  21.5 16.5 %collective-permute-start.5 = (bf16[1280,256]{1,0:T(8,128)(2,1)S(1)}, bf16[1280,256]{1,0:T(8,128)(2,1)S(1)}, u32[]{:S(2)}, u32[]{:S(2)}) collective-permute-start(bf16[1280,256]{1,0:T(8,128)(2,1)S(1)} %lower.1.refs_0_), channel_id=1, source_target_pairs={{0,3},{1,0},{2,1},{3,2},{4,7},{5,4},{6,5},{7,6},{8,11},{9,8},{10,9... | collective-permute-start | bytes 1966088 | tf_op jit(solution)/shard_map/ppermute | solution.py:33
  34.7 8.8 %collective-permute-start.13 = (bf16[160,1024]{1,0:T(8,128)(2,1)S(1)}, bf16[160,1024]{1,0:T(8,128)(2,1)S(1)}, u32[]{:S(2)}, u32[]{:S(2)}) collective-permute-start(bf16[160,1024]{1,0:T(8,128)(2,1)S(1)} %slice.84), channel_id=1, source_target_pairs={{0,4},{1,5},{2,6},{3,7},{4,8},{5,9},{6,10},{7,11},{8,12},{9,13},{1... | collective-permute-start | bytes 983048 | tf_op jit(solution)/shard_map/ppermute | solution.py:33
  34.8 8.7 %collective-permute-start.14 = (bf16[160,1024]{1,0:T(8,128)(2,1)S(1)}, bf16[160,1024]{1,0:T(8,128)(2,1)S(1)}, u32[]{:S(2)}, u32[]{:S(2)}) collective-permute-start(bf16[160,1024]{1,0:T(8,128)(2,1)S(1)} %slice.85), channel_id=1, source_target_pairs={{0,12},{1,13},{2,14},{3,15},{4,0},{5,1},{6,2},{7,3},{8,4},{9,5},{1... | collective-permute-start | bytes 983048 | tf_op jit(solution)/shard_map/ppermute | solution.py:33
  38.1 8.6 %collective-permute-start.6 = (bf16[640,256]{1,0:T(8,128)(2,1)S(1)}, bf16[640,256]{1,0:T(8,128)(2,1)S(1)}, u32[]{:S(2)}, u32[]{:S(2)}) collective-permute-start(bf16[640,256]{1,0:T(8,128)(2,1)S(1)} %slice.65), channel_id=1, source_target_pairs={{0,1},{1,2},{2,3},{3,0},{4,5},{5,6},{6,7},{7,4},{8,9},{9,10},{10,1... | collective-permute-start | bytes 983048 | tf_op jit(solution)/shard_map/ppermute | solution.py:33
  50.1 12.0 %collective-permute-start.15 = (bf16[128,2048]{1,0:T(8,128)(2,1)S(1)}, bf16[128,2048]{1,0:T(8,128)(2,1)S(1)}, u32[]{:S(2)}, u32[]{:S(2)}) collective-permute-start(bf16[128,2048]{1,0:T(8,128)(2,1)S(1)} %get-tuple-element.40), channel_id=1, source_target_pairs={{0,4},{1,5},{2,6},{3,7},{4,8},{5,9},{6,10},{7,11},{8,12},{9,13},{1... | collective-permute-start | bytes 1572872 | tf_op jit(solution)/shard_map/ppermute | solution.py:33
  50.1 12.1 %collective-permute-start.16 = (bf16[128,2048]{1,0:T(8,128)(2,1)S(1)}, bf16[128,2048]{1,0:T(8,128)(2,1)S(1)}, u32[]{:S(2)}, u32[]{:S(2)}) collective-permute-start(bf16[128,2048]{1,0:T(8,128)(2,1)S(1)} %get-tuple-element.40), channel_id=1, source_target_pairs={{0,12},{1,13},{2,14},{3,15},{4,0},{5,1},{6,2},{7,3},{8,4},{9,5},{1... | collective-permute-start | bytes 1572872 | tf_op jit(solution)/shard_map/ppermute | solution.py:33
  53.3 12.2 %collective-permute-start.19 = (bf16[128,2048]{1,0:T(8,128)(2,1)S(1)}, bf16[128,2048]{1,0:T(8,128)(2,1)S(1)}, u32[]{:S(2)}, u32[]{:S(2)}) collective-permute-start(bf16[128,2048]{1,0:T(8,128)(2,1)S(1)} %get-tuple-element.40), channel_id=1, source_target_pairs={{0,1},{1,2},{2,3},{3,0},{4,5},{5,6},{6,7},{7,4},{8,9},{9,10},{10,1... | collective-permute-start | bytes 1572872 | tf_op jit(solution)/shard_map/ppermute | solution.py:33
  53.5 12.5 %collective-permute-start.20 = (bf16[128,2048]{1,0:T(8,128)(2,1)S(1)}, bf16[128,2048]{1,0:T(8,128)(2,1)S(1)}, u32[]{:S(2)}, u32[]{:S(2)}) collective-permute-start(bf16[128,2048]{1,0:T(8,128)(2,1)S(1)} %get-tuple-element.40), channel_id=1, source_target_pairs={{0,3},{1,0},{2,1},{3,2},{4,7},{5,4},{6,5},{7,6},{8,11},{9,8},{10,9... | collective-permute-start | bytes 1572872 | tf_op jit(solution)/shard_map/ppermute | solution.py:33
  62.1 7.7 %collective-permute-start.17 = (bf16[64,2048]{1,0:T(8,128)(2,1)S(1)}, bf16[64,2048]{1,0:T(8,128)(2,1)S(1)}, u32[]{:S(2)}, u32[]{:S(2)}) collective-permute-start(bf16[64,2048]{1,0:T(8,128)(2,1)S(1)} %slice.86), channel_id=1, source_target_pairs={{0,4},{1,5},{2,6},{3,7},{4,8},{5,9},{6,10},{7,11},{8,12},{9,13},{1... | collective-permute-start | bytes 786440 | tf_op jit(solution)/shard_map/ppermute | solution.py:33
  62.2 7.6 %collective-permute-start.18 = (bf16[64,2048]{1,0:T(8,128)(2,1)S(1)}, bf16[64,2048]{1,0:T(8,128)(2,1)S(1)}, u32[]{:S(2)}, u32[]{:S(2)}) collective-permute-start(bf16[64,2048]{1,0:T(8,128)(2,1)S(1)} %slice.87), channel_id=1, source_target_pairs={{0,12},{1,13},{2,14},{3,15},{4,0},{5,1},{6,2},{7,3},{8,4},{9,5},{1... | collective-permute-start | bytes 786440 | tf_op jit(solution)/shard_map/ppermute | solution.py:33
  65.5 7.8 %collective-permute-start.21 = (bf16[64,2048]{1,0:T(8,128)(2,1)S(1)}, bf16[64,2048]{1,0:T(8,128)(2,1)S(1)}, u32[]{:S(2)}, u32[]{:S(2)}) collective-permute-start(bf16[64,2048]{1,0:T(8,128)(2,1)S(1)} %slice.88), channel_id=1, source_target_pairs={{0,1},{1,2},{2,3},{3,0},{4,5},{5,6},{6,7},{7,4},{8,9},{9,10},{10,1... | collective-permute-start | bytes 786440 | tf_op jit(solution)/shard_map/ppermute | solution.py:33
  74.7 8.4 %collective-permute-start.24 = (bf16[256,512]{1,0:T(8,128)(2,1)S(1)}, bf16[256,512]{1,0:T(8,128)(2,1)S(1)}, u32[]{:S(2)}, u32[]{:S(2)}) collective-permute-start(bf16[256,512]{1,0:T(8,128)(2,1)S(1)} %tile.3), channel_id=1, source_target_pairs={{0,64},{16,80},{32,96},{48,112},{64,0},{80,16},{96,32},{112,48},{1... | collective-permute-start | bytes 786440 | tf_op jit(solution)/shard_map/ppermute | solution.py:38
  79.3 8.0 %collective-permute-start.23 = (bf16[256,512]{1,0:T(8,128)(2,1)S(1)}, bf16[256,512]{1,0:T(8,128)(2,1)S(1)}, u32[]{:S(2)}, u32[]{:S(2)}) collective-permute-start(bf16[256,512]{1,0:T(8,128)(2,1)S(1)} %tile.2), channel_id=1, source_target_pairs={{0,64},{16,80},{32,96},{48,112},{64,0},{80,16},{96,32},{112,48},{1... | collective-permute-start | bytes 786440 | tf_op jit(solution)/shard_map/ppermute | solution.py:38
  83.1 13.0 %collective-permute-start.25 = (bf16[256,512]{1,0:T(8,128)(2,1)S(1)}, bf16[256,512]{1,0:T(8,128)(2,1)S(1)}, u32[]{:S(2)}, u32[]{:S(2)}) collective-permute-start(bf16[256,512]{1,0:T(8,128)(2,1)S(1)} %collective-permute-done.24), channel_id=1, source_target_pairs={{0,4},{1,5},{2,6},{3,7},{4,8},{5,9},{6,10},{7,11},{8,12},{9,13},{1... | collective-permute-start | bytes 786440 | tf_op jit(solution)/shard_map/ppermute | solution.py:33
  83.1 13.1 %collective-permute-start.26 = (bf16[256,512]{1,0:T(8,128)(2,1)S(1)}, bf16[256,512]{1,0:T(8,128)(2,1)S(1)}, u32[]{:S(2)}, u32[]{:S(2)}) collective-permute-start(bf16[256,512]{1,0:T(8,128)(2,1)S(1)} %collective-permute-done.24), channel_id=1, source_target_pairs={{0,12},{1,13},{2,14},{3,15},{4,0},{5,1},{6,2},{7,3},{8,4},{9,5},{1... | collective-permute-start | bytes 786440 | tf_op jit(solution)/shard_map/ppermute | solution.py:33
  87.2 12.3 %collective-permute-start.34 = (bf16[256,512]{1,0:T(8,128)(2,1)S(1)}, bf16[256,512]{1,0:T(8,128)(2,1)S(1)}, u32[]{:S(2)}, u32[]{:S(2)}) collective-permute-start(bf16[256,512]{1,0:T(8,128)(2,1)S(1)} %collective-permute-done.23), channel_id=1, source_target_pairs={{0,8},{1,9},{2,10},{3,11},{4,12},{5,13},{6,14},{7,15},{8,0},{9,1},... | collective-permute-start | bytes 786440 | tf_op jit(solution)/shard_map/ppermute | solution.py:33
  87.2 12.3 %collective-permute-start.33 = (bf16[256,512]{1,0:T(8,128)(2,1)S(1)}, bf16[256,512]{1,0:T(8,128)(2,1)S(1)}, u32[]{:S(2)}, u32[]{:S(2)}) collective-permute-start(bf16[256,512]{1,0:T(8,128)(2,1)S(1)} %collective-permute-done.23), channel_id=1, source_target_pairs={{0,12},{1,13},{2,14},{3,15},{4,0},{5,1},{6,2},{7,3},{8,4},{9,5},{1... | collective-permute-start | bytes 786440 | tf_op jit(solution)/shard_map/ppermute | solution.py:33
  88.7 11.6 %collective-permute-start.32 = (bf16[256,512]{1,0:T(8,128)(2,1)S(1)}, bf16[256,512]{1,0:T(8,128)(2,1)S(1)}, u32[]{:S(2)}, u32[]{:S(2)}) collective-permute-start(bf16[256,512]{1,0:T(8,128)(2,1)S(1)} %collective-permute-done.23), channel_id=1, source_target_pairs={{0,4},{1,5},{2,6},{3,7},{4,8},{5,9},{6,10},{7,11},{8,12},{9,13},{1... | collective-permute-start | bytes 786440 | tf_op jit(solution)/shard_map/ppermute | solution.py:33
  96.1 9.5 %collective-permute-start.27 = (bf16[128,512]{1,0:T(8,128)(2,1)S(1)}, bf16[128,512]{1,0:T(8,128)(2,1)S(1)}, u32[]{:S(2)}, u32[]{:S(2)}) collective-permute-start(bf16[128,512]{1,0:T(8,128)(2,1)S(1)} %slice.90), channel_id=1, source_target_pairs={{0,4},{1,5},{2,6},{3,7},{4,8},{5,9},{6,10},{7,11},{8,12},{9,13},{1... | collective-permute-start | bytes 393224 | tf_op jit(solution)/shard_map/ppermute | solution.py:33
  96.3 9.4 %collective-permute-start.28 = (bf16[128,512]{1,0:T(8,128)(2,1)S(1)}, bf16[128,512]{1,0:T(8,128)(2,1)S(1)}, u32[]{:S(2)}, u32[]{:S(2)}) collective-permute-start(bf16[128,512]{1,0:T(8,128)(2,1)S(1)} %slice.91), channel_id=1, source_target_pairs={{0,12},{1,13},{2,14},{3,15},{4,0},{5,1},{6,2},{7,3},{8,4},{9,5},{1... | collective-permute-start | bytes 393224 | tf_op jit(solution)/shard_map/ppermute | solution.py:33
  101.2 8.9 %collective-permute-start.35 = (bf16[3,256,128]{2,1,0:T(8,128)(2,1)S(1)}, bf16[3,256,128]{2,1,0:T(8,128)(2,1)S(1)}, u32[]{:S(2)}, u32[]{:S(2)}) collective-permute-start(bf16[3,256,128]{2,1,0:T(8,128)(2,1)S(1)} %get-tuple-element.53), channel_id=1, source_target_pairs={{0,1},{1,2},{2,3},{3,0},{4,5},{5,6},{6,7},{7,4},{8,9},{9,10},{10,1... | collective-permute-start | bytes 589832 | tf_op jit(solution)/shard_map/ppermute | solution.py:33
  101.3 11.0 %collective-permute-start.36 = (bf16[3,256,128]{2,1,0:T(8,128)(2,1)S(1)}, bf16[3,256,128]{2,1,0:T(8,128)(2,1)S(1)}, u32[]{:S(2)}, u32[]{:S(2)}) collective-permute-start(bf16[3,256,128]{2,1,0:T(8,128)(2,1)S(1)} %get-tuple-element.52), channel_id=1, source_target_pairs={{0,2},{1,3},{2,0},{3,1},{4,6},{5,7},{6,4},{7,5},{8,10},{9,11},{10,... | collective-permute-start | bytes 589832 | tf_op jit(solution)/shard_map/ppermute | solution.py:33
  106.4 7.9 %collective-permute-start.29 = (bf16[3,256,128]{2,1,0:T(8,128)(2,1)S(1)}, bf16[3,256,128]{2,1,0:T(8,128)(2,1)S(1)}, u32[]{:S(2)}, u32[]{:S(2)}) collective-permute-start(bf16[3,256,128]{2,1,0:T(8,128)(2,1)S(1)} %get-tuple-element.50), channel_id=1, source_target_pairs={{0,1},{1,2},{2,3},{3,0},{4,5},{5,6},{6,7},{7,4},{8,9},{9,10},{10,1... | collective-permute-start | bytes 589832 | tf_op jit(solution)/shard_map/ppermute | solution.py:33
  108.4 8.0 %collective-permute-start.30 = (bf16[3,256,128]{2,1,0:T(8,128)(2,1)S(1)}, bf16[3,256,128]{2,1,0:T(8,128)(2,1)S(1)}, u32[]{:S(2)}, u32[]{:S(2)}) collective-permute-start(bf16[3,256,128]{2,1,0:T(8,128)(2,1)S(1)} %get-tuple-element.49), channel_id=1, source_target_pairs={{0,2},{1,3},{2,0},{3,1},{4,6},{5,7},{6,4},{7,5},{8,10},{9,11},{10,... | collective-permute-start | bytes 589832 | tf_op jit(solution)/shard_map/ppermute | solution.py:33
  (13 other events, 101.1 us)
